TPU v7x, 32 devices: a whole 2x2x4 slice. The times are simulated.
32 devices in a mesh: dp: 8 (over z, y), seq: 4 (over x, core).
Axes of the slice: x: 2, y: 2, z: 4, core: 2. Of those that a mesh axis runs over, the one named last changes fastest.
Arguments:
- tokens: bfloat16 [8, 1024, 896], P('dp', 'seq'), may hold values from -6 to 6
- cotangent: bfloat16 [8, 1024, 896], P('dp', 'seq'), may hold values from -6 to 6
- span_order: int32 [8, 4], P('dp'), may hold values from 0 to 3, each once within a row
- attn_gain: bfloat16 [2, 896], P(None, ('dp', 'seq')), may hold values from 0.099609375 to 1.8984375
- joined_weight: bfloat16 [2, 896, 1152], P(None, ('dp', 'seq')), may hold values from -0.1875 to 0.1875
- joined_bias: bfloat16 [2, 1152], P(None, ('dp', 'seq')), may hold values from -3 to 3
- out_weight: bfloat16 [2, 896, 896], P(None, ('dp', 'seq')), may hold values from -1 to 1
- mlp_gain: bfloat16 [2, 896], P(None, ('dp', 'seq')), may hold values from 0.099609375 to 1.8984375
- gate_up_weight: bfloat16 [2, 896, 9728], P(None, ('dp', 'seq')), may hold values from -0.1875 to 0.1875
- down_weight: bfloat16 [2, 4864, 896], P(None, ('dp', 'seq')), may hold values from -0.125 to 0.125
Outputs:
- activations: bfloat16 [8, 1024, 896], P('dp', 'seq')
- input_grad: float32 [8, 1024, 896], P('dp', 'seq')
- attn_gain_grad: float32 [2, 896], P(None, ('dp', 'seq'))
- joined_weight_grad: float32 [2, 896, 1152], P(None, ('dp', 'seq'))
- joined_bias_grad: float32 [2, 1024], P(None, ('dp', 'seq'))
- value_bias_grad: float32 [2, 128], P(None, ('dp', 'seq'))
- out_weight_grad: float32 [2, 896, 896], P(None, ('dp', 'seq'))
- mlp_gain_grad: float32 [2, 896], P(None, ('dp', 'seq'))
- gate_up_grad: float32 [2, 896, 9728], P(None, ('dp', 'seq'))
- down_grad: float32 [2, 4864, 896], P(None, ('dp', 'seq'))
Inputs may be any that keep to these rules, and one draw needn't show every extreme that they name: Each row of span_order holds every number below 4 once.
All inputs are finite; a program needn't handle non-finite values.
Results may differ from a plain program's by a relative error of at most 0.023.
Values may be sent and summed in bfloat16 or wider, within the bound.
No kernel may reach another device: no remote copies, remote signals or barrier semaphores. Data moves between devices by JAX's collectives and lax.ppermute only.
A program may use at most 256 MiB of HBM per device.

v0:
```python
import jax
import jax.numpy as jnp
from jax import lax
from jax.sharding import PartitionSpec as P

D = 896
HEADS = 14
KV_HEADS = 2
HEAD = 64
LAYERS = 2


EPS = 1e-06
THETA = 1000000.0
NEGATIVE = -1e30


def token_places(order_cols, span_len, num_devices):
    inside = jnp.arange(2 * span_len, dtype=jnp.int32)
    lower_part = inside < span_len
    offsets = jnp.where(lower_part, inside, inside - span_len)
    picked = jnp.where(
        lower_part[None, None, :],
        order_cols[..., None],
        2 * num_devices - 1 - order_cols[..., None],
    )
    return (picked * span_len + offsets[None, None, :]).reshape(order_cols.shape[0], -1)


def rotary_tables(positions):
    half_head = HEAD // 2
    frequency = THETA ** (-2.0 * jnp.arange(half_head, dtype=jnp.float32) / HEAD)
    angles = positions.astype(jnp.float32)[..., None] * frequency
    return (jnp.cos(angles), jnp.sin(angles))


def rotate(values_in, cos_table, sin_table):
    half_head = HEAD // 2
    upper_half = values_in[..., :half_head]
    lower_half = values_in[..., half_head:]
    cos_part = cos_table[..., None, :]
    sin_part = sin_table[..., None, :]
    return jnp.concatenate(
        [
            upper_half * cos_part - lower_half * sin_part,
            lower_half * cos_part + upper_half * sin_part,
        ],
        axis=-1,
    )


def norm_forward(residual, gain_row):
    inv_root = lax.rsqrt(jnp.mean(residual * residual, axis=-1, keepdims=True) + EPS)
    return (inv_root, (residual * inv_root * gain_row.astype(jnp.float32)).astype(jnp.bfloat16))


def norm_backward(residual, inv_root, gain_row, upstream):
    normal = residual * inv_root
    weighted = upstream * gain_row.astype(jnp.float32)
    gain_grad = jnp.sum(upstream * normal, axis=0)
    inner_sum = jnp.mean(weighted * normal, axis=-1, keepdims=True)
    return (gain_grad, inv_root * (weighted - normal * inner_sum))


def head_slices(queries, keys_all, kv_index, group_size):
    head_query = queries[:, :, kv_index * group_size : (kv_index + 1) * group_size, :]
    head_key = keys_all[:, :, kv_index * HEAD : (kv_index + 1) * HEAD]
    value_start = (KV_HEADS + kv_index) * HEAD
    head_value = keys_all[:, :, value_start : value_start + HEAD]
    return (head_query, head_key, head_value)


def masked_scores(head_query, head_key, allowed, score_scale):
    scores = (
        jnp.einsum("sqgd,std->sgqt", head_query, head_key, preferred_element_type=jnp.float32)
        * score_scale
    )
    return jnp.where(allowed[:, None], scores, NEGATIVE)


def attend_forward(queries, keys_all, allowed, kv_index, group_size, score_scale):
    head_query, head_key, head_value = head_slices(queries, keys_all, kv_index, group_size)
    scores = masked_scores(head_query, head_key, allowed, score_scale)
    highest = jnp.max(scores, axis=-1, keepdims=True)
    exponent = jnp.exp(scores - highest)
    row_sum = jnp.sum(exponent, axis=-1, keepdims=True)
    prob_low = (exponent / row_sum).astype(jnp.bfloat16)
    mixed_part = jnp.einsum(
        "sgqt,std->sqgd", prob_low, head_value, preferred_element_type=jnp.float32
    )
    return (mixed_part, highest + jnp.log(row_sum))


def attend_backward(
    queries, keys_all, allowed, log_sum, grad_mixed, kv_index, group_size, score_scale
):
    head_query, head_key, head_value = head_slices(queries, keys_all, kv_index, group_size)
    scores = masked_scores(head_query, head_key, allowed, score_scale)
    prob_full = jnp.exp(scores - log_sum)
    prob_low = prob_full.astype(jnp.bfloat16)
    head_grad = grad_mixed[:, :, kv_index * group_size : (kv_index + 1) * group_size, :]
    grad_probs = jnp.einsum(
        "sqgd,std->sgqt", head_grad, head_value, preferred_element_type=jnp.float32
    )
    inner_sum = jnp.sum(grad_probs * prob_full, axis=-1, keepdims=True)
    grad_scores = (prob_full * (grad_probs - inner_sum)).astype(jnp.bfloat16)
    grad_value = jnp.einsum(
        "sgqt,sqgd->std", prob_low, head_grad, preferred_element_type=jnp.float32
    )
    grad_query = (
        jnp.einsum("sgqt,std->sqgd", grad_scores, head_key, preferred_element_type=jnp.float32)
        * score_scale
    )
    grad_key = (
        jnp.einsum("sgqt,sqgd->std", grad_scores, head_query, preferred_element_type=jnp.float32)
        * score_scale
    )
    return (grad_query, grad_key, grad_value)


def body(
    tokens,
    cotangent,
    span_order,
    attn_gain,
    joined_weight,
    joined_bias,
    out_weight,
    mlp_gain,
    gate_up_weight,
    down_weight,
):
    seq_count, tok_len, model_width = tokens.shape
    row_count = seq_count * tok_len
    span_len = tok_len // 2
    group_size = HEADS // KV_HEADS
    score_scale = HEAD ** (-0.5)
    kv_width = KV_HEADS * HEAD
    split_col = D + kv_width
    seq_place = lax.axis_index("seq")
    key_places = token_places(span_order, span_len, lax.axis_size("seq"))
    own_order = lax.dynamic_slice_in_dim(span_order, seq_place, 1, 1)
    query_places = token_places(own_order, span_len, lax.axis_size("seq"))
    allowed = query_places[:, :, None] >= key_places[:, None, :]
    cos_table, sin_table = rotary_tables(query_places)
    group_count = lax.axis_size("dp")
    seq_devices = lax.axis_size("seq")
    unit_rows = down_weight.shape[1]
    width_rows = gate_up_weight.shape[1]

    def group_rows(values):
        gathered = lax.all_gather(
            values.reshape(seq_count, tok_len, values.shape[-1]), "seq", axis=1, tiled=True
        )
        return gathered.reshape(-1, values.shape[-1])

    def group_sums(values):
        summed = lax.psum_scatter(
            values.reshape(seq_count, -1, model_width).astype(jnp.bfloat16),
            "seq",
            scatter_dimension=1,
            tiled=True,
        ).astype(jnp.float32)
        return summed.reshape(row_count, model_width)

    residual = tokens.astype(jnp.float32).reshape(row_count, model_width)
    kept_state = []
    for layer_index in range(LAYERS):
        attn_set = (
            lax.all_gather(attn_gain[layer_index], ("dp", "seq"), axis=0, tiled=True),
            lax.all_gather(joined_weight[layer_index], ("dp", "seq"), axis=0, tiled=True),
            lax.all_gather(joined_bias[layer_index], ("dp", "seq"), axis=0, tiled=True),
            lax.all_gather(out_weight[layer_index], ("dp", "seq"), axis=0, tiled=True),
        )
        gain_full, joined_full, bias_full, out_full = attn_set
        inv_one, normed = norm_forward(residual, gain_full)
        joined_proj = jnp.dot(
            normed, joined_full, preferred_element_type=jnp.float32
        ) + bias_full.astype(jnp.float32)
        queries = rotate(
            joined_proj[:, :D].reshape(seq_count, tok_len, HEADS, HEAD), cos_table, sin_table
        ).astype(jnp.bfloat16)
        key_part = rotate(
            joined_proj[:, D : D + kv_width].reshape(seq_count, tok_len, KV_HEADS, HEAD),
            cos_table,
            sin_table,
        ).astype(jnp.bfloat16)
        value_part = joined_proj[:, D + kv_width :].astype(jnp.bfloat16)
        local_kv = jnp.concatenate(
            [
                key_part.reshape(seq_count, tok_len, kv_width),
                value_part.reshape(seq_count, tok_len, kv_width),
            ],
            axis=-1,
        )
        keys_all = lax.all_gather(local_kv, "seq", axis=1, tiled=True)
        pieces = []
        log_sums = []
        for kv_index in range(KV_HEADS):
            mixed_part, log_sum = attend_forward(
                queries, keys_all, allowed, kv_index, group_size, score_scale
            )
            pieces.append(mixed_part)
            log_sums.append(log_sum)
        mixed_out = (
            jnp.concatenate(pieces, axis=2).reshape(row_count, model_width).astype(jnp.bfloat16)
        )
        middle = residual + jnp.dot(mixed_out, out_full, preferred_element_type=jnp.float32)
        shaped = gate_up_weight[layer_index].reshape(
            width_rows, 2, group_count, seq_devices, unit_rows
        )
        gain_copies = jnp.broadcast_to(
            mlp_gain[layer_index].reshape(width_rows, 1, 1, 1, 1),
            (width_rows, 1, 1, seq_devices, 1),
        )
        gain_cols = lax.all_to_all(gain_copies, "seq", split_axis=3, concat_axis=0, tiled=True)
        gate_cols = lax.all_to_all(shaped, "seq", split_axis=3, concat_axis=0, tiled=True)
        gain_whole = lax.all_gather(gain_cols, "dp", axis=0, tiled=True)
        gate_whole = lax.all_gather(gate_cols, "dp", axis=0, tiled=True)
        down_whole = lax.all_gather(down_weight[layer_index], "dp", axis=0, tiled=True)
        mlp_set = (gain_whole.reshape(-1), gate_whole.reshape(gate_whole.shape[0], -1), down_whole)
        mlp_gain_full, gate_up_full, down_full = mlp_set
        inv_two, normed_own = norm_forward(middle, mlp_gain_full)
        normed_two = group_rows(normed_own)
        unit_count = gate_up_full.shape[1] // 2
        gate_up = jnp.dot(normed_two, gate_up_full, preferred_element_type=jnp.float32)
        hidden = (jax.nn.silu(gate_up[:, :unit_count]) * gate_up[:, unit_count:]).astype(
            jnp.bfloat16
        )
        branch_out = group_sums(jnp.dot(hidden, down_full, preferred_element_type=jnp.float32))
        kept_state.append(
            (
                residual,
                inv_one,
                normed,
                queries,
                keys_all,
                log_sums,
                mixed_out,
                middle,
                inv_two,
                normed_two,
                gate_up,
                hidden,
                attn_set,
                mlp_set,
            )
        )
        residual = middle + branch_out
    activations = residual.astype(jnp.bfloat16).reshape(seq_count, tok_len, model_width)
    upstream = cotangent.astype(jnp.float32).reshape(row_count, model_width)
    attn_results = [None] * LAYERS
    mlp_results = [None] * LAYERS
    for layer_index in reversed(range(LAYERS)):
        (
            layer_input,
            inv_one,
            normed,
            queries,
            keys_all,
            log_sums,
            mixed_out,
            middle,
            inv_two,
            normed_two,
            gate_up,
            hidden,
            attn_set,
            mlp_set,
        ) = kept_state[layer_index]
        mlp_gain_full, gate_up_full, down_full = mlp_set
        unit_count = gate_up_full.shape[1] // 2
        grad_low = group_rows(upstream.astype(jnp.bfloat16))
        down_part = jnp.einsum("rf,rd->fd", hidden, grad_low, preferred_element_type=jnp.float32)
        grad_hidden = jnp.einsum(
            "rd,fd->rf", grad_low, down_full, preferred_element_type=jnp.float32
        )
        gate_part = gate_up[:, :unit_count]
        up_part = gate_up[:, unit_count:]
        sigmoid_gate = jax.nn.sigmoid(gate_part)
        grad_gate = grad_hidden * up_part * sigmoid_gate * (1.0 + gate_part * (1.0 - sigmoid_gate))
        grad_up = grad_hidden * gate_part * sigmoid_gate
        grad_gu = jnp.concatenate([grad_gate, grad_up], axis=1).astype(jnp.bfloat16)
        gate_up_part = jnp.einsum(
            "rk,rf->kf", normed_two, grad_gu, preferred_element_type=jnp.float32
        )
        grad_normed_two = group_sums(
            jnp.einsum("rf,kf->rk", grad_gu, gate_up_full, preferred_element_type=jnp.float32)
        )
        mlp_gain_part, norm_two_grad = norm_backward(
            middle, inv_two, mlp_gain_full, grad_normed_two
        )
        grad_middle = upstream + norm_two_grad
        gain_sum, gate_sum, down_sum = (
            lax.psum_scatter(
                mlp_gain_part.astype(jnp.bfloat16), "dp", scatter_dimension=0, tiled=True
            ).astype(jnp.float32),
            lax.psum_scatter(
                gate_up_part.reshape(model_width, 2, group_count, 1, unit_rows).astype(
                    jnp.bfloat16
                ),
                "dp",
                scatter_dimension=0,
                tiled=True,
            ).astype(jnp.float32),
            lax.psum_scatter(
                down_part.astype(jnp.bfloat16), "dp", scatter_dimension=0, tiled=True
            ).astype(jnp.float32),
        )
        gain_terms, gate_owned = (
            lax.all_to_all(
                gain_sum.reshape(-1, 1, 1, 1, 1).astype(jnp.bfloat16),
                "seq",
                split_axis=0,
                concat_axis=3,
                tiled=True,
            ).astype(jnp.float32),
            lax.all_to_all(
                gate_sum.astype(jnp.bfloat16), "seq", split_axis=0, concat_axis=3, tiled=True
            ).astype(gate_sum.dtype),
        )
        mlp_results[layer_index] = (
            jnp.sum(gain_terms, axis=3).reshape(-1),
            gate_owned.reshape(gate_owned.shape[0], -1),
            down_sum,
        )
        attn_set = (
            lax.all_gather(attn_gain[layer_index], ("dp", "seq"), axis=0, tiled=True),
            lax.all_gather(joined_weight[layer_index], ("dp", "seq"), axis=0, tiled=True),
            lax.all_gather(joined_bias[layer_index], ("dp", "seq"), axis=0, tiled=True),
            lax.all_gather(out_weight[layer_index], ("dp", "seq"), axis=0, tiled=True),
        )
        gain_full, joined_full, bias_full, out_full = attn_set
        grad_out_low = grad_middle.astype(jnp.bfloat16)
        out_part = jnp.einsum(
            "rk,rd->kd", mixed_out, grad_out_low, preferred_element_type=jnp.float32
        )
        grad_mixed = jnp.einsum(
            "rd,kd->rk", grad_out_low, out_full, preferred_element_type=jnp.float32
        ).astype(jnp.bfloat16)
        grad_mixed = grad_mixed.reshape(seq_count, tok_len, HEADS, HEAD)
        query_pieces = []
        key_pieces = []
        value_pieces = []
        for kv_index in range(KV_HEADS):
            grad_query, grad_key, grad_value = attend_backward(
                queries,
                keys_all,
                allowed,
                log_sums[kv_index],
                grad_mixed,
                kv_index,
                group_size,
                score_scale,
            )
            query_pieces.append(grad_query)
            key_pieces.append(grad_key)
            value_pieces.append(grad_value)
        kv_terms = jnp.concatenate(key_pieces + value_pieces, axis=-1)
        kv_owned = lax.psum_scatter(
            kv_terms.astype(jnp.bfloat16), "seq", scatter_dimension=1, tiled=True
        ).astype(jnp.float32)
        grad_keys_own = kv_owned[..., :kv_width].reshape(seq_count, tok_len, KV_HEADS, HEAD)
        grad_values_own = kv_owned[..., kv_width:].reshape(row_count, kv_width)
        grad_queries = jnp.concatenate(query_pieces, axis=2)
        grad_joined = jnp.concatenate(
            [
                rotate(grad_queries, cos_table, -sin_table).reshape(row_count, D),
                rotate(grad_keys_own, cos_table, -sin_table).reshape(row_count, kv_width),
                grad_values_own,
            ],
            axis=1,
        ).astype(jnp.bfloat16)
        bias_part = jnp.sum(grad_joined.astype(jnp.float32), axis=0)
        front_bias_part = bias_part[:split_col]
        value_bias_part = bias_part[split_col:]
        joined_part = jnp.einsum(
            "rk,rf->kf", normed, grad_joined, preferred_element_type=jnp.float32
        )
        grad_normed = jnp.einsum(
            "rf,kf->rk", grad_joined, joined_full, preferred_element_type=jnp.float32
        )
        attn_gain_part, norm_one_grad = norm_backward(layer_input, inv_one, gain_full, grad_normed)
        upstream = grad_middle + norm_one_grad
        attn_results[layer_index] = (
            lax.psum_scatter(attn_gain_part, ("dp", "seq"), scatter_dimension=0, tiled=True),
            lax.psum_scatter(joined_part, ("dp", "seq"), scatter_dimension=0, tiled=True),
            lax.psum_scatter(front_bias_part, ("dp", "seq"), scatter_dimension=0, tiled=True),
            lax.psum_scatter(value_bias_part, ("dp", "seq"), scatter_dimension=0, tiled=True),
            lax.psum_scatter(out_part, ("dp", "seq"), scatter_dimension=0, tiled=True),
        )
    input_grad = upstream.reshape(seq_count, tok_len, model_width)
    attn_gain_grad = jnp.stack([entry[0] for entry in attn_results])
    joined_weight_grad = jnp.stack([entry[1] for entry in attn_results])
    joined_bias_grad = jnp.stack([entry[2] for entry in attn_results])
    value_bias_grad = jnp.stack([entry[3] for entry in attn_results])
    out_weight_grad = jnp.stack([entry[4] for entry in attn_results])
    mlp_gain_grad = jnp.stack([entry[0] for entry in mlp_results])
    gate_up_grad = jnp.stack([entry[1] for entry in mlp_results])
    down_grad = jnp.stack([entry[2] for entry in mlp_results])
    return (
        activations,
        input_grad,
        attn_gain_grad,
        joined_weight_grad,
        joined_bias_grad,
        value_bias_grad,
        out_weight_grad,
        mlp_gain_grad,
        gate_up_grad,
        down_grad,
    )


def solution(mesh):
    in_specs = (
        P("dp", "seq", None),
        P("dp", "seq", None),
        P("dp", None),
        P(None, ("dp", "seq")),
        P(None, ("dp", "seq"), None),
        P(None, ("dp", "seq")),
        P(None, ("dp", "seq"), None),
        P(None, ("dp", "seq")),
        P(None, ("dp", "seq"), None),
        P(None, ("dp", "seq"), None),
    )
    out_specs = (
        P("dp", "seq", None),
        P("dp", "seq", None),
        P(None, ("dp", "seq")),
        P(None, ("dp", "seq"), None),
        P(None, ("dp", "seq")),
        P(None, ("dp", "seq")),
        P(None, ("dp", "seq"), None),
        P(None, ("dp", "seq")),
        P(None, ("dp", "seq"), None),
        P(None, ("dp", "seq"), None),
    )
    return jax.shard_map(body, mesh=mesh, in_specs=in_specs, out_specs=out_specs, check_vma=False)
```

profile of v0, /device:TPU:0, one launch (start us, length us, event | category | flops | bytes accessed | tf_op | source)
XLA Modules:
  0.0 1555.8 jit_solution(14968614911038476941)
XLA Ops:
  25.2 13.0 all-to-all-done.1
  43.7 42.6 %all-reduce.25 = (bf16[1152]{0:T(1024)(128)(2,1)S(1)}, bf16[896]{0:T(1024)(128)(2,1)S(1)}, bf16[1152]{0:T(1024)(128)(2,1)S(1)}, bf16[896]{0:T(1024)(128)(2,1)S(1)}) all-reduce(bf16[1152]{0:T(1024)(128)(2,1)S(1)} %dynamic-update-slice.1, bf16[896]{0:T(1024)(128)(2,1)S(1)} %dynamic-update-slice, ...), channel_id=4, replica_groups=mesh['dp'=8,'seq'=4] {'dp','seq'}, use_global_device_ids=true, to_apply=%add.1 | all-reduce | flops 4096 | bytes 16384
  100.5 20.4 %all-reduce.27 = (bf16[896]{0:T(1024)(128)(2,1)S(1)}, bf16[896]{0:T(1024)(128)(2,1)S(1)}) all-reduce(bf16[896]{0:T(1024)(128)(2,1)S(1)} %dynamic-update-slice.2, bf16[896]{0:T(1024)(128)(2,1)S(1)} %dynamic-update-slice.5), channel_id=1, replica_groups=mesh['dp'=8,'seq'=4] {'dp'}, use_global_device_ids=true, to_apply=%add.2 | all-reduce | flops 1792 | bytes 7168
  126.6 6.8 all_gather.69
  148.2 104.7 %all-gather.26.cloned.1.call-done = bf16[896,2,8,1,152]{4,2,3,1,0:T(8,128)(2,1)} async-done(((bf16[112,2,8,1,152]{4,2,3,1,0:T(8,128)(2,1)}), bf16[896,2,8,1,152]{4,2,3,1,0:T(8,128)(2,1)}) %all-gather.26.cloned.1.call-update) | async-done | bytes 4358160 | tf_op jit(solution)/shard_map/all_gather | solution.py:219
  253.0 11.3 copy.211
  264.3 10.0 all-gather.36.cloned.1.call-done
  274.3 8.3 fusion.260
  289.8 37.3 %all-gather.38.cloned.1.call-done = bf16[1,1216,896]{2,1,0:T(8,128)(2,1)} async-done(((bf16[1,152,896]{2,1,0:T(8,128)(2,1)}), bf16[1,1216,896]{2,1,0:T(8,128)(2,1)}) %all-gather.38.cloned.1.call-update) | async-done | bytes 2179088 | tf_op jit(solution)/shard_map/all_gather | solution.py:220
  337.8 19.2 %all_to_all.108 = bf16[28,2,8,4,152]{4,2,1,0,3:T(8,128)(2,1)} all-to-all(bf16[28,2,8,4,152]{4,2,1,0,3:T(8,128)(2,1)S(1)} %copy.221), channel_id=1, replica_groups=mesh['dp'=8,'seq'=4] {'seq'}, dimensions={3} | all-to-all | bytes 1089536 | tf_op jit(solution)/shard_map/all_to_all | solution.py:217
  357.1 7.7 reduce-scatter.27.cloned.1.call-done
  366.1 62.0 %all-gather.40.cloned.1.call-done = bf16[1,896,1152]{2,0,1:T(2,128)(2,1)} async-done(((bf16[1,28,1152]{2,0,1:T(2,128)(2,1)}), bf16[1,896,1152]{2,0,1:T(2,128)(2,1)}) %all-gather.40.cloned.1.call-update) | async-done | bytes 2064400 | tf_op jit(solution)/shard_map/all_gather | solution.py:171
  434.7 7.4 all_gather.78
  451.3 38.0 %all-gather.42.cloned.1.call-done = bf16[1,896,896]{2,0,1:T(2,128)(2,1)} async-done(((bf16[1,28,896]{2,0,1:T(2,128)(2,1)}), bf16[1,896,896]{2,0,1:T(2,128)(2,1)}) %all-gather.42.cloned.1.call-update) | async-done | bytes 1605648 | tf_op jit(solution)/shard_map/all_gather | solution.py:173
  494.6 108.1 %all-gather.28.cloned.1.call-done = bf16[896,2,8,1,152]{4,2,3,1,0:T(8,128)(2,1)} async-done(((bf16[112,2,8,1,152]{4,2,3,1,0:T(8,128)(2,1)}), bf16[896,2,8,1,152]{4,2,3,1,0:T(8,128)(2,1)}) %all-gather.28.cloned.1.call-update) | async-done | bytes 4358160 | tf_op jit(solution)/shard_map/all_gather | solution.py:219
  602.7 11.4 copy.223
  614.0 10.0 all-gather.44.cloned.1.call-done
  624.1 10.5 fusion.261
  634.5 12.3 all-gather.30.cloned.1.call-done
  646.9 52.5 %all-gather.46.cloned.1.call-done = bf16[1,1216,896]{2,1,0:T(8,128)(2,1)} async-done(((bf16[1,152,896]{2,1,0:T(8,128)(2,1)}), bf16[1,1216,896]{2,1,0:T(8,128)(2,1)}) %all-gather.46.cloned.1.call-update) | async-done | bytes 2179088 | tf_op jit(solution)/shard_map/all_gather | solution.py:220
  699.4 9.4 multiply_convert_fusion.3
  711.1 9.0 convert_bitcast_fusion.3
  720.2 6.5 convert_bitcast_fusion.4
  727.3 21.3 %reduce-scatter.31.cloned.1.call-done = bf16[1,256,896]{2,1,0:T(8,128)(2,1)} async-done(((bf16[1,1024,896]{2,1,0:T(8,128)(2,1)}), bf16[1,256,896]{2,1,0:T(8,128)(2,1)}) %reduce-scatter.31.cloned.1.call-update) | async-done | bytes 458768 | tf_op jit(solution)/shard_map/reduce_scatter | solution.py:158
  750.6 30.2 %reduce-scatter.29.cloned.1.call-done = bf16[1,256,896]{2,1,0:T(8,128)(2,1)} async-done(((bf16[1,1024,896]{2,1,0:T(8,128)(2,1)}), bf16[1,256,896]{2,1,0:T(8,128)(2,1)}) %reduce-scatter.29.cloned.1.call-update) | async-done | bytes 458768 | tf_op jit(solution)/shard_map/reduce_scatter | solution.py:158
  791.4 8.1 fusion.10
  829.4 17.4 %reduce-scatter.33.cloned.1.call-done = bf16[1,256,256]{1,2,0:T(8,128)(2,1)} async-done(((bf16[1,1024,256]{1,2,0:T(8,128)(2,1)}), bf16[1,256,256]{1,2,0:T(8,128)(2,1)}) %reduce-scatter.33.cloned.1.call-update) | async-done | bytes 131088 | tf_op jit(solution)/shard_map/reduce_scatter | solution.py:360
  852.2 21.2 %all-gather.48.cloned.1.call-done = bf16[1024,896]{1,0:T(8,128)(2,1)} async-done(((bf16[256,896]{1,0:T(8,128)(2,1)}), bf16[1024,896]{1,0:T(8,128)(2,1)}) %all-gather.48.cloned.1.call-update) | async-done | bytes 1835024 | tf_op jit(solution)/shard_map/all_gather | solution.py:152
  873.4 9.3 multiply_convert_fusion.1
  885.1 9.0 convert_bitcast_fusion.2
  900.7 7.9 copy.255
  908.5 9.2 convert_bitcast_fusion
  917.7 12.2 copy.315
  929.9 13.1 reshape.1237
  956.8 7.6 copy.252
  964.4 6.5 convolution_convert_fusion.1
  976.4 7.5 fusion.4
  989.7 7.6 fusion.7
  997.3 6.7 fusion.38
  1010.7 9.2 convert_bitcast_fusion.1
  1020.0 12.1 copy.313
  1032.1 13.1 reshape.1235
  1074.0 21.3 %all-reduce.26 = (bf16[896]{0:T(1024)(128)(2,1)S(1)}, bf16[896]{0:T(1024)(128)(2,1)S(1)}) all-reduce(bf16[896]{0:T(1024)(128)(2,1)S(1)} %copy-done.71, bf16[896]{0:T(1024)(128)(2,1)S(1)} %get-tuple-element.52), channel_id=32, replica_groups=mesh['dp'=8,'seq'=4] {'dp'}, use_global_device_ids=true, to_apply=%region_44.45.clone | all-reduce | flops 1792 | bytes 7168
  1116.9 71.3 %reduce-scatter.43.cloned.1.call-done = bf16[152,896]{1,0:T(8,128)(2,1)} async-done(((bf16[1216,896]{1,0:T(8,128)(2,1)}), bf16[152,896]{1,0:T(8,128)(2,1)}) %reduce-scatter.43.cloned.1.call-update) | async-done | bytes 272400
  1190.2 21.7 %reduce-scatter.37.cloned.1.call-done = bf16[1,256,256]{1,2,0:T(8,128)(2,1)} async-done(((bf16[1,1024,256]{1,2,0:T(8,128)(2,1)}), bf16[1,256,256]{1,2,0:T(8,128)(2,1)}) %reduce-scatter.37.cloned.1.call-update) | async-done | bytes 131088 | tf_op jit(solution)/shard_map/reduce_scatter | solution.py:360
  1218.3 189.8 %fusion.247 = (f32[32,1152]{1,0:T(8,128)S(1)}, f32[32,1152]{1,0:T(8,128)S(1)}, f32[32,896]{1,0:T(8,128)}, f32[32,896]{1,0:T(8,128)}) fusion(f32[896,1152]{1,0:T(8,128)} %fusion.246, f32[896,1152]{1,0:T(8,128)} %fusion.225, f32[896,896]{1,0:T(8,128)S(1)} %fusion.222, f32[896,896]{1,0:T(8,128)} %fusion.219), kind=kCustom, calls=%all-reduce-scatter.4 | all-reduce-scatter fusion | flops 4194305 | bytes 15204352
  1421.0 42.7 %all-reduce.24 = (f32[896]{0:T(1024)S(1)}, f32[896]{0:T(1024)S(1)}, f32[1024]{0:T(1024)S(1)}, f32[1024]{0:T(1024)S(1)}, f32[128]{0:T(128)S(1)}, /*index=5*/f32[128]{0:T(128)S(1)}) all-reduce(f32[896]{0:T(1024)S(1)} %get-tuple-element.50, f32[896]{0:T(1024)S(1)} %get-tuple-element.56, ...), channel_id=22, replica_groups=mesh['dp'=8,'seq'=4] {'dp','seq'}, use_global_device_ids=true, to_apply=%region_29.30.clone | all-reduce | flops 4096 | bytes 32768
  1530.6 12.1 all-to-all-done.6
  (478 shorter events, 331.0 us)
Async XLA Ops:
  7.2 113.7 %all-gather.32.cloned.1.call-start = ((), (), s32[]{:S(2)}) async-start(), calls=%async_computation.27 | async-start | bytes 4257792 | tf_op jit(solution)/shard_map/all_gather | solution.py:171
  9.1 132.6 %all-gather.34.cloned.1.call-start = ((), (), s32[]{:S(2)}) async-start(), calls=%async_computation.28 | async-start | bytes 3311616 | tf_op jit(solution)/shard_map/all_gather | solution.py:173
  20.9 17.3 %all-to-all-start.1 = ((bf16[28,2,8,4,152]{4,2,1,0,3:T(8,128)(2,1)}), bf16[28,2,8,4,152]{4,2,1,0,3:T(8,128)(2,1)S(1)}, u32[]{:S(2)}, u32[]{:S(2)}) async-start(bf16[28,2,8,4,152]{4,2,1,0,3:T(8,128)(2,1)} %copy.209), calls=%async_computation.1 | async-start | bytes 1835008 | tf_op jit(solution)/shard_map/all_to_all | solution.py:217
  38.8 53.4 %all-to-all-start = ((bf16[28,1,1,4,1]{0,4,2,1,3:T(2,128)(2,1)}), bf16[28,1,1,4,1]{0,4,2,1,3:T(2,128)(2,1)S(1)}, u32[]{:S(2)}, u32[]{:S(2)}) async-start(bf16[28,1,1,4,1]{0,4,2,1,3:T(2,128)(2,1)} %broadcast_in_dim.181), calls=%async_computation | async-start | bytes 4096 | tf_op jit(solution)/shard_map/all_to_all | solution.py:216
  42.0 211.0 %all-gather.26.cloned.1.call-start = ((), (), s32[]{:S(2)}) async-start(), calls=%async_computation.18 | async-start | bytes 8257536 | tf_op jit(solution)/shard_map/all_gather | solution.py:219
  92.7 7.2 all-to-all-start.2
  96.3 178.0 %all-gather.36.cloned.1.call-start = ((), (), s32[]{:S(2)}) async-start(), calls=%async_computation.29 | async-start | bytes 2293760 | tf_op jit(solution)/shard_map/all_gather | solution.py:152
  144.6 220.2 %copy-start.9 = (f32[256,896]{1,0:T(8,128)}, f32[256,896]{1,0:T(8,128)S(1)}, u32[]{:S(2)}) copy-start(f32[256,896]{1,0:T(8,128)S(1)} %get-tuple-element.137) | copy-start | bytes 2752516
  145.7 181.4 %all-gather.38.cloned.1.call-start = ((), (), s32[]{:S(2)}) async-start(), calls=%async_computation.30 | async-start | bytes 2451456 | tf_op jit(solution)/shard_map/all_gather | solution.py:220
  147.7 217.2 %reduce-scatter.27.cloned.1.call-start = ((), (), s32[]{:S(2)}) async-start(), calls=%async_computation.19 | async-start | bytes 2293760 | tf_op jit(solution)/shard_map/reduce_scatter | solution.py:158
  333.7 94.4 %all-gather.40.cloned.1.call-start = ((), (), s32[]{:S(2)}) async-start(), calls=%async_computation.31 | async-start | bytes 4257792 | tf_op jit(solution)/shard_map/all_gather | solution.py:171
  334.4 154.9 %all-gather.42.cloned.1.call-start = ((), (), s32[]{:S(2)}) async-start(), calls=%async_computation.32 | async-start | bytes 3311616 | tf_op jit(solution)/shard_map/all_gather | solution.py:173
  335.2 267.5 %all-gather.28.cloned.1.call-start = ((), (), s32[]{:S(2)}) async-start(), calls=%async_computation.20 | async-start | bytes 8257536 | tf_op jit(solution)/shard_map/all_gather | solution.py:219
  357.0 267.0 %all-gather.44.cloned.1.call-start = ((), (), s32[]{:S(2)}) async-start(), calls=%async_computation.33 | async-start | bytes 2293760 | tf_op jit(solution)/shard_map/all_gather | solution.py:152
  366.1 485.0 %copy-start.11 = (f32[256,896]{1,0:T(8,128)}, f32[256,896]{1,0:T(8,128)S(1)}, u32[]{:S(2)}) copy-start(f32[256,896]{1,0:T(8,128)S(1)} %get-tuple-element.85) | copy-start | bytes 2752516
  493.0 153.9 %all-gather.30.cloned.1.call-start = ((), (), s32[]{:S(2)}) async-start(), calls=%async_computation.22 | async-start | bytes 2293760 | tf_op jit(solution)/shard_map/all_gather | solution.py:152
  493.7 205.6 %all-gather.46.cloned.1.call-start = ((), (), s32[]{:S(2)}) async-start(), calls=%async_computation.34 | async-start | bytes 2451456 | tf_op jit(solution)/shard_map/all_gather | solution.py:220
  494.3 254.3 %reduce-scatter.31.cloned.1.call-start = ((), (), s32[]{:S(2)}) async-start(), calls=%async_computation.23 | async-start | bytes 2293760 | tf_op jit(solution)/shard_map/reduce_scatter | solution.py:158
  720.2 60.7 %reduce-scatter.29.cloned.1.call-start = ((), (), s32[]{:S(2)}) async-start(), calls=%async_computation.21 | async-start | bytes 2293760 | tf_op jit(solution)/shard_map/reduce_scatter | solution.py:158
  726.8 120.1 %reduce-scatter.33.cloned.1.call-start = ((), (), s32[]{:S(2)}) async-start(), calls=%async_computation.24 | async-start | bytes 655360 | tf_op jit(solution)/shard_map/reduce_scatter | solution.py:360
  825.0 48.4 %all-gather.48.cloned.1.call-start = ((), (), s32[]{:S(2)}) async-start(), calls=%async_computation.35 | async-start | bytes 2293760 | tf_op jit(solution)/shard_map/all_gather | solution.py:152
  852.1 119.3 %reduce-scatter.35.cloned.1.call-start = ((), (), s32[]{:S(2)}) async-start(), calls=%async_computation.25 | async-start | bytes 2293760 | tf_op jit(solution)/shard_map/reduce_scatter | solution.py:158
  894.2 151.7 %reduce-scatter.41.cloned.1.call-start = ((), (), s32[]{:S(2)}) async-start(), calls=%async_computation.37 | async-start | bytes 4902912
  943.1 173.8 %reduce-scatter.45.cloned.1.call-start = ((), (), s32[]{:S(2)}) async-start(), calls=%async_computation.39 | async-start | bytes 2451456
  950.4 237.7 %reduce-scatter.43.cloned.1.call-start = ((), (), s32[]{:S(2)}) async-start(), calls=%async_computation.38 | async-start | bytes 2451456
  970.9 241.0 %reduce-scatter.37.cloned.1.call-start = ((), (), s32[]{:S(2)}) async-start(), calls=%async_computation.26 | async-start | bytes 655360 | tf_op jit(solution)/shard_map/reduce_scatter | solution.py:360
  1010.5 509.9 %reduce-scatter.39.cloned.1.call-start = ((), (), s32[]{:S(2)}) async-start(), calls=%async_computation.36 | async-start | bytes 4902912
  1050.2 17.4 %all-to-all-start.7 = ((bf16[112,2,8,1,152]{4,2,1,3,0:T(8,128)(2,1)}), bf16[112,2,8,1,152]{4,2,1,3,0:T(8,128)(2,1)}, u32[]{:S(2)}, u32[]{:S(2)}) async-start(bf16[112,2,8,1,152]{4,2,1,3,0:T(8,128)(2,1)} %bitcast.195), calls=%async_computation.13 | async-start | bytes 1835008 | tf_op jit(solution)/shard_map/all_to_all | solution.py:318
  1096.1 11.8 all-to-all-start.4
  1107.9 7.3 all-to-all-start.5
  1214.2 193.9 %copy-start.64 = (f32[1152]{0:T(1024)}, f32[1152]{0:T(1024)S(1)}, u32[]{:S(2)}) copy-start(f32[1152]{0:T(1024)S(1)} %convert_reduce_fusion.1) | copy-start | bytes 13828
  1409.2 66.8 %collective-permute-start.11 = (f32[28,896]{1,0:T(8,128)S(1)}, f32[28,896]{1,0:T(8,128)S(1)}, u32[]{:S(2)}, u32[]{:S(2)}) collective-permute-start(f32[28,896]{1,0:T(8,128)S(1)} %slice.336), channel_id=1, source_target_pairs={{0,4},{1,5},{2,6},{3,7},{4,8},{5,9},{6,10},{7,11},{8,12},{9,13},{1... | collective-permute-start | bytes 301064
  1415.3 69.5 %collective-permute-start.14 = (f32[32,896]{1,0:T(8,128)}, f32[32,896]{1,0:T(8,128)S(1)}, u32[]{:S(2)}, u32[]{:S(2)}) collective-permute-start(f32[32,896]{1,0:T(8,128)} %get-tuple-element.80), channel_id=1, source_target_pairs={{0,3},{1,4},{2,5},{3,6},{4,7},{5,8},{6,9},{7,10},{8,11},{9,12},{10... | collective-permute-start | bytes 344072
  1465.7 20.5 %collective-permute-start.13 = (f32[32,896]{1,0:T(8,128)S(1)}, f32[32,896]{1,0:T(8,128)S(1)}, u32[]{:S(2)}, u32[]{:S(2)}) collective-permute-start(f32[32,896]{1,0:T(8,128)S(1)} %copy-done.41), channel_id=1, source_target_pairs={{0,2},{1,3},{2,4},{3,5},{4,6},{5,7},{6,8},{7,9},{8,10},{9,11},{10,... | collective-permute-start | bytes 344072
  1469.9 22.4 %collective-permute-start.12 = (f32[32,896]{1,0:T(8,128)S(1)}, f32[32,896]{1,0:T(8,128)S(1)}, u32[]{:S(2)}, u32[]{:S(2)}) collective-permute-start(f32[32,896]{1,0:T(8,128)S(1)} %copy-done.41), channel_id=1, source_target_pairs={{0,1},{1,2},{2,3},{3,4},{4,5},{5,6},{6,7},{7,8},{8,9},{9,10},{10,1... | collective-permute-start | bytes 344072
  1471.2 25.4 %collective-permute-start.10 = (f32[32,896]{1,0:T(8,128)S(1)}, f32[32,896]{1,0:T(8,128)S(1)}, u32[]{:S(2)}, u32[]{:S(2)}) collective-permute-start(f32[32,896]{1,0:T(8,128)S(1)} %copy-done.40), channel_id=1, source_target_pairs={{0,3},{1,4},{2,5},{3,6},{4,7},{5,8},{6,9},{7,10},{8,11},{9,12},{10... | collective-permute-start | bytes 344072
  1475.9 5.4 collective-permute-start.15
  1481.3 18.8 %collective-permute-start.9 = (f32[32,896]{1,0:T(8,128)S(1)}, f32[32,896]{1,0:T(8,128)S(1)}, u32[]{:S(2)}, u32[]{:S(2)}) collective-permute-start(f32[32,896]{1,0:T(8,128)S(1)} %copy-done.40), channel_id=1, source_target_pairs={{0,2},{1,3},{2,4},{3,5},{4,6},{5,7},{6,8},{7,9},{8,10},{9,11},{10,... | collective-permute-start | bytes 344072
  1484.7 16.7 %collective-permute-start.8 = (f32[32,896]{1,0:T(8,128)S(1)}, f32[32,896]{1,0:T(8,128)S(1)}, u32[]{:S(2)}, u32[]{:S(2)}) collective-permute-start(f32[32,896]{1,0:T(8,128)S(1)} %copy-done.40), channel_id=1, source_target_pairs={{0,1},{1,2},{2,3},{3,4},{4,5},{5,6},{6,7},{7,8},{8,9},{9,10},{10,1... | collective-permute-start | bytes 344072
  1486.1 25.3 %collective-permute-start.6 = (f32[32,1152]{1,0:T(8,128)S(1)}, f32[32,1152]{1,0:T(8,128)S(1)}, u32[]{:S(2)}, u32[]{:S(2)}) collective-permute-start(f32[32,1152]{1,0:T(8,128)S(1)} %get-tuple-element.78), channel_id=1, source_target_pairs={{0,3},{1,4},{2,5},{3,6},{4,7},{5,8},{6,9},{7,10},{8,11},{9,12},{10... | collective-permute-start | bytes 442376
  1492.3 20.4 %collective-permute-start.5 = (f32[32,1152]{1,0:T(8,128)S(1)}, f32[32,1152]{1,0:T(8,128)S(1)}, u32[]{:S(2)}, u32[]{:S(2)}) collective-permute-start(f32[32,1152]{1,0:T(8,128)S(1)} %get-tuple-element.78), channel_id=1, source_target_pairs={{0,2},{1,3},{2,4},{3,5},{4,6},{5,7},{6,8},{7,9},{8,10},{9,11},{10,... | collective-permute-start | bytes 442376
  1496.5 11.7 collective-permute-start.7
  1500.1 17.7 %collective-permute-start.4 = (f32[32,1152]{1,0:T(8,128)S(1)}, f32[32,1152]{1,0:T(8,128)S(1)}, u32[]{:S(2)}, u32[]{:S(2)}) collective-permute-start(f32[32,1152]{1,0:T(8,128)S(1)} %get-tuple-element.78), channel_id=1, source_target_pairs={{0,1},{1,2},{2,3},{3,4},{4,5},{5,6},{6,7},{7,8},{8,9},{9,10},{10,1... | collective-permute-start | bytes 442376
  1501.5 18.2 %collective-permute-start.2 = (f32[32,1152]{1,0:T(8,128)S(1)}, f32[32,1152]{1,0:T(8,128)S(1)}, u32[]{:S(2)}, u32[]{:S(2)}) collective-permute-start(f32[32,1152]{1,0:T(8,128)S(1)} %get-tuple-element.79), channel_id=1, source_target_pairs={{0,3},{1,4},{2,5},{3,6},{4,7},{5,8},{6,9},{7,10},{8,11},{9,12},{10... | collective-permute-start | bytes 442376
  1508.3 11.4 collective-permute-start.1
  1511.4 8.3 collective-permute-start
  1512.7 7.0 collective-permute-start.3
  1524.8 17.9 %all-to-all-start.6 = ((bf16[112,2,8,1,152]{4,2,1,3,0:T(8,128)(2,1)}), bf16[112,2,8,1,152]{4,2,1,3,0:T(8,128)(2,1)S(1)}, u32[]{:S(2)}, u32[]{:S(2)}) async-start(bf16[112,2,8,1,152]{4,2,1,3,0:T(8,128)(2,1)} %bitcast.192), calls=%async_computation.12 | async-start | bytes 1835008 | tf_op jit(solution)/shard_map/all_to_all | solution.py:318
  (87 other events, 1953.4 us)
Sparse Core Ops, SparseCore 0:
  11.5 64.6 all-gather.31
  79.7 59.7 all-gather.33
  142.2 110.7 all-gather.25
  255.0 19.2 all-gather.35
  276.9 50.1 all-gather.37
  333.8 30.9 reduce-scatter.26
  368.8 59.3 all-gather.39
  431.4 57.8 all-gather.41
  491.7 110.8 all-gather.27
  604.7 19.2 all-gather.43
  625.7 21.1 all-gather.29
  649.2 50.1 all-gather.45
  720.3 28.2 reduce-scatter.30
  751.0 29.8 reduce-scatter.28
  825.2 21.6 reduce-scatter.32
  852.2 21.1 all-gather.47
  894.3 29.8 reduce-scatter.34
  943.2 89.7 reduce-scatter.40
  1037.4 73.6 reduce-scatter.44
  1114.4 73.7 reduce-scatter.42
  1190.8 21.1 reduce-scatter.36
  1215.5 135.2 reduce-scatter.38
where the time goes:
time: 1570 us; the launch traced here: 1560 us
  waiting for transfers between devices  670 us (43%)
  blocking collectives  350 us (22%)
  matrix products  196 us (12%)
  local copies, waits for them, and re-layouts  163 us (10%)
  starting transfers between devices  83.9 us (5%)
  other arithmetic  74.1 us (5%)
  between operations  18.1 us (1%)
    unnamed x5, blocking collectives  317 us
    all_gather x2, waiting for transfers between devices, body(): gate_whole = lax.all_gather(gate_cols, 'dp', axis=0, tiled=True)  213 us
    all_gather x2, waiting for transfers between devices, body(): lax.all_gather(down_weight[layer_index], 'dp', axis=0, tiled=True)  89.8 us
    unnamed x210, local copies, waits for them, and re-layouts  88.3 us
    unnamed x42, waiting for transfers between devices  77.8 us
    all_gather x2, waiting for transfers between devices, body(): lax.all_gather(joined_weight[layer_index], ('dp', 'seq'), axis=0, tiled=T...  62.1 us
    reduce_scatter x4, waiting for transfers between devices, group_sums(): lax.psum_scatter(values.reshape(seq_count, -1, model_width).astype(jnp.bf...  59.3 us
    unnamed x20, starting transfers between devices  54.7 us
  transfers between devices with their start and end apart: 45, of which 23 were waited for; matrix products, arithmetic and copies ran while one was open for 32% of the time, Pallas kernels for 0%

commit v1 on v0

v1 whole, which is shorter than its diff:
```python
import jax
import jax.numpy as jnp
from jax import lax
from jax.experimental import pallas as pl
from jax.experimental.pallas import tpu as pltpu
from jax.sharding import PartitionSpec as P

D = 896
HEADS = 14
KV_HEADS = 2
HEAD = 64
LAYERS = 2


EPS = 1e-06
THETA = 1000000.0
NEGATIVE = -1e30


def rotary_tables(positions):
    half_head = HEAD // 2
    frequency = THETA ** (-2.0 * jnp.arange(half_head, dtype=jnp.float32) / HEAD)
    angles = positions.astype(jnp.float32)[..., None] * frequency
    return (jnp.cos(angles), jnp.sin(angles))


NT = (((1,), (1,)), ((), ()))
TN = (((0,), (0,)), ((), ()))
FULL = pl.BlockSpec(memory_space=pltpu.VMEM)
SCALE = HEAD ** (-0.5)
GROUP = HEADS // KV_HEADS
KV_WIDTH = KV_HEADS * HEAD
SPLIT = D + KV_WIDTH
TILE = 384


def dot(left, right, dims=(((1,), (0,)), ((), ()))):
    return lax.dot_general(left, right, dims, preferred_element_type=jnp.float32)


def call(kernel, outs, micros, scratch=(), limit=40, **grid):
    return pl.pallas_call(
        kernel,
        out_shape=[jax.ShapeDtypeStruct(shape, kind) for shape, kind in outs],
        scratch_shapes=list(scratch),
        compiler_params=pltpu.CompilerParams(vmem_limit_bytes=limit * 2**20),
        name=kernel.__qualname__.split(".")[0],
        cost_estimate=pl.CostEstimate(
            flops=0, bytes_accessed=int(micros * 4e5), transcendentals=0
        ),
        **grid,
    )


def turn(block, cos_wide, sin_wide):
    lane = lax.broadcasted_iota(jnp.int32, block.shape, 1)
    width = block.shape[1]
    partner = jnp.where(
        lane % HEAD < HEAD // 2,
        pltpu.roll(block, width - HEAD // 2, 1),
        pltpu.roll(block, HEAD // 2, 1),
    )
    return block * cos_wide + partner * sin_wide


def inverse_root(rows):
    return lax.rsqrt(jnp.mean(rows * rows, axis=-1, keepdims=True) + EPS)


def before_attention(terms, gain, first_full, second_full, bias_first, bias_second, cos_wide, sin_wide):
    count = len(terms)
    rows = terms[0].shape[0]
    span = rows // 2

    def kernel(*refs):
        parts = refs[:count]
        gain_ref, first_ref, second_ref, bias_one, bias_two, cos_ref, sin_ref = refs[count : count + 7]
        x_ref, n_ref, q_ref, kv_ref = refs[count + 7 :]
        x = parts[0][...].astype(jnp.float32)
        for part in parts[1:]:
            x = x + part[...].astype(jnp.float32)
        x_ref[...] = x
        normed = (x * inverse_root(x) * gain_ref[...]).astype(jnp.bfloat16)
        n_ref[...] = normed
        cos_w, sin_w = cos_ref[...], sin_ref[...]
        for tile in range(SPLIT // 128):
            lanes = slice(tile * 128, tile * 128 + 128)
            block = dot(normed, first_ref[:, lanes]) + bias_one[:, lanes]
            turned = turn(block, cos_w, sin_w)
            if tile * 128 < D:
                for part in range(2):
                    head = 2 * tile + part
                    piece = turned[:, part * HEAD : part * HEAD + HEAD].astype(jnp.bfloat16)
                    place = (head % GROUP) * span
                    for half in range(2):
                        q_ref[head // GROUP, half, place : place + span, :] = piece[
                            half * span : half * span + span
                        ]
            else:
                kv_ref[:, :KV_WIDTH] = turned.astype(jnp.bfloat16)
        kv_ref[:, KV_WIDTH:] = (
            dot(normed, second_ref[:, :KV_WIDTH]) + bias_two[...]
        ).astype(jnp.bfloat16)

    return call(
        kernel,
        [
            ((rows, D), jnp.float32),
            ((rows, D), jnp.bfloat16),
            ((KV_HEADS, 2, GROUP * span, HEAD), jnp.bfloat16),
            ((rows, 2 * KV_WIDTH), jnp.bfloat16),
        ],
        4.0,
    )(*terms, gain, first_full, second_full, bias_first, bias_second, cos_wide, sin_wide)


def key_part(kv_refs, half, lanes):
    span = kv_refs[0].shape[0] // 2
    return jnp.concatenate(
        [ref[half * span : half * span + span, lanes] for ref in kv_refs], axis=0
    )


def attention(queries, kv_blocks, biases, x, second_full, gain):
    rows = x.shape[0]
    span = rows // 2

    def kernel(q_ref, kv0, kv1, kv2, kv3, bias_ref, x_ref, w_ref, gain_ref, mixed_ref, mid_ref, n_ref):
        kvs = (kv0, kv1, kv2, kv3)
        for group in range(KV_HEADS):
            key_lanes = slice(group * HEAD, group * HEAD + HEAD)
            value_lanes = slice(KV_WIDTH + group * HEAD, KV_WIDTH + group * HEAD + HEAD)
            keys = [key_part(kvs, half, key_lanes) for half in range(2)]
            values = []
            for half in range(2):
                block = key_part(kvs, half, value_lanes)
                values.append(jnp.concatenate([block, jnp.ones_like(block)], axis=1))
            for half in range(2):
                bias = bias_ref[half]
                for member in range(GROUP):
                    query = q_ref[group, half, member * span : member * span + span, :] * jnp.bfloat16(SCALE)
                    near = dot(query, keys[half], NT) + bias
                    top = jnp.max(near, axis=-1, keepdims=True)
                    if half == 1:
                        far = dot(query, keys[0], NT)
                        top = jnp.maximum(top, jnp.max(far, axis=-1, keepdims=True))
                    total = dot(jnp.exp(near - top).astype(jnp.bfloat16), values[half])
                    if half == 1:
                        total = total + dot(jnp.exp(far - top).astype(jnp.bfloat16), values[0])
                    out = total[:, :HEAD] / total[:, HEAD : 2 * HEAD]
                    head = group * GROUP + member
                    mixed_ref[half * span : half * span + span, head * HEAD : head * HEAD + HEAD] = (
                        out.astype(jnp.bfloat16)
                    )
        middle = x_ref[...] + dot(mixed_ref[...], w_ref[:, KV_WIDTH:])
        mid_ref[...] = middle
        n_ref[...] = (middle * inverse_root(middle) * gain_ref[...]).astype(jnp.bfloat16)

    return call(
        kernel,
        [((rows, D), jnp.bfloat16), ((rows, D), jnp.float32), ((rows, D), jnp.bfloat16)],
        10.5,
    )(queries, *kv_blocks, biases, x, second_full, gain)


def feed_forward(parts, gate_up_full, down_full):
    count = len(parts)
    part_rows = parts[0].shape[0]
    rows = count * part_rows
    units = down_full.shape[0]
    steps = pl.cdiv(units, TILE)
    last = units - (steps - 1) * TILE

    def kernel(*refs):
        part_refs = refs[:count]
        w_ref, d_ref, gu_ref = refs[count : count + 3]
        out_refs, total = refs[count + 3 : -1], refs[-1]
        step = pl.program_id(0)
        n2 = jnp.concatenate([ref[...] for ref in part_refs], axis=0)

        @pl.when(step == 0)
        def _():
            total[...] = jnp.zeros_like(total)

        @pl.when(step < steps - 1)
        def _():
            both = dot(n2, w_ref[...])
            gu_ref[...] = both.astype(jnp.bfloat16)
            gate, up = both[:, :TILE], both[:, TILE:]
            hidden = (gate * jax.nn.sigmoid(gate) * up).astype(jnp.bfloat16)
            total[...] += dot(hidden, d_ref[...])

        @pl.when(step == steps - 1)
        def _():
            both = dot(n2, w_ref[:, : 2 * last])
            gu_ref[:, : 2 * last] = both.astype(jnp.bfloat16)
            gate, up = both[:, :last], both[:, last:]
            hidden = (gate * jax.nn.sigmoid(gate) * up).astype(jnp.bfloat16)
            summed = (total[...] + dot(hidden, d_ref[:last, :])).astype(jnp.bfloat16)
            for place in range(count):
                out_refs[place][...] = summed[place * part_rows : place * part_rows + part_rows]

    whole = lambda step: (0, 0)
    return call(
        kernel,
        [((rows, 2 * units), jnp.bfloat16)] + [((part_rows, D), jnp.bfloat16)] * count,
        9.0,
        [pltpu.VMEM((rows, D), jnp.float32)],
        grid=(steps,),
        in_specs=[pl.BlockSpec((part_rows, D), whole)] * count
        + [
            pl.BlockSpec((D, 2 * TILE), lambda step: (0, step)),
            pl.BlockSpec((TILE, D), lambda step: (step, 0)),
        ],
        out_specs=[
            pl.BlockSpec((rows, 2 * TILE), lambda step: (0, step)),
        ]
        + [pl.BlockSpec((part_rows, D), whole)] * count,
    )(*parts, gate_up_full, down_full)


def feed_back(gz_parts, n2_parts, gu_parts, gate_up_full, down_full, dp_place, group_count):
    line = group_count // 2
    half = line // 2
    chunk = D // group_count
    count = len(gz_parts)
    gu_count = len(gu_parts)
    part_rows = gz_parts[0].shape[0]
    rows = count * part_rows
    units = down_full.shape[0]
    steps = pl.cdiv(units, TILE)
    last = units - (steps - 1) * TILE

    def kernel(*refs):
        place_ref, *refs = refs
        gz_refs = refs[:count]
        n2_refs = refs[count : 2 * count]
        gu_refs = refs[2 * count : 2 * count + gu_count]
        w_ref, d_ref = refs[2 * count + gu_count : 2 * count + gu_count + 2]
        keep_near, keep_far, send_near, send_far, down_ref, own_ref, across_ref, pair_ref = refs[
            2 * count + gu_count + 2 : 2 * count + gu_count + 10
        ]
        total, gz, n2t = refs[-3:]
        side, mine = place_ref[0] % 2, place_ref[0] // 2
        step = pl.program_id(0)

        @pl.when(step == 0)
        def _():
            total[...] = jnp.zeros_like(total)
            for place in range(count):
                here = slice(place * part_rows, place * part_rows + part_rows)
                gz[here, :] = gz_refs[place][...]
                n2t[:, here] = n2_refs[place][...].T

        def work(width):
            gu = jnp.concatenate([ref[:, : 2 * width] for ref in gu_refs], axis=0).astype(jnp.float32)
            gate, up = gu[:, :width], gu[:, width:]
            sig = jax.nn.sigmoid(gate)
            act = gate * sig
            hidden = (act * up).astype(jnp.bfloat16)
            down_ref[:width, :] = dot(hidden, gz[...], TN).astype(jnp.bfloat16)
            grad = dot(gz[...], d_ref[:width, :], NT)
            d_gate = grad * up * (sig + act * (1.0 - sig))
            d_up = grad * act
            both = jnp.concatenate([d_gate, d_up], axis=1).astype(jnp.bfloat16)
            part = dot(n2t[...], both)
            for spot in range(line):
                even = part[2 * spot * chunk : (2 * spot + 1) * chunk].astype(jnp.bfloat16)
                odd = part[(2 * spot + 1) * chunk : (2 * spot + 2) * chunk].astype(jnp.bfloat16)
                keep = jnp.where(side == 0, even, odd)
                send = jnp.where(side == 0, odd, even)
                slot = mine ^ spot

                @pl.when(slot < half)
                def _():
                    keep_near[slot, :, : 2 * width] = keep
                    send_near[slot, :, : 2 * width] = send

                @pl.when(slot >= half)
                def _():
                    keep_far[slot - half, :, : 2 * width] = keep
                    send_far[slot - half, :, : 2 * width] = send

            return dot(both, w_ref[:, : 2 * width], NT)

        @pl.when(step < steps - 1)
        def _():
            total[...] += work(TILE)

        @pl.when(step == steps - 1)
        def _():
            summed = (total[...] + work(last)).astype(jnp.bfloat16)
            own_ref[...] = summed[:part_rows]
            pair_ref[0] = summed[part_rows : 2 * part_rows]
            across_ref[...] = summed[2 * part_rows : 3 * part_rows]
            pair_ref[1] = summed[3 * part_rows :]

    whole = lambda step: (0, 0)
    return call(
        kernel,
        [
            ((half, chunk, 2 * units), jnp.bfloat16),
            ((half, chunk, 2 * units), jnp.bfloat16),
            ((half, chunk, 2 * units), jnp.bfloat16),
            ((half, chunk, 2 * units), jnp.bfloat16),
            ((units, D), jnp.bfloat16),
            ((part_rows, D), jnp.bfloat16),
            ((part_rows, D), jnp.bfloat16),
            ((2, part_rows, D), jnp.bfloat16),
        ],
        25.0,
        [
            pltpu.VMEM((rows, D), jnp.float32),
            pltpu.VMEM((rows, D), jnp.bfloat16),
            pltpu.VMEM((D, rows), jnp.bfloat16),
        ],
        limit=56,
        grid=(steps,),
        in_specs=[pl.BlockSpec(memory_space=pltpu.SMEM)]
        + [pl.BlockSpec((part_rows, D), whole)] * (2 * count)
        + [pl.BlockSpec((rows // gu_count, 2 * TILE), lambda step: (0, step))] * gu_count
        + [
            pl.BlockSpec((D, 2 * TILE), lambda step: (0, step)),
            pl.BlockSpec((TILE, D), lambda step: (step, 0)),
        ],
        out_specs=[
            pl.BlockSpec((half, chunk, 2 * TILE), lambda step: (0, 0, step)),
            pl.BlockSpec((half, chunk, 2 * TILE), lambda step: (0, 0, step)),
            pl.BlockSpec((half, chunk, 2 * TILE), lambda step: (0, 0, step)),
            pl.BlockSpec((half, chunk, 2 * TILE), lambda step: (0, 0, step)),
            pl.BlockSpec((TILE, D), lambda step: (step, 0)),
            pl.BlockSpec((part_rows, D), whole),
            pl.BlockSpec((part_rows, D), whole),
            pl.BlockSpec((2, part_rows, D), lambda step: (0, 0, 0)),
        ],
    )(dp_place.reshape(1).astype(jnp.int32), *gz_parts, *n2_parts, *gu_parts, gate_up_full, down_full)


def norm_back(rows, gain, grad):
    inv_root = inverse_root(rows)
    normal = rows * inv_root
    gain_part = jnp.sum(grad * normal, axis=0, keepdims=True)
    weighted = grad * gain
    inner = jnp.mean(weighted * normal, axis=-1, keepdims=True)
    return gain_part, inv_root * (weighted - normal * inner)


def attention_back(upstream, middle, gain, terms, second_full, queries, kv_blocks, biases, cos_wide, sin_wide):
    count = len(terms)
    rows = middle.shape[0]
    span = rows // 2
    wide = GROUP * span

    def kernel(*refs):
        up_ref, mid_ref, gain_ref = refs[:3]
        term_refs = refs[3 : 3 + count]
        w_ref, q_ref, kv0, kv1, kv2, kv3, bias_ref, cos_ref, sin_ref = refs[3 + count : 12 + count]
        gm_ref, gy_ref, dgain_ref, gq_ref, own_ref, d1, d2, d3, go_ref, dkv = refs[12 + count :]
        kvs = (kv0, kv1, kv2, kv3)
        grad = term_refs[0][...].astype(jnp.float32)
        for term in term_refs[1:]:
            grad = grad + term[...].astype(jnp.float32)
        gain_part, back = norm_back(mid_ref[...], gain_ref[...], grad)
        dgain_ref[...] = gain_part
        grad_middle = up_ref[...].astype(jnp.float32) + back
        gm_ref[...] = grad_middle
        grad_low = grad_middle.astype(jnp.bfloat16)
        gy_ref[...] = grad_low
        for tile in range(D // 128):
            start = KV_WIDTH
            block = dot(grad_low, w_ref[tile * 128 : tile * 128 + 128, start:], NT).astype(jnp.bfloat16)
            for part in range(2):
                head = 2 * tile + part
                place = (head % GROUP) * span
                for half in range(2):
                    go_ref[head // GROUP, half, place : place + span, :] = block[
                        half * span : half * span + span, part * HEAD : part * HEAD + HEAD
                    ]
        for group in range(KV_HEADS):
            key_lanes = slice(group * HEAD, group * HEAD + HEAD)
            value_lanes = slice(KV_WIDTH + group * HEAD, KV_WIDTH + group * HEAD + HEAD)
            keys = [key_part(kvs, half, key_lanes) for half in range(2)]
            values = [key_part(kvs, half, value_lanes) for half in range(2)]
            for half in range(2):
                query = q_ref[group, half] * jnp.bfloat16(SCALE)
                grad_out = go_ref[group, half]
                bias = jnp.concatenate([bias_ref[half]] * GROUP, axis=1)
                use = [half] if half == 0 else [1, 0]
                scores = []
                top = None
                for which in use:
                    score = dot(keys[which], query, NT)
                    if which == half:
                        score = score + bias
                    scores.append(score)
                    best = jnp.max(score, axis=0, keepdims=True)
                    top = best if top is None else jnp.maximum(top, best)
                weights = [jnp.exp(score - top) for score in scores]
                total = sum(jnp.sum(weight, axis=0, keepdims=True) for weight in weights)
                scale = 1.0 / total
                probs = [weight * scale for weight in weights]
                grads = [dot(values[which], grad_out, NT) for which in use]
                inner = sum(
                    jnp.sum(prob * grad_prob, axis=0, keepdims=True)
                    for prob, grad_prob in zip(probs, grads)
                )
                grad_query = None
                for which, prob, grad_prob in zip(use, probs, grads):
                    grad_score = (prob * (grad_prob - inner)).astype(jnp.bfloat16)
                    value_grad = dot(prob.astype(jnp.bfloat16), grad_out)
                    key_grad = dot(grad_score, query)
                    if half == 0:
                        dkv[group, which] = key_grad
                        dkv[KV_HEADS + group, which] = value_grad
                    elif which == 0:
                        dkv[group, which] += key_grad
                        dkv[KV_HEADS + group, which] += value_grad
                    else:
                        dkv[group, which] = key_grad
                        dkv[KV_HEADS + group, which] = value_grad
                    term = dot(keys[which].T, grad_score)
                    grad_query = term if grad_query is None else grad_query + term
                grad_query = grad_query * SCALE
                cos_w = cos_ref[half * span : half * span + span, :]
                sin_w = sin_ref[half * span : half * span + span, :]
                for member in range(GROUP):
                    head = group * GROUP + member
                    piece = grad_query[:, member * span : member * span + span].T
                    pair = jnp.concatenate([piece, piece], axis=1)
                    turned = turn(pair, cos_w, -sin_w)[:, :HEAD]
                    gq_ref[half * span : half * span + span, head * HEAD : head * HEAD + HEAD] = (
                        turned.astype(jnp.bfloat16)
                    )
        for place, out in enumerate((own_ref, d1, d2, d3)):
            for half in range(2):
                block = jnp.concatenate(
                    [dkv[lane, half, place * span : place * span + span, :] for lane in range(2 * KV_HEADS)],
                    axis=1,
                )
                out[half * span : half * span + span, :] = block.astype(out.dtype)

    return call(
        kernel,
        [
            ((rows, D), jnp.float32),
            ((rows, D), jnp.bfloat16),
            ((1, D), jnp.float32),
            ((rows, D), jnp.bfloat16),
            ((rows, 2 * KV_WIDTH), jnp.float32),
        ]
        + [((rows, 2 * KV_WIDTH), jnp.bfloat16)] * 3,
        13.0,
        [
            pltpu.VMEM((KV_HEADS, 2, wide, HEAD), jnp.bfloat16),
            pltpu.VMEM((2 * KV_HEADS, 2, 4 * span, HEAD), jnp.float32),
        ],
    )(upstream, middle, gain, *terms, second_full, queries, *kv_blocks, biases, cos_wide, sin_wide)


def before_back(kv_terms, gq, x, gain, grad_middle, first_full, second_full, cos_wide, sin_wide):
    rows = x.shape[0]
    count = len(kv_terms)

    def kernel(*refs):
        kv_refs = refs[:count]
        gq_ref, x_ref, gain_ref, gm_ref, w1_ref, w2_ref, cos_ref, sin_ref = refs[count : count + 8]
        up_ref, low_ref, gkv_ref, dgain_ref, bias_one, bias_two = refs[count + 8 :]
        grad = kv_refs[0][...].astype(jnp.float32)
        for ref in kv_refs[1:]:
            grad = grad + ref[...].astype(jnp.float32)
        grad_key = turn(grad[:, :KV_WIDTH], cos_ref[...], -sin_ref[...]).astype(jnp.bfloat16)
        grad_value = grad[:, KV_WIDTH:].astype(jnp.bfloat16)
        gkv_ref[:, :KV_WIDTH] = grad_key
        gkv_ref[:, KV_WIDTH:] = grad_value
        grad_query = gq_ref[...]
        bias_one[:, :D] = jnp.sum(grad_query.astype(jnp.float32), axis=0, keepdims=True)
        bias_one[:, D:] = jnp.sum(grad_key.astype(jnp.float32), axis=0, keepdims=True)
        bias_two[...] = jnp.sum(grad_value.astype(jnp.float32), axis=0, keepdims=True)
        grad_normed = (
            dot(grad_query, w1_ref[:, :D], NT)
            + dot(grad_key, w1_ref[:, D:], NT)
            + dot(grad_value, w2_ref[:, :KV_WIDTH], NT)
        )
        gain_part, back = norm_back(x_ref[...], gain_ref[...], grad_normed)
        dgain_ref[...] = gain_part
        upstream = gm_ref[...] + back
        up_ref[...] = upstream
        low_ref[...] = upstream.astype(jnp.bfloat16)

    return call(
        kernel,
        [
            ((rows, D), jnp.float32),
            ((rows, D), jnp.bfloat16),
            ((rows, 2 * KV_WIDTH), jnp.bfloat16),
            ((1, D), jnp.float32),
            ((1, SPLIT), jnp.float32),
            ((1, KV_WIDTH), jnp.float32),
        ],
        2.4,
    )(*kv_terms, gq, x, gain, grad_middle, first_full, second_full, cos_wide, sin_wide)


def unit_pieces(unit_rows, group_count, seq_devices):
    units = unit_rows * group_count
    steps = pl.cdiv(units, TILE)
    pieces = []
    for owner in range(seq_devices):
        for kind in range(2):
            for group in range(group_count):
                unit = group * unit_rows
                stop = unit + unit_rows
                column = kind * units * seq_devices + (group * seq_devices + owner) * unit_rows
                while unit < stop:
                    step = unit // TILE
                    end = min(stop, (step + 1) * TILE)
                    width = TILE if step < steps - 1 else units - (steps - 1) * TILE
                    inside = 2 * step * TILE + kind * width + unit - step * TILE
                    pieces.append((owner, inside, column, end - unit))
                    column += end - unit
                    unit = end
    return pieces


def spread_columns(weight, place, unit_rows, group_count, seq_devices):
    layers, rows, columns = weight.shape
    quarter = columns // seq_devices
    pieces = unit_pieces(unit_rows, group_count, seq_devices)

    def kernel(place_ref, w_ref, *refs):
        outs, wide, narrow = refs[:seq_devices], refs[-2], refs[-1]
        for layer in range(layers):
            wide[...] = w_ref[layer].astype(jnp.float32)
            for owner in range(seq_devices):
                for who, inside, column, width in pieces:
                    if who == owner:
                        narrow[:, inside : inside + width] = wide[:, column : column + width]
                block = narrow[...].astype(jnp.bfloat16)
                for bit in range(seq_devices):

                    @pl.when(place_ref[0] == owner ^ bit)
                    def _():
                        outs[bit][layer] = block

    return call(
        kernel,
        [((layers, rows, quarter), jnp.bfloat16)] * seq_devices,
        2.5,
        [pltpu.VMEM((rows, columns), jnp.float32), pltpu.VMEM((rows, quarter), jnp.float32)],
        in_specs=[pl.BlockSpec(memory_space=pltpu.SMEM), FULL],
        out_specs=[FULL] * seq_devices,
    )(place.reshape(1).astype(jnp.int32), weight)


def collect_columns(blocks, place, unit_rows, group_count):
    count = len(blocks)
    rows, quarter = blocks[0].shape
    pieces = unit_pieces(unit_rows, group_count, count)

    def kernel(place_ref, *refs):
        out_ref, narrow = refs[count:]
        me = place_ref[0]
        for owner in range(count):
            for bit in range(count):

                @pl.when(me == owner ^ bit)
                def _():
                    narrow[...] = refs[bit][...].astype(jnp.float32)

            for who, inside, column, width in pieces:
                if who == owner:
                    out_ref[:, column : column + width] = narrow[:, inside : inside + width]

    return call(
        kernel,
        [((rows, count * quarter), jnp.float32)],
        1.5,
        [pltpu.VMEM((rows, quarter), jnp.float32)],
        in_specs=[pl.BlockSpec(memory_space=pltpu.SMEM)] + [FULL] * count,
        out_specs=[FULL],
    )(place.reshape(1).astype(jnp.int32), *blocks)[0]


def join_rows(blocks, place):
    owners = len(blocks)
    layers, rows, columns = blocks[0].shape

    def kernel(place_ref, *refs):
        ins, outs = refs[:owners], refs[owners:]
        for layer in range(layers):
            parts = []
            for owner in range(owners):
                part = ins[0][layer].astype(jnp.float32)
                for bit in range(1, owners):
                    part = jnp.where(
                        place_ref[0] == owner ^ bit, ins[bit][layer].astype(jnp.float32), part
                    )
                parts.append(part)
            outs[layer][0] = jnp.concatenate(parts, axis=0).astype(jnp.bfloat16)

    return call(
        kernel,
        [((1, owners * rows, columns), jnp.bfloat16)] * layers,
        2.0,
        in_specs=[pl.BlockSpec(memory_space=pltpu.SMEM)] + [FULL] * owners,
        out_specs=[FULL] * layers,
    )(place.reshape(1).astype(jnp.int32), *blocks)


def split_rows(terms, place, count):
    number, total_rows, columns = terms.shape
    rows = total_rows // count

    def kernel(place_ref, in_ref, *outs):
        total = in_ref[0].astype(jnp.float32)
        for k in range(1, number):
            total = total + in_ref[k].astype(jnp.float32)
        for owner in range(count):
            block = total[owner * rows : owner * rows + rows].astype(jnp.bfloat16)
            for bit in range(count):

                @pl.when(place_ref[0] == owner ^ bit)
                def _():
                    outs[bit][...] = block

    return call(
        kernel,
        [((rows, columns), jnp.bfloat16)] * count,
        2.0,
        in_specs=[pl.BlockSpec(memory_space=pltpu.SMEM), FULL],
        out_specs=[FULL] * count,
    )(place.reshape(1).astype(jnp.int32), terms)


def lay_out(blocks, places):
    total = len(places)
    shape = blocks[0].shape[-2:]
    count = len(blocks)

    def kernel(place_ref, *refs):
        ins, out, sems = refs[:count], refs[count], refs[-1]
        copies = []
        spot = 0
        for which in range(count):
            many = blocks[which].shape[0] if blocks[which].ndim == 3 else 1
            for k in range(many):
                source = ins[which].at[k] if blocks[which].ndim == 3 else ins[which]
                copies.append(
                    pltpu.make_async_copy(source, out.at[place_ref[spot]], sems.at[spot])
                )
                spot += 1
        for copy in copies:
            copy.start()
        for copy in copies:
            copy.wait()

    outside = pl.BlockSpec(memory_space=pltpu.HBM)
    return call(
        kernel,
        [((total,) + shape, blocks[0].dtype)],
        2.5,
        [pltpu.SemaphoreType.DMA((total,))],
        in_specs=[pl.BlockSpec(memory_space=pltpu.SMEM)] + [outside] * count,
        out_specs=[outside],
    )(jnp.stack(places).astype(jnp.int32), *blocks)[0]


def assemble(parts, places, chip_rows):
    line, rows, width = parts[0].shape

    def kernel(place_ref, *refs):
        ins = refs[:8]
        first_ref, second_ref, small_ref = refs[8:]
        here, chip, side = place_ref[0] == 0, place_ref[1] == 0, place_ref[2] % 2 == 0
        mine = place_ref[2] // 2
        small = jnp.zeros((rows - chip_rows, width), jnp.float32)
        for spot in range(line):
            halves = []
            for half in range(2):
                pieces = []
                blocks = [ins[4 * half + k][spot].astype(jnp.float32) for k in range(4)]
                for block in blocks:
                    small = small + block[chip_rows:]
                lower = [jnp.where(side, blocks[2 * x], blocks[2 * x + 1]) for x in range(2)]
                upper = [jnp.where(side, blocks[2 * x + 1], blocks[2 * x]) for x in range(2)]
                for pair in (lower, upper):
                    pieces.append(jnp.where(chip, pair[0], pair[1])[:chip_rows])
                    pieces.append(jnp.where(chip, pair[1], pair[0])[:chip_rows])
                halves.append(jnp.concatenate(pieces, axis=0).astype(jnp.bfloat16))
            first_ref[mine ^ spot] = jnp.where(here, halves[0], halves[1])
            second_ref[mine ^ spot] = jnp.where(here, halves[1], halves[0])
        small_ref[...] = small

    first, second, small = call(
        kernel,
        [
            ((line, 4 * chip_rows, width), jnp.bfloat16),
            ((line, 4 * chip_rows, width), jnp.bfloat16),
            ((rows - chip_rows, width), jnp.float32),
        ],
        4.0,
        in_specs=[pl.BlockSpec(memory_space=pltpu.SMEM)] + [FULL] * 8,
        out_specs=[FULL] * 3,
    )(jnp.stack(places).astype(jnp.int32), *parts)
    return first.reshape(-1, width), second.reshape(-1, width), small


def projection_grads(normed, grad_query, grad_kv, mixed, grad_low, gain_one, gain_two, bias_one, bias_two, places, chip_rows, line):
    width = SPLIT

    def kernel(place_ref, n_ref, gq_ref, gkv_ref, mixed_ref, gy_ref, g1_ref, g2_ref, b1_ref, b2_ref, keep0, keep1, send0, send1, pad):
        here, chip, side = place_ref[0] == 0, place_ref[1] == 0, place_ref[2] % 2
        mine = place_ref[2] // 2
        turned = n_ref[...].T
        pad[...] = jnp.zeros_like(pad)
        pad[0:1, :D] = g1_ref[...]
        pad[1:2, :D] = g2_ref[...]
        pad[2:3, :] = b1_ref[...]
        pad[3:4, :KV_WIDTH] = b2_ref[...]
        small = pad[...]
        first = jnp.concatenate(
            [dot(turned, gq_ref[...]), dot(turned, gkv_ref[:, :KV_WIDTH])], axis=1
        )
        second = jnp.concatenate(
            [dot(turned, gkv_ref[:, KV_WIDTH:]), dot(mixed_ref[...], gy_ref[...], TN)], axis=1
        )

        def chunk(part, number):
            rows = part[number * chip_rows : (number + 1) * chip_rows]
            return jnp.concatenate([rows, small], axis=0).astype(jnp.bfloat16)

        for spot in range(line):
            for pair in range(2):
                slot = side ^ pair
                firsts = [chunk(first, 4 * spot + 2 * pair + x) for x in range(2)]
                seconds = [chunk(second, 4 * spot + 2 * pair + x) for x in range(2)]
                keeps = [jnp.where(here, one, two) for one, two in zip(firsts, seconds)]
                sends = [jnp.where(here, two, one) for one, two in zip(firsts, seconds)]
                keep0[slot, mine ^ spot] = jnp.where(chip, keeps[0], keeps[1])
                keep1[slot, mine ^ spot] = jnp.where(chip, keeps[1], keeps[0])
                send0[slot, mine ^ spot] = jnp.where(chip, sends[0], sends[1])
                send1[slot, mine ^ spot] = jnp.where(chip, sends[1], sends[0])

    return call(
        kernel,
        [((2, line, chip_rows + 8, width), jnp.bfloat16)] * 4,
        6.0,
        [pltpu.VMEM((8, width), jnp.float32)],
        in_specs=[pl.BlockSpec(memory_space=pltpu.SMEM)] + [FULL] * 9,
        out_specs=[FULL] * 4,
    )(
        jnp.stack(places).astype(jnp.int32),
        normed,
        grad_query,
        grad_kv,
        mixed,
        grad_low,
        gain_one,
        gain_two,
        bias_one,
        bias_two,
    )


def swap(values, axis, bit):
    size = lax.axis_size(axis)
    return lax.ppermute(values, axis, [(i, i ^ bit) for i in range(size)])


def after(values, *others):
    return lax.optimization_barrier((values,) + tuple(others))[0]


def line_bits():
    bits = [1]
    while 4 * bits[-1] < lax.axis_size("dp"):
        bits.append(2 * bits[-1])
    return bits


def line_gather(values, bits):
    for bit in bits:
        values = jnp.concatenate([values, swap(values, "dp", 2 * bit)], axis=0)
    return values


def line_scatter(values, bits):
    for bit in bits[:0:-1]:
        values = add_low(values[:bit], swap(values[bit:], "dp", 2 * bit))
    return [values[0], swap(values[1], "dp", 2)]


def add_low(left, right):
    return (left.astype(jnp.float32) + right.astype(jnp.float32)).astype(jnp.bfloat16)


def group_rows(values):
    beside = swap(values, "seq", 1)
    across = swap(values, "seq", 2)
    return [values, beside, across, swap(across, "seq", 1)]


def placed(values, offset, width):
    return lax.dynamic_update_slice(jnp.zeros((width,), values.dtype), values, (offset,))


def body(
    tokens,
    cotangent,
    span_order,
    attn_gain,
    joined_weight,
    joined_bias,
    out_weight,
    mlp_gain,
    gate_up_weight,
    down_weight,
):
    seq_count, tok_len, model_width = tokens.shape
    span_len = tok_len // 2
    group_count = lax.axis_size("dp")
    seq_devices = lax.axis_size("seq")
    unit_rows = down_weight.shape[1]
    width_rows = gate_up_weight.shape[1]
    units = group_count * unit_rows
    dp_place = lax.axis_index("dp")
    seq_place = lax.axis_index("seq")
    core = seq_place % 2
    chip_x = seq_place // 2
    device = dp_place * seq_devices + seq_place
    chip_rows = 2 * width_rows
    line = group_count // 2
    side = dp_place % 2

    order = [lax.dynamic_slice(span_order, (0, seq_place ^ bit), (1, 1))[0, 0] for bit in range(4)]
    inside = jnp.arange(span_len, dtype=jnp.int32)
    own_places = jnp.concatenate(
        [order[0] * span_len + inside, (2 * seq_devices - 1 - order[0]) * span_len + inside]
    )
    half_biases = []
    for half in range(2):
        blocks = []
        for bit in range(4):
            ahead = order[bit] < order[0] if half == 0 else order[bit] > order[0]
            allowed = ahead | ((order[bit] == order[0]) & (inside[:, None] >= inside[None, :]))
            blocks.append(jnp.where(allowed, 0.0, NEGATIVE).astype(jnp.float32))
        half_biases.append(jnp.concatenate(blocks, axis=1))
    biases = jnp.stack(half_biases)
    biases_turned = jnp.swapaxes(biases, 1, 2)
    cos_table, sin_table = rotary_tables(own_places)
    cos_wide = jnp.concatenate([cos_table] * 4, axis=1)
    sin_wide = jnp.concatenate([-sin_table, sin_table] * 2, axis=1)

    def attn_shard(layer):
        first = joined_weight[layer][:, :SPLIT]
        second = jnp.concatenate([joined_weight[layer][:, SPLIT:], out_weight[layer]], axis=1)
        got = swap(jnp.where(core == 0, second, first), "seq", 1)
        mine = jnp.where(core == 0, first, second)
        rows = jnp.where(core == 0, jnp.stack([mine, got]), jnp.stack([got, mine])).reshape(
            chip_rows, -1
        )
        bias_all = placed(joined_bias[layer], device * joined_bias.shape[1], SPLIT + KV_WIDTH)
        extra = jnp.zeros((8, SPLIT), jnp.bfloat16)
        extra = extra.at[0].set(placed(attn_gain[layer], device * width_rows, SPLIT))
        extra = extra.at[1].set(placed(mlp_gain[layer], device * width_rows, SPLIT))
        extra = extra.at[2].set(bias_all[:SPLIT])
        extra = extra.at[3, :KV_WIDTH].set(bias_all[SPLIT:])
        return jnp.concatenate([rows, extra], axis=0)

    def attn_finish(near):
        far = swap(near, "dp", 1)
        across = swap(near, "seq", 2)
        parts = [near, far, across, swap(far, "seq", 2)]
        parts = parts + [swap(part, "seq", 1) for part in parts]
        first_full, second_full, small = assemble(parts, [core, chip_x, dp_place], chip_rows)
        return (
            first_full,
            second_full,
            small[0:1, :model_width],
            small[1:2, :model_width],
            small[2:3],
            small[3:4, :KV_WIDTH],
        )

    bits = line_bits()
    spread = spread_columns(gate_up_weight, seq_place, unit_rows, group_count, seq_devices)
    shards = [attn_shard(layer)[None] for layer in range(LAYERS)]
    down_full = [
        lax.all_gather(down_weight[layer], "dp", axis=0, tiled=True) for layer in range(LAYERS)
    ]
    gate_blocks = [spread[0]] + [swap(spread[bit], "seq", bit) for bit in range(1, 4)]
    gate_shards = join_rows(gate_blocks, seq_place)
    attn_near = [line_gather(after(shards[0], *spread), bits)]
    attn_near.append(line_gather(after(shards[1], attn_near[0]), bits))
    gate_near = []
    gate_far = []
    gate_near_pair = []
    started = attn_near[0]
    for layer in range(LAYERS):
        gate_near.append(line_gather(after(gate_shards[layer], started), bits[:-1]))
        gate_far.append(swap(gate_near[layer], "dp", 2 * bits[-1]))
        gate_near_pair.append(swap(gate_near[layer], "dp", 1))
        started = gate_far[layer]
    attn_sets = [attn_finish(after(attn_near[0], *gate_shards)), attn_finish(attn_near[1])]
    half = line // 2
    offsets = [dp_place ^ (2 * k) for k in range(line)]
    places = offsets + [offset ^ 1 for offset in offsets]

    def gate_finish(layer):
        far_pair = swap(gate_far[layer], "dp", 1)
        blocks = [gate_near[layer], gate_far[layer], gate_near_pair[layer], far_pair]
        return lay_out(blocks, places).reshape(model_width, 2 * units)

    terms = [tokens.reshape(tok_len, model_width)]
    kept_state = []
    gate_up_full = []
    for layer in range(LAYERS):
        first_full, second_full, gain_full, mlp_gain_full, bias_first, bias_second = attn_sets[layer]
        x, normed, queries, own_kv = before_attention(
            terms,
            after(gain_full, gate_near[0], attn_near[1]) if layer == 0 else after(gain_full, gate_far[1]),
            first_full,
            second_full,
            bias_first,
            bias_second,
            cos_wide,
            sin_wide,
        )
        kv_blocks = [own_kv] + [swap(own_kv, "seq", bit) for bit in range(1, 4)]
        waited = (gate_near_pair[layer],)
        mixed, middle, n2 = attention(
            queries, kv_blocks, biases, x, second_full, after(mlp_gain_full, *waited)
        )
        n2_parts = group_rows(n2)
        gate_up_full.append(gate_finish(layer))
        gu_near, *outs_near = feed_forward(n2_parts[:2], gate_up_full[layer], down_full[layer])
        gu_far, *outs_far = feed_forward(n2_parts[2:], gate_up_full[layer], down_full[layer])
        far = add_low(outs_far[0], swap(outs_far[1], "seq", 1))
        terms = [middle, outs_near[0], swap(outs_near[1], "seq", 1), swap(far, "seq", 2)]
        kept_state.append((x, normed, queries, kv_blocks, mixed, middle, n2_parts, [gu_near, gu_far]))
    activations = sum(term.astype(jnp.float32) for term in terms).astype(jnp.bfloat16)
    upstream = cotangent.reshape(tok_len, model_width)
    upstream_low = upstream
    results = [None] * LAYERS
    before = None

    def send_attn(state, pair, *waited):
        near, far, got_near, got_far = state["attn_parts"]
        return swap(after(add_low(far[pair], got_far[pair]), *waited), "seq", 2)

    def sum_attn(state, arrived, *waited):
        near, far, got_near, got_far = state["attn_parts"]
        sums = [
            (
                near[pair].astype(jnp.float32)
                + got_near[pair].astype(jnp.float32)
                + after(arrived[pair], *waited).astype(jnp.float32)
            ).astype(jnp.bfloat16)
            for pair in range(2)
        ]
        return add_low(sums[0], swap(sums[1], "dp", 1))

    def sum_gate(state, *waited):
        near = add_low(state["keep_near"], after(state["near_got"], *waited))
        return add_low(near, after(state["gate_got"], *waited))

    def finish(state, gate_sum, attn_sum, *waited):
        gate_terms = jnp.stack(line_scatter(gate_sum, bits[:-1]))
        gate_rows = split_rows(after(gate_terms, *waited), seq_place, seq_devices)
        gate_owned = collect_columns(
            [gate_rows[0]] + [swap(gate_rows[bit], "seq", bit) for bit in range(1, 4)],
            seq_place,
            unit_rows,
            group_count,
        )
        owned = sum(
            term.astype(jnp.float32) for term in line_scatter(attn_sum, bits)
        )
        extra = owned[chip_rows:]
        halves = owned[:chip_rows].reshape(2, width_rows, -1)
        mine = lax.dynamic_index_in_dim(halves, core, 0, keepdims=False)
        theirs = swap(
            lax.dynamic_index_in_dim(halves, 1 - core, 0, keepdims=False), "seq", 1
        )
        first_own = jnp.where(core == 0, mine, theirs)
        second_own = jnp.where(core == 0, theirs, mine)

        def cut(row, width, stop):
            return lax.dynamic_slice(extra[row, :stop], (device * width,), (width,))

        results[state["layer"]] = (
            cut(0, width_rows, model_width),
            jnp.concatenate([first_own, second_own[:, :KV_WIDTH]], axis=1),
            cut(2, SPLIT // (group_count * seq_devices), SPLIT),
            cut(3, KV_WIDTH // (group_count * seq_devices), KV_WIDTH),
            second_own[:, KV_WIDTH:],
            cut(1, width_rows, model_width),
            gate_owned,
            state["down_sum"],
        )

    for layer in reversed(range(LAYERS)):
        x, normed, queries, kv_blocks, mixed, middle, n2_parts, gu_parts = kept_state[layer]
        first_full, second_full, gain_full, mlp_gain_full, _, _ = attn_sets[layer]
        low_parts = group_rows(upstream_low)
        if before is not None:
            low_parts[0] = after(low_parts[0], before["attn_parts"][3])
        keep_near, keep_far, send_near, send_far, down_part, own_out, across_out, pair_out = feed_back(
            low_parts,
            n2_parts,
            gu_parts,
            gate_up_full[layer],
            down_full[layer],
            dp_place,
            group_count,
        )
        got = swap(pair_out, "seq", 1)
        out_terms = [own_out, got[0], swap(add_low(across_out, got[1]), "seq", 2)]
        down_sum = lax.psum_scatter(down_part, "dp", scatter_dimension=0, tiled=True).astype(
            jnp.float32
        )
        got_far = swap(send_far, "dp", 1)
        gate_far_sum = add_low(keep_far, got_far)
        near_got = swap(after(send_near, got_far), "dp", 1)
        if before is not None:
            attn_far = send_attn(before, 1, out_terms[2])
            gate_before = sum_gate(before, own_out)
        grad_middle, grad_low, mlp_gain_part, grad_query, own_term, *kv_terms = attention_back(
            upstream,
            middle,
            mlp_gain_full,
            out_terms,
            second_full,
            queries,
            kv_blocks,
            biases_turned,
            cos_wide,
            sin_wide,
        )
        kv_terms = [own_term] + [swap(kv_terms[bit - 1], "seq", bit) for bit in range(1, 4)]
        if before is not None:
            attn_near_sent = send_attn(before, 0, *kv_terms[1:])
        upstream, upstream_low, grad_kv, attn_gain_part, bias_first, bias_second = before_back(
            kv_terms,
            grad_query,
            x,
            after(gain_full, gate_far_sum)
            if before is None
            else after(gain_full, gate_far_sum, gate_before),
            grad_middle,
            first_full,
            second_full,
            cos_wide,
            sin_wide,
        )
        near, far, near_other, far_other = projection_grads(
            normed,
            grad_query,
            grad_kv,
            mixed,
            grad_low,
            attn_gain_part,
            mlp_gain_part,
            bias_first,
            bias_second,
            [core, chip_x, dp_place],
            chip_rows,
            line,
        )
        got_far_other = swap(far_other, "seq", 1)
        got_near_other = swap(near_other, "seq", 1)
        state = {
            "layer": layer,
            "keep_near": keep_near,
            "near_got": near_got,
            "gate_got": swap(after(gate_far_sum, upstream_low), "dp", 2 * bits[-1]),
            "attn_parts": (near, far, got_near_other, got_far_other),
            "down_sum": down_sum,
        }
        if before is not None:
            attn_sum = sum_attn(before, [attn_near_sent, attn_far], grad_low)
            finish(before, gate_before, attn_sum, near)
        before = state
    arrived = [None, send_attn(before, 1)]
    arrived[0] = send_attn(before, 0)
    finish(before, sum_gate(before), sum_attn(before, arrived))
    return (
        activations.reshape(seq_count, tok_len, model_width),
        upstream.reshape(seq_count, tok_len, model_width),
    ) + tuple(jnp.stack([results[layer][k] for layer in range(LAYERS)]) for k in range(8))


def solution(mesh):
    in_specs = (
        P("dp", "seq", None),
        P("dp", "seq", None),
        P("dp", None),
        P(None, ("dp", "seq")),
        P(None, ("dp", "seq"), None),
        P(None, ("dp", "seq")),
        P(None, ("dp", "seq"), None),
        P(None, ("dp", "seq")),
        P(None, ("dp", "seq"), None),
        P(None, ("dp", "seq"), None),
    )
    out_specs = (
        P("dp", "seq", None),
        P("dp", "seq", None),
        P(None, ("dp", "seq")),
        P(None, ("dp", "seq"), None),
        P(None, ("dp", "seq")),
        P(None, ("dp", "seq")),
        P(None, ("dp", "seq"), None),
        P(None, ("dp", "seq")),
        P(None, ("dp", "seq"), None),
        P(None, ("dp", "seq"), None),
    )
    return jax.shard_map(body, mesh=mesh, in_specs=in_specs, out_specs=out_specs, check_vma=False)
```

time: 1570 us -> 676 us (0.43)
  waiting for transfers between devices: 670 us -> 302 us
  blocking collectives: 350 us -> 0 us
  matrix products: 196 us -> 0 us
  Pallas kernels: 0 us -> 177 us
  local copies, waits for them, and re-layouts: 163 us -> 64.1 us
  other arithmetic: 74.1 us -> 31.2 us
  starting transfers between devices: 83.9 us -> 67.2 us
    all_gather x12 -> x2, waiting for transfers between devices: 456 us -> 0.01 us  [body(): lax.all_gather(down_weight[layer], 'dp', axis=0, tiled=True)]
    unnamed x5 -> x0, blocking collectives: 317 us -> none
    ppermute x0 -> x95, waiting for transfers between devices: none -> 302 us  [swap(): return lax.ppermute(values, axis, [(i, i ^ bit) for i in range(size)])]
    dot_general x48 -> x0, matrix products: 196 us -> none  [the longest x4 28 us: attend_backward(): jnp.einsum('sqgd,std->sgqt', head_grad, head_value, preferred_element_typ...]
    pallas_call x0 -> x26, Pallas kernels: none -> 177 us  [the longest x2 61 us: feed_back(): call(kernel, [((half, chunk, 2 * units), jnp.bfloat16), ((half, chunk, 2...]
    reduce_scatter x6 -> x0, waiting for transfers between devices: 98.4 us -> none  [the longest x4 59.3 us: group_sums(): lax.psum_scatter(values.reshape(seq_count, -1, model_width).astype(jnp.bf...]
    unnamed x42 -> x6, waiting for transfers between devices: 77.8 us -> 0.07 us
    ppermute x0 -> x95, starting transfers between devices: none -> 67.1 us  [swap(): return lax.ppermute(values, axis, [(i, i ^ bit) for i in range(size)])]
  transfers between devices with their start and end apart: 45 -> 99, of which waited for: 23 -> 35; matrix products, arithmetic and copies ran while one was open for 32% -> 8% of each run, Pallas kernels for 0% -> 22%
where the time goes in v1:
time: 676 us; the launch traced here: 670 us
  waiting for transfers between devices  302 us (45%)
  Pallas kernels  177 us (26%)
  starting transfers between devices  67.2 us (10%)
  local copies, waits for them, and re-layouts  64.1 us (9%)
  other arithmetic  31.2 us (5%)
  between operations  27.9 us (4%)
    ppermute x95, waiting for transfers between devices, swap(): return lax.ppermute(values, axis, [(i, i ^ bit) for i in range(size)])  302 us
    ppermute x95, starting transfers between devices, swap(): return lax.ppermute(values, axis, [(i, i ^ bit) for i in range(size)])  67.1 us
    pallas_call x2, Pallas kernels, feed_back(): call(kernel, [((half, chunk, 2 * units), jnp.bfloat16), ((half, chunk, 2...  61 us
    unnamed x240, local copies, waits for them, and re-layouts  48.4 us
    pallas_call x4, Pallas kernels, feed_forward(): call(kernel, [((rows, 2 * units), jnp.bfloat16)] + [((part_rows, D), jnp....  36 us
    pallas_call x2, Pallas kernels, attention_back(): call(kernel, [((rows, D), jnp.float32), ((rows, D), jnp.bfloat16), ((1, D...  26.7 us
    pallas_call x2, Pallas kernels, attention(): call(kernel, [((rows, D), jnp.bfloat16), ((rows, D), jnp.float32), ((rows...  22.7 us
    convert_element_type x14, other arithmetic, add_low(): (left.astype(jnp.float32) + right.astype(jnp.float32)).astype(jnp.bfloat16)  15.4 us
  transfers between devices with their start and end apart: 99, of which 35 were waited for; matrix products, arithmetic and copies ran while one was open for 8% of the time, Pallas kernels for 22%

profile of v1, /device:TPU:0, one launch (start us, length us, event | category | flops | bytes accessed | tf_op | source)
XLA Modules:
  0.0 669.6 jit_solution(17210647342204666385)
XLA Ops:
  10.6 2.2 spread_columns.1
  13.4 2.6 collective-permute-start.4
  24.0 2.3 collective-permute-start.1
  32.3 2.4 collective-permute-done.1
  38.2 24.0 %collective-permute-done.2 = bf16[2,64,1024]{2,1,0:T(8,128)(2,1)} collective-permute-done((bf16[2,64,1024]{2,1,0:T(8,128)(2,1)}, bf16[2,64,1024]{2,1,0:T(8,128)(2,1)}, u32[]{:S(2)}, u32[]{:S(2)}) %collective-permute-start.2) | collective-permute-done | bytes 262176 | tf_op jit(solution)/shard_map/ppermute | solution.py:767
  63.2 3.5 collective-permute-start.6
  71.1 13.5 %collective-permute-done.15 = bf16[1,64,1024]{2,1,0:T(8,128)(2,1)S(1)} collective-permute-done((bf16[1,64,1024]{2,1,0:T(8,128)(2,1)S(1)}, bf16[1,64,1024]{2,1,0:T(8,128)(2,1)S(1)}, u32[]{:S(2)}, u32[]{:S(2)}) %collective-permute-start.15) | collective-permute-done | bytes 131104 | tf_op jit(solution)/shard_map/ppermute | solution.py:767
  93.6 8.7 %collective-permute-done.16 = bf16[2,64,1024]{2,1,0:T(8,128)(2,1)} collective-permute-done((bf16[2,64,1024]{2,1,0:T(8,128)(2,1)}, bf16[2,64,1024]{2,1,0:T(8,128)(2,1)}, u32[]{:S(2)}, u32[]{:S(2)}) %collective-permute-start.16) | collective-permute-done | bytes 262176 | tf_op jit(solution)/shard_map/ppermute | solution.py:767
  125.5 12.1 %attention.2 = (bf16[256,896]{1,0:T(8,128)(2,1)S(1)}, f32[256,896]{1,0:T(8,128)S(1)}, bf16[256,896]{1,0:T(8,128)(2,1)}) custom-call(bf16[2,2,896,64]{3,2,1,0:T(8,128)(2,1)S(1)} %copy-done.17, bf16[256,256]{1,0:T(8,128)(2,1)S(1)} %get-tuple-element.240.kv0.refs_8_, bf16[256,256]{1,0:T(8,128)(2,1)S(1)} %collective-permute-done.17.kv1.refs_9_, ...), custom_call_target="tpu_custom_call" | custom-call | bytes 4200000 | tf_op jit(solution)/shard_map/attention/pallas_call | solution.py:159
  139.9 30.5 %collective-permute-done.22.refs_1_ = bf16[2,112,2432]{2,1,0:T(8,128)(2,1)} collective-permute-done((bf16[2,112,2432]{2,1,0:T(8,128)(2,1)}, bf16[2,112,2432]{2,1,0:T(8,128)(2,1)}, u32[]{:S(2)}, u32[]{:S(2)}) %collective-permute-start.22) | collective-permute-done | bytes 1089568 | tf_op jit(solution)/shard_map/ppermute | solution.py:767
  174.6 33.3 %collective-permute-done.29.refs_1_ = bf16[4,64,1024]{2,1,0:T(8,128)(2,1)} collective-permute-done((bf16[4,64,1024]{2,1,0:T(8,128)(2,1)}, bf16[4,64,1024]{2,1,0:T(8,128)(2,1)}, u32[]{:S(2)}, u32[]{:S(2)}) %collective-permute-start.29) | collective-permute-done | bytes 524320 | tf_op jit(solution)/shard_map/ppermute | solution.py:767
  212.7 2.5 lay_out.2
  217.3 2.2 copy-done.1
  223.1 8.0 %feed_forward.5 = (bf16[512,2432]{1,0:T(8,128)(2,1)S(1)}, bf16[256,896]{1,0:T(8,128)(2,1)S(1)}, bf16[256,896]{1,0:T(8,128)(2,1)S(1)}) custom-call(bf16[256,896]{1,0:T(8,128)(2,1)S(1)} %copy-done.37, bf16[256,896]{1,0:T(8,128)(2,1)S(1)} %copy-done.39, bf16[896,2432]{1,0:T(8,128)(2,1)S(1)} %bitcast.153, bf16[1216,896]{1,0:T(8,128)(2,1)S(1)} %bitcast.167), custom_call_target="tpu_custom_call" | custom-call | bytes 3600000 | tf_op jit(solution)/shard_map/feed_forward/pallas_call | solution.py:204
  235.1 9.2 %feed_forward.4 = (bf16[512,2432]{1,0:T(8,128)(2,1)S(1)}, bf16[256,896]{1,0:T(8,128)(2,1)S(1)}, bf16[256,896]{1,0:T(8,128)(2,1)S(1)}) custom-call(bf16[256,896]{1,0:T(8,128)(2,1)} %get-tuple-element.244.refs_0_.refs_5_, bf16[256,896]{1,0:T(8,128)(2,1)} %collective-permute-done.21.refs_1_.refs_6_, bf16[896,2432]{1,0:T(8,128)(2,1)S(1)} %bitcast.154, ...), custom_call_target="tpu_custom_call" | custom-call | bytes 3600000 | tf_op jit(solution)/shard_map/feed_forward/pallas_call | solution.py:204
  245.4 3.5 assemble.3
  248.9 12.7 %collective-permute-done.37.refs_1_ = bf16[2,112,2432]{2,1,0:T(8,128)(2,1)} collective-permute-done((bf16[2,112,2432]{2,1,0:T(8,128)(2,1)}, bf16[2,112,2432]{2,1,0:T(8,128)(2,1)}, u32[]{:S(2)}, u32[]{:S(2)}) %collective-permute-start.37) | collective-permute-done | bytes 1089568 | tf_op jit(solution)/shard_map/ppermute | solution.py:767
  267.1 4.5 collective-permute-done.39.kv2.refs_10_
  273.5 10.6 %attention.3 = (bf16[256,896]{1,0:T(8,128)(2,1)S(1)}, f32[256,896]{1,0:T(8,128)S(1)}, bf16[256,896]{1,0:T(8,128)(2,1)}) custom-call(bf16[2,2,896,64]{3,2,1,0:T(8,128)(2,1)S(1)} %get-tuple-element.254.q_ref.refs_7_, bf16[256,256]{1,0:T(8,128)(2,1)S(1)} %get-tuple-element.255.kv0.refs_8_, bf16[256,256]{1,0:T(8,128)(2,1)S(1)} %collective-permute-done.38.kv1.refs_9_, ...), custom_call_target="tpu_custom_call" | custom-call | bytes 4200000 | tf_op jit(solution)/shard_map/attention/pallas_call | solution.py:159
  287.9 11.5 %collective-permute-done.45.refs_0_.refs_7_ = bf16[256,896]{1,0:T(8,128)(2,1)S(1)} collective-permute-done((bf16[256,896]{1,0:T(8,128)(2,1)}, bf16[256,896]{1,0:T(8,128)(2,1)S(1)}, u32[]{:S(2)}, u32[]{:S(2)}) %collective-permute-start.45) | collective-permute-done | bytes 458784 | tf_op jit(solution)/shard_map/ppermute | solution.py:767
  299.9 9.1 %collective-permute-done.50.refs_3_ = bf16[256,896]{1,0:T(8,128)(2,1)} collective-permute-done((bf16[256,896]{1,0:T(8,128)(2,1)}, bf16[256,896]{1,0:T(8,128)(2,1)}, u32[]{:S(2)}, u32[]{:S(2)}) %collective-permute-start.50) | collective-permute-done | bytes 458784 | tf_op jit(solution)/shard_map/ppermute | solution.py:767
  313.2 2.2 copy-done.4
  317.1 9.7 %feed_forward.6 = (bf16[512,2432]{1,0:T(8,128)(2,1)S(1)}, bf16[256,896]{1,0:T(8,128)(2,1)S(1)}, bf16[256,896]{1,0:T(8,128)(2,1)S(1)}) custom-call(bf16[256,896]{1,0:T(8,128)(2,1)} %get-tuple-element.259.refs_0_.refs_5_, bf16[256,896]{1,0:T(8,128)(2,1)} %collective-permute-done.42.refs_1_.refs_6_, bf16[896,2432]{1,0:T(8,128)(2,1)S(1)} %bitcast.156, ...), custom_call_target="tpu_custom_call" | custom-call | bytes 3600000 | tf_op jit(solution)/shard_map/feed_forward/pallas_call | solution.py:204
  328.3 9.1 %feed_forward.7 = (bf16[512,2432]{1,0:T(8,128)(2,1)S(1)}, bf16[256,896]{1,0:T(8,128)(2,1)S(1)}, bf16[256,896]{1,0:T(8,128)(2,1)S(1)}) custom-call(bf16[256,896]{1,0:T(8,128)(2,1)S(1)} %collective-permute-done.45.refs_0_.refs_7_, bf16[256,896]{1,0:T(8,128)(2,1)} %collective-permute-done.46.refs_1_.refs_8_, bf16[896,2432]{1,0:T(8,128)(2,1)S(1)} %bitcast.157, ...), custom_call_target="tpu_custom_call" | custom-call | bytes 3600000 | tf_op jit(solution)/shard_map/feed_forward/pallas_call | solution.py:204
  340.4 30.5 %feed_back.2 = (bf16[2,112,2432]{2,1,0:T(8,128)(2,1)}, bf16[2,112,2432]{2,1,0:T(8,128)(2,1)}, bf16[2,112,2432]{2,1,0:T(8,128)(2,1)}, bf16[2,112,2432]{2,1,0:T(8,...) custom-call(s32[1]{0:T(128)} %bitcast.3.refs_0_, ...), custom_call_target="tpu_custom_call" | custom-call | bytes 10000000 | tf_op jit(solution)/shard_map/feed_back/pallas_call | solution.py:299
  375.8 12.2 %collective-permute-done.53.refs_5_ = bf16[256,896]{1,0:T(8,128)(2,1)S(1)} collective-permute-done((bf16[256,896]{1,0:T(8,128)(2,1)S(1)}, bf16[256,896]{1,0:T(8,128)(2,1)S(1)}, u32[]{:S(2)}, u32[]{:S(2)}) %collective-permute-start.53) | collective-permute-done | bytes 458784 | tf_op jit(solution)/shard_map/ppermute | solution.py:767
  389.0 13.3 %attention_back.2 = (f32[256,896]{1,0:T(8,128)S(1)}, bf16[256,896]{1,0:T(8,128)(2,1)S(1)}, f32[1,896]{1,0:T(1,128)S(1)}, bf16[256,896]{1,0:T(8,128)(2,1)S(1)}, f...) custom-call(bf16[256,896]{1,0:T(8,128)(2,1)} %bitcast.48.refs_1_.ref, ...), custom_call_target="tpu_custom_call" | custom-call | bytes 5200000 | tf_op jit(solution)/shard_map/attention_back/pallas_call | solution.py:442
  406.2 2.5 collective-permute-done.55.refs_2_
  412.1 3.4 projection_grads.2
  418.7 12.0 %collective-permute-done.60.refs_3_ = bf16[256,896]{1,0:T(8,128)(2,1)} collective-permute-done((bf16[256,896]{1,0:T(8,128)(2,1)S(1)}, bf16[256,896]{1,0:T(8,128)(2,1)}, u32[]{:S(2)}, u32[]{:S(2)}) %collective-permute-start.60) | collective-permute-done | bytes 458784 | tf_op jit(solution)/shard_map/ppermute | solution.py:767
  432.9 30.4 %feed_back.3 = (bf16[2,112,2432]{2,1,0:T(8,128)(2,1)}, bf16[2,112,2432]{2,1,0:T(8,128)(2,1)}, bf16[2,112,2432]{2,1,0:T(8,128)(2,1)}, bf16[2,112,2432]{2,1,0:T(8,...) custom-call(s32[1]{0:T(128)} %bitcast.3.refs_0_, ...), custom_call_target="tpu_custom_call" | custom-call | bytes 10000000 | tf_op jit(solution)/shard_map/feed_back/pallas_call | solution.py:299
  463.8 16.4 %collective-permute-done.69 = bf16[2,112,2432]{2,1,0:T(8,128)(2,1)} collective-permute-done((bf16[2,112,2432]{2,1,0:T(8,128)(2,1)}, bf16[2,112,2432]{2,1,0:T(8,128)(2,1)}, u32[]{:S(2)}, u32[]{:S(2)}) %collective-permute-start.69) | collective-permute-done | bytes 1089568 | tf_op jit(solution)/shard_map/ppermute | solution.py:767
  485.7 11.1 %collective-permute-done.63.refs_5_ = bf16[256,896]{1,0:T(8,128)(2,1)S(1)} collective-permute-done((bf16[256,896]{1,0:T(8,128)(2,1)S(1)}, bf16[256,896]{1,0:T(8,128)(2,1)S(1)}, u32[]{:S(2)}, u32[]{:S(2)}) %collective-permute-start.63) | collective-permute-done | bytes 458784 | tf_op jit(solution)/shard_map/ppermute | solution.py:767
  496.8 13.5 %attention_back.3 = (f32[256,896]{1,0:T(8,128)S(1)}, bf16[256,896]{1,0:T(8,128)(2,1)S(1)}, f32[1,896]{1,0:T(1,128)S(1)}, bf16[256,896]{1,0:T(8,128)(2,1)S(1)}, f...) custom-call(f32[256,896]{1,0:T(8,128)S(1)} %copy-done.48, ...), custom_call_target="tpu_custom_call" | custom-call | bytes 5200000 | tf_op jit(solution)/shard_map/attention_back/pallas_call | solution.py:442
  513.8 2.9 collective-permute-done.65.refs_2_
  520.4 2.4 before_back.3
  527.1 2.8 fusion.8
  533.5 14.0 %collective-permute-done.94.refs_3_ = bf16[28,2432]{1,0:T(8,128)(2,1)} collective-permute-done((bf16[28,2432]{1,0:T(8,128)(2,1)}, bf16[28,2432]{1,0:T(8,128)(2,1)}, u32[]{:S(2)}, u32[]{:S(2)}) %collective-permute-start.94) | collective-permute-done | bytes 136224 | tf_op jit(solution)/shard_map/ppermute | solution.py:767
  557.8 4.7 collective-permute-done.78
  564.0 7.8 %collective-permute-done.86 = bf16[2,112,2432]{2,1,0:T(8,128)(2,1)} collective-permute-done((bf16[2,112,2432]{2,1,0:T(8,128)(2,1)}, bf16[2,112,2432]{2,1,0:T(8,128)(2,1)}, u32[]{:S(2)}, u32[]{:S(2)}) %collective-permute-start.86) | collective-permute-done | bytes 1089568 | tf_op jit(solution)/shard_map/ppermute | solution.py:767
  573.9 2.5 collective-permute-done.80
  582.0 17.6 %collective-permute-done.81 = bf16[2,64,1024]{2,1,0:T(8,128)(2,1)S(1)} collective-permute-done((bf16[2,64,1024]{2,1,0:T(8,128)(2,1)S(1)}, bf16[2,64,1024]{2,1,0:T(8,128)(2,1)S(1)}, u32[]{:S(2)}, u32[]{:S(2)}) %collective-permute-start.81) | collective-permute-done | bytes 262176 | tf_op jit(solution)/shard_map/ppermute | solution.py:767
  603.9 3.0 collective-permute-done.82
  616.9 3.0 copy.60
  619.9 5.6 collective-permute-done.72
  625.5 6.5 collective-permute-done.74
  634.7 16.1 %collective-permute-done.75 = bf16[2,64,1024]{2,1,0:T(8,128)(2,1)S(1)} collective-permute-done((bf16[2,64,1024]{2,1,0:T(8,128)(2,1)S(1)}, bf16[2,64,1024]{2,1,0:T(8,128)(2,1)S(1)}, u32[]{:S(2)}, u32[]{:S(2)}) %collective-permute-start.75) | collective-permute-done | bytes 262176 | tf_op jit(solution)/shard_map/ppermute | solution.py:767
  651.1 4.9 collective-permute-done.76
  (557 shorter events, 172.7 us)
Async XLA Ops:
  7.2 210.1 %all-gather.5.cloned.1.call-start = ((), (), s32[]{:S(2)}) async-start(), calls=%async_computation.2 | async-start | bytes 2451456 | tf_op jit(solution)/shard_map/all_gather | solution.py:889
  9.2 304.0 %all-gather.7.cloned.1.call-start = ((), (), s32[]{:S(2)}) async-start(), calls=%async_computation.3 | async-start | bytes 2451456 | tf_op jit(solution)/shard_map/all_gather | solution.py:889
  12.8 24.8 %collective-permute-start.3 = (bf16[2,28,2432]{2,1,0:T(8,128)(2,1)S(1)}, bf16[2,28,2432]{2,1,0:T(8,128)(2,1)S(1)}, u32[]{:S(2)}, u32[]{:S(2)}) collective-permute-start(bf16[2,28,2432]{2,1,0:T(8,128)(2,1)S(1)} %get-tuple-element.226), channel_id=1, source_target_pairs={{0,1},{1,0},{2,3},{3,2},{4,5},{5,4},{6,7},{7,6},{8,9},{9,8},{10,11... | collective-permute-start | bytes 817160 | tf_op jit(solution)/shard_map/ppermute | solution.py:767
  13.4 24.3 %collective-permute-start.4 = (bf16[2,28,2432]{2,1,0:T(8,128)(2,1)S(1)}, bf16[2,28,2432]{2,1,0:T(8,128)(2,1)S(1)}, u32[]{:S(2)}, u32[]{:S(2)}) collective-permute-start(bf16[2,28,2432]{2,1,0:T(8,128)(2,1)S(1)} %get-tuple-element.227), channel_id=1, source_target_pairs={{0,2},{1,3},{2,0},{3,1},{4,6},{5,7},{6,4},{7,5},{8,10},{9,11},{10,... | collective-permute-start | bytes 817160 | tf_op jit(solution)/shard_map/ppermute | solution.py:767
  15.9 21.8 %collective-permute-start.5 = (bf16[2,28,2432]{2,1,0:T(8,128)(2,1)S(1)}, bf16[2,28,2432]{2,1,0:T(8,128)(2,1)S(1)}, u32[]{:S(2)}, u32[]{:S(2)}) collective-permute-start(bf16[2,28,2432]{2,1,0:T(8,128)(2,1)S(1)} %get-tuple-element.228), channel_id=1, source_target_pairs={{0,3},{1,2},{2,1},{3,0},{4,7},{5,6},{6,5},{7,4},{8,11},{9,10},{10,... | collective-permute-start | bytes 817160 | tf_op jit(solution)/shard_map/ppermute | solution.py:767
  16.3 644.4 %reduce-scatter.9.cloned.1.call-start = ((), (), s32[]{:S(2)}) async-start(), calls=%async_computation.5 | async-start | bytes 2451456
  35.4 26.8 %collective-permute-start.2 = (bf16[2,64,1024]{2,1,0:T(8,128)(2,1)}, bf16[2,64,1024]{2,1,0:T(8,128)(2,1)}, u32[]{:S(2)}, u32[]{:S(2)}) collective-permute-start(bf16[2,64,1024]{2,1,0:T(8,128)(2,1)} %pad_maximum_fusion.7), channel_id=1, source_target_pairs={{0,16},{4,20},{8,24},{12,28},{16,0},{20,4},{24,8},{28,12},{1,17},{... | collective-permute-start | bytes 786440 | tf_op jit(solution)/shard_map/ppermute | solution.py:767
  63.2 23.3 %collective-permute-start.6 = (bf16[4,64,1024]{2,1,0:T(8,128)(2,1)S(1)}, bf16[4,64,1024]{2,1,0:T(8,128)(2,1)S(1)}, u32[]{:S(2)}, u32[]{:S(2)}) collective-permute-start(bf16[4,64,1024]{2,1,0:T(8,128)(2,1)S(1)} %constant_dynamic-update-slice_fusion.refs_0_), channel_id=1, source_target_pairs={{0,4},{4,0},{8,12},{12,8},{16,20},{20,16},{24,28},{28,24},{1,5},{5... | collective-permute-start | bytes 1572872 | tf_op jit(solution)/shard_map/ppermute | solution.py:767
  66.7 35.6 %collective-permute-start.7 = (bf16[4,64,1024]{2,1,0:T(8,128)(2,1)S(1)}, bf16[4,64,1024]{2,1,0:T(8,128)(2,1)S(1)}, u32[]{:S(2)}, u32[]{:S(2)}) collective-permute-start(bf16[4,64,1024]{2,1,0:T(8,128)(2,1)S(1)} %constant_dynamic-update-slice_fusion.refs_0_), channel_id=1, source_target_pairs={{0,2},{1,3},{2,0},{3,1},{4,6},{5,7},{6,4},{7,5},{8,10},{9,11},{10,... | collective-permute-start | bytes 1572872 | tf_op jit(solution)/shard_map/ppermute | solution.py:767
  68.3 34.6 %collective-permute-start.9 = (bf16[4,64,1024]{2,1,0:T(8,128)(2,1)S(1)}, bf16[4,64,1024]{2,1,0:T(8,128)(2,1)S(1)}, u32[]{:S(2)}, u32[]{:S(2)}) collective-permute-start(bf16[4,64,1024]{2,1,0:T(8,128)(2,1)S(1)} %constant_dynamic-update-slice_fusion.refs_0_), channel_id=1, source_target_pairs={{0,1},{1,0},{2,3},{3,2},{4,5},{5,4},{6,7},{7,6},{8,9},{9,8},{10,11... | collective-permute-start | bytes 1572872 | tf_op jit(solution)/shard_map/ppermute | solution.py:767
  89.0 30.9 %collective-permute-start.20 = (bf16[2,112,2432]{2,1,0:T(8,128)(2,1)}, bf16[2,112,2432]{2,1,0:T(8,128)(2,1)}, u32[]{:S(2)}, u32[]{:S(2)}) collective-permute-start(bf16[2,112,2432]{2,1,0:T(8,128)(2,1)} %constant_dynamic-update-slice_fusion.3.refs_0_), channel_id=1, source_target_pairs={{0,4},{4,0},{8,12},{12,8},{16,20},{20,16},{24,28},{28,24},{1,5},{5... | collective-permute-start | bytes 3268616 | tf_op jit(solution)/shard_map/ppermute | solution.py:767
  102.8 67.5 %collective-permute-start.22 = (bf16[2,112,2432]{2,1,0:T(8,128)(2,1)}, bf16[2,112,2432]{2,1,0:T(8,128)(2,1)}, u32[]{:S(2)}, u32[]{:S(2)}) collective-permute-start(bf16[2,112,2432]{2,1,0:T(8,128)(2,1)} %constant_dynamic-update-slice_fusion.3.refs_0_), channel_id=1, source_target_pairs={{0,16},{4,20},{8,24},{12,28},{16,0},{20,4},{24,8},{28,12},{1,17},{... | collective-permute-start | bytes 3268616 | tf_op jit(solution)/shard_map/ppermute | solution.py:767
  138.4 34.0 %collective-permute-start.25 = (bf16[256,896]{1,0:T(8,128)(2,1)}, bf16[256,896]{1,0:T(8,128)(2,1)S(1)}, u32[]{:S(2)}, u32[]{:S(2)}) collective-permute-start(bf16[256,896]{1,0:T(8,128)(2,1)} %get-tuple-element.244.refs_0_.refs_5_), channel_id=1, source_target_pairs={{0,2},{1,3},{2,0},{3,1},{4,6},{5,7},{6,4},{7,5},{8,10},{9,11},{10,... | collective-permute-start | bytes 1376264 | tf_op jit(solution)/shard_map/ppermute | solution.py:767
  170.4 40.0 %collective-permute-start.23 = (bf16[2,112,2432]{2,1,0:T(8,128)(2,1)}, bf16[2,112,2432]{2,1,0:T(8,128)(2,1)S(1)}, u32[]{:S(2)}, u32[]{:S(2)}) collective-permute-start(bf16[2,112,2432]{2,1,0:T(8,128)(2,1)} %collective-permute-done.22.refs_1_), channel_id=1, source_target_pairs={{0,4},{4,0},{8,12},{12,8},{16,20},{20,16},{24,28},{28,24},{1,5},{5... | collective-permute-start | bytes 3268616 | tf_op jit(solution)/shard_map/ppermute | solution.py:767
  171.8 36.2 %collective-permute-start.36 = (bf16[1,112,2432]{2,1,0:T(8,128)(2,1)S(1)}, bf16[1,112,2432]{2,1,0:T(8,128)(2,1)S(1)}, u32[]{:S(2)}, u32[]{:S(2)}) collective-permute-start(bf16[1,112,2432]{2,1,0:T(8,128)(2,1)S(1)} %copy-done.50), channel_id=1, source_target_pairs={{0,8},{4,12},{8,0},{12,4},{16,24},{20,28},{24,16},{28,20},{1,9},{5... | collective-permute-start | bytes 1634312 | tf_op jit(solution)/shard_map/ppermute | solution.py:767
  171.8 36.1 %collective-permute-start.29 = (bf16[4,64,1024]{2,1,0:T(8,128)(2,1)}, bf16[4,64,1024]{2,1,0:T(8,128)(2,1)}, u32[]{:S(2)}, u32[]{:S(2)}) collective-permute-start(bf16[4,64,1024]{2,1,0:T(8,128)(2,1)} %constant_dynamic-update-slice_fusion.5.refs_0_), channel_id=1, source_target_pairs={{0,4},{4,0},{8,12},{12,8},{16,20},{20,16},{24,28},{28,24},{1,5},{5... | collective-permute-start | bytes 1572872 | tf_op jit(solution)/shard_map/ppermute | solution.py:767
  172.4 36.8 %collective-permute-start.26 = (bf16[256,896]{1,0:T(8,128)(2,1)S(1)}, bf16[256,896]{1,0:T(8,128)(2,1)S(1)}, u32[]{:S(2)}, u32[]{:S(2)}) collective-permute-start(bf16[256,896]{1,0:T(8,128)(2,1)S(1)} %collective-permute-done.25.refs_0_.refs_7_), channel_id=1, source_target_pairs={{0,1},{1,0},{2,3},{3,2},{4,5},{5,4},{6,7},{7,6},{8,9},{9,8},{10,11... | collective-permute-start | bytes 1376264 | tf_op jit(solution)/shard_map/ppermute | solution.py:767
  172.4 60.1 %collective-permute-start.30 = (bf16[4,64,1024]{2,1,0:T(8,128)(2,1)}, bf16[4,64,1024]{2,1,0:T(8,128)(2,1)}, u32[]{:S(2)}, u32[]{:S(2)}) collective-permute-start(bf16[4,64,1024]{2,1,0:T(8,128)(2,1)} %constant_dynamic-update-slice_fusion.5.refs_0_), channel_id=1, source_target_pairs={{0,2},{1,3},{2,0},{3,1},{4,6},{5,7},{6,4},{7,5},{8,10},{9,11},{10,... | collective-permute-start | bytes 1572872 | tf_op jit(solution)/shard_map/ppermute | solution.py:767
  207.9 24.9 %collective-permute-start.32 = (bf16[4,64,1024]{2,1,0:T(8,128)(2,1)}, bf16[4,64,1024]{2,1,0:T(8,128)(2,1)}, u32[]{:S(2)}, u32[]{:S(2)}) collective-permute-start(bf16[4,64,1024]{2,1,0:T(8,128)(2,1)} %constant_dynamic-update-slice_fusion.5.refs_0_), channel_id=1, source_target_pairs={{0,1},{1,0},{2,3},{3,2},{4,5},{5,4},{6,7},{7,6},{8,9},{9,8},{10,11... | collective-permute-start | bytes 1572872 | tf_op jit(solution)/shard_map/ppermute | solution.py:767
  207.9 25.2 %collective-permute-start.31 = (bf16[4,64,1024]{2,1,0:T(8,128)(2,1)}, bf16[4,64,1024]{2,1,0:T(8,128)(2,1)}, u32[]{:S(2)}, u32[]{:S(2)}) collective-permute-start(bf16[4,64,1024]{2,1,0:T(8,128)(2,1)} %collective-permute-done.29.refs_1_), channel_id=1, source_target_pairs={{0,2},{1,3},{2,0},{3,1},{4,6},{5,7},{6,4},{7,5},{8,10},{9,11},{10,... | collective-permute-start | bytes 1572872 | tf_op jit(solution)/shard_map/ppermute | solution.py:767
  209.3 24.1 %collective-permute-start.21 = (bf16[256,896]{1,0:T(8,128)(2,1)}, bf16[256,896]{1,0:T(8,128)(2,1)}, u32[]{:S(2)}, u32[]{:S(2)}) collective-permute-start(bf16[256,896]{1,0:T(8,128)(2,1)} %get-tuple-element.244.refs_0_.refs_5_), channel_id=1, source_target_pairs={{0,1},{1,0},{2,3},{3,2},{4,5},{5,4},{6,7},{7,6},{8,9},{9,8},{10,11... | collective-permute-start | bytes 1376264 | tf_op jit(solution)/shard_map/ppermute | solution.py:767
  211.4 50.2 %collective-permute-start.37 = (bf16[2,112,2432]{2,1,0:T(8,128)(2,1)}, bf16[2,112,2432]{2,1,0:T(8,128)(2,1)}, u32[]{:S(2)}, u32[]{:S(2)}) collective-permute-start(bf16[2,112,2432]{2,1,0:T(8,128)(2,1)} %constant_dynamic-update-slice_fusion.8.refs_0_), channel_id=1, source_target_pairs={{0,16},{4,20},{8,24},{12,28},{16,0},{20,4},{24,8},{28,12},{1,17},{... | collective-permute-start | bytes 3268616 | tf_op jit(solution)/shard_map/ppermute | solution.py:767
  233.4 33.7 %collective-permute-start.41 = (bf16[2,112,2432]{2,1,0:T(8,128)(2,1)}, bf16[2,112,2432]{2,1,0:T(8,128)(2,1)S(1)}, u32[]{:S(2)}, u32[]{:S(2)}) collective-permute-start(bf16[2,112,2432]{2,1,0:T(8,128)(2,1)} %constant_dynamic-update-slice_fusion.8.refs_0_), channel_id=1, source_target_pairs={{0,4},{4,0},{8,12},{12,8},{16,20},{20,16},{24,28},{28,24},{1,5},{5... | collective-permute-start | bytes 3268616 | tf_op jit(solution)/shard_map/ppermute | solution.py:767
  261.6 47.4 %collective-permute-start.43 = (bf16[2,112,2432]{2,1,0:T(8,128)(2,1)}, bf16[2,112,2432]{2,1,0:T(8,128)(2,1)S(1)}, u32[]{:S(2)}, u32[]{:S(2)}) collective-permute-start(bf16[2,112,2432]{2,1,0:T(8,128)(2,1)} %collective-permute-done.37.refs_1_), channel_id=1, source_target_pairs={{0,4},{4,0},{8,12},{12,8},{16,20},{20,16},{24,28},{28,24},{1,5},{5... | collective-permute-start | bytes 3268616 | tf_op jit(solution)/shard_map/ppermute | solution.py:767
  286.4 22.6 %collective-permute-start.50 = (bf16[256,896]{1,0:T(8,128)(2,1)}, bf16[256,896]{1,0:T(8,128)(2,1)}, u32[]{:S(2)}, u32[]{:S(2)}) collective-permute-start(bf16[256,896]{1,0:T(8,128)(2,1)} %bitcast.48.refs_1_.refs_0_), channel_id=1, source_target_pairs={{0,2},{1,3},{2,0},{3,1},{4,6},{5,7},{6,4},{7,5},{8,10},{9,11},{10,... | collective-permute-start | bytes 1376264 | tf_op jit(solution)/shard_map/ppermute | solution.py:767
  287.9 25.3 %collective-permute-start.42 = (bf16[256,896]{1,0:T(8,128)(2,1)}, bf16[256,896]{1,0:T(8,128)(2,1)}, u32[]{:S(2)}, u32[]{:S(2)}) collective-permute-start(bf16[256,896]{1,0:T(8,128)(2,1)} %get-tuple-element.259.refs_0_.refs_5_), channel_id=1, source_target_pairs={{0,1},{1,0},{2,3},{3,2},{4,5},{5,4},{6,7},{7,6},{8,9},{9,8},{10,11... | collective-permute-start | bytes 1376264 | tf_op jit(solution)/shard_map/ppermute | solution.py:767
  299.4 28.9 %collective-permute-start.46 = (bf16[256,896]{1,0:T(8,128)(2,1)S(1)}, bf16[256,896]{1,0:T(8,128)(2,1)}, u32[]{:S(2)}, u32[]{:S(2)}) collective-permute-start(bf16[256,896]{1,0:T(8,128)(2,1)S(1)} %collective-permute-done.45.refs_0_.refs_7_), channel_id=1, source_target_pairs={{0,1},{1,0},{2,3},{3,2},{4,5},{5,4},{6,7},{7,6},{8,9},{9,8},{10,11... | collective-permute-start | bytes 1376264 | tf_op jit(solution)/shard_map/ppermute | solution.py:767
  299.4 41.0 %collective-permute-start.49 = (bf16[256,896]{1,0:T(8,128)(2,1)}, bf16[256,896]{1,0:T(8,128)(2,1)}, u32[]{:S(2)}, u32[]{:S(2)}) collective-permute-start(bf16[256,896]{1,0:T(8,128)(2,1)} %bitcast.48.refs_1_.refs_0_), channel_id=1, source_target_pairs={{0,1},{1,0},{2,3},{3,2},{4,5},{5,4},{6,7},{7,6},{8,9},{9,8},{10,11... | collective-permute-start | bytes 1376264 | tf_op jit(solution)/shard_map/ppermute | solution.py:767
  309.0 31.4 %collective-permute-start.51 = (bf16[256,896]{1,0:T(8,128)(2,1)}, bf16[256,896]{1,0:T(8,128)(2,1)}, u32[]{:S(2)}, u32[]{:S(2)}) collective-permute-start(bf16[256,896]{1,0:T(8,128)(2,1)} %collective-permute-done.50.refs_3_), channel_id=1, source_target_pairs={{0,1},{1,0},{2,3},{3,2},{4,5},{5,4},{6,7},{7,6},{8,9},{9,8},{10,11... | collective-permute-start | bytes 1376264 | tf_op jit(solution)/shard_map/ppermute | solution.py:767
  371.5 33.1 %collective-permute-start.57 = (bf16[2,112,2432]{2,1,0:T(8,128)(2,1)}, bf16[2,112,2432]{2,1,0:T(8,128)(2,1)S(1)}, u32[]{:S(2)}, u32[]{:S(2)}) collective-permute-start(bf16[2,112,2432]{2,1,0:T(8,128)(2,1)} %get-tuple-element.275), channel_id=1, source_target_pairs={{0,4},{4,0},{8,12},{12,8},{16,20},{20,16},{24,28},{28,24},{1,5},{5... | collective-permute-start | bytes 3268616 | tf_op jit(solution)/shard_map/ppermute | solution.py:767
  405.9 57.6 %collective-permute-start.68 = (bf16[2,112,2432]{2,1,0:T(8,128)(2,1)}, bf16[2,112,2432]{2,1,0:T(8,128)(2,1)}, u32[]{:S(2)}, u32[]{:S(2)}) collective-permute-start(bf16[2,112,2432]{2,1,0:T(8,128)(2,1)} %get-tuple-element.304), channel_id=1, source_target_pairs={{0,4},{4,0},{8,12},{12,8},{16,20},{20,16},{24,28},{28,24},{1,5},{5... | collective-permute-start | bytes 3268616 | tf_op jit(solution)/shard_map/ppermute | solution.py:767
  412.0 68.3 %collective-permute-start.69 = (bf16[2,112,2432]{2,1,0:T(8,128)(2,1)}, bf16[2,112,2432]{2,1,0:T(8,128)(2,1)}, u32[]{:S(2)}, u32[]{:S(2)}) collective-permute-start(bf16[2,112,2432]{2,1,0:T(8,128)(2,1)} %add_convert_fusion.5), channel_id=1, source_target_pairs={{0,16},{4,20},{8,24},{12,28},{16,0},{20,4},{24,8},{28,12},{1,17},{... | collective-permute-start | bytes 3268616 | tf_op jit(solution)/shard_map/ppermute | solution.py:767
  430.7 230.0 %reduce-scatter.7.cloned.1.call-start = ((), (), s32[]{:S(2)}) async-start(), calls=%async_computation.4 | async-start | bytes 2451456
  430.8 95.5 %collective-permute-start.44 = (bf16[256,896]{1,0:T(8,128)(2,1)}, bf16[256,896]{1,0:T(8,128)(2,1)S(1)}, u32[]{:S(2)}, u32[]{:S(2)}) collective-permute-start(bf16[256,896]{1,0:T(8,128)(2,1)} %copy-done.93), channel_id=1, source_target_pairs={{0,1},{1,0},{2,3},{3,2},{4,5},{5,4},{6,7},{7,6},{8,9},{9,8},{10,11... | collective-permute-start | bytes 1376264 | tf_op jit(solution)/shard_map/ppermute | solution.py:767
  431.4 52.3 %collective-permute-start.47 = (bf16[256,896]{1,0:T(8,128)(2,1)}, bf16[256,896]{1,0:T(8,128)(2,1)S(1)}, u32[]{:S(2)}, u32[]{:S(2)}) collective-permute-start(bf16[256,896]{1,0:T(8,128)(2,1)} %copy-done.94), channel_id=1, source_target_pairs={{0,1},{1,0},{2,3},{3,2},{4,5},{5,4},{6,7},{7,6},{8,9},{9,8},{10,11... | collective-permute-start | bytes 1376264 | tf_op jit(solution)/shard_map/ppermute | solution.py:767
  463.5 47.2 %collective-permute-start.67 = (bf16[2,112,2432]{2,1,0:T(8,128)(2,1)}, bf16[2,112,2432]{2,1,0:T(8,128)(2,1)S(1)}, u32[]{:S(2)}, u32[]{:S(2)}) collective-permute-start(bf16[2,112,2432]{2,1,0:T(8,128)(2,1)} %get-tuple-element.301), channel_id=1, source_target_pairs={{0,4},{4,0},{8,12},{12,8},{16,20},{20,16},{24,28},{28,24},{1,5},{5... | collective-permute-start | bytes 3268616 | tf_op jit(solution)/shard_map/ppermute | solution.py:767
  482.3 28.1 %collective-permute-start.91 = (bf16[112,2432]{1,0:T(8,128)(2,1)S(1)}, bf16[112,2432]{1,0:T(8,128)(2,1)S(1)}, u32[]{:S(2)}, u32[]{:S(2)}) collective-permute-start(bf16[112,2432]{1,0:T(8,128)(2,1)S(1)} %get-tuple-element.391), channel_id=1, source_target_pairs={{0,8},{4,12},{8,0},{12,4},{16,24},{20,28},{24,16},{28,20},{1,9},{5... | collective-permute-start | bytes 1634312 | tf_op jit(solution)/shard_map/ppermute | solution.py:767
  483.8 42.5 %collective-permute-start.48 = (bf16[256,896]{1,0:T(8,128)(2,1)S(1)}, bf16[256,896]{1,0:T(8,128)(2,1)S(1)}, u32[]{:S(2)}, u32[]{:S(2)}) collective-permute-start(bf16[256,896]{1,0:T(8,128)(2,1)S(1)} %add_convert_fusion.13), channel_id=1, source_target_pairs={{0,2},{1,3},{2,0},{3,1},{4,6},{5,7},{6,4},{7,5},{8,10},{9,11},{10,... | collective-permute-start | bytes 1376264 | tf_op jit(solution)/shard_map/ppermute | solution.py:767
  513.5 42.7 %collective-permute-start.77 = (bf16[2,4,64,1024]{3,2,1,0:T(8,128)(2,1)}, bf16[2,4,64,1024]{3,2,1,0:T(8,128)(2,1)}, u32[]{:S(2)}, u32[]{:S(2)}) collective-permute-start(bf16[2,4,64,1024]{3,2,1,0:T(8,128)(2,1)} %get-tuple-element.324), channel_id=1, source_target_pairs={{0,1},{1,0},{2,3},{3,2},{4,5},{5,4},{6,7},{7,6},{8,9},{9,8},{10,11... | collective-permute-start | bytes 3145736 | tf_op jit(solution)/shard_map/ppermute | solution.py:767
  516.7 55.0 %collective-permute-start.86 = (bf16[2,112,2432]{2,1,0:T(8,128)(2,1)}, bf16[2,112,2432]{2,1,0:T(8,128)(2,1)}, u32[]{:S(2)}, u32[]{:S(2)}) collective-permute-start(bf16[2,112,2432]{2,1,0:T(8,128)(2,1)} %add_convert_fusion.4), channel_id=1, source_target_pairs={{0,16},{4,20},{8,24},{12,28},{16,0},{20,4},{24,8},{28,12},{1,17},{... | collective-permute-start | bytes 3268616 | tf_op jit(solution)/shard_map/ppermute | solution.py:767
  518.6 53.1 %collective-permute-start.85 = (bf16[2,112,2432]{2,1,0:T(8,128)(2,1)}, bf16[2,112,2432]{2,1,0:T(8,128)(2,1)}, u32[]{:S(2)}, u32[]{:S(2)}) collective-permute-start(bf16[2,112,2432]{2,1,0:T(8,128)(2,1)} %get-tuple-element.332), channel_id=1, source_target_pairs={{0,4},{4,0},{8,12},{12,8},{16,20},{20,16},{24,28},{28,24},{1,5},{5... | collective-permute-start | bytes 3268616 | tf_op jit(solution)/shard_map/ppermute | solution.py:767
  530.6 24.9 %collective-permute-start.79 = (bf16[4,64,1024]{2,1,0:T(8,128)(2,1)}, bf16[4,64,1024]{2,1,0:T(8,128)(2,1)}, u32[]{:S(2)}, u32[]{:S(2)}) collective-permute-start(bf16[4,64,1024]{2,1,0:T(8,128)(2,1)} %get-tuple-element.328), channel_id=1, source_target_pairs={{0,2},{1,3},{2,0},{3,1},{4,6},{5,7},{6,4},{7,5},{8,10},{9,11},{10,... | collective-permute-start | bytes 1572872 | tf_op jit(solution)/shard_map/ppermute | solution.py:767
  555.5 23.7 %collective-permute-start.71 = (bf16[2,4,64,1024]{3,2,1,0:T(8,128)(2,1)}, bf16[2,4,64,1024]{3,2,1,0:T(8,128)(2,1)S(1)}, u32[]{:S(2)}, u32[]{:S(2)}) collective-permute-start(bf16[2,4,64,1024]{3,2,1,0:T(8,128)(2,1)} %copy-done.92), channel_id=1, source_target_pairs={{0,1},{1,0},{2,3},{3,2},{4,5},{5,4},{6,7},{7,6},{8,9},{9,8},{10,11... | collective-permute-start | bytes 3145736 | tf_op jit(solution)/shard_map/ppermute | solution.py:767
  556.2 57.5 %collective-permute-start.70 = (bf16[2,4,64,1024]{3,2,1,0:T(8,128)(2,1)}, bf16[2,4,64,1024]{3,2,1,0:T(8,128)(2,1)}, u32[]{:S(2)}, u32[]{:S(2)}) collective-permute-start(bf16[2,4,64,1024]{3,2,1,0:T(8,128)(2,1)} %copy-done.91), channel_id=1, source_target_pairs={{0,1},{1,0},{2,3},{3,2},{4,5},{5,4},{6,7},{7,6},{8,9},{9,8},{10,11... | collective-permute-start | bytes 3145736 | tf_op jit(solution)/shard_map/ppermute | solution.py:767
  573.8 27.8 %collective-permute-start.87 = (bf16[112,2432]{1,0:T(8,128)(2,1)S(1)}, bf16[112,2432]{1,0:T(8,128)(2,1)S(1)}, u32[]{:S(2)}, u32[]{:S(2)}) collective-permute-start(bf16[112,2432]{1,0:T(8,128)(2,1)S(1)} %get-tuple-element.389), channel_id=1, source_target_pairs={{0,8},{4,12},{8,0},{12,4},{16,24},{20,28},{24,16},{28,20},{1,9},{5... | collective-permute-start | bytes 1634312 | tf_op jit(solution)/shard_map/ppermute | solution.py:767
  578.0 21.6 %collective-permute-start.81 = (bf16[2,64,1024]{2,1,0:T(8,128)(2,1)S(1)}, bf16[2,64,1024]{2,1,0:T(8,128)(2,1)S(1)}, u32[]{:S(2)}, u32[]{:S(2)}) collective-permute-start(bf16[2,64,1024]{2,1,0:T(8,128)(2,1)S(1)} %slice.458), channel_id=1, source_target_pairs={{0,16},{4,20},{8,24},{12,28},{16,0},{20,4},{24,8},{28,12},{1,17},{... | collective-permute-start | bytes 786440 | tf_op jit(solution)/shard_map/ppermute | solution.py:767
  580.6 33.0 %collective-permute-start.73 = (bf16[4,64,1024]{2,1,0:T(8,128)(2,1)}, bf16[4,64,1024]{2,1,0:T(8,128)(2,1)}, u32[]{:S(2)}, u32[]{:S(2)}) collective-permute-start(bf16[4,64,1024]{2,1,0:T(8,128)(2,1)} %get-tuple-element.385), channel_id=1, source_target_pairs={{0,2},{1,3},{2,0},{3,1},{4,6},{5,7},{6,4},{7,5},{8,10},{9,11},{10,... | collective-permute-start | bytes 1572872 | tf_op jit(solution)/shard_map/ppermute | solution.py:767
  611.3 23.4 %collective-permute-start.84 = (f32[28,1024]{1,0:T(8,128)S(1)}, f32[28,1024]{1,0:T(8,128)S(1)}, u32[]{:S(2)}, u32[]{:S(2)}) collective-permute-start(f32[28,1024]{1,0:T(8,128)S(1)} %dynamic-slice_bitcast_fusion), channel_id=1, source_target_pairs={{0,1},{1,0},{2,3},{3,2},{4,5},{5,4},{6,7},{7,6},{8,9},{9,8},{10,11... | collective-permute-start | bytes 344072 | tf_op jit(solution)/shard_map/ppermute | solution.py:767
  (166 other events, 1886.5 us)
Sparse Core Ops, SparseCore 0:
  10.2 57.7 all-gather.4
  70.2 86.0 all-gather.6
  430.8 85.9 reduce-scatter.8
  551.0 97.8 reduce-scatter.6

commit v2 on v1

--- a/solution.py
+++ b/solution.py
@@ -46,7 +46,7 @@
         compiler_params=pltpu.CompilerParams(vmem_limit_bytes=limit * 2**20),
         name=kernel.__qualname__.split(".")[0],
         cost_estimate=pl.CostEstimate(
-            flops=0, bytes_accessed=int(micros * 4e5), transcendentals=0
+            flops=0, bytes_accessed=int(micros * 4e3), transcendentals=0
         ),
         **grid,
     )
@@ -206,6 +206,7 @@
         [((rows, 2 * units), jnp.bfloat16)] + [((part_rows, D), jnp.bfloat16)] * count,
         9.0,
         [pltpu.VMEM((rows, D), jnp.float32)],
+        limit=60,
         grid=(steps,),
         in_specs=[pl.BlockSpec((part_rows, D), whole)] * count
         + [
@@ -217,6 +218,12 @@
         ]
         + [pl.BlockSpec((part_rows, D), whole)] * count,
     )(*parts, gate_up_full, down_full)
+
+
+def far_slot(mine, place, line):
+    if line == 4:
+        return jnp.where(mine < 2, place - 2, 1 - place)
+    return (mine ^ place) - line // 2
 
 
 def feed_back(gz_parts, n2_parts, gu_parts, gate_up_full, down_full, dp_place, group_count):
@@ -270,6 +277,7 @@
                 keep = jnp.where(side == 0, even, odd)
                 send = jnp.where(side == 0, odd, even)
                 slot = mine ^ spot
+                beyond = far_slot(mine, spot, line)
 
                 @pl.when(slot < half)
                 def _():
@@ -278,8 +286,8 @@
 
                 @pl.when(slot >= half)
                 def _():
-                    keep_far[slot - half, :, : 2 * width] = keep
-                    send_far[slot - half, :, : 2 * width] = send
+                    keep_far[beyond, :, : 2 * width] = keep
+                    send_far[beyond, :, : 2 * width] = send
 
             return dot(both, w_ref[:, : 2 * width], NT)
 
@@ -554,26 +562,27 @@
 
 def collect_columns(blocks, place, unit_rows, group_count):
     count = len(blocks)
-    rows, quarter = blocks[0].shape
+    layers, rows, quarter = blocks[0].shape
     pieces = unit_pieces(unit_rows, group_count, count)
 
     def kernel(place_ref, *refs):
         out_ref, narrow = refs[count:]
         me = place_ref[0]
-        for owner in range(count):
-            for bit in range(count):
-
-                @pl.when(me == owner ^ bit)
-                def _():
-                    narrow[...] = refs[bit][...].astype(jnp.float32)
-
-            for who, inside, column, width in pieces:
-                if who == owner:
-                    out_ref[:, column : column + width] = narrow[:, inside : inside + width]
+        for layer in range(layers):
+            for owner in range(count):
+                for bit in range(count):
+
+                    @pl.when(me == owner ^ bit)
+                    def _():
+                        narrow[...] = refs[bit][layer].astype(jnp.float32)
+
+                for who, inside, column, width in pieces:
+                    if who == owner:
+                        out_ref[layer, :, column : column + width] = narrow[:, inside : inside + width]
 
     return call(
         kernel,
-        [((rows, count * quarter), jnp.float32)],
+        [((layers, rows, count * quarter), jnp.float32)],
         1.5,
         [pltpu.VMEM((rows, quarter), jnp.float32)],
         in_specs=[pl.BlockSpec(memory_space=pltpu.SMEM)] + [FULL] * count,
@@ -607,29 +616,34 @@
     )(place.reshape(1).astype(jnp.int32), *blocks)
 
 
-def split_rows(terms, place, count):
-    number, total_rows, columns = terms.shape
-    rows = total_rows // count
-
-    def kernel(place_ref, in_ref, *outs):
-        total = in_ref[0].astype(jnp.float32)
-        for k in range(1, number):
-            total = total + in_ref[k].astype(jnp.float32)
-        for owner in range(count):
-            block = total[owner * rows : owner * rows + rows].astype(jnp.bfloat16)
-            for bit in range(count):
-
-                @pl.when(place_ref[0] == owner ^ bit)
-                def _():
-                    outs[bit][...] = block
+def split_rows(terms, layers, place, count):
+    number = len(terms)
+    layer_rows = terms[0].shape[0] // layers
+    columns = terms[0].shape[1]
+    rows = layer_rows // count
+
+    def kernel(place_ref, *refs):
+        ins, outs = refs[:number], refs[number:]
+        for layer in range(layers):
+            here = slice(layer * layer_rows, (layer + 1) * layer_rows)
+            total = ins[0][here, :].astype(jnp.float32)
+            for ref in ins[1:]:
+                total = total + ref[here, :].astype(jnp.float32)
+            for owner in range(count):
+                block = total[owner * rows : owner * rows + rows].astype(jnp.bfloat16)
+                for bit in range(count):
+
+                    @pl.when(place_ref[0] == owner ^ bit)
+                    def _():
+                        outs[bit][layer] = block
 
     return call(
         kernel,
-        [((rows, columns), jnp.bfloat16)] * count,
+        [((layers, rows, columns), jnp.bfloat16)] * count,
         2.0,
-        in_specs=[pl.BlockSpec(memory_space=pltpu.SMEM), FULL],
+        in_specs=[pl.BlockSpec(memory_space=pltpu.SMEM)] + [FULL] * number,
         out_specs=[FULL] * count,
-    )(place.reshape(1).astype(jnp.int32), terms)
+    )(place.reshape(1).astype(jnp.int32), *terms)
 
 
 def lay_out(blocks, places):
@@ -784,6 +798,19 @@
     return values
 
 
+def line_steps(values, moves):
+    return lax.ppermute(
+        values, "dp", [(2 * here + side, 2 * there + side) for here, there in moves for side in range(2)]
+    )
+
+
+def cross_middle(values):
+    line = lax.axis_size("dp") // 2
+    if line == 4:
+        return line_steps(values, [(1, 2), (2, 1)])
+    return swap(values, "dp", line)
+
+
 def line_scatter(values, bits):
     for bit in bits[:0:-1]:
         values = add_low(values[:bit], swap(values[bit:], "dp", 2 * bit))
@@ -794,10 +821,10 @@
     return (left.astype(jnp.float32) + right.astype(jnp.float32)).astype(jnp.bfloat16)
 
 
-def group_rows(values):
+def group_rows(values, *waited):
     beside = swap(values, "seq", 1)
     across = swap(values, "seq", 2)
-    return [values, beside, across, swap(across, "seq", 1)]
+    return [values, beside, across, swap(after(across, *waited), "seq", 1)]
 
 
 def placed(values, offset, width):
@@ -831,6 +858,7 @@
     chip_rows = 2 * width_rows
     line = group_count // 2
     side = dp_place % 2
+    line_place = dp_place // 2
 
     order = [lax.dynamic_slice(span_order, (0, seq_place ^ bit), (1, 1))[0, 0] for bit in range(4)]
     inside = jnp.arange(span_len, dtype=jnp.int32)
@@ -867,10 +895,9 @@
         extra = extra.at[3, :KV_WIDTH].set(bias_all[SPLIT:])
         return jnp.concatenate([rows, extra], axis=0)
 
-    def attn_finish(near):
-        far = swap(near, "dp", 1)
-        across = swap(near, "seq", 2)
-        parts = [near, far, across, swap(far, "seq", 2)]
+    def attn_finish(own_side, other_side, *waited):
+        parts = [own_side, other_side]
+        parts = parts + [swap(after(part, *waited), "seq", 2) for part in parts]
         parts = parts + [swap(part, "seq", 1) for part in parts]
         first_full, second_full, small = assemble(parts, [core, chip_x, dp_place], chip_rows)
         return (
@@ -885,40 +912,41 @@
     bits = line_bits()
     spread = spread_columns(gate_up_weight, seq_place, unit_rows, group_count, seq_devices)
     shards = [attn_shard(layer)[None] for layer in range(LAYERS)]
-    down_full = [
-        lax.all_gather(down_weight[layer], "dp", axis=0, tiled=True) for layer in range(LAYERS)
-    ]
     gate_blocks = [spread[0]] + [swap(spread[bit], "seq", bit) for bit in range(1, 4)]
     gate_shards = join_rows(gate_blocks, seq_place)
-    attn_near = [line_gather(after(shards[0], *spread), bits)]
-    attn_near.append(line_gather(after(shards[1], attn_near[0]), bits))
-    gate_near = []
-    gate_far = []
-    gate_near_pair = []
-    started = attn_near[0]
-    for layer in range(LAYERS):
-        gate_near.append(line_gather(after(gate_shards[layer], started), bits[:-1]))
-        gate_far.append(swap(gate_near[layer], "dp", 2 * bits[-1]))
-        gate_near_pair.append(swap(gate_near[layer], "dp", 1))
-        started = gate_far[layer]
-    attn_sets = [attn_finish(after(attn_near[0], *gate_shards)), attn_finish(attn_near[1])]
+    attn_line = line_gather(after(shards[0], *spread), bits)
+    attn_other = swap(after(attn_line, *gate_shards), "dp", 1)
+    near = [line_gather(after(gate_shards[0], attn_line), bits[:-1])]
+    far = [swap(near[0], "dp", 2 * bits[-1])]
+    near_pair = [swap(after(near[0], attn_other), "dp", 1)]
+    down_full = [
+        lax.all_gather(
+            down_weight[layer] if layer == 0 else after(down_weight[layer], near_pair[0]),
+            "dp",
+            axis=0,
+            tiled=True,
+        )
+        for layer in range(LAYERS)
+    ]
+    offsets = [dp_place ^ (2 * k) for k in range(line)]
     half = line // 2
-    offsets = [dp_place ^ (2 * k) for k in range(line)]
-    places = offsets + [offset ^ 1 for offset in offsets]
-
-    def gate_finish(layer):
-        far_pair = swap(gate_far[layer], "dp", 1)
-        blocks = [gate_near[layer], gate_far[layer], gate_near_pair[layer], far_pair]
-        return lay_out(blocks, places).reshape(model_width, 2 * units)
+    gate_places = offsets + [offset ^ 1 for offset in offsets]
+
+    def mlp_finish(layer, *waited):
+        far_pair = swap(after(far[layer], *waited), "dp", 1)
+        blocks = [near[layer], far[layer], near_pair[layer], far_pair]
+        gate_up = lay_out(blocks, gate_places).reshape(model_width, 2 * units)
+        return gate_up, down_full[layer], far_pair
 
     terms = [tokens.reshape(tok_len, model_width)]
     kept_state = []
-    gate_up_full = []
+    mlp_sets = []
+    attn_sets = [attn_finish(attn_line, attn_other)]
     for layer in range(LAYERS):
         first_full, second_full, gain_full, mlp_gain_full, bias_first, bias_second = attn_sets[layer]
         x, normed, queries, own_kv = before_attention(
             terms,
-            after(gain_full, gate_near[0], attn_near[1]) if layer == 0 else after(gain_full, gate_far[1]),
+            after(gain_full, near[0]) if layer == 0 else gain_full,
             first_full,
             second_full,
             bias_first,
@@ -927,21 +955,36 @@
             sin_wide,
         )
         kv_blocks = [own_kv] + [swap(own_kv, "seq", bit) for bit in range(1, 4)]
-        waited = (gate_near_pair[layer],)
+        waited = (near_pair[0],) if layer == 0 else ()
         mixed, middle, n2 = attention(
             queries, kv_blocks, biases, x, second_full, after(mlp_gain_full, *waited)
         )
-        n2_parts = group_rows(n2)
-        gate_up_full.append(gate_finish(layer))
-        gu_near, *outs_near = feed_forward(n2_parts[:2], gate_up_full[layer], down_full[layer])
-        gu_far, *outs_far = feed_forward(n2_parts[2:], gate_up_full[layer], down_full[layer])
-        far = add_low(outs_far[0], swap(outs_far[1], "seq", 1))
-        terms = [middle, outs_near[0], swap(outs_near[1], "seq", 1), swap(far, "seq", 2)]
+        n2_parts = group_rows(n2 if layer == 0 else after(n2, mlp_sets[1][2]))
+        if layer + 1 == LAYERS:
+            low_parts = group_rows(after(cotangent.reshape(tok_len, model_width), n2_parts[3]))
+        if layer == 0:
+            second_line = line_gather(after(shards[1], own_kv), bits[:1])
+            for bit in bits[1:]:
+                second_line = line_gather(after(second_line, n2), [bit])
+            second_other = swap(after(second_line, n2_parts[3]), "dp", 1)
+            near.append(line_gather(after(gate_shards[1], n2), bits[:-1]))
+            far.append(swap(after(near[1], n2_parts[3]), "dp", 2 * bits[-1]))
+            near_pair.append(swap(after(near[1], n2_parts[3]), "dp", 1))
+            mlp_sets.append(mlp_finish(0, n2))
+            n2_parts[0] = after(n2_parts[0], near[1])
+        gu_near, *outs_near = feed_forward(n2_parts[:2], *mlp_sets[layer][:2])
+        gu_far, *outs_far = feed_forward(n2_parts[2:], *mlp_sets[layer][:2])
+        if layer == 0:
+            attn_sets.append(attn_finish(second_line, second_other, gu_near))
+            mlp_sets.append(mlp_finish(1, outs_far[0]))
+            outs_far[0] = after(outs_far[0], far[1], near_pair[1])
+        across_sum = add_low(outs_far[0], swap(outs_far[1], "seq", 1))
+        terms = [middle, outs_near[0], swap(outs_near[1], "seq", 1)]
+        if layer + 1 < LAYERS:
+            terms.append(swap(across_sum, "seq", 2))
         kept_state.append((x, normed, queries, kv_blocks, mixed, middle, n2_parts, [gu_near, gu_far]))
-    activations = sum(term.astype(jnp.float32) for term in terms).astype(jnp.bfloat16)
     upstream = cotangent.reshape(tok_len, model_width)
-    upstream_low = upstream
-    results = [None] * LAYERS
+    states = [None] * LAYERS
     before = None
 
     def send_attn(state, pair, *waited):
@@ -950,7 +993,7 @@
 
     def sum_attn(state, arrived, *waited):
         near, far, got_near, got_far = state["attn_parts"]
-        sums = [
+        return [
             (
                 near[pair].astype(jnp.float32)
                 + got_near[pair].astype(jnp.float32)
@@ -958,73 +1001,103 @@
             ).astype(jnp.bfloat16)
             for pair in range(2)
         ]
-        return add_low(sums[0], swap(sums[1], "dp", 1))
-
-    def sum_gate(state, *waited):
-        near = add_low(state["keep_near"], after(state["near_got"], *waited))
-        return add_low(near, after(state["gate_got"], *waited))
-
-    def finish(state, gate_sum, attn_sum, *waited):
-        gate_terms = jnp.stack(line_scatter(gate_sum, bits[:-1]))
-        gate_rows = split_rows(after(gate_terms, *waited), seq_place, seq_devices)
+
+    def half_of(values, which):
+        count = values.shape[0] // 2
+        return lax.dynamic_slice_in_dim(values, which * count, count, 0)
+
+    def halve_down(values, bit):
+        upper = (line_place // bit) % 2
+        return half_of(values, upper), swap(half_of(values, 1 - upper), "dp", 2 * bit)
+
+    def step_one(state, *waited):
+        far_sum = state["far_sum"]
+        if line == 4:
+            far_sum = add_low(far_sum, after(state["inward"], *waited))
+        state["crossed"] = cross_middle(far_sum)
+        state["near_sum"] = add_low(state["keep_near"], after(state["near_got"], *waited))
+
+    def step_two(state, *waited):
+        state["near_sum"] = add_low(state["near_sum"], after(state["crossed"], *waited))
+
+    def step_three(state, *waited):
+        down = add_low(state["down_keep"], after(state["down_got"], *waited))
+        state["down_kept"], state["down_got"] = halve_down(down, bits[-1])
+
+    def finish(states):
+        other_side = swap(jnp.concatenate([state["attn_sums"][1] for state in states], axis=1), "dp", 1)
+        own_side = jnp.concatenate([state["attn_sums"][0] for state in states], axis=1)
+        owned = sum(
+            term.astype(jnp.float32) for term in line_scatter(add_low(own_side, other_side), bits)
+        ).reshape(LAYERS, chip_rows + 8, -1)
+        extra = owned[:, chip_rows:]
+        halves = owned[:, :chip_rows].reshape(LAYERS, 2, width_rows, -1)
+        mine = lax.dynamic_index_in_dim(halves, core, 1, keepdims=False)
+        theirs = swap(
+            lax.dynamic_index_in_dim(halves, 1 - core, 1, keepdims=False), "seq", 1
+        )
+        first_own = jnp.where(core == 0, mine, theirs)
+        second_own = jnp.where(core == 0, theirs, mine)
+
+        def cut(row, width, stop):
+            start = (0, row, device * width)
+            return lax.dynamic_slice(extra[:, :, :stop], start, (LAYERS, 1, width))[:, 0]
+
+        near_sums = jnp.concatenate([state["near_sum"] for state in states], axis=1)
+        gate_rows = split_rows(
+            line_scatter(near_sums, bits[:-1]), len(states), seq_place, seq_devices
+        )
         gate_owned = collect_columns(
             [gate_rows[0]] + [swap(gate_rows[bit], "seq", bit) for bit in range(1, 4)],
             seq_place,
             unit_rows,
             group_count,
         )
-        owned = sum(
-            term.astype(jnp.float32) for term in line_scatter(attn_sum, bits)
-        )
-        extra = owned[chip_rows:]
-        halves = owned[:chip_rows].reshape(2, width_rows, -1)
-        mine = lax.dynamic_index_in_dim(halves, core, 0, keepdims=False)
-        theirs = swap(
-            lax.dynamic_index_in_dim(halves, 1 - core, 0, keepdims=False), "seq", 1
-        )
-        first_own = jnp.where(core == 0, mine, theirs)
-        second_own = jnp.where(core == 0, theirs, mine)
-
-        def cut(row, width, stop):
-            return lax.dynamic_slice(extra[row, :stop], (device * width,), (width,))
-
-        results[state["layer"]] = (
+        down = jnp.concatenate(
+            [add_low(state["down_kept"], state["down_got"]) for state in states], axis=1
+        )
+        for bit in bits[-2::-1]:
+            kept, got = halve_down(down, bit)
+            down = kept.astype(jnp.float32) + got.astype(jnp.float32)
+            if bit > 1:
+                down = down.astype(jnp.bfloat16)
+        down_owned = down.reshape(len(states), unit_rows, model_width)
+        return (
             cut(0, width_rows, model_width),
-            jnp.concatenate([first_own, second_own[:, :KV_WIDTH]], axis=1),
+            jnp.concatenate([first_own, second_own[:, :, :KV_WIDTH]], axis=2),
             cut(2, SPLIT // (group_count * seq_devices), SPLIT),
             cut(3, KV_WIDTH // (group_count * seq_devices), KV_WIDTH),
-            second_own[:, KV_WIDTH:],
+            second_own[:, :, KV_WIDTH:],
             cut(1, width_rows, model_width),
             gate_owned,
-            state["down_sum"],
+            down_owned,
         )
 
     for layer in reversed(range(LAYERS)):
         x, normed, queries, kv_blocks, mixed, middle, n2_parts, gu_parts = kept_state[layer]
         first_full, second_full, gain_full, mlp_gain_full, _, _ = attn_sets[layer]
-        low_parts = group_rows(upstream_low)
         if before is not None:
-            low_parts[0] = after(low_parts[0], before["attn_parts"][3])
+            low_parts = group_rows(upstream_low, before["near_got"])
+            low_parts[0] = after(low_parts[0], *before["attn_parts"][2:])
+            attn_sent = [send_attn(before, pair, low_parts[3]) for pair in range(2)]
+            last_across = swap(after(across_sum, low_parts[3]), "seq", 2)
         keep_near, keep_far, send_near, send_far, down_part, own_out, across_out, pair_out = feed_back(
             low_parts,
             n2_parts,
             gu_parts,
-            gate_up_full[layer],
-            down_full[layer],
+            *mlp_sets[layer][:2],
             dp_place,
             group_count,
         )
+        if before is not None:
+            pair_out = after(pair_out, last_across, *attn_sent, before["down_got"])
         got = swap(pair_out, "seq", 1)
         out_terms = [own_out, got[0], swap(add_low(across_out, got[1]), "seq", 2)]
-        down_sum = lax.psum_scatter(down_part, "dp", scatter_dimension=0, tiled=True).astype(
-            jnp.float32
-        )
         got_far = swap(send_far, "dp", 1)
-        gate_far_sum = add_low(keep_far, got_far)
-        near_got = swap(after(send_near, got_far), "dp", 1)
+        near_got = swap(after(send_near, got), "dp", 1)
         if before is not None:
-            attn_far = send_attn(before, 1, out_terms[2])
-            gate_before = sum_gate(before, own_out)
+            step_one(before, own_out)
+            before["attn_sums"] = sum_attn(before, attn_sent, own_out)
         grad_middle, grad_low, mlp_gain_part, grad_query, own_term, *kv_terms = attention_back(
             upstream,
             middle,
@@ -1037,23 +1110,39 @@
             cos_wide,
             sin_wide,
         )
+        if before is not None:
+            kv_terms[2] = after(kv_terms[2], before["crossed"])
         kv_terms = [own_term] + [swap(kv_terms[bit - 1], "seq", bit) for bit in range(1, 4)]
+        far_sum = add_low(keep_far, after(got_far, grad_low))
+        waited = (far_sum,)
         if before is not None:
-            attn_near_sent = send_attn(before, 0, *kv_terms[1:])
+            step_two(before, grad_low)
+        state = {
+            "layer": layer,
+            "far_sum": far_sum,
+            "keep_near": keep_near,
+            "near_got": near_got,
+        }
+        if line == 4:
+            state["inward"] = line_steps(far_sum, [(0, 1), (3, 2)])
+        by_side = down_part.reshape(line, 2, unit_rows, model_width)
+        down_send = lax.dynamic_index_in_dim(by_side, 1 - side, 1, keepdims=False)
+        state["down_keep"] = lax.dynamic_index_in_dim(by_side, side, 1, keepdims=False)
+        state["down_got"] = swap(
+            after(down_send, *(out_terms[2:] if before is None else kv_terms[1:])), "dp", 1
+        )
         upstream, upstream_low, grad_kv, attn_gain_part, bias_first, bias_second = before_back(
             kv_terms,
             grad_query,
             x,
-            after(gain_full, gate_far_sum)
-            if before is None
-            else after(gain_full, gate_far_sum, gate_before),
+            after(gain_full, *waited),
             grad_middle,
             first_full,
             second_full,
             cos_wide,
             sin_wide,
         )
-        near, far, near_other, far_other = projection_grads(
+        near_x, far_x, near_other, far_other = projection_grads(
             normed,
             grad_query,
             grad_kv,
@@ -1069,25 +1158,23 @@
         )
         got_far_other = swap(far_other, "seq", 1)
         got_near_other = swap(near_other, "seq", 1)
-        state = {
-            "layer": layer,
-            "keep_near": keep_near,
-            "near_got": near_got,
-            "gate_got": swap(after(gate_far_sum, upstream_low), "dp", 2 * bits[-1]),
-            "attn_parts": (near, far, got_near_other, got_far_other),
-            "down_sum": down_sum,
-        }
+        state["attn_parts"] = (near_x, far_x, got_near_other, got_far_other)
         if before is not None:
-            attn_sum = sum_attn(before, [attn_near_sent, attn_far], grad_low)
-            finish(before, gate_before, attn_sum, near)
-        before = state
+            step_three(before, upstream)
+        states[layer] = before = state
+    step_one(before)
+    step_two(before)
+    step_three(before)
     arrived = [None, send_attn(before, 1)]
     arrived[0] = send_attn(before, 0)
-    finish(before, sum_gate(before), sum_attn(before, arrived))
+    before["attn_sums"] = sum_attn(before, arrived)
+    grads = finish(states)
+    terms.append(last_across)
+    activations = sum(term.astype(jnp.float32) for term in terms).astype(jnp.bfloat16)
     return (
         activations.reshape(seq_count, tok_len, model_width),
         upstream.reshape(seq_count, tok_len, model_width),
-    ) + tuple(jnp.stack([results[layer][k] for layer in range(LAYERS)]) for k in range(8))
+    ) + grads
 
 
 def solution(mesh):

time: 676 us -> 706 us (1.044)
  starting transfers between devices: 67.2 us -> 81.4 us
  waiting for transfers between devices: 302 us -> 316 us
  local copies, waits for them, and re-layouts: 64.1 us -> 53.9 us
  Pallas kernels: 177 us -> 187 us
    unnamed x240 -> x196, local copies, waits for them, and re-layouts: 48.4 us -> 22 us
    pallas_call x4, Pallas kernels: 36 us -> 49.3 us  [feed_forward(): call(kernel, [((rows, 2 * units), jnp.bfloat16)] + [((part_rows, D), jnp....]
    ppermute x0 -> x4, waiting for transfers between devices: none -> 9.76 us  [line_steps(): lax.ppermute(values, 'dp', [(2 * here + side, 2 * there + side) for here,...]
    ppermute x95 -> x90, starting transfers between devices: 67.1 us -> 75.6 us  [swap(): return lax.ppermute(values, axis, [(i, i ^ bit) for i in range(size)])]
    ppermute x95 -> x90, waiting for transfers between devices: 302 us -> 306 us  [swap(): return lax.ppermute(values, axis, [(i, i ^ bit) for i in range(size)])]
    convert_element_type x14 -> x18, other arithmetic: 15.4 us -> 17.2 us  [add_low(): (left.astype(jnp.float32) + right.astype(jnp.float32)).astype(jnp.bfloat16)]
  transfers between devices with their start and end apart: 99 -> 96, of which waited for: 35 -> 36; matrix products, arithmetic and copies ran while one was open for 8% -> 9% of each run, Pallas kernels for 22% -> 22%
where the time goes in v2:
time: 706 us; the launch traced here: 696 us
  waiting for transfers between devices  316 us (45%)
  Pallas kernels  187 us (26%)
  starting transfers between devices  81.4 us (12%)
  local copies, waits for them, and re-layouts  53.9 us (8%)
  between operations  29.2 us (4%)
  other arithmetic  28.4 us (4%)
    ppermute x90, waiting for transfers between devices, swap(): return lax.ppermute(values, axis, [(i, i ^ bit) for i in range(size)])  306 us
    ppermute x90, starting transfers between devices, swap(): return lax.ppermute(values, axis, [(i, i ^ bit) for i in range(size)])  75.6 us
    pallas_call x2, Pallas kernels, feed_back(): call(kernel, [((half, chunk, 2 * units), jnp.bfloat16), ((half, chunk, 2...  60.8 us
    pallas_call x4, Pallas kernels, feed_forward(): call(kernel, [((rows, 2 * units), jnp.bfloat16)] + [((part_rows, D), jnp....  49.3 us
    pallas_call x2, Pallas kernels, attention_back(): call(kernel, [((rows, D), jnp.float32), ((rows, D), jnp.bfloat16), ((1, D...  26.8 us
    unnamed x196, local copies, waits for them, and re-layouts  22 us
    pallas_call x2, Pallas kernels, attention(): call(kernel, [((rows, D), jnp.bfloat16), ((rows, D), jnp.float32), ((rows...  20.7 us
    convert_element_type x18, other arithmetic, add_low(): (left.astype(jnp.float32) + right.astype(jnp.float32)).astype(jnp.bfloat16)  17.2 us
  transfers between devices with their start and end apart: 96, of which 36 were waited for; matrix products, arithmetic and copies ran while one was open for 9% of the time, Pallas kernels for 22%

profile of v2, /device:TPU:0, one launch (start us, length us, event | category | flops | bytes accessed | tf_op | source)
XLA Modules:
  0.0 695.9 jit_solution(9444478976879821690)
XLA Ops:
  14.1 2.9 collective-permute-start.4
  24.4 3.8 collective-permute-done.1
  28.9 2.8 collective-permute-start.2
  44.3 7.2 %collective-permute-done.2 = bf16[2,64,1024]{2,1,0:T(8,128)(2,1)} collective-permute-done((bf16[2,64,1024]{2,1,0:T(8,128)(2,1)}, bf16[2,64,1024]{2,1,0:T(8,128)(2,1)}, u32[]{:S(2)}, u32[]{:S(2)}) %collective-permute-start.2) | collective-permute-done | bytes 262176 | tf_op jit(solution)/shard_map/ppermute | solution.py:781
  56.4 21.1 %collective-permute-done.6.refs_1_ = bf16[4,64,1024]{2,1,0:T(8,128)(2,1)S(1)} collective-permute-done((bf16[4,64,1024]{2,1,0:T(8,128)(2,1)S(1)}, bf16[4,64,1024]{2,1,0:T(8,128)(2,1)S(1)}, u32[]{:S(2)}, u32[]{:S(2)}) %collective-permute-start.6) | collective-permute-done | bytes 524320 | tf_op jit(solution)/shard_map/ppermute | solution.py:781
  79.9 2.7 collective-permute-done.13
  85.5 4.2 collective-permute-done.8.refs_3_
  92.9 2.9 assemble.2
  119.5 10.8 %attention.2 = (bf16[256,896]{1,0:T(8,128)(2,1)S(1)}, f32[256,896]{1,0:T(8,128)S(1)}, bf16[256,896]{1,0:T(8,128)(2,1)S(1)}) custom-call(bf16[2,2,896,64]{3,2,1,0:T(8,128)(2,1)S(1)} %copy-done.9, bf16[256,256]{1,0:T(8,128)(2,1)S(1)} %get-tuple-element.254.kv0.refs_8_, bf16[256,256]{1,0:T(8,128)(2,1)S(1)} %collective-permute-done.14.kv1.refs_9_, ...), custom_call_target="tpu_custom_call" | custom-call | bytes 42000 | tf_op jit(solution)/shard_map/attention/pallas_call | solution.py:159
  135.3 3.2 collective-permute-done.20.refs_1_
  138.6 2.6 collective-permute-start.21
  143.5 9.3 %collective-permute-done.30 = bf16[1,64,1024]{2,1,0:T(8,128)(2,1)S(1)} collective-permute-done((bf16[1,64,1024]{2,1,0:T(8,128)(2,1)S(1)}, bf16[1,64,1024]{2,1,0:T(8,128)(2,1)S(1)}, u32[]{:S(2)}, u32[]{:S(2)}) %collective-permute-start.30) | collective-permute-done | bytes 131104 | tf_op jit(solution)/shard_map/ppermute | solution.py:781
  156.8 2.6 collective-permute-start.26
  160.1 40.0 %collective-permute-done.31 = bf16[2,64,1024]{2,1,0:T(8,128)(2,1)} collective-permute-done((bf16[2,64,1024]{2,1,0:T(8,128)(2,1)S(1)}, bf16[2,64,1024]{2,1,0:T(8,128)(2,1)}, u32[]{:S(2)}, u32[]{:S(2)}) %collective-permute-start.31) | collective-permute-done | bytes 262176 | tf_op jit(solution)/shard_map/ppermute | solution.py:781
  201.8 2.6 collective-permute-start.32
  204.5 2.8 lay_out.2
  209.4 10.2 %feed_forward.5 = (bf16[512,2432]{1,0:T(8,128)(2,1)}, bf16[256,896]{1,0:T(8,128)(2,1)}, bf16[256,896]{1,0:T(8,128)(2,1)}) custom-call(bf16[256,896]{1,0:T(8,128)(2,1)} %copy-done.62, bf16[256,896]{1,0:T(8,128)(2,1)} %copy-done.63, bf16[896,2432]{1,0:T(8,128)(2,1)} %bitcast.152, bf16[1216,896]{1,0:T(8,128)(2,1)} %bitcast.171), custom_call_target="tpu_custom_call" | custom-call | bytes 36000 | tf_op jit(solution)/shard_map/feed_forward/pallas_call | solution.py:204
  220.1 18.7 %feed_forward.4 = (bf16[512,2432]{1,0:T(8,128)(2,1)}, bf16[256,896]{1,0:T(8,128)(2,1)}, bf16[256,896]{1,0:T(8,128)(2,1)}) custom-call(bf16[256,896]{1,0:T(8,128)(2,1)} %copy-done.24, bf16[256,896]{1,0:T(8,128)(2,1)} %collective-permute-done.19.refs_1_.refs_6_, bf16[896,2432]{1,0:T(8,128)(2,1)} %bitcast.153, bf16[1216,896]{1,0:T(8,128)(2,1)} %bitcast.172), custom_call_target="tpu_custom_call" | custom-call | bytes 36000 | tf_op jit(solution)/shard_map/feed_forward/pallas_call | solution.py:204
  244.0 9.9 %collective-permute-done.33.refs_2_ = bf16[4,64,1024]{2,1,0:T(8,128)(2,1)S(1)} collective-permute-done((bf16[4,64,1024]{2,1,0:T(8,128)(2,1)}, bf16[4,64,1024]{2,1,0:T(8,128)(2,1)S(1)}, u32[]{:S(2)}, u32[]{:S(2)}) %collective-permute-start.33) | collective-permute-done | bytes 524320 | tf_op jit(solution)/shard_map/ppermute | solution.py:781
  253.9 10.3 %collective-permute-done.34.refs_3_ = bf16[4,64,1024]{2,1,0:T(8,128)(2,1)S(1)} collective-permute-done((bf16[4,64,1024]{2,1,0:T(8,128)(2,1)}, bf16[4,64,1024]{2,1,0:T(8,128)(2,1)S(1)}, u32[]{:S(2)}, u32[]{:S(2)}) %collective-permute-start.34) | collective-permute-done | bytes 524320 | tf_op jit(solution)/shard_map/ppermute | solution.py:781
  267.7 2.8 assemble.3
  270.6 8.0 %collective-permute-done.28.refs_3_ = bf16[256,896]{1,0:T(8,128)(2,1)S(1)} collective-permute-done((bf16[256,896]{1,0:T(8,128)(2,1)S(1)}, bf16[256,896]{1,0:T(8,128)(2,1)S(1)}, u32[]{:S(2)}, u32[]{:S(2)}) %collective-permute-start.28) | collective-permute-done | bytes 458784 | tf_op jit(solution)/shard_map/ppermute | solution.py:781
  282.3 4.5 collective-permute-done.40.kv2.refs_10_
  288.7 9.9 %attention.3 = (bf16[256,896]{1,0:T(8,128)(2,1)S(1)}, f32[256,896]{1,0:T(8,128)S(1)}, bf16[256,896]{1,0:T(8,128)(2,1)S(1)}) custom-call(bf16[2,2,896,64]{3,2,1,0:T(8,128)(2,1)S(1)} %get-tuple-element.278.q_ref.refs_7_, bf16[256,256]{1,0:T(8,128)(2,1)S(1)} %get-tuple-element.279.kv0.refs_8_, bf16[256,256]{1,0:T(8,128)(2,1)S(1)} %collective-permute-done.39.kv1.refs_9_, ...), custom_call_target="tpu_custom_call" | custom-call | bytes 42000 | tf_op jit(solution)/shard_map/attention/pallas_call | solution.py:159
  301.9 11.1 %collective-permute-done.45.refs_0_.refs_7_ = bf16[256,896]{1,0:T(8,128)(2,1)S(1)} collective-permute-done((bf16[256,896]{1,0:T(8,128)(2,1)S(1)}, bf16[256,896]{1,0:T(8,128)(2,1)S(1)}, u32[]{:S(2)}, u32[]{:S(2)}) %collective-permute-start.45) | collective-permute-done | bytes 458784 | tf_op jit(solution)/shard_map/ppermute | solution.py:781
  316.9 10.8 %collective-permute-done.49.refs_3_ = bf16[256,896]{1,0:T(8,128)(2,1)} collective-permute-done((bf16[256,896]{1,0:T(8,128)(2,1)}, bf16[256,896]{1,0:T(8,128)(2,1)}, u32[]{:S(2)}, u32[]{:S(2)}) %collective-permute-start.49) | collective-permute-done | bytes 458784 | tf_op jit(solution)/shard_map/ppermute | solution.py:781
  332.7 10.2 %feed_forward.6 = (bf16[512,2432]{1,0:T(8,128)(2,1)}, bf16[256,896]{1,0:T(8,128)(2,1)}, bf16[256,896]{1,0:T(8,128)(2,1)}) custom-call(bf16[256,896]{1,0:T(8,128)(2,1)} %copy-done.25, bf16[256,896]{1,0:T(8,128)(2,1)} %collective-permute-done.43.refs_1_.refs_6_, bf16[896,2432]{1,0:T(8,128)(2,1)} %bitcast.155, ...), custom_call_target="tpu_custom_call" | custom-call | bytes 36000 | tf_op jit(solution)/shard_map/feed_forward/pallas_call | solution.py:204
  342.9 10.2 %feed_forward.7 = (bf16[512,2432]{1,0:T(8,128)(2,1)}, bf16[256,896]{1,0:T(8,128)(2,1)}, bf16[256,896]{1,0:T(8,128)(2,1)}) custom-call(bf16[256,896]{1,0:T(8,128)(2,1)} %copy-done.64, bf16[256,896]{1,0:T(8,128)(2,1)} %copy-done.65, bf16[896,2432]{1,0:T(8,128)(2,1)} %bitcast.156, bf16[1216,896]{1,0:T(8,128)(2,1)} %all-gather.4.cloned.1.call-done.refs_3_.refs_12_), custom_call_target="tpu_custom_call" | custom-call | bytes 36000 | tf_op jit(solution)/shard_map/feed_forward/pallas_call | solution.py:204
  353.1 30.5 %feed_back.2 = (bf16[2,112,2432]{2,1,0:T(8,128)(2,1)}, bf16[2,112,2432]{2,1,0:T(8,128)(2,1)}, bf16[2,112,2432]{2,1,0:T(8,128)(2,1)}, bf16[2,112,2432]{2,1,0:T(8,...) custom-call(s32[1]{0:T(128)} %bitcast.3.refs_0_, ...), custom_call_target="tpu_custom_call" | custom-call | bytes 100000 | tf_op jit(solution)/shard_map/feed_back/pallas_call | solution.py:307
  389.8 10.9 %collective-permute-done.52.refs_5_ = bf16[256,896]{1,0:T(8,128)(2,1)S(1)} collective-permute-done((bf16[256,896]{1,0:T(8,128)(2,1)S(1)}, bf16[256,896]{1,0:T(8,128)(2,1)S(1)}, u32[]{:S(2)}, u32[]{:S(2)}) %collective-permute-start.52) | collective-permute-done | bytes 458784 | tf_op jit(solution)/shard_map/ppermute | solution.py:781
  401.7 13.3 %attention_back.2 = (f32[256,896]{1,0:T(8,128)S(1)}, bf16[256,896]{1,0:T(8,128)(2,1)S(1)}, f32[1,896]{1,0:T(1,128)S(1)}, bf16[256,896]{1,0:T(8,128)(2,1)S(1)}, f...) custom-call(bf16[256,896]{1,0:T(8,128)(2,1)} %bitcast.47.refs_1_.ref, ...), custom_call_target="tpu_custom_call" | custom-call | bytes 52000 | tf_op jit(solution)/shard_map/attention_back/pallas_call | solution.py:450
  418.5 3.3 collective-permute-done.54.refs_2_
  425.1 3.5 projection_grads.2
  432.9 10.9 %collective-permute-done.57.refs_3_ = bf16[256,896]{1,0:T(8,128)(2,1)} collective-permute-done((bf16[256,896]{1,0:T(8,128)(2,1)S(1)}, bf16[256,896]{1,0:T(8,128)(2,1)}, u32[]{:S(2)}, u32[]{:S(2)}) %collective-permute-start.57) | collective-permute-done | bytes 458784 | tf_op jit(solution)/shard_map/ppermute | solution.py:781
  448.1 2.6 fusion.14
  455.2 30.3 %feed_back.3 = (bf16[2,112,2432]{2,1,0:T(8,128)(2,1)}, bf16[2,112,2432]{2,1,0:T(8,128)(2,1)}, bf16[2,112,2432]{2,1,0:T(8,128)(2,1)}, bf16[2,112,2432]{2,1,0:T(8,...) custom-call(s32[1]{0:T(128)} %bitcast.3.refs_0_, ...), custom_call_target="tpu_custom_call" | custom-call | bytes 100000 | tf_op jit(solution)/shard_map/feed_back/pallas_call | solution.py:307
  498.5 7.6 %collective-permute-done.68.refs_5_ = bf16[256,896]{1,0:T(8,128)(2,1)S(1)} collective-permute-done((bf16[256,896]{1,0:T(8,128)(2,1)S(1)}, bf16[256,896]{1,0:T(8,128)(2,1)S(1)}, u32[]{:S(2)}, u32[]{:S(2)}) %collective-permute-start.68) | collective-permute-done | bytes 458784 | tf_op jit(solution)/shard_map/ppermute | solution.py:781
  506.2 13.5 %attention_back.3 = (f32[256,896]{1,0:T(8,128)S(1)}, bf16[256,896]{1,0:T(8,128)(2,1)S(1)}, f32[1,896]{1,0:T(1,128)S(1)}, bf16[256,896]{1,0:T(8,128)(2,1)S(1)}, f...) custom-call(f32[256,896]{1,0:T(8,128)S(1)} %get-tuple-element.312.re, ...), custom_call_target="tpu_custom_call" | custom-call | bytes 52000 | tf_op jit(solution)/shard_map/attention_back/pallas_call | solution.py:450
  535.2 4.2 collective-permute-done.83
  539.6 9.8 %collective-permute-done.84 = bf16[2,112,2432]{2,1,0:T(8,128)(2,1)S(1)} collective-permute-done((bf16[2,112,2432]{2,1,0:T(8,128)(2,1)S(1)}, bf16[2,112,2432]{2,1,0:T(8,128)(2,1)S(1)}, u32[]{:S(2)}, u32[]{:S(2)}) %collective-permute-start.84) | collective-permute-done | bytes 1089568 | tf_op jit(solution)/shard_map/ppermute | solution.py:802
  552.5 9.8 %collective-permute-done.90 = bf16[4,152,896]{2,1,0:T(8,128)(2,1)S(1)} collective-permute-done((bf16[4,152,896]{2,1,0:T(8,128)(2,1)S(1)}, bf16[4,152,896]{2,1,0:T(8,128)(2,1)S(1)}, u32[]{:S(2)}, u32[]{:S(2)}) %collective-permute-start.90) | collective-permute-done | bytes 1089568 | tf_op jit(solution)/shard_map/ppermute | solution.py:781
  564.3 8.8 %collective-permute-done.92 = bf16[2,152,896]{2,1,0:T(8,128)(2,1)S(1)} collective-permute-done((bf16[2,152,896]{2,1,0:T(8,128)(2,1)S(1)}, bf16[2,152,896]{2,1,0:T(8,128)(2,1)S(1)}, u32[]{:S(2)}, u32[]{:S(2)}) %collective-permute-start.92) | collective-permute-done | bytes 544800 | tf_op jit(solution)/shard_map/ppermute | solution.py:781
  578.4 33.9 %collective-permute-done.91 = bf16[2,152,896]{2,1,0:T(8,128)(2,1)S(1)} collective-permute-done((bf16[2,152,896]{2,1,0:T(8,128)(2,1)S(1)}, bf16[2,152,896]{2,1,0:T(8,128)(2,1)S(1)}, u32[]{:S(2)}, u32[]{:S(2)}) %collective-permute-start.91) | collective-permute-done | bytes 544800 | tf_op jit(solution)/shard_map/ppermute | solution.py:781
  618.1 18.8 %collective-permute-done.80 = bf16[2,128,1024]{2,1,0:T(8,128)(2,1)S(1)} collective-permute-done((bf16[2,128,1024]{2,1,0:T(8,128)(2,1)S(1)}, bf16[2,128,1024]{2,1,0:T(8,128)(2,1)S(1)}, u32[]{:S(2)}, u32[]{:S(2)}) %collective-permute-start.80) | collective-permute-done | bytes 524320 | tf_op jit(solution)/shard_map/ppermute | solution.py:781
  637.2 26.4 %collective-permute-done.93 = bf16[1,304,896]{2,1,0:T(8,128)(2,1)S(1)} collective-permute-done((bf16[1,304,896]{2,1,0:T(8,128)(2,1)S(1)}, bf16[1,304,896]{2,1,0:T(8,128)(2,1)S(1)}, u32[]{:S(2)}, u32[]{:S(2)}) %collective-permute-start.93) | collective-permute-done | bytes 544800 | tf_op jit(solution)/shard_map/ppermute | solution.py:781
  670.4 5.4 collective-permute-done.88.refs_2_
  675.9 5.8 collective-permute-done.89.refs_3_
  683.7 3.0 copy.70
  (485 shorter events, 176.3 us)
Async XLA Ops:
  7.2 202.2 %all-gather.6.cloned.1.call-start = ((), (), s32[]{:S(2)}) async-start(), calls=%async_computation.1 | async-start | bytes 2451456 | tf_op jit(solution)/shard_map/all_gather | solution.py:923
  14.0 29.8 %collective-permute-start.3 = (bf16[2,28,2432]{2,1,0:T(8,128)(2,1)S(1)}, bf16[2,28,2432]{2,1,0:T(8,128)(2,1)S(1)}, u32[]{:S(2)}, u32[]{:S(2)}) collective-permute-start(bf16[2,28,2432]{2,1,0:T(8,128)(2,1)S(1)} %get-tuple-element.241), channel_id=1, source_target_pairs={{0,1},{1,0},{2,3},{3,2},{4,5},{5,4},{6,7},{7,6},{8,9},{9,8},{10,11... | collective-permute-start | bytes 817160 | tf_op jit(solution)/shard_map/ppermute | solution.py:781
  14.1 29.7 %collective-permute-start.4 = (bf16[2,28,2432]{2,1,0:T(8,128)(2,1)S(1)}, bf16[2,28,2432]{2,1,0:T(8,128)(2,1)S(1)}, u32[]{:S(2)}, u32[]{:S(2)}) collective-permute-start(bf16[2,28,2432]{2,1,0:T(8,128)(2,1)S(1)} %get-tuple-element.242), channel_id=1, source_target_pairs={{0,2},{1,3},{2,0},{3,1},{4,6},{5,7},{6,4},{7,5},{8,10},{9,11},{10,... | collective-permute-start | bytes 817160 | tf_op jit(solution)/shard_map/ppermute | solution.py:781
  17.0 26.8 %collective-permute-start.5 = (bf16[2,28,2432]{2,1,0:T(8,128)(2,1)S(1)}, bf16[2,28,2432]{2,1,0:T(8,128)(2,1)S(1)}, u32[]{:S(2)}, u32[]{:S(2)}) collective-permute-start(bf16[2,28,2432]{2,1,0:T(8,128)(2,1)S(1)} %get-tuple-element.243), channel_id=1, source_target_pairs={{0,3},{1,2},{2,1},{3,0},{4,7},{5,6},{6,5},{7,4},{8,11},{9,10},{10,... | collective-permute-start | bytes 817160 | tf_op jit(solution)/shard_map/ppermute | solution.py:781
  17.9 314.7 %all-gather.4.cloned.1.call-start = ((), (), s32[]{:S(2)}) async-start(), calls=%async_computation | async-start | bytes 2451456 | tf_op jit(solution)/shard_map/all_gather | solution.py:923
  28.9 22.6 %collective-permute-start.2 = (bf16[2,64,1024]{2,1,0:T(8,128)(2,1)}, bf16[2,64,1024]{2,1,0:T(8,128)(2,1)}, u32[]{:S(2)}, u32[]{:S(2)}) collective-permute-start(bf16[2,64,1024]{2,1,0:T(8,128)(2,1)} %pad_maximum_fusion.6), channel_id=1, source_target_pairs={{0,16},{4,20},{8,24},{12,28},{16,0},{20,4},{24,8},{28,12},{1,17},{... | collective-permute-start | bytes 786440 | tf_op jit(solution)/shard_map/ppermute | solution.py:781
  52.5 25.0 %collective-permute-start.6 = (bf16[4,64,1024]{2,1,0:T(8,128)(2,1)S(1)}, bf16[4,64,1024]{2,1,0:T(8,128)(2,1)S(1)}, u32[]{:S(2)}, u32[]{:S(2)}) collective-permute-start(bf16[4,64,1024]{2,1,0:T(8,128)(2,1)S(1)} %constant_dynamic-update-slice_fusion.refs_0_), channel_id=1, source_target_pairs={{0,4},{4,0},{8,12},{12,8},{16,20},{20,16},{24,28},{28,24},{1,5},{5... | collective-permute-start | bytes 1572872 | tf_op jit(solution)/shard_map/ppermute | solution.py:781
  54.3 28.3 %collective-permute-start.13 = (bf16[1,112,2432]{2,1,0:T(8,128)(2,1)S(1)}, bf16[1,112,2432]{2,1,0:T(8,128)(2,1)S(1)}, u32[]{:S(2)}, u32[]{:S(2)}) collective-permute-start(bf16[1,112,2432]{2,1,0:T(8,128)(2,1)S(1)} %get-tuple-element.249), channel_id=1, source_target_pairs={{0,8},{4,12},{8,0},{12,4},{16,24},{20,28},{24,16},{28,20},{1,9},{5... | collective-permute-start | bytes 1634312 | tf_op jit(solution)/shard_map/ppermute | solution.py:781
  54.9 35.5 %collective-permute-start.9 = (bf16[4,64,1024]{2,1,0:T(8,128)(2,1)S(1)}, bf16[4,64,1024]{2,1,0:T(8,128)(2,1)S(1)}, u32[]{:S(2)}, u32[]{:S(2)}) collective-permute-start(bf16[4,64,1024]{2,1,0:T(8,128)(2,1)S(1)} %constant_dynamic-update-slice_fusion.refs_0_), channel_id=1, source_target_pairs={{0,1},{1,0},{2,3},{3,2},{4,5},{5,4},{6,7},{7,6},{8,9},{9,8},{10,11... | collective-permute-start | bytes 1572872 | tf_op jit(solution)/shard_map/ppermute | solution.py:781
  55.0 30.1 %collective-permute-start.7 = (bf16[4,64,1024]{2,1,0:T(8,128)(2,1)S(1)}, bf16[4,64,1024]{2,1,0:T(8,128)(2,1)}, u32[]{:S(2)}, u32[]{:S(2)}) collective-permute-start(bf16[4,64,1024]{2,1,0:T(8,128)(2,1)S(1)} %constant_dynamic-update-slice_fusion.refs_0_), channel_id=1, source_target_pairs={{0,2},{1,3},{2,0},{3,1},{4,6},{5,7},{6,4},{7,5},{8,10},{9,11},{10,... | collective-permute-start | bytes 1572872 | tf_op jit(solution)/shard_map/ppermute | solution.py:781
  83.5 33.6 %collective-permute-start.17 = (bf16[2,112,2432]{2,1,0:T(8,128)(2,1)}, bf16[2,112,2432]{2,1,0:T(8,128)(2,1)}, u32[]{:S(2)}, u32[]{:S(2)}) collective-permute-start(bf16[2,112,2432]{2,1,0:T(8,128)(2,1)} %constant_dynamic-update-slice_fusion.3.refs_0_), channel_id=1, source_target_pairs={{0,4},{4,0},{8,12},{12,8},{16,20},{20,16},{24,28},{28,24},{1,5},{5... | collective-permute-start | bytes 3268616 | tf_op jit(solution)/shard_map/ppermute | solution.py:781
  90.4 48.1 %collective-permute-start.20 = (bf16[2,112,2432]{2,1,0:T(8,128)(2,1)}, bf16[2,112,2432]{2,1,0:T(8,128)(2,1)}, u32[]{:S(2)}, u32[]{:S(2)}) collective-permute-start(bf16[2,112,2432]{2,1,0:T(8,128)(2,1)} %constant_dynamic-update-slice_fusion.3.refs_0_), channel_id=1, source_target_pairs={{0,16},{4,20},{8,24},{12,28},{16,0},{20,4},{24,8},{28,12},{1,17},{... | collective-permute-start | bytes 3268616 | tf_op jit(solution)/shard_map/ppermute | solution.py:781
  132.4 21.3 %collective-permute-start.18 = (bf16[1,112,2432]{2,1,0:T(8,128)(2,1)S(1)}, bf16[1,112,2432]{2,1,0:T(8,128)(2,1)S(1)}, u32[]{:S(2)}, u32[]{:S(2)}) collective-permute-start(bf16[1,112,2432]{2,1,0:T(8,128)(2,1)S(1)} %copy-done.31), channel_id=1, source_target_pairs={{0,8},{4,12},{8,0},{12,4},{16,24},{20,28},{24,16},{28,20},{1,9},{5... | collective-permute-start | bytes 1634312 | tf_op jit(solution)/shard_map/ppermute | solution.py:781
  138.6 65.9 %collective-permute-start.21 = (bf16[2,112,2432]{2,1,0:T(8,128)(2,1)}, bf16[2,112,2432]{2,1,0:T(8,128)(2,1)}, u32[]{:S(2)}, u32[]{:S(2)}) collective-permute-start(bf16[2,112,2432]{2,1,0:T(8,128)(2,1)} %collective-permute-done.20.refs_1_), channel_id=1, source_target_pairs={{0,4},{4,0},{8,12},{12,8},{16,20},{20,16},{24,28},{28,24},{1,5},{5... | collective-permute-start | bytes 3268616 | tf_op jit(solution)/shard_map/ppermute | solution.py:781
  152.9 47.3 %collective-permute-start.31 = (bf16[2,64,1024]{2,1,0:T(8,128)(2,1)S(1)}, bf16[2,64,1024]{2,1,0:T(8,128)(2,1)}, u32[]{:S(2)}, u32[]{:S(2)}) collective-permute-start(bf16[2,64,1024]{2,1,0:T(8,128)(2,1)S(1)} %pad_maximum_fusion.7), channel_id=1, source_target_pairs={{0,16},{4,20},{8,24},{12,28},{16,0},{20,4},{24,8},{28,12},{1,17},{... | collective-permute-start | bytes 786440 | tf_op jit(solution)/shard_map/ppermute | solution.py:781
  154.6 86.4 %collective-permute-start.25 = (bf16[2,112,2432]{2,1,0:T(8,128)(2,1)}, bf16[2,112,2432]{2,1,0:T(8,128)(2,1)}, u32[]{:S(2)}, u32[]{:S(2)}) collective-permute-start(bf16[2,112,2432]{2,1,0:T(8,128)(2,1)} %constant_dynamic-update-slice_fusion.5.refs_0_), channel_id=1, source_target_pairs={{0,16},{4,20},{8,24},{12,28},{16,0},{20,4},{24,8},{28,12},{1,17},{... | collective-permute-start | bytes 3268616 | tf_op jit(solution)/shard_map/ppermute | solution.py:781
  156.8 84.2 %collective-permute-start.26 = (bf16[2,112,2432]{2,1,0:T(8,128)(2,1)}, bf16[2,112,2432]{2,1,0:T(8,128)(2,1)}, u32[]{:S(2)}, u32[]{:S(2)}) collective-permute-start(bf16[2,112,2432]{2,1,0:T(8,128)(2,1)} %constant_dynamic-update-slice_fusion.5.refs_0_), channel_id=1, source_target_pairs={{0,4},{4,0},{8,12},{12,8},{16,20},{20,16},{24,28},{28,24},{1,5},{5... | collective-permute-start | bytes 3268616 | tf_op jit(solution)/shard_map/ppermute | solution.py:781
  201.8 38.7 %collective-permute-start.32 = (bf16[4,64,1024]{2,1,0:T(8,128)(2,1)}, bf16[4,64,1024]{2,1,0:T(8,128)(2,1)}, u32[]{:S(2)}, u32[]{:S(2)}) collective-permute-start(bf16[4,64,1024]{2,1,0:T(8,128)(2,1)} %constant_dynamic-update-slice_fusion.7.refs_0_), channel_id=1, source_target_pairs={{0,4},{4,0},{8,12},{12,8},{16,20},{20,16},{24,28},{28,24},{1,5},{5... | collective-permute-start | bytes 1572872 | tf_op jit(solution)/shard_map/ppermute | solution.py:781
  219.6 21.9 %collective-permute-start.27 = (bf16[256,896]{1,0:T(8,128)(2,1)}, bf16[256,896]{1,0:T(8,128)(2,1)}, u32[]{:S(2)}, u32[]{:S(2)}) collective-permute-start(bf16[256,896]{1,0:T(8,128)(2,1)} %get-tuple-element.268), channel_id=1, source_target_pairs={{0,1},{1,0},{2,3},{3,2},{4,5},{5,4},{6,7},{7,6},{8,9},{9,8},{10,11... | collective-permute-start | bytes 1376264 | tf_op jit(solution)/shard_map/ppermute | solution.py:781
  240.5 23.7 %collective-permute-start.34 = (bf16[4,64,1024]{2,1,0:T(8,128)(2,1)}, bf16[4,64,1024]{2,1,0:T(8,128)(2,1)S(1)}, u32[]{:S(2)}, u32[]{:S(2)}) collective-permute-start(bf16[4,64,1024]{2,1,0:T(8,128)(2,1)} %collective-permute-done.32.refs_1_), channel_id=1, source_target_pairs={{0,2},{1,3},{2,0},{3,1},{4,6},{5,7},{6,4},{7,5},{8,10},{9,11},{10,... | collective-permute-start | bytes 1572872 | tf_op jit(solution)/shard_map/ppermute | solution.py:781
  240.9 24.5 %collective-permute-start.35 = (bf16[4,64,1024]{2,1,0:T(8,128)(2,1)}, bf16[4,64,1024]{2,1,0:T(8,128)(2,1)S(1)}, u32[]{:S(2)}, u32[]{:S(2)}) collective-permute-start(bf16[4,64,1024]{2,1,0:T(8,128)(2,1)} %constant_dynamic-update-slice_fusion.7.refs_0_), channel_id=1, source_target_pairs={{0,1},{1,0},{2,3},{3,2},{4,5},{5,4},{6,7},{7,6},{8,9},{9,8},{10,11... | collective-permute-start | bytes 1572872 | tf_op jit(solution)/shard_map/ppermute | solution.py:781
  241.0 25.1 %collective-permute-start.36 = (bf16[4,64,1024]{2,1,0:T(8,128)(2,1)}, bf16[4,64,1024]{2,1,0:T(8,128)(2,1)S(1)}, u32[]{:S(2)}, u32[]{:S(2)}) collective-permute-start(bf16[4,64,1024]{2,1,0:T(8,128)(2,1)} %collective-permute-done.32.refs_1_), channel_id=1, source_target_pairs={{0,1},{1,0},{2,3},{3,2},{4,5},{5,4},{6,7},{7,6},{8,9},{9,8},{10,11... | collective-permute-start | bytes 1572872 | tf_op jit(solution)/shard_map/ppermute | solution.py:781
  241.5 58.8 %collective-permute-start.42 = (bf16[2,112,2432]{2,1,0:T(8,128)(2,1)}, bf16[2,112,2432]{2,1,0:T(8,128)(2,1)S(1)}, u32[]{:S(2)}, u32[]{:S(2)}) collective-permute-start(bf16[2,112,2432]{2,1,0:T(8,128)(2,1)} %collective-permute-done.25.refs_1_), channel_id=1, source_target_pairs={{0,4},{4,0},{8,12},{12,8},{16,20},{20,16},{24,28},{28,24},{1,5},{5... | collective-permute-start | bytes 3268616 | tf_op jit(solution)/shard_map/ppermute | solution.py:781
  316.4 36.6 %collective-permute-start.48 = (bf16[256,896]{1,0:T(8,128)(2,1)}, bf16[256,896]{1,0:T(8,128)(2,1)}, u32[]{:S(2)}, u32[]{:S(2)}) collective-permute-start(bf16[256,896]{1,0:T(8,128)(2,1)} %bitcast.47.refs_1_.refs_0_), channel_id=1, source_target_pairs={{0,1},{1,0},{2,3},{3,2},{4,5},{5,4},{6,7},{7,6},{8,9},{9,8},{10,11... | collective-permute-start | bytes 1376264 | tf_op jit(solution)/shard_map/ppermute | solution.py:781
  327.7 25.3 %collective-permute-start.50 = (bf16[256,896]{1,0:T(8,128)(2,1)}, bf16[256,896]{1,0:T(8,128)(2,1)}, u32[]{:S(2)}, u32[]{:S(2)}) collective-permute-start(bf16[256,896]{1,0:T(8,128)(2,1)} %collective-permute-done.49.refs_3_), channel_id=1, source_target_pairs={{0,1},{1,0},{2,3},{3,2},{4,5},{5,4},{6,7},{7,6},{8,9},{9,8},{10,11... | collective-permute-start | bytes 1376264 | tf_op jit(solution)/shard_map/ppermute | solution.py:781
  384.2 33.1 %collective-permute-start.56 = (bf16[2,112,2432]{2,1,0:T(8,128)(2,1)}, bf16[2,112,2432]{2,1,0:T(8,128)(2,1)S(1)}, u32[]{:S(2)}, u32[]{:S(2)}) collective-permute-start(bf16[2,112,2432]{2,1,0:T(8,128)(2,1)} %get-tuple-element.302), channel_id=1, source_target_pairs={{0,4},{4,0},{8,12},{12,8},{16,20},{20,16},{24,28},{28,24},{1,5},{5... | collective-permute-start | bytes 3268616 | tf_op jit(solution)/shard_map/ppermute | solution.py:781
  389.4 54.4 %collective-permute-start.58 = (bf16[2,112,2432]{2,1,0:T(8,128)(2,1)}, bf16[2,112,2432]{2,1,0:T(8,128)(2,1)}, u32[]{:S(2)}, u32[]{:S(2)}) collective-permute-start(bf16[2,112,2432]{2,1,0:T(8,128)(2,1)} %get-tuple-element.309), channel_id=1, source_target_pairs={{0,4},{4,0},{8,12},{12,8},{16,20},{20,16},{24,28},{28,24},{1,5},{5... | collective-permute-start | bytes 3268616 | tf_op jit(solution)/shard_map/ppermute | solution.py:781
  446.4 39.1 %collective-permute-start.71 = (bf16[2,112,2432]{2,1,0:T(8,128)(2,1)S(1)}, bf16[2,112,2432]{2,1,0:T(8,128)(2,1)S(1)}, u32[]{:S(2)}, u32[]{:S(2)}) collective-permute-start(bf16[2,112,2432]{2,1,0:T(8,128)(2,1)S(1)} %copy-done.59), channel_id=1, source_target_pairs={{0,8},{4,12},{24,16},{28,20},{1,9},{5,13},{25,17},{29,21},{2,10},{... | collective-permute-start | bytes 3268616 | tf_op jit(solution)/shard_map/ppermute | solution.py:802
  447.8 37.8 %collective-permute-start.66 = (bf16[4,152,896]{2,1,0:T(8,128)(2,1)S(1)}, bf16[4,152,896]{2,1,0:T(8,128)(2,1)}, u32[]{:S(2)}, u32[]{:S(2)}) collective-permute-start(bf16[4,152,896]{2,1,0:T(8,128)(2,1)S(1)} %dynamic-slice_bitcast_fusion.1), channel_id=1, source_target_pairs={{0,4},{4,0},{8,12},{12,8},{16,20},{20,16},{24,28},{28,24},{1,5},{5... | collective-permute-start | bytes 3268616 | tf_op jit(solution)/shard_map/ppermute | solution.py:781
  450.7 35.0 %collective-permute-start.64 = (bf16[4,64,1024]{2,1,0:T(8,128)(2,1)}, bf16[4,64,1024]{2,1,0:T(8,128)(2,1)S(1)}, u32[]{:S(2)}, u32[]{:S(2)}) collective-permute-start(bf16[4,64,1024]{2,1,0:T(8,128)(2,1)} %get-tuple-element.327), channel_id=1, source_target_pairs={{0,2},{1,3},{2,0},{3,1},{4,6},{5,7},{6,4},{7,5},{8,10},{9,11},{10,... | collective-permute-start | bytes 1572872 | tf_op jit(solution)/shard_map/ppermute | solution.py:781
  452.3 33.4 %collective-permute-start.65 = (bf16[4,64,1024]{2,1,0:T(8,128)(2,1)}, bf16[4,64,1024]{2,1,0:T(8,128)(2,1)S(1)}, u32[]{:S(2)}, u32[]{:S(2)}) collective-permute-start(bf16[4,64,1024]{2,1,0:T(8,128)(2,1)} %get-tuple-element.328), channel_id=1, source_target_pairs={{0,2},{1,3},{2,0},{3,1},{4,6},{5,7},{6,4},{7,5},{8,10},{9,11},{10,... | collective-permute-start | bytes 1572872 | tf_op jit(solution)/shard_map/ppermute | solution.py:781
  453.6 32.1 %collective-permute-start.60 = (bf16[256,896]{1,0:T(8,128)(2,1)}, bf16[256,896]{1,0:T(8,128)(2,1)}, u32[]{:S(2)}, u32[]{:S(2)}) collective-permute-start(bf16[256,896]{1,0:T(8,128)(2,1)} %add_convert_fusion.17), channel_id=1, source_target_pairs={{0,2},{1,3},{2,0},{3,1},{4,6},{5,7},{6,4},{7,5},{8,10},{9,11},{10,... | collective-permute-start | bytes 1376264 | tf_op jit(solution)/shard_map/ppermute | solution.py:781
  487.1 34.3 %collective-permute-start.72 = (bf16[2,112,2432]{2,1,0:T(8,128)(2,1)}, bf16[2,112,2432]{2,1,0:T(8,128)(2,1)}, u32[]{:S(2)}, u32[]{:S(2)}) collective-permute-start(bf16[2,112,2432]{2,1,0:T(8,128)(2,1)} %add_convert_fusion.6), channel_id=1, source_target_pairs={{8,16},{12,20},{16,8},{20,12},{9,17},{13,21},{17,9},{21,13},{10,18... | collective-permute-start | bytes 3268616 | tf_op jit(solution)/shard_map/ppermute | solution.py:802
  488.9 32.6 %collective-permute-start.74 = (bf16[2,112,2432]{2,1,0:T(8,128)(2,1)}, bf16[2,112,2432]{2,1,0:T(8,128)(2,1)}, u32[]{:S(2)}, u32[]{:S(2)}) collective-permute-start(bf16[2,112,2432]{2,1,0:T(8,128)(2,1)} %get-tuple-element.341), channel_id=1, source_target_pairs={{0,4},{4,0},{8,12},{12,8},{16,20},{20,16},{24,28},{28,24},{1,5},{5... | collective-permute-start | bytes 3268616 | tf_op jit(solution)/shard_map/ppermute | solution.py:781
  497.0 42.3 %collective-permute-start.83 = (bf16[2,112,2432]{2,1,0:T(8,128)(2,1)S(1)}, bf16[2,112,2432]{2,1,0:T(8,128)(2,1)S(1)}, u32[]{:S(2)}, u32[]{:S(2)}) collective-permute-start(bf16[2,112,2432]{2,1,0:T(8,128)(2,1)S(1)} %copy-done.90), channel_id=1, source_target_pairs={{0,4},{4,0},{8,12},{12,8},{16,20},{20,16},{24,28},{28,24},{1,5},{5... | collective-permute-start | bytes 3268616 | tf_op jit(solution)/shard_map/ppermute | solution.py:781
  523.2 26.2 %collective-permute-start.84 = (bf16[2,112,2432]{2,1,0:T(8,128)(2,1)S(1)}, bf16[2,112,2432]{2,1,0:T(8,128)(2,1)S(1)}, u32[]{:S(2)}, u32[]{:S(2)}) collective-permute-start(bf16[2,112,2432]{2,1,0:T(8,128)(2,1)S(1)} %add_convert_fusion.5), channel_id=1, source_target_pairs={{0,8},{4,12},{24,16},{28,20},{1,9},{5,13},{25,17},{29,21},{2,10},{... | collective-permute-start | bytes 3268616 | tf_op jit(solution)/shard_map/ppermute | solution.py:802
  533.2 42.7 %collective-permute-start.75 = (bf16[2,4,64,1024]{3,2,1,0:T(8,128)(2,1)S(1)}, bf16[2,4,64,1024]{3,2,1,0:T(8,128)(2,1)S(1)}, u32[]{:S(2)}, u32[]{:S(2)}) collective-permute-start(bf16[2,4,64,1024]{3,2,1,0:T(8,128)(2,1)S(1)} %get-tuple-element.355), channel_id=1, source_target_pairs={{0,1},{1,0},{2,3},{3,2},{4,5},{5,4},{6,7},{7,6},{8,9},{9,8},{10,11... | collective-permute-start | bytes 3145736 | tf_op jit(solution)/shard_map/ppermute | solution.py:781
  533.2 29.1 %collective-permute-start.90 = (bf16[4,152,896]{2,1,0:T(8,128)(2,1)S(1)}, bf16[4,152,896]{2,1,0:T(8,128)(2,1)S(1)}, u32[]{:S(2)}, u32[]{:S(2)}) collective-permute-start(bf16[4,152,896]{2,1,0:T(8,128)(2,1)S(1)} %dynamic-slice_bitcast_fusion), channel_id=1, source_target_pairs={{0,4},{4,0},{8,12},{12,8},{16,20},{20,16},{24,28},{28,24},{1,5},{5... | collective-permute-start | bytes 3268616 | tf_op jit(solution)/shard_map/ppermute | solution.py:781
  539.4 33.7 %collective-permute-start.92 = (bf16[2,152,896]{2,1,0:T(8,128)(2,1)S(1)}, bf16[2,152,896]{2,1,0:T(8,128)(2,1)S(1)}, u32[]{:S(2)}, u32[]{:S(2)}) collective-permute-start(bf16[2,152,896]{2,1,0:T(8,128)(2,1)S(1)} %constant_dynamic-slice_fusion), channel_id=1, source_target_pairs={{0,16},{4,20},{8,24},{12,28},{16,0},{20,4},{24,8},{28,12},{1,17},{... | collective-permute-start | bytes 1634312 | tf_op jit(solution)/shard_map/ppermute | solution.py:781
  549.6 62.8 %collective-permute-start.85 = (bf16[2,112,2432]{2,1,0:T(8,128)(2,1)S(1)}, bf16[2,112,2432]{2,1,0:T(8,128)(2,1)S(1)}, u32[]{:S(2)}, u32[]{:S(2)}) collective-permute-start(bf16[2,112,2432]{2,1,0:T(8,128)(2,1)S(1)} %add_convert_fusion.3), channel_id=1, source_target_pairs={{8,16},{12,20},{16,8},{20,12},{9,17},{13,21},{17,9},{21,13},{10,18... | collective-permute-start | bytes 3268616 | tf_op jit(solution)/shard_map/ppermute | solution.py:802
  550.8 22.5 %collective-permute-start.77 = (bf16[4,64,1024]{2,1,0:T(8,128)(2,1)S(1)}, bf16[4,64,1024]{2,1,0:T(8,128)(2,1)S(1)}, u32[]{:S(2)}, u32[]{:S(2)}) collective-permute-start(bf16[4,64,1024]{2,1,0:T(8,128)(2,1)S(1)} %get-tuple-element.408), channel_id=1, source_target_pairs={{0,2},{1,3},{2,0},{3,1},{4,6},{5,7},{6,4},{7,5},{8,10},{9,11},{10,... | collective-permute-start | bytes 1572872 | tf_op jit(solution)/shard_map/ppermute | solution.py:781
  573.1 39.1 %collective-permute-start.91 = (bf16[2,152,896]{2,1,0:T(8,128)(2,1)S(1)}, bf16[2,152,896]{2,1,0:T(8,128)(2,1)S(1)}, u32[]{:S(2)}, u32[]{:S(2)}) collective-permute-start(bf16[2,152,896]{2,1,0:T(8,128)(2,1)S(1)} %constant_dynamic-slice_fusion.1), channel_id=1, source_target_pairs={{0,16},{4,20},{8,24},{12,28},{16,0},{20,4},{24,8},{28,12},{1,17},{... | collective-permute-start | bytes 1634312 | tf_op jit(solution)/shard_map/ppermute | solution.py:781
  573.3 42.8 %collective-permute-start.44 = (bf16[256,896]{1,0:T(8,128)(2,1)S(1)}, bf16[256,896]{1,0:T(8,128)(2,1)S(1)}, u32[]{:S(2)}, u32[]{:S(2)}) collective-permute-start(bf16[256,896]{1,0:T(8,128)(2,1)S(1)} %copy-done.91), channel_id=1, source_target_pairs={{0,1},{1,0},{2,3},{3,2},{4,5},{5,4},{6,7},{7,6},{8,9},{9,8},{10,11... | collective-permute-start | bytes 1376264 | tf_op jit(solution)/shard_map/ppermute | solution.py:781
  576.6 36.2 %collective-permute-start.79 = (bf16[4,128,1024]{2,1,0:T(8,128)(2,1)S(1)}, bf16[4,128,1024]{2,1,0:T(8,128)(2,1)S(1)}, u32[]{:S(2)}, u32[]{:S(2)}) collective-permute-start(bf16[4,128,1024]{2,1,0:T(8,128)(2,1)S(1)} %pad_maximum_fusion.1), channel_id=1, source_target_pairs={{0,4},{4,0},{8,12},{12,8},{16,20},{20,16},{24,28},{28,24},{1,5},{5... | collective-permute-start | bytes 3145736 | tf_op jit(solution)/shard_map/ppermute | solution.py:781
  613.3 23.6 %collective-permute-start.80 = (bf16[2,128,1024]{2,1,0:T(8,128)(2,1)S(1)}, bf16[2,128,1024]{2,1,0:T(8,128)(2,1)S(1)}, u32[]{:S(2)}, u32[]{:S(2)}) collective-permute-start(bf16[2,128,1024]{2,1,0:T(8,128)(2,1)S(1)} %slice.390), channel_id=1, source_target_pairs={{0,16},{4,20},{8,24},{12,28},{16,0},{20,4},{24,8},{28,12},{1,17},{... | collective-permute-start | bytes 1572872 | tf_op jit(solution)/shard_map/ppermute | solution.py:781
  613.6 51.1 %collective-permute-start.86 = (bf16[224,2432]{1,0:T(8,128)(2,1)S(1)}, bf16[224,2432]{1,0:T(8,128)(2,1)S(1)}, u32[]{:S(2)}, u32[]{:S(2)}) collective-permute-start(bf16[224,2432]{1,0:T(8,128)(2,1)S(1)} %get-tuple-element.404), channel_id=1, source_target_pairs={{0,8},{4,12},{8,0},{12,4},{16,24},{20,28},{24,16},{28,20},{1,9},{5... | collective-permute-start | bytes 3268616 | tf_op jit(solution)/shard_map/ppermute | solution.py:781
  615.9 47.7 %collective-permute-start.93 = (bf16[1,304,896]{2,1,0:T(8,128)(2,1)S(1)}, bf16[1,304,896]{2,1,0:T(8,128)(2,1)S(1)}, u32[]{:S(2)}, u32[]{:S(2)}) collective-permute-start(bf16[1,304,896]{2,1,0:T(8,128)(2,1)S(1)} %fusion.11), channel_id=1, source_target_pairs={{0,8},{4,12},{8,0},{12,4},{16,24},{20,28},{24,16},{28,20},{1,9},{5... | collective-permute-start | bytes 1634312 | tf_op jit(solution)/shard_map/ppermute | solution.py:781
  637.1 30.4 %collective-permute-start.81 = (bf16[128,1024]{1,0:T(8,128)(2,1)S(1)}, bf16[128,1024]{1,0:T(8,128)(2,1)S(1)}, u32[]{:S(2)}, u32[]{:S(2)}) collective-permute-start(bf16[128,1024]{1,0:T(8,128)(2,1)S(1)} %slice_bitcast_fusion.5), channel_id=1, source_target_pairs={{0,8},{4,12},{8,0},{12,4},{16,24},{20,28},{24,16},{28,20},{1,9},{5... | collective-permute-start | bytes 786440 | tf_op jit(solution)/shard_map/ppermute | solution.py:781
  (141 other events, 1637.9 us)
Sparse Core Ops, SparseCore 0:
  18.0 67.3 all-gather.5
  159.5 79.0 all-gather.3

commit v3 on v2

--- a/solution.py
+++ b/solution.py
@@ -235,6 +235,9 @@
     part_rows = gz_parts[0].shape[0]
     rows = count * part_rows
     units = down_full.shape[0]
+    unit_rows = units // group_count
+    packed = chunk + unit_rows * D // (2 * units)
+    once = pl.Buffered(1)
     steps = pl.cdiv(units, TILE)
     last = units - (steps - 1) * TILE
 
@@ -244,10 +247,10 @@
         n2_refs = refs[count : 2 * count]
         gu_refs = refs[2 * count : 2 * count + gu_count]
         w_ref, d_ref = refs[2 * count + gu_count : 2 * count + gu_count + 2]
-        keep_near, keep_far, send_near, send_far, down_ref, own_ref, across_ref, pair_ref = refs[
-            2 * count + gu_count + 2 : 2 * count + gu_count + 10
+        keep_near, keep_far, send_near, send_far, own_ref, across_ref, pair_ref = refs[
+            2 * count + gu_count + 2 : 2 * count + gu_count + 9
         ]
-        total, gz, n2t = refs[-3:]
+        total, gz, n2t, down = refs[-4:]
         side, mine = place_ref[0] % 2, place_ref[0] // 2
         step = pl.program_id(0)
 
@@ -259,13 +262,29 @@
                 gz[here, :] = gz_refs[place][...]
                 n2t[:, here] = n2_refs[place][...].T
 
+        def write(spot, even, odd, rows, lanes):
+            keep = jnp.where(side == 0, even, odd)
+            send = jnp.where(side == 0, odd, even)
+            slot = mine ^ spot
+            beyond = far_slot(mine, spot, line)
+
+            @pl.when(slot < half)
+            def _():
+                keep_near[slot, rows, lanes] = keep
+                send_near[slot, rows, lanes] = send
+
+            @pl.when(slot >= half)
+            def _():
+                keep_far[beyond, rows, lanes] = keep
+                send_far[beyond, rows, lanes] = send
+
         def work(width):
             gu = jnp.concatenate([ref[:, : 2 * width] for ref in gu_refs], axis=0).astype(jnp.float32)
             gate, up = gu[:, :width], gu[:, width:]
             sig = jax.nn.sigmoid(gate)
             act = gate * sig
             hidden = (act * up).astype(jnp.bfloat16)
-            down_ref[:width, :] = dot(hidden, gz[...], TN).astype(jnp.bfloat16)
+            down[pl.ds(pl.multiple_of(step * TILE, 128), width), :] = dot(hidden, gz[...], TN)
             grad = dot(gz[...], d_ref[:width, :], NT)
             d_gate = grad * up * (sig + act * (1.0 - sig))
             d_up = grad * act
@@ -274,20 +293,7 @@
             for spot in range(line):
                 even = part[2 * spot * chunk : (2 * spot + 1) * chunk].astype(jnp.bfloat16)
                 odd = part[(2 * spot + 1) * chunk : (2 * spot + 2) * chunk].astype(jnp.bfloat16)
-                keep = jnp.where(side == 0, even, odd)
-                send = jnp.where(side == 0, odd, even)
-                slot = mine ^ spot
-                beyond = far_slot(mine, spot, line)
-
-                @pl.when(slot < half)
-                def _():
-                    keep_near[slot, :, : 2 * width] = keep
-                    send_near[slot, :, : 2 * width] = send
-
-                @pl.when(slot >= half)
-                def _():
-                    keep_far[beyond, :, : 2 * width] = keep
-                    send_far[beyond, :, : 2 * width] = send
+                write(spot, even, odd, slice(0, chunk), pl.ds(pl.multiple_of(step * 2 * TILE, 128), 2 * width))
 
             return dot(both, w_ref[:, : 2 * width], NT)
 
@@ -298,6 +304,14 @@
         @pl.when(step == steps - 1)
         def _():
             summed = (total[...] + work(last)).astype(jnp.bfloat16)
+            for spot in range(line):
+                even, odd = (
+                    fold(down[place * unit_rows : place * unit_rows + unit_rows, :], 2 * units).astype(
+                        jnp.bfloat16
+                    )
+                    for place in (2 * spot, 2 * spot + 1)
+                )
+                write(spot, even, odd, slice(chunk, packed), slice(0, 2 * units))
             own_ref[...] = summed[:part_rows]
             pair_ref[0] = summed[part_rows : 2 * part_rows]
             across_ref[...] = summed[2 * part_rows : 3 * part_rows]
@@ -307,11 +321,10 @@
     return call(
         kernel,
         [
-            ((half, chunk, 2 * units), jnp.bfloat16),
-            ((half, chunk, 2 * units), jnp.bfloat16),
-            ((half, chunk, 2 * units), jnp.bfloat16),
-            ((half, chunk, 2 * units), jnp.bfloat16),
-            ((units, D), jnp.bfloat16),
+            ((half, packed, 2 * units), jnp.bfloat16),
+            ((half, packed, 2 * units), jnp.bfloat16),
+            ((half, packed, 2 * units), jnp.bfloat16),
+            ((half, packed, 2 * units), jnp.bfloat16),
             ((part_rows, D), jnp.bfloat16),
             ((part_rows, D), jnp.bfloat16),
             ((2, part_rows, D), jnp.bfloat16),
@@ -321,25 +334,25 @@
             pltpu.VMEM((rows, D), jnp.float32),
             pltpu.VMEM((rows, D), jnp.bfloat16),
             pltpu.VMEM((D, rows), jnp.bfloat16),
+            pltpu.VMEM((units, D), jnp.float32),
         ],
-        limit=56,
+        limit=60,
         grid=(steps,),
         in_specs=[pl.BlockSpec(memory_space=pltpu.SMEM)]
-        + [pl.BlockSpec((part_rows, D), whole)] * (2 * count)
+        + [pl.BlockSpec((part_rows, D), whole, pipeline_mode=once)] * (2 * count)
         + [pl.BlockSpec((rows // gu_count, 2 * TILE), lambda step: (0, step))] * gu_count
         + [
             pl.BlockSpec((D, 2 * TILE), lambda step: (0, step)),
             pl.BlockSpec((TILE, D), lambda step: (step, 0)),
         ],
         out_specs=[
-            pl.BlockSpec((half, chunk, 2 * TILE), lambda step: (0, 0, step)),
-            pl.BlockSpec((half, chunk, 2 * TILE), lambda step: (0, 0, step)),
-            pl.BlockSpec((half, chunk, 2 * TILE), lambda step: (0, 0, step)),
-            pl.BlockSpec((half, chunk, 2 * TILE), lambda step: (0, 0, step)),
-            pl.BlockSpec((TILE, D), lambda step: (step, 0)),
-            pl.BlockSpec((part_rows, D), whole),
-            pl.BlockSpec((part_rows, D), whole),
-            pl.BlockSpec((2, part_rows, D), lambda step: (0, 0, 0)),
+            pl.BlockSpec((half, packed, 2 * units), lambda step: (0, 0, 0), pipeline_mode=once),
+            pl.BlockSpec((half, packed, 2 * units), lambda step: (0, 0, 0), pipeline_mode=once),
+            pl.BlockSpec((half, packed, 2 * units), lambda step: (0, 0, 0), pipeline_mode=once),
+            pl.BlockSpec((half, packed, 2 * units), lambda step: (0, 0, 0), pipeline_mode=once),
+            pl.BlockSpec((part_rows, D), whole, pipeline_mode=once),
+            pl.BlockSpec((part_rows, D), whole, pipeline_mode=once),
+            pl.BlockSpec((2, part_rows, D), lambda step: (0, 0, 0), pipeline_mode=once),
         ],
     )(dp_place.reshape(1).astype(jnp.int32), *gz_parts, *n2_parts, *gu_parts, gate_up_full, down_full)
 
@@ -590,11 +603,42 @@
     )(place.reshape(1).astype(jnp.int32), *blocks)[0]
 
 
-def join_rows(blocks, place):
+def fold(rows, columns):
+    high = rows.shape[0] * 128 // columns
+    wide = rows.shape[1] // 128
+    return jnp.concatenate(
+        [
+            jnp.concatenate(
+                [rows[high * r : high * r + high, 128 * c : 128 * c + 128] for r in range(columns // 128)],
+                axis=1,
+            )
+            for c in range(wide)
+        ],
+        axis=0,
+    )
+
+
+def unfold(rows, width):
+    high = rows.shape[0] * 128 // width
+    wide = rows.shape[1] // 128
+    return jnp.concatenate(
+        [
+            jnp.concatenate(
+                [rows[high * c : high * c + high, 128 * r : 128 * r + 128] for c in range(width // 128)],
+                axis=1,
+            )
+            for r in range(wide)
+        ],
+        axis=0,
+    )
+
+
+def pack_rows(blocks, down, place):
     owners = len(blocks)
     layers, rows, columns = blocks[0].shape
-
-    def kernel(place_ref, *refs):
+    total = owners * rows + down.shape[1] * down.shape[2] // columns
+
+    def kernel(place_ref, down_ref, *refs):
         ins, outs = refs[:owners], refs[owners:]
         for layer in range(layers):
             parts = []
@@ -605,30 +649,56 @@
                         place_ref[0] == owner ^ bit, ins[bit][layer].astype(jnp.float32), part
                     )
                 parts.append(part)
+            parts.append(fold(down_ref[layer].astype(jnp.float32), columns))
             outs[layer][0] = jnp.concatenate(parts, axis=0).astype(jnp.bfloat16)
 
     return call(
         kernel,
-        [((1, owners * rows, columns), jnp.bfloat16)] * layers,
-        2.0,
-        in_specs=[pl.BlockSpec(memory_space=pltpu.SMEM)] + [FULL] * owners,
+        [((1, total, columns), jnp.bfloat16)] * layers,
+        3.0,
+        in_specs=[pl.BlockSpec(memory_space=pltpu.SMEM)] + [FULL] * (owners + 1),
         out_specs=[FULL] * layers,
-    )(place.reshape(1).astype(jnp.int32), *blocks)
-
-
-def split_rows(terms, layers, place, count):
-    number = len(terms)
-    layer_rows = terms[0].shape[0] // layers
-    columns = terms[0].shape[1]
-    rows = layer_rows // count
+    )(place.reshape(1).astype(jnp.int32), down, *blocks)
+
+
+def unpack(parts, places, chunk):
+    count, total, columns = parts[0].shape
+    number = count * len(parts)
+    unit_rows = (total - chunk) * columns // D
 
     def kernel(place_ref, *refs):
-        ins, outs = refs[:number], refs[number:]
+        ins, gate_ref, down_ref = refs[: len(parts)], refs[-2], refs[-1]
+        for which in range(len(parts)):
+            for k in range(count):
+                spot = place_ref[which * count + k]
+                gate_ref[spot] = ins[which][k, :chunk, :]
+                down_ref[spot] = unfold(ins[which][k, chunk:, :].astype(jnp.float32), D).astype(
+                    jnp.bfloat16
+                )
+
+    gate, down = call(
+        kernel,
+        [((number, chunk, columns), jnp.bfloat16), ((number, unit_rows, D), jnp.bfloat16)],
+        5.0,
+        in_specs=[pl.BlockSpec(memory_space=pltpu.SMEM)] + [FULL] * len(parts),
+        out_specs=[FULL] * 2,
+    )(jnp.stack(places).astype(jnp.int32), *parts)
+    return gate.reshape(number * chunk, columns), down.reshape(number * unit_rows, D)
+
+
+def split_rows(terms, chunk, place, count):
+    layers = len(terms)
+    total_rows, columns = terms[0][0].shape
+    rows = chunk // count
+    unit_rows = (total_rows - chunk) * columns // D
+
+    def kernel(place_ref, *refs):
+        ins, outs, down_ref = refs[: 2 * layers], refs[2 * layers : -1], refs[-1]
         for layer in range(layers):
-            here = slice(layer * layer_rows, (layer + 1) * layer_rows)
-            total = ins[0][here, :].astype(jnp.float32)
-            for ref in ins[1:]:
-                total = total + ref[here, :].astype(jnp.float32)
+            total = ins[2 * layer][...].astype(jnp.float32) + ins[2 * layer + 1][...].astype(
+                jnp.float32
+            )
+            down_ref[layer] = unfold(total[chunk:], D)
             for owner in range(count):
                 block = total[owner * rows : owner * rows + rows].astype(jnp.bfloat16)
                 for bit in range(count):
@@ -637,46 +707,15 @@
                     def _():
                         outs[bit][layer] = block
 
-    return call(
-        kernel,
-        [((layers, rows, columns), jnp.bfloat16)] * count,
-        2.0,
-        in_specs=[pl.BlockSpec(memory_space=pltpu.SMEM)] + [FULL] * number,
-        out_specs=[FULL] * count,
-    )(place.reshape(1).astype(jnp.int32), *terms)
-
-
-def lay_out(blocks, places):
-    total = len(places)
-    shape = blocks[0].shape[-2:]
-    count = len(blocks)
-
-    def kernel(place_ref, *refs):
-        ins, out, sems = refs[:count], refs[count], refs[-1]
-        copies = []
-        spot = 0
-        for which in range(count):
-            many = blocks[which].shape[0] if blocks[which].ndim == 3 else 1
-            for k in range(many):
-                source = ins[which].at[k] if blocks[which].ndim == 3 else ins[which]
-                copies.append(
-                    pltpu.make_async_copy(source, out.at[place_ref[spot]], sems.at[spot])
-                )
-                spot += 1
-        for copy in copies:
-            copy.start()
-        for copy in copies:
-            copy.wait()
-
-    outside = pl.BlockSpec(memory_space=pltpu.HBM)
-    return call(
-        kernel,
-        [((total,) + shape, blocks[0].dtype)],
-        2.5,
-        [pltpu.SemaphoreType.DMA((total,))],
-        in_specs=[pl.BlockSpec(memory_space=pltpu.SMEM)] + [outside] * count,
-        out_specs=[outside],
-    )(jnp.stack(places).astype(jnp.int32), *blocks)[0]
+    *blocks, down = call(
+        kernel,
+        [((layers, rows, columns), jnp.bfloat16)] * count
+        + [((layers, unit_rows, D), jnp.float32)],
+        3.0,
+        in_specs=[pl.BlockSpec(memory_space=pltpu.SMEM)] + [FULL] * (2 * layers),
+        out_specs=[FULL] * (count + 1),
+    )(place.reshape(1).astype(jnp.int32), *[term for pair in terms for term in pair])
+    return blocks, down
 
 
 def assemble(parts, places, chip_rows):
@@ -913,30 +952,33 @@
     spread = spread_columns(gate_up_weight, seq_place, unit_rows, group_count, seq_devices)
     shards = [attn_shard(layer)[None] for layer in range(LAYERS)]
     gate_blocks = [spread[0]] + [swap(spread[bit], "seq", bit) for bit in range(1, 4)]
-    gate_shards = join_rows(gate_blocks, seq_place)
+    gate_shards = pack_rows(gate_blocks, down_weight, seq_place)
     attn_line = line_gather(after(shards[0], *spread), bits)
     attn_other = swap(after(attn_line, *gate_shards), "dp", 1)
+    def outward(crossed):
+        if line != 4:
+            return crossed
+        passed = line_steps(crossed, [(1, 0), (2, 3)])
+        return jnp.where((line_place == 1) | (line_place == 2), crossed, passed)
+
     near = [line_gather(after(gate_shards[0], attn_line), bits[:-1])]
-    far = [swap(near[0], "dp", 2 * bits[-1])]
+    near.append(line_gather(after(gate_shards[1], near[0]), bits[:-1]))
     near_pair = [swap(after(near[0], attn_other), "dp", 1)]
-    down_full = [
-        lax.all_gather(
-            down_weight[layer] if layer == 0 else after(down_weight[layer], near_pair[0]),
-            "dp",
-            axis=0,
-            tiled=True,
-        )
-        for layer in range(LAYERS)
-    ]
+    crossed = [cross_middle(near[0])]
+    far = []
     offsets = [dp_place ^ (2 * k) for k in range(line)]
     half = line // 2
-    gate_places = offsets + [offset ^ 1 for offset in offsets]
-
-    def mlp_finish(layer, *waited):
-        far_pair = swap(after(far[layer], *waited), "dp", 1)
-        blocks = [near[layer], far[layer], near_pair[layer], far_pair]
-        gate_up = lay_out(blocks, gate_places).reshape(model_width, 2 * units)
-        return gate_up, down_full[layer], far_pair
+    if line == 4:
+        beyond = [jnp.where(line_place < 2, 2 + k, 1 - k) * 2 + side for k in range(2)]
+    else:
+        beyond = offsets[half:]
+    places = offsets[:half] + beyond
+    places = [offsets[:half], beyond, [spot ^ 1 for spot in offsets[:half]], [spot ^ 1 for spot in beyond]]
+    places = [spot for group in places for spot in group]
+
+    def mlp_finish(layer, far_pair):
+        parts = [near[layer], far[layer], near_pair[layer], far_pair]
+        return unpack(parts, places, seq_devices * width_rows)
 
     terms = [tokens.reshape(tok_len, model_width)]
     kept_state = []
@@ -946,7 +988,7 @@
         first_full, second_full, gain_full, mlp_gain_full, bias_first, bias_second = attn_sets[layer]
         x, normed, queries, own_kv = before_attention(
             terms,
-            after(gain_full, near[0]) if layer == 0 else gain_full,
+            after(gain_full, *near) if layer == 0 else after(gain_full, near_pair[1]),
             first_full,
             second_full,
             bias_first,
@@ -959,25 +1001,29 @@
         mixed, middle, n2 = attention(
             queries, kv_blocks, biases, x, second_full, after(mlp_gain_full, *waited)
         )
-        n2_parts = group_rows(n2 if layer == 0 else after(n2, mlp_sets[1][2]))
-        if layer + 1 == LAYERS:
-            low_parts = group_rows(after(cotangent.reshape(tok_len, model_width), n2_parts[3]))
+        n2_parts = group_rows(n2)
         if layer == 0:
             second_line = line_gather(after(shards[1], own_kv), bits[:1])
             for bit in bits[1:]:
                 second_line = line_gather(after(second_line, n2), [bit])
             second_other = swap(after(second_line, n2_parts[3]), "dp", 1)
-            near.append(line_gather(after(gate_shards[1], n2), bits[:-1]))
-            far.append(swap(after(near[1], n2_parts[3]), "dp", 2 * bits[-1]))
-            near_pair.append(swap(after(near[1], n2_parts[3]), "dp", 1))
-            mlp_sets.append(mlp_finish(0, n2))
-            n2_parts[0] = after(n2_parts[0], near[1])
-        gu_near, *outs_near = feed_forward(n2_parts[:2], *mlp_sets[layer][:2])
-        gu_far, *outs_far = feed_forward(n2_parts[2:], *mlp_sets[layer][:2])
+            far.append(outward(after(crossed[0], n2)))
+            far_pair = swap(far[0], "dp", 1)
+            crossed.append(cross_middle(after(near[1], n2)))
+            attn_sets.append(attn_finish(second_line, second_other, n2_parts[3]))
+            near_pair.append(swap(after(near[1], far_pair), "dp", 1))
+            n2_parts[0] = after(n2_parts[0], attn_sets[1][2], crossed[1])
+        mlp_sets.append(mlp_finish(layer, far_pair))
+        gu_near, *outs_near = feed_forward(n2_parts[:2], *mlp_sets[layer])
+        if layer + 1 == LAYERS:
+            low_parts = group_rows(
+                after(cotangent.reshape(tok_len, model_width), n2_parts[3]), gu_near
+            )
+        gu_far, *outs_far = feed_forward(n2_parts[2:], *mlp_sets[layer])
         if layer == 0:
-            attn_sets.append(attn_finish(second_line, second_other, gu_near))
-            mlp_sets.append(mlp_finish(1, outs_far[0]))
-            outs_far[0] = after(outs_far[0], far[1], near_pair[1])
+            far.append(outward(crossed[1]))
+            outs_far[0] = after(outs_far[0], far[1])
+            far_pair = swap(after(far[1], outs_far[0]), "dp", 1)
         across_sum = add_low(outs_far[0], swap(outs_far[1], "seq", 1))
         terms = [middle, outs_near[0], swap(outs_near[1], "seq", 1)]
         if layer + 1 < LAYERS:
@@ -1002,14 +1048,6 @@
             for pair in range(2)
         ]
 
-    def half_of(values, which):
-        count = values.shape[0] // 2
-        return lax.dynamic_slice_in_dim(values, which * count, count, 0)
-
-    def halve_down(values, bit):
-        upper = (line_place // bit) % 2
-        return half_of(values, upper), swap(half_of(values, 1 - upper), "dp", 2 * bit)
-
     def step_one(state, *waited):
         far_sum = state["far_sum"]
         if line == 4:
@@ -1018,14 +1056,12 @@
         state["near_sum"] = add_low(state["keep_near"], after(state["near_got"], *waited))
 
     def step_two(state, *waited):
-        state["near_sum"] = add_low(state["near_sum"], after(state["crossed"], *waited))
-
-    def step_three(state, *waited):
-        down = add_low(state["down_keep"], after(state["down_got"], *waited))
-        state["down_kept"], state["down_got"] = halve_down(down, bits[-1])
+        near_sum = add_low(state["near_sum"], after(state["crossed"], *waited))
+        state["terms"] = line_scatter(near_sum, bits[:-1])
 
     def finish(states):
-        other_side = swap(jnp.concatenate([state["attn_sums"][1] for state in states], axis=1), "dp", 1)
+        other_side = jnp.concatenate([state["attn_sums"][1] for state in states], axis=1)
+        other_side = swap(after(other_side, states[0]["near_got"]), "dp", 1)
         own_side = jnp.concatenate([state["attn_sums"][0] for state in states], axis=1)
         owned = sum(
             term.astype(jnp.float32) for term in line_scatter(add_low(own_side, other_side), bits)
@@ -1043,9 +1079,8 @@
             start = (0, row, device * width)
             return lax.dynamic_slice(extra[:, :, :stop], start, (LAYERS, 1, width))[:, 0]
 
-        near_sums = jnp.concatenate([state["near_sum"] for state in states], axis=1)
-        gate_rows = split_rows(
-            line_scatter(near_sums, bits[:-1]), len(states), seq_place, seq_devices
+        gate_rows, down_owned = split_rows(
+            [state["terms"] for state in states], seq_devices * width_rows, seq_place, seq_devices
         )
         gate_owned = collect_columns(
             [gate_rows[0]] + [swap(gate_rows[bit], "seq", bit) for bit in range(1, 4)],
@@ -1053,15 +1088,6 @@
             unit_rows,
             group_count,
         )
-        down = jnp.concatenate(
-            [add_low(state["down_kept"], state["down_got"]) for state in states], axis=1
-        )
-        for bit in bits[-2::-1]:
-            kept, got = halve_down(down, bit)
-            down = kept.astype(jnp.float32) + got.astype(jnp.float32)
-            if bit > 1:
-                down = down.astype(jnp.bfloat16)
-        down_owned = down.reshape(len(states), unit_rows, model_width)
         return (
             cut(0, width_rows, model_width),
             jnp.concatenate([first_own, second_own[:, :, :KV_WIDTH]], axis=2),
@@ -1077,24 +1103,24 @@
         x, normed, queries, kv_blocks, mixed, middle, n2_parts, gu_parts = kept_state[layer]
         first_full, second_full, gain_full, mlp_gain_full, _, _ = attn_sets[layer]
         if before is not None:
-            low_parts = group_rows(upstream_low, before["near_got"])
+            low_parts = group_rows(upstream_low)
             low_parts[0] = after(low_parts[0], *before["attn_parts"][2:])
             attn_sent = [send_attn(before, pair, low_parts[3]) for pair in range(2)]
             last_across = swap(after(across_sum, low_parts[3]), "seq", 2)
-        keep_near, keep_far, send_near, send_far, down_part, own_out, across_out, pair_out = feed_back(
+        keep_near, keep_far, send_near, send_far, own_out, across_out, pair_out = feed_back(
             low_parts,
             n2_parts,
             gu_parts,
-            *mlp_sets[layer][:2],
+            *mlp_sets[layer],
             dp_place,
             group_count,
         )
         if before is not None:
-            pair_out = after(pair_out, last_across, *attn_sent, before["down_got"])
+            pair_out = after(pair_out, last_across, *attn_sent, before["near_got"], before["inward"])
         got = swap(pair_out, "seq", 1)
         out_terms = [own_out, got[0], swap(add_low(across_out, got[1]), "seq", 2)]
         got_far = swap(send_far, "dp", 1)
-        near_got = swap(after(send_near, got), "dp", 1)
+        near_got = swap(after(send_near, got_far), "dp", 1)
         if before is not None:
             step_one(before, own_out)
             before["attn_sums"] = sum_attn(before, attn_sent, own_out)
@@ -1110,38 +1136,28 @@
             cos_wide,
             sin_wide,
         )
-        if before is not None:
-            kv_terms[2] = after(kv_terms[2], before["crossed"])
         kv_terms = [own_term] + [swap(kv_terms[bit - 1], "seq", bit) for bit in range(1, 4)]
-        far_sum = add_low(keep_far, after(got_far, grad_low))
-        waited = (far_sum,)
-        if before is not None:
-            step_two(before, grad_low)
+        upstream, upstream_low, grad_kv, attn_gain_part, bias_first, bias_second = before_back(
+            kv_terms,
+            grad_query,
+            x,
+            gain_full,
+            grad_middle,
+            first_full,
+            second_full,
+            cos_wide,
+            sin_wide,
+        )
+        far_sum = add_low(keep_far, after(got_far, upstream))
         state = {
             "layer": layer,
             "far_sum": far_sum,
             "keep_near": keep_near,
             "near_got": near_got,
+            "inward": line_steps(far_sum, [(0, 1), (3, 2)]) if line == 4 else far_sum,
         }
-        if line == 4:
-            state["inward"] = line_steps(far_sum, [(0, 1), (3, 2)])
-        by_side = down_part.reshape(line, 2, unit_rows, model_width)
-        down_send = lax.dynamic_index_in_dim(by_side, 1 - side, 1, keepdims=False)
-        state["down_keep"] = lax.dynamic_index_in_dim(by_side, side, 1, keepdims=False)
-        state["down_got"] = swap(
-            after(down_send, *(out_terms[2:] if before is None else kv_terms[1:])), "dp", 1
-        )
-        upstream, upstream_low, grad_kv, attn_gain_part, bias_first, bias_second = before_back(
-            kv_terms,
-            grad_query,
-            x,
-            after(gain_full, *waited),
-            grad_middle,
-            first_full,
-            second_full,
-            cos_wide,
-            sin_wide,
-        )
+        if before is not None:
+            step_two(before, far_sum)
         near_x, far_x, near_other, far_other = projection_grads(
             normed,
             grad_query,
@@ -1159,12 +1175,9 @@
         got_far_other = swap(far_other, "seq", 1)
         got_near_other = swap(near_other, "seq", 1)
         state["attn_parts"] = (near_x, far_x, got_near_other, got_far_other)
-        if before is not None:
-            step_three(before, upstream)
         states[layer] = before = state
     step_one(before)
     step_two(before)
-    step_three(before)
     arrived = [None, send_attn(before, 1)]
     arrived[0] = send_attn(before, 0)
     before["attn_sums"] = sum_attn(before, arrived)

time: 706 us -> 696 us (0.986)
  between operations: 29.2 us -> 15.6 us
    unnamed x196 -> x200, local copies, waits for them, and re-layouts: 22 us -> 39.5 us
    ppermute x4 -> x8, starting transfers between devices: 5.79 us -> 18.1 us  [line_steps(): lax.ppermute(values, 'dp', [(2 * here + side, 2 * there + side) for here,...]
    ppermute x90 -> x84, starting transfers between devices: 75.6 us -> 66.5 us  [swap(): return lax.ppermute(values, axis, [(i, i ^ bit) for i in range(size)])]
    pallas_call x4, Pallas kernels: 49.3 us -> 41.5 us  [feed_forward(): call(kernel, [((rows, 2 * units), jnp.bfloat16)] + [((part_rows, D), jnp....]
    ppermute x90 -> x84, waiting for transfers between devices: 306 us -> 312 us  [swap(): return lax.ppermute(values, axis, [(i, i ^ bit) for i in range(size)])]
    convert_element_type x18 -> x14, other arithmetic: 17.2 us -> 19.1 us  [add_low(): (left.astype(jnp.float32) + right.astype(jnp.float32)).astype(jnp.bfloat16)]
  transfers between devices with their start and end apart: 96 -> 92, of which waited for: 36 -> 39; matrix products, arithmetic and copies ran while one was open for 9% -> 7% of each run, Pallas kernels for 22% -> 22%
where the time goes in v3:
time: 696 us; the launch traced here: 689 us
  waiting for transfers between devices  317 us (46%)
  Pallas kernels  185 us (27%)
  starting transfers between devices  84.6 us (12%)
  local copies, waits for them, and re-layouts  55.5 us (8%)
  other arithmetic  31.4 us (5%)
  between operations  15.6 us (2%)
    ppermute x84, waiting for transfers between devices, swap(): return lax.ppermute(values, axis, [(i, i ^ bit) for i in range(size)])  312 us
    ppermute x84, starting transfers between devices, swap(): return lax.ppermute(values, axis, [(i, i ^ bit) for i in range(size)])  66.5 us
    pallas_call x2, Pallas kernels, feed_back(): call(kernel, [((half, packed, 2 * units), jnp.bfloat16), ((half, packed,...  65.4 us
    pallas_call x4, Pallas kernels, feed_forward(): call(kernel, [((rows, 2 * units), jnp.bfloat16)] + [((part_rows, D), jnp....  41.5 us
    unnamed x200, local copies, waits for them, and re-layouts  39.5 us
    pallas_call x2, Pallas kernels, attention_back(): call(kernel, [((rows, D), jnp.float32), ((rows, D), jnp.bfloat16), ((1, D...  26.3 us
    pallas_call x2, Pallas kernels, attention(): call(kernel, [((rows, D), jnp.bfloat16), ((rows, D), jnp.float32), ((rows...  21.4 us
    convert_element_type x14, other arithmetic, add_low(): (left.astype(jnp.float32) + right.astype(jnp.float32)).astype(jnp.bfloat16)  19.1 us
  transfers between devices with their start and end apart: 92, of which 39 were waited for; matrix products, arithmetic and copies ran while one was open for 7% of the time, Pallas kernels for 22%

profile of v3, /device:TPU:0, one launch (start us, length us, event | category | flops | bytes accessed | tf_op | source)
XLA Modules:
  0.0 688.9 jit_solution(13345033860777317403)
XLA Ops:
  7.5 2.9 collective-permute-start.4
  16.9 4.3 collective-permute-done.1
  21.3 2.8 collective-permute-start.2
  28.1 7.9 %collective-permute-done.2 = bf16[2,64,1024]{2,1,0:T(8,128)(2,1)S(1)} collective-permute-done((bf16[2,64,1024]{2,1,0:T(8,128)(2,1)S(1)}, bf16[2,64,1024]{2,1,0:T(8,128)(2,1)S(1)}, u32[]{:S(2)}, u32[]{:S(2)}) %collective-permute-start.2) | collective-permute-done | bytes 262176 | tf_op jit(solution)/shard_map/ppermute | solution.py:820
  59.7 6.2 collective-permute-done.7.refs_2_
  66.6 10.1 %collective-permute-done.8.refs_3_ = bf16[4,64,1024]{2,1,0:T(8,128)(2,1)S(1)} collective-permute-done((bf16[4,64,1024]{2,1,0:T(8,128)(2,1)S(1)}, bf16[4,64,1024]{2,1,0:T(8,128)(2,1)S(1)}, u32[]{:S(2)}, u32[]{:S(2)}) %collective-permute-start.8) | collective-permute-done | bytes 524320 | tf_op jit(solution)/shard_map/ppermute | solution.py:820
  83.3 13.3 %collective-permute-done.14 = bf16[1,168,2432]{2,1,0:T(8,128)(2,1)S(1)} collective-permute-done((bf16[1,168,2432]{2,1,0:T(8,128)(2,1)S(1)}, bf16[1,168,2432]{2,1,0:T(8,128)(2,1)S(1)}, u32[]{:S(2)}, u32[]{:S(2)}) %collective-permute-start.14) | collective-permute-done | bytes 817184 | tf_op jit(solution)/shard_map/ppermute | solution.py:820
  109.7 11.6 %attention.2 = (bf16[256,896]{1,0:T(8,128)(2,1)S(1)}, f32[256,896]{1,0:T(8,128)S(1)}, bf16[256,896]{1,0:T(8,128)(2,1)}) custom-call(bf16[2,2,896,64]{3,2,1,0:T(8,128)(2,1)S(1)} %get-tuple-element.251.q_ref.refs_7_, bf16[256,256]{1,0:T(8,128)(2,1)S(1)} %get-tuple-element.252.kv0.refs_8_, bf16[256,256]{1,0:T(8,128)(2,1)S(1)} %collective-permute-done.15.kv1.refs_9_, ...), custom_call_target="tpu_custom_call" | custom-call | bytes 42000 | tf_op jit(solution)/shard_map/attention/pallas_call | solution.py:159
  130.9 5.8 collective-permute-start.20
  136.7 29.1 %collective-permute-done.20 = bf16[1,64,1024]{2,1,0:T(8,128)(2,1)S(1)} collective-permute-done((bf16[1,64,1024]{2,1,0:T(8,128)(2,1)S(1)}, bf16[1,64,1024]{2,1,0:T(8,128)(2,1)S(1)}, u32[]{:S(2)}, u32[]{:S(2)}) %collective-permute-start.20) | collective-permute-done | bytes 131104 | tf_op jit(solution)/shard_map/ppermute | solution.py:820
  169.4 12.7 %collective-permute-done.21 = bf16[2,64,1024]{2,1,0:T(8,128)(2,1)S(1)} collective-permute-done((bf16[2,64,1024]{2,1,0:T(8,128)(2,1)S(1)}, bf16[2,64,1024]{2,1,0:T(8,128)(2,1)S(1)}, u32[]{:S(2)}, u32[]{:S(2)}) %collective-permute-start.21) | collective-permute-done | bytes 262176 | tf_op jit(solution)/shard_map/ppermute | solution.py:820
  186.5 31.7 %collective-permute-done.24.refs_1_ = bf16[4,64,1024]{2,1,0:T(8,128)(2,1)S(1)} collective-permute-done((bf16[4,64,1024]{2,1,0:T(8,128)(2,1)S(1)}, bf16[4,64,1024]{2,1,0:T(8,128)(2,1)S(1)}, u32[]{:S(2)}, u32[]{:S(2)}) %collective-permute-start.24) | collective-permute-done | bytes 524320 | tf_op jit(solution)/shard_map/ppermute | solution.py:820
  221.9 10.1 %collective-permute-done.26.refs_3_ = bf16[4,64,1024]{2,1,0:T(8,128)(2,1)} collective-permute-done((bf16[4,64,1024]{2,1,0:T(8,128)(2,1)S(1)}, bf16[4,64,1024]{2,1,0:T(8,128)(2,1)}, u32[]{:S(2)}, u32[]{:S(2)}) %collective-permute-start.26) | collective-permute-done | bytes 524320 | tf_op jit(solution)/shard_map/ppermute | solution.py:820
  238.4 3.2 assemble.3
  244.6 2.9 unpack.2
  250.9 10.2 %feed_forward.4 = (bf16[512,2432]{1,0:T(8,128)(2,1)}, bf16[256,896]{1,0:T(8,128)(2,1)}, bf16[256,896]{1,0:T(8,128)(2,1)}) custom-call(bf16[256,896]{1,0:T(8,128)(2,1)} %get-tuple-element.264.refs_0_.refs_5_, bf16[256,896]{1,0:T(8,128)(2,1)} %collective-permute-done.32.refs_1_.refs_6_, bf16[896,2432]{1,0:T(8,128)(2,1)} %bitcast.140, bf16[1216,896]{1,0:T(8,128)(2,1)} %bitcast.154), custom_call_target="tpu_custom_call" | custom-call | bytes 36000 | tf_op jit(solution)/shard_map/feed_forward/pallas_call | solution.py:204
  261.1 10.4 %feed_forward.5 = (bf16[512,2432]{1,0:T(8,128)(2,1)}, bf16[256,896]{1,0:T(8,128)(2,1)}, bf16[256,896]{1,0:T(8,128)(2,1)}) custom-call(bf16[256,896]{1,0:T(8,128)(2,1)} %collective-permute-done.22.refs_0_.refs_7_, bf16[256,896]{1,0:T(8,128)(2,1)} %copy-done.70, bf16[896,2432]{1,0:T(8,128)(2,1)} %bitcast.141, bf16[1216,896]{1,0:T(8,128)(2,1)} %bitcast.155), custom_call_target="tpu_custom_call" | custom-call | bytes 36000 | tf_op jit(solution)/shard_map/feed_forward/pallas_call | solution.py:204
  277.1 5.8 collective-permute-done.40.refs_2_
  283.0 3.8 collective-permute-done.39.refs_3_
  286.8 2.8 before_attention.3
  292.2 4.4 collective-permute-done.42.kv2.refs_10_
  298.7 9.8 %attention.3 = (bf16[256,896]{1,0:T(8,128)(2,1)S(1)}, f32[256,896]{1,0:T(8,128)S(1)}, bf16[256,896]{1,0:T(8,128)(2,1)S(1)}) custom-call(bf16[2,2,896,64]{3,2,1,0:T(8,128)(2,1)S(1)} %get-tuple-element.277.q_ref.refs_7_, bf16[256,256]{1,0:T(8,128)(2,1)S(1)} %get-tuple-element.278.kv0.refs_8_, bf16[256,256]{1,0:T(8,128)(2,1)S(1)} %collective-permute-done.41.kv1.refs_9_, ...), custom_call_target="tpu_custom_call" | custom-call | bytes 42000 | tf_op jit(solution)/shard_map/attention/pallas_call | solution.py:159
  311.8 11.4 %collective-permute-done.47.refs_0_.refs_7_ = bf16[256,896]{1,0:T(8,128)(2,1)S(1)} collective-permute-done((bf16[256,896]{1,0:T(8,128)(2,1)S(1)}, bf16[256,896]{1,0:T(8,128)(2,1)S(1)}, u32[]{:S(2)}, u32[]{:S(2)}) %collective-permute-start.47) | collective-permute-done | bytes 458784 | tf_op jit(solution)/shard_map/ppermute | solution.py:820
  333.1 10.7 %feed_forward.6 = (bf16[512,2432]{1,0:T(8,128)(2,1)}, bf16[256,896]{1,0:T(8,128)(2,1)}, bf16[256,896]{1,0:T(8,128)(2,1)}) custom-call(bf16[256,896]{1,0:T(8,128)(2,1)} %copy-done.33, bf16[256,896]{1,0:T(8,128)(2,1)} %copy-done.73, bf16[896,2432]{1,0:T(8,128)(2,1)} %bitcast.143, bf16[1216,896]{1,0:T(8,128)(2,1)} %bitcast.157), custom_call_target="tpu_custom_call" | custom-call | bytes 36000 | tf_op jit(solution)/shard_map/feed_forward/pallas_call | solution.py:204
  344.3 10.2 %feed_forward.7 = (bf16[512,2432]{1,0:T(8,128)(2,1)}, bf16[256,896]{1,0:T(8,128)(2,1)}, bf16[256,896]{1,0:T(8,128)(2,1)}) custom-call(bf16[256,896]{1,0:T(8,128)(2,1)} %copy-done.71, bf16[256,896]{1,0:T(8,128)(2,1)} %copy-done.72, bf16[896,2432]{1,0:T(8,128)(2,1)} %bitcast.144, bf16[1216,896]{1,0:T(8,128)(2,1)} %bitcast.158), custom_call_target="tpu_custom_call" | custom-call | bytes 36000 | tf_op jit(solution)/shard_map/feed_forward/pallas_call | solution.py:204
  355.3 32.8 %feed_back.2 = (bf16[2,168,2432]{2,1,0:T(8,128)(2,1)}, bf16[2,168,2432]{2,1,0:T(8,128)(2,1)}, bf16[2,168,2432]{2,1,0:T(8,128)(2,1)}, bf16[2,168,2432]{2,1,0:T(8,...) custom-call(s32[1]{0:T(128)} %bitcast.3.refs_0_, ...), custom_call_target="tpu_custom_call" | custom-call | bytes 100000 | tf_op jit(solution)/shard_map/feed_back/pallas_call | solution.py:321
  392.6 12.0 %collective-permute-done.54.refs_5_ = bf16[256,896]{1,0:T(8,128)(2,1)S(1)} collective-permute-done((bf16[256,896]{1,0:T(8,128)(2,1)S(1)}, bf16[256,896]{1,0:T(8,128)(2,1)S(1)}, u32[]{:S(2)}, u32[]{:S(2)}) %collective-permute-start.54) | collective-permute-done | bytes 458784 | tf_op jit(solution)/shard_map/ppermute | solution.py:820
  407.0 13.2 %attention_back.2 = (f32[256,896]{1,0:T(8,128)S(1)}, bf16[256,896]{1,0:T(8,128)(2,1)S(1)}, f32[1,896]{1,0:T(1,128)S(1)}, bf16[256,896]{1,0:T(8,128)(2,1)S(1)}, f...) custom-call(bf16[256,896]{1,0:T(8,128)(2,1)} %bitcast.47.refs_1_.ref, ...), custom_call_target="tpu_custom_call" | custom-call | bytes 52000 | tf_op jit(solution)/shard_map/attention_back/pallas_call | solution.py:463
  422.5 4.1 collective-permute-done.56.refs_2_
  435.1 8.4 %collective-permute-done.58.refs_3_ = bf16[256,896]{1,0:T(8,128)(2,1)S(1)} collective-permute-done((bf16[256,896]{1,0:T(8,128)(2,1)S(1)}, bf16[256,896]{1,0:T(8,128)(2,1)S(1)}, u32[]{:S(2)}, u32[]{:S(2)}) %collective-permute-start.58) | collective-permute-done | bytes 458784 | tf_op jit(solution)/shard_map/ppermute | solution.py:820
  445.2 5.6 collective-permute-start.68
  457.7 32.6 %feed_back.3 = (bf16[2,168,2432]{2,1,0:T(8,128)(2,1)}, bf16[2,168,2432]{2,1,0:T(8,128)(2,1)}, bf16[2,168,2432]{2,1,0:T(8,128)(2,1)}, bf16[2,168,2432]{2,1,0:T(8,...) custom-call(s32[1]{0:T(128)} %bitcast.3.refs_0_, ...), custom_call_target="tpu_custom_call" | custom-call | bytes 100000 | tf_op jit(solution)/shard_map/feed_back/pallas_call | solution.py:321
  500.2 6.8 collective-permute-done.70.refs_5_
  507.0 13.1 %attention_back.3 = (f32[256,896]{1,0:T(8,128)S(1)}, bf16[256,896]{1,0:T(8,128)(2,1)S(1)}, f32[1,896]{1,0:T(1,128)S(1)}, bf16[256,896]{1,0:T(8,128)(2,1)S(1)}, f...) custom-call(f32[256,896]{1,0:T(8,128)S(1)} %copy-done.39, ...), custom_call_target="tpu_custom_call" | custom-call | bytes 52000 | tf_op jit(solution)/shard_map/attention_back/pallas_call | solution.py:463
  522.0 6.8 collective-permute-done.78
  530.4 2.7 before_back.3
  536.8 2.7 collective-permute-start.84
  545.6 10.9 %collective-permute-done.76 = bf16[4,64,1024]{2,1,0:T(8,128)(2,1)} collective-permute-done((bf16[4,64,1024]{2,1,0:T(8,128)(2,1)}, bf16[4,64,1024]{2,1,0:T(8,128)(2,1)}, u32[]{:S(2)}, u32[]{:S(2)}) %collective-permute-start.76) | collective-permute-done | bytes 524320 | tf_op jit(solution)/shard_map/ppermute | solution.py:820
  556.5 10.3 %collective-permute-done.77 = bf16[4,64,1024]{2,1,0:T(8,128)(2,1)} collective-permute-done((bf16[4,64,1024]{2,1,0:T(8,128)(2,1)}, bf16[4,64,1024]{2,1,0:T(8,128)(2,1)}, u32[]{:S(2)}, u32[]{:S(2)}) %collective-permute-start.77) | collective-permute-done | bytes 524320 | tf_op jit(solution)/shard_map/ppermute | solution.py:820
  569.6 4.8 collective-permute-done.84
  577.5 2.6 add_convert_fusion
  580.1 13.2 %collective-permute-done.80 = bf16[4,128,1024]{2,1,0:T(8,128)(2,1)S(1)} collective-permute-done((bf16[4,128,1024]{2,1,0:T(8,128)(2,1)S(1)}, bf16[4,128,1024]{2,1,0:T(8,128)(2,1)S(1)}, u32[]{:S(2)}, u32[]{:S(2)}) %collective-permute-start.80) | collective-permute-done | bytes 1048608 | tf_op jit(solution)/shard_map/ppermute | solution.py:820
  595.4 45.1 %collective-permute-done.81 = bf16[2,128,1024]{2,1,0:T(8,128)(2,1)S(1)} collective-permute-done((bf16[2,128,1024]{2,1,0:T(8,128)(2,1)S(1)}, bf16[2,128,1024]{2,1,0:T(8,128)(2,1)S(1)}, u32[]{:S(2)}, u32[]{:S(2)}) %collective-permute-start.81) | collective-permute-done | bytes 524320 | tf_op jit(solution)/shard_map/ppermute | solution.py:820
  647.2 2.9 collective-permute-done.82
  652.7 12.9 %collective-permute-done.86.refs_1_ = bf16[168,2432]{1,0:T(8,128)(2,1)S(1)} collective-permute-done((bf16[168,2432]{1,0:T(8,128)(2,1)S(1)}, bf16[168,2432]{1,0:T(8,128)(2,1)S(1)}, u32[]{:S(2)}, u32[]{:S(2)}) %collective-permute-start.86) | collective-permute-done | bytes 817184 | tf_op jit(solution)/shard_map/ppermute | solution.py:820
  671.3 6.4 collective-permute-done.90.refs_2_
  677.7 5.9 collective-permute-done.91.refs_3_
  685.6 3.0 copy.67
  (471 shorter events, 180.3 us)
Async XLA Ops:
  7.4 16.7 %collective-permute-start.3 = (bf16[2,28,2432]{2,1,0:T(8,128)(2,1)S(1)}, bf16[2,28,2432]{2,1,0:T(8,128)(2,1)S(1)}, u32[]{:S(2)}, u32[]{:S(2)}) collective-permute-start(bf16[2,28,2432]{2,1,0:T(8,128)(2,1)S(1)} %get-tuple-element.238), channel_id=1, source_target_pairs={{0,1},{1,0},{2,3},{3,2},{4,5},{5,4},{6,7},{7,6},{8,9},{9,8},{10,11... | collective-permute-start | bytes 817160 | tf_op jit(solution)/shard_map/ppermute | solution.py:820
  7.5 16.6 %collective-permute-start.4 = (bf16[2,28,2432]{2,1,0:T(8,128)(2,1)S(1)}, bf16[2,28,2432]{2,1,0:T(8,128)(2,1)S(1)}, u32[]{:S(2)}, u32[]{:S(2)}) collective-permute-start(bf16[2,28,2432]{2,1,0:T(8,128)(2,1)S(1)} %get-tuple-element.239), channel_id=1, source_target_pairs={{0,2},{1,3},{2,0},{3,1},{4,6},{5,7},{6,4},{7,5},{8,10},{9,11},{10,... | collective-permute-start | bytes 817160 | tf_op jit(solution)/shard_map/ppermute | solution.py:820
  36.0 19.3 %collective-permute-start.13 = (bf16[1,168,2432]{2,1,0:T(8,128)(2,1)S(1)}, bf16[1,168,2432]{2,1,0:T(8,128)(2,1)}, u32[]{:S(2)}, u32[]{:S(2)}) collective-permute-start(bf16[1,168,2432]{2,1,0:T(8,128)(2,1)S(1)} %get-tuple-element.246), channel_id=1, source_target_pairs={{0,8},{4,12},{8,0},{12,4},{16,24},{20,28},{24,16},{28,20},{1,9},{5... | collective-permute-start | bytes 2451464 | tf_op jit(solution)/shard_map/ppermute | solution.py:820
  37.5 16.2 %collective-permute-start.6 = (bf16[4,64,1024]{2,1,0:T(8,128)(2,1)S(1)}, bf16[4,64,1024]{2,1,0:T(8,128)(2,1)S(1)}, u32[]{:S(2)}, u32[]{:S(2)}) collective-permute-start(bf16[4,64,1024]{2,1,0:T(8,128)(2,1)S(1)} %constant_dynamic-update-slice_fusion.refs_0_), channel_id=1, source_target_pairs={{0,4},{4,0},{8,12},{12,8},{16,20},{20,16},{24,28},{28,24},{1,5},{5... | collective-permute-start | bytes 1572872 | tf_op jit(solution)/shard_map/ppermute | solution.py:820
  51.1 15.5 %collective-permute-start.9 = (bf16[4,64,1024]{2,1,0:T(8,128)(2,1)S(1)}, bf16[4,64,1024]{2,1,0:T(8,128)(2,1)S(1)}, u32[]{:S(2)}, u32[]{:S(2)}) collective-permute-start(bf16[4,64,1024]{2,1,0:T(8,128)(2,1)S(1)} %constant_dynamic-update-slice_fusion.refs_0_), channel_id=1, source_target_pairs={{0,1},{1,0},{2,3},{3,2},{4,5},{5,4},{6,7},{7,6},{8,9},{9,8},{10,11... | collective-permute-start | bytes 1572872 | tf_op jit(solution)/shard_map/ppermute | solution.py:820
  51.2 14.8 %collective-permute-start.7 = (bf16[4,64,1024]{2,1,0:T(8,128)(2,1)S(1)}, bf16[4,64,1024]{2,1,0:T(8,128)(2,1)S(1)}, u32[]{:S(2)}, u32[]{:S(2)}) collective-permute-start(bf16[4,64,1024]{2,1,0:T(8,128)(2,1)S(1)} %constant_dynamic-update-slice_fusion.refs_0_), channel_id=1, source_target_pairs={{0,2},{1,3},{2,0},{3,1},{4,6},{5,7},{6,4},{7,5},{8,10},{9,11},{10,... | collective-permute-start | bytes 1572872 | tf_op jit(solution)/shard_map/ppermute | solution.py:820
  53.7 23.0 %collective-permute-start.8 = (bf16[4,64,1024]{2,1,0:T(8,128)(2,1)S(1)}, bf16[4,64,1024]{2,1,0:T(8,128)(2,1)S(1)}, u32[]{:S(2)}, u32[]{:S(2)}) collective-permute-start(bf16[4,64,1024]{2,1,0:T(8,128)(2,1)S(1)} %collective-permute-done.6.refs_1_), channel_id=1, source_target_pairs={{0,2},{1,3},{2,0},{3,1},{4,6},{5,7},{6,4},{7,5},{8,10},{9,11},{10,... | collective-permute-start | bytes 1572872 | tf_op jit(solution)/shard_map/ppermute | solution.py:820
  54.2 23.9 %collective-permute-start.10 = (bf16[4,64,1024]{2,1,0:T(8,128)(2,1)S(1)}, bf16[4,64,1024]{2,1,0:T(8,128)(2,1)S(1)}, u32[]{:S(2)}, u32[]{:S(2)}) collective-permute-start(bf16[4,64,1024]{2,1,0:T(8,128)(2,1)S(1)} %collective-permute-done.6.refs_1_), channel_id=1, source_target_pairs={{0,1},{1,0},{2,3},{3,2},{4,5},{5,4},{6,7},{7,6},{8,9},{9,8},{10,11... | collective-permute-start | bytes 1572872 | tf_op jit(solution)/shard_map/ppermute | solution.py:820
  57.4 65.6 %collective-permute-start.33 = (bf16[2,168,2432]{2,1,0:T(8,128)(2,1)}, bf16[2,168,2432]{2,1,0:T(8,128)(2,1)}, u32[]{:S(2)}, u32[]{:S(2)}) collective-permute-start(bf16[2,168,2432]{2,1,0:T(8,128)(2,1)} %constant_dynamic-update-slice_fusion.3.refs_0_), channel_id=1, source_target_pairs={{8,16},{12,20},{16,8},{20,12},{9,17},{13,21},{17,9},{21,13},{10,18... | collective-permute-start | bytes 4902920 | tf_op jit(solution)/shard_map/ppermute | solution.py:841
  66.0 38.3 %collective-permute-start.18 = (bf16[2,168,2432]{2,1,0:T(8,128)(2,1)}, bf16[2,168,2432]{2,1,0:T(8,128)(2,1)}, u32[]{:S(2)}, u32[]{:S(2)}) collective-permute-start(bf16[2,168,2432]{2,1,0:T(8,128)(2,1)} %constant_dynamic-update-slice_fusion.3.refs_0_), channel_id=1, source_target_pairs={{0,4},{4,0},{8,12},{12,8},{16,20},{20,16},{24,28},{28,24},{1,5},{5... | collective-permute-start | bytes 4902920 | tf_op jit(solution)/shard_map/ppermute | solution.py:820
  76.7 19.9 %collective-permute-start.14 = (bf16[1,168,2432]{2,1,0:T(8,128)(2,1)S(1)}, bf16[1,168,2432]{2,1,0:T(8,128)(2,1)S(1)}, u32[]{:S(2)}, u32[]{:S(2)}) collective-permute-start(bf16[1,168,2432]{2,1,0:T(8,128)(2,1)S(1)} %get-tuple-element.247), channel_id=1, source_target_pairs={{0,8},{4,12},{8,0},{12,4},{16,24},{20,28},{24,16},{28,20},{1,9},{5... | collective-permute-start | bytes 2451464 | tf_op jit(solution)/shard_map/ppermute | solution.py:820
  123.0 44.2 %collective-permute-start.34 = (bf16[2,168,2432]{2,1,0:T(8,128)(2,1)}, bf16[2,168,2432]{2,1,0:T(8,128)(2,1)}, u32[]{:S(2)}, u32[]{:S(2)}) collective-permute-start(bf16[2,168,2432]{2,1,0:T(8,128)(2,1)} %collective-permute-done.33), channel_id=1, source_target_pairs={{8,0},{12,4},{16,24},{20,28},{9,1},{13,5},{17,25},{21,29},{10,2},{... | collective-permute-start | bytes 4902920 | tf_op jit(solution)/shard_map/ppermute | solution.py:841
  127.0 55.7 %collective-permute-start.31 = (bf16[2,168,2432]{2,1,0:T(8,128)(2,1)}, bf16[2,168,2432]{2,1,0:T(8,128)(2,1)}, u32[]{:S(2)}, u32[]{:S(2)}) collective-permute-start(bf16[2,168,2432]{2,1,0:T(8,128)(2,1)} %constant_dynamic-update-slice_fusion.5.refs_0_), channel_id=1, source_target_pairs={{8,16},{12,20},{16,8},{20,12},{9,17},{13,21},{17,9},{21,13},{10,18... | collective-permute-start | bytes 4902920 | tf_op jit(solution)/shard_map/ppermute | solution.py:841
  129.1 38.0 %collective-permute-start.22 = (bf16[256,896]{1,0:T(8,128)(2,1)}, bf16[256,896]{1,0:T(8,128)(2,1)}, u32[]{:S(2)}, u32[]{:S(2)}) collective-permute-start(bf16[256,896]{1,0:T(8,128)(2,1)} %get-tuple-element.264.refs_0_.refs_5_), channel_id=1, source_target_pairs={{0,2},{1,3},{2,0},{3,1},{4,6},{5,7},{6,4},{7,5},{8,10},{9,11},{10,... | collective-permute-start | bytes 1376264 | tf_op jit(solution)/shard_map/ppermute | solution.py:820
  130.9 34.9 %collective-permute-start.20 = (bf16[1,64,1024]{2,1,0:T(8,128)(2,1)S(1)}, bf16[1,64,1024]{2,1,0:T(8,128)(2,1)S(1)}, u32[]{:S(2)}, u32[]{:S(2)}) collective-permute-start(bf16[1,64,1024]{2,1,0:T(8,128)(2,1)S(1)} %maximum_bitcast_fusion.1), channel_id=1, source_target_pairs={{0,8},{4,12},{8,0},{12,4},{16,24},{20,28},{24,16},{28,20},{1,9},{5... | collective-permute-start | bytes 393224 | tf_op jit(solution)/shard_map/ppermute | solution.py:820
  165.8 16.3 %collective-permute-start.21 = (bf16[2,64,1024]{2,1,0:T(8,128)(2,1)S(1)}, bf16[2,64,1024]{2,1,0:T(8,128)(2,1)S(1)}, u32[]{:S(2)}, u32[]{:S(2)}) collective-permute-start(bf16[2,64,1024]{2,1,0:T(8,128)(2,1)S(1)} %pad_maximum_fusion.6), channel_id=1, source_target_pairs={{0,16},{4,20},{8,24},{12,28},{16,0},{20,4},{24,8},{28,12},{1,17},{... | collective-permute-start | bytes 786440 | tf_op jit(solution)/shard_map/ppermute | solution.py:820
  167.1 15.0 %collective-permute-start.23 = (bf16[256,896]{1,0:T(8,128)(2,1)}, bf16[256,896]{1,0:T(8,128)(2,1)S(1)}, u32[]{:S(2)}, u32[]{:S(2)}) collective-permute-start(bf16[256,896]{1,0:T(8,128)(2,1)} %collective-permute-done.22.refs_0_.refs_7_), channel_id=1, source_target_pairs={{0,1},{1,0},{2,3},{3,2},{4,5},{5,4},{6,7},{7,6},{8,9},{9,8},{10,11... | collective-permute-start | bytes 1376264 | tf_op jit(solution)/shard_map/ppermute | solution.py:820
  168.8 75.3 %collective-permute-start.35 = (bf16[2,168,2432]{2,1,0:T(8,128)(2,1)S(1)}, bf16[2,168,2432]{2,1,0:T(8,128)(2,1)}, u32[]{:S(2)}, u32[]{:S(2)}) collective-permute-start(bf16[2,168,2432]{2,1,0:T(8,128)(2,1)S(1)} %broadcast_select_fusion.1.refs_1_), channel_id=1, source_target_pairs={{0,4},{4,0},{8,12},{12,8},{16,20},{20,16},{24,28},{28,24},{1,5},{5... | collective-permute-start | bytes 4902920 | tf_op jit(solution)/shard_map/ppermute | solution.py:820
  182.1 36.1 %collective-permute-start.24 = (bf16[4,64,1024]{2,1,0:T(8,128)(2,1)S(1)}, bf16[4,64,1024]{2,1,0:T(8,128)(2,1)S(1)}, u32[]{:S(2)}, u32[]{:S(2)}) collective-permute-start(bf16[4,64,1024]{2,1,0:T(8,128)(2,1)S(1)} %constant_dynamic-update-slice_fusion.7.refs_0_), channel_id=1, source_target_pairs={{0,4},{4,0},{8,12},{12,8},{16,20},{20,16},{24,28},{28,24},{1,5},{5... | collective-permute-start | bytes 1572872 | tf_op jit(solution)/shard_map/ppermute | solution.py:820
  182.7 89.4 %collective-permute-start.37 = (bf16[2,168,2432]{2,1,0:T(8,128)(2,1)}, bf16[2,168,2432]{2,1,0:T(8,128)(2,1)}, u32[]{:S(2)}, u32[]{:S(2)}) collective-permute-start(bf16[2,168,2432]{2,1,0:T(8,128)(2,1)} %collective-permute-done.31), channel_id=1, source_target_pairs={{8,0},{12,4},{16,24},{20,28},{9,1},{13,5},{17,25},{21,29},{10,2},{... | collective-permute-start | bytes 4902920 | tf_op jit(solution)/shard_map/ppermute | solution.py:841
  184.0 35.7 %collective-permute-start.27 = (bf16[4,64,1024]{2,1,0:T(8,128)(2,1)S(1)}, bf16[4,64,1024]{2,1,0:T(8,128)(2,1)S(1)}, u32[]{:S(2)}, u32[]{:S(2)}) collective-permute-start(bf16[4,64,1024]{2,1,0:T(8,128)(2,1)S(1)} %constant_dynamic-update-slice_fusion.7.refs_0_), channel_id=1, source_target_pairs={{0,1},{1,0},{2,3},{3,2},{4,5},{5,4},{6,7},{7,6},{8,9},{9,8},{10,11... | collective-permute-start | bytes 1572872 | tf_op jit(solution)/shard_map/ppermute | solution.py:820
  184.1 37.3 %collective-permute-start.25 = (bf16[4,64,1024]{2,1,0:T(8,128)(2,1)S(1)}, bf16[4,64,1024]{2,1,0:T(8,128)(2,1)}, u32[]{:S(2)}, u32[]{:S(2)}) collective-permute-start(bf16[4,64,1024]{2,1,0:T(8,128)(2,1)S(1)} %constant_dynamic-update-slice_fusion.7.refs_0_), channel_id=1, source_target_pairs={{0,2},{1,3},{2,0},{3,1},{4,6},{5,7},{6,4},{7,5},{8,10},{9,11},{10,... | collective-permute-start | bytes 1572872 | tf_op jit(solution)/shard_map/ppermute | solution.py:820
  232.7 18.1 %collective-permute-start.32 = (bf16[256,896]{1,0:T(8,128)(2,1)}, bf16[256,896]{1,0:T(8,128)(2,1)}, u32[]{:S(2)}, u32[]{:S(2)}) collective-permute-start(bf16[256,896]{1,0:T(8,128)(2,1)} %get-tuple-element.264.refs_0_.refs_5_), channel_id=1, source_target_pairs={{0,1},{1,0},{2,3},{3,2},{4,5},{5,4},{6,7},{7,6},{8,9},{9,8},{10,11... | collective-permute-start | bytes 1376264 | tf_op jit(solution)/shard_map/ppermute | solution.py:820
  244.1 38.9 %collective-permute-start.40 = (bf16[2,168,2432]{2,1,0:T(8,128)(2,1)}, bf16[2,168,2432]{2,1,0:T(8,128)(2,1)}, u32[]{:S(2)}, u32[]{:S(2)}) collective-permute-start(bf16[2,168,2432]{2,1,0:T(8,128)(2,1)} %constant_dynamic-update-slice_fusion.5.refs_0_), channel_id=1, source_target_pairs={{0,4},{4,0},{8,12},{12,8},{16,20},{20,16},{24,28},{28,24},{1,5},{5... | collective-permute-start | bytes 4902920 | tf_op jit(solution)/shard_map/ppermute | solution.py:820
  261.1 21.9 %collective-permute-start.36 = (bf16[256,896]{1,0:T(8,128)(2,1)}, bf16[256,896]{1,0:T(8,128)(2,1)}, u32[]{:S(2)}, u32[]{:S(2)}) collective-permute-start(bf16[256,896]{1,0:T(8,128)(2,1)} %get-tuple-element.269), channel_id=1, source_target_pairs={{0,1},{1,0},{2,3},{3,2},{4,5},{5,4},{6,7},{7,6},{8,9},{9,8},{10,11... | collective-permute-start | bytes 1376264 | tf_op jit(solution)/shard_map/ppermute | solution.py:820
  275.6 50.9 %collective-permute-start.45 = (bf16[2,168,2432]{2,1,0:T(8,128)(2,1)S(1)}, bf16[2,168,2432]{2,1,0:T(8,128)(2,1)S(1)}, u32[]{:S(2)}, u32[]{:S(2)}) collective-permute-start(bf16[2,168,2432]{2,1,0:T(8,128)(2,1)S(1)} %broadcast_select_fusion.refs_1_), channel_id=1, source_target_pairs={{0,4},{4,0},{8,12},{12,8},{16,20},{20,16},{24,28},{28,24},{1,5},{5... | collective-permute-start | bytes 4902920 | tf_op jit(solution)/shard_map/ppermute | solution.py:820
  325.0 18.8 %collective-permute-start.51 = (bf16[256,896]{1,0:T(8,128)(2,1)}, bf16[256,896]{1,0:T(8,128)(2,1)}, u32[]{:S(2)}, u32[]{:S(2)}) collective-permute-start(bf16[256,896]{1,0:T(8,128)(2,1)} %bitcast.47.refs_1_.refs_0_), channel_id=1, source_target_pairs={{0,2},{1,3},{2,0},{3,1},{4,6},{5,7},{6,4},{7,5},{8,10},{9,11},{10,... | collective-permute-start | bytes 1376264 | tf_op jit(solution)/shard_map/ppermute | solution.py:820
  388.2 45.3 %collective-permute-start.66 = (bf16[2,168,2432]{2,1,0:T(8,128)(2,1)}, bf16[2,168,2432]{2,1,0:T(8,128)(2,1)S(1)}, u32[]{:S(2)}, u32[]{:S(2)}) collective-permute-start(bf16[2,168,2432]{2,1,0:T(8,128)(2,1)} %get-tuple-element.324), channel_id=1, source_target_pairs={{0,4},{4,0},{8,12},{12,8},{16,20},{20,16},{24,28},{28,24},{1,5},{5... | collective-permute-start | bytes 4902920 | tf_op jit(solution)/shard_map/ppermute | solution.py:820
  433.5 17.9 %collective-permute-start.62 = (bf16[2,4,64,1024]{3,2,1,0:T(8,128)(2,1)S(1)}, bf16[2,4,64,1024]{3,2,1,0:T(8,128)(2,1)S(1)}, u32[]{:S(2)}, u32[]{:S(2)}) collective-permute-start(bf16[2,4,64,1024]{3,2,1,0:T(8,128)(2,1)S(1)} %get-tuple-element.314), channel_id=1, source_target_pairs={{0,1},{1,0},{2,3},{3,2},{4,5},{5,4},{6,7},{7,6},{8,9},{9,8},{10,11... | collective-permute-start | bytes 3145736 | tf_op jit(solution)/shard_map/ppermute | solution.py:820
  433.6 56.8 %collective-permute-start.67 = (bf16[2,168,2432]{2,1,0:T(8,128)(2,1)}, bf16[2,168,2432]{2,1,0:T(8,128)(2,1)}, u32[]{:S(2)}, u32[]{:S(2)}) collective-permute-start(bf16[2,168,2432]{2,1,0:T(8,128)(2,1)} %get-tuple-element.325), channel_id=1, source_target_pairs={{0,4},{4,0},{8,12},{12,8},{16,20},{20,16},{24,28},{28,24},{1,5},{5... | collective-permute-start | bytes 4902920 | tf_op jit(solution)/shard_map/ppermute | solution.py:820
  445.2 45.2 %collective-permute-start.68 = (bf16[2,168,2432]{2,1,0:T(8,128)(2,1)}, bf16[2,168,2432]{2,1,0:T(8,128)(2,1)}, u32[]{:S(2)}, u32[]{:S(2)}) collective-permute-start(bf16[2,168,2432]{2,1,0:T(8,128)(2,1)} %add_convert_fusion.7), channel_id=1, source_target_pairs={{0,8},{4,12},{24,16},{28,20},{1,9},{5,13},{25,17},{29,21},{2,10},{... | collective-permute-start | bytes 4902920 | tf_op jit(solution)/shard_map/ppermute | solution.py:841
  454.1 36.3 %collective-permute-start.64 = (bf16[4,64,1024]{2,1,0:T(8,128)(2,1)}, bf16[4,64,1024]{2,1,0:T(8,128)(2,1)}, u32[]{:S(2)}, u32[]{:S(2)}) collective-permute-start(bf16[4,64,1024]{2,1,0:T(8,128)(2,1)} %get-tuple-element.321), channel_id=1, source_target_pairs={{0,2},{1,3},{2,0},{3,1},{4,6},{5,7},{6,4},{7,5},{8,10},{9,11},{10,... | collective-permute-start | bytes 1572872 | tf_op jit(solution)/shard_map/ppermute | solution.py:820
  454.8 35.6 %collective-permute-start.65 = (bf16[4,64,1024]{2,1,0:T(8,128)(2,1)}, bf16[4,64,1024]{2,1,0:T(8,128)(2,1)}, u32[]{:S(2)}, u32[]{:S(2)}) collective-permute-start(bf16[4,64,1024]{2,1,0:T(8,128)(2,1)} %get-tuple-element.322), channel_id=1, source_target_pairs={{0,2},{1,3},{2,0},{3,1},{4,6},{5,7},{6,4},{7,5},{8,10},{9,11},{10,... | collective-permute-start | bytes 1572872 | tf_op jit(solution)/shard_map/ppermute | solution.py:820
  457.0 33.4 %collective-permute-start.60 = (bf16[256,896]{1,0:T(8,128)(2,1)}, bf16[256,896]{1,0:T(8,128)(2,1)}, u32[]{:S(2)}, u32[]{:S(2)}) collective-permute-start(bf16[256,896]{1,0:T(8,128)(2,1)} %add_convert_fusion.15), channel_id=1, source_target_pairs={{0,2},{1,3},{2,0},{3,1},{4,6},{5,7},{6,4},{7,5},{8,10},{9,11},{10,... | collective-permute-start | bytes 1376264 | tf_op jit(solution)/shard_map/ppermute | solution.py:820
  490.5 38.3 %collective-permute-start.78 = (bf16[2,168,2432]{2,1,0:T(8,128)(2,1)}, bf16[2,168,2432]{2,1,0:T(8,128)(2,1)S(1)}, u32[]{:S(2)}, u32[]{:S(2)}) collective-permute-start(bf16[2,168,2432]{2,1,0:T(8,128)(2,1)} %get-tuple-element.353), channel_id=1, source_target_pairs={{0,4},{4,0},{8,12},{12,8},{16,20},{20,16},{24,28},{28,24},{1,5},{5... | collective-permute-start | bytes 4902920 | tf_op jit(solution)/shard_map/ppermute | solution.py:820
  498.1 44.7 %collective-permute-start.87 = (bf16[2,168,2432]{2,1,0:T(8,128)(2,1)S(1)}, bf16[2,168,2432]{2,1,0:T(8,128)(2,1)}, u32[]{:S(2)}, u32[]{:S(2)}) collective-permute-start(bf16[2,168,2432]{2,1,0:T(8,128)(2,1)S(1)} %add_convert_fusion.1), channel_id=1, source_target_pairs={{8,16},{12,20},{16,8},{20,12},{9,17},{13,21},{17,9},{21,13},{10,18... | collective-permute-start | bytes 4902920 | tf_op jit(solution)/shard_map/ppermute | solution.py:841
  528.8 40.2 %collective-permute-start.79 = (bf16[2,168,2432]{2,1,0:T(8,128)(2,1)}, bf16[2,168,2432]{2,1,0:T(8,128)(2,1)}, u32[]{:S(2)}, u32[]{:S(2)}) collective-permute-start(bf16[2,168,2432]{2,1,0:T(8,128)(2,1)} %get-tuple-element.354), channel_id=1, source_target_pairs={{0,4},{4,0},{8,12},{12,8},{16,20},{20,16},{24,28},{28,24},{1,5},{5... | collective-permute-start | bytes 4902920 | tf_op jit(solution)/shard_map/ppermute | solution.py:820
  536.8 37.6 %collective-permute-start.84 = (bf16[2,168,2432]{2,1,0:T(8,128)(2,1)}, bf16[2,168,2432]{2,1,0:T(8,128)(2,1)}, u32[]{:S(2)}, u32[]{:S(2)}) collective-permute-start(bf16[2,168,2432]{2,1,0:T(8,128)(2,1)} %add_convert_fusion.5), channel_id=1, source_target_pairs={{0,8},{4,12},{24,16},{28,20},{1,9},{5,13},{25,17},{29,21},{2,10},{... | collective-permute-start | bytes 4902920 | tf_op jit(solution)/shard_map/ppermute | solution.py:841
  539.5 27.3 %collective-permute-start.74 = (bf16[2,4,64,1024]{3,2,1,0:T(8,128)(2,1)S(1)}, bf16[2,4,64,1024]{3,2,1,0:T(8,128)(2,1)}, u32[]{:S(2)}, u32[]{:S(2)}) collective-permute-start(bf16[2,4,64,1024]{3,2,1,0:T(8,128)(2,1)S(1)} %get-tuple-element.346), channel_id=1, source_target_pairs={{0,1},{1,0},{2,3},{3,2},{4,5},{5,4},{6,7},{7,6},{8,9},{9,8},{10,11... | collective-permute-start | bytes 3145736 | tf_op jit(solution)/shard_map/ppermute | solution.py:820
  541.4 15.1 %collective-permute-start.76 = (bf16[4,64,1024]{2,1,0:T(8,128)(2,1)}, bf16[4,64,1024]{2,1,0:T(8,128)(2,1)}, u32[]{:S(2)}, u32[]{:S(2)}) collective-permute-start(bf16[4,64,1024]{2,1,0:T(8,128)(2,1)} %get-tuple-element.400), channel_id=1, source_target_pairs={{0,2},{1,3},{2,0},{3,1},{4,6},{5,7},{6,4},{7,5},{8,10},{9,11},{10,... | collective-permute-start | bytes 1572872 | tf_op jit(solution)/shard_map/ppermute | solution.py:820
  542.8 24.1 %collective-permute-start.77 = (bf16[4,64,1024]{2,1,0:T(8,128)(2,1)}, bf16[4,64,1024]{2,1,0:T(8,128)(2,1)}, u32[]{:S(2)}, u32[]{:S(2)}) collective-permute-start(bf16[4,64,1024]{2,1,0:T(8,128)(2,1)} %get-tuple-element.401), channel_id=1, source_target_pairs={{0,2},{1,3},{2,0},{3,1},{4,6},{5,7},{6,4},{7,5},{8,10},{9,11},{10,... | collective-permute-start | bytes 1572872 | tf_op jit(solution)/shard_map/ppermute | solution.py:820
  556.5 88.7 %collective-permute-start.46 = (bf16[256,896]{1,0:T(8,128)(2,1)S(1)}, bf16[256,896]{1,0:T(8,128)(2,1)S(1)}, u32[]{:S(2)}, u32[]{:S(2)}) collective-permute-start(bf16[256,896]{1,0:T(8,128)(2,1)S(1)} %copy-done.93), channel_id=1, source_target_pairs={{0,1},{1,0},{2,3},{3,2},{4,5},{5,4},{6,7},{7,6},{8,9},{9,8},{10,11... | collective-permute-start | bytes 1376264 | tf_op jit(solution)/shard_map/ppermute | solution.py:820
  569.0 24.3 %collective-permute-start.80 = (bf16[4,128,1024]{2,1,0:T(8,128)(2,1)S(1)}, bf16[4,128,1024]{2,1,0:T(8,128)(2,1)S(1)}, u32[]{:S(2)}, u32[]{:S(2)}) collective-permute-start(bf16[4,128,1024]{2,1,0:T(8,128)(2,1)S(1)} %pad_maximum_fusion), channel_id=1, source_target_pairs={{0,4},{4,0},{8,12},{12,8},{16,20},{20,16},{24,28},{28,24},{1,5},{5... | collective-permute-start | bytes 3145736 | tf_op jit(solution)/shard_map/ppermute | solution.py:820
  576.7 64.1 %collective-permute-start.85 = (bf16[2,168,2432]{2,1,0:T(8,128)(2,1)S(1)}, bf16[2,168,2432]{2,1,0:T(8,128)(2,1)S(1)}, u32[]{:S(2)}, u32[]{:S(2)}) collective-permute-start(bf16[2,168,2432]{2,1,0:T(8,128)(2,1)S(1)} %add_convert_fusion.4), channel_id=1, source_target_pairs={{8,16},{12,20},{16,8},{20,12},{9,17},{13,21},{17,9},{21,13},{10,18... | collective-permute-start | bytes 4902920 | tf_op jit(solution)/shard_map/ppermute | solution.py:841
  593.8 46.7 %collective-permute-start.81 = (bf16[2,128,1024]{2,1,0:T(8,128)(2,1)S(1)}, bf16[2,128,1024]{2,1,0:T(8,128)(2,1)S(1)}, u32[]{:S(2)}, u32[]{:S(2)}) collective-permute-start(bf16[2,128,1024]{2,1,0:T(8,128)(2,1)S(1)} %slice.390), channel_id=1, source_target_pairs={{0,16},{4,20},{8,24},{12,28},{16,0},{20,4},{24,8},{28,12},{1,17},{... | collective-permute-start | bytes 1572872 | tf_op jit(solution)/shard_map/ppermute | solution.py:820
  594.0 58.7 %collective-permute-start.88 = (bf16[168,2432]{1,0:T(8,128)(2,1)S(1)}, bf16[168,2432]{1,0:T(8,128)(2,1)S(1)}, u32[]{:S(2)}, u32[]{:S(2)}) collective-permute-start(bf16[168,2432]{1,0:T(8,128)(2,1)S(1)} %get-tuple-element.406), channel_id=1, source_target_pairs={{0,8},{4,12},{8,0},{12,4},{16,24},{20,28},{24,16},{28,20},{1,9},{5... | collective-permute-start | bytes 2451464 | tf_op jit(solution)/shard_map/ppermute | solution.py:820
  643.1 22.5 %collective-permute-start.86 = (bf16[168,2432]{1,0:T(8,128)(2,1)S(1)}, bf16[168,2432]{1,0:T(8,128)(2,1)S(1)}, u32[]{:S(2)}, u32[]{:S(2)}) collective-permute-start(bf16[168,2432]{1,0:T(8,128)(2,1)S(1)} %get-tuple-element.408), channel_id=1, source_target_pairs={{0,8},{4,12},{8,0},{12,4},{16,24},{20,28},{24,16},{28,20},{1,9},{5... | collective-permute-start | bytes 2451464 | tf_op jit(solution)/shard_map/ppermute | solution.py:820
  650.7 18.7 %collective-permute-start.83 = (f32[2,28,1024]{2,1,0:T(8,128)S(1)}, f32[2,28,1024]{2,1,0:T(8,128)S(1)}, u32[]{:S(2)}, u32[]{:S(2)}) collective-permute-start(f32[2,28,1024]{2,1,0:T(8,128)S(1)} %bitcast.170), channel_id=1, source_target_pairs={{0,1},{1,0},{2,3},{3,2},{4,5},{5,4},{6,7},{7,6},{8,9},{9,8},{10,11... | collective-permute-start | bytes 688136 | tf_op jit(solution)/shard_map/ppermute | solution.py:820
  (139 other events, 1362.0 us)

commit v4 on v3

--- a/solution.py
+++ b/solution.py
@@ -831,9 +831,9 @@
     return bits
 
 
-def line_gather(values, bits):
+def line_gather(values, bits, *waited):
     for bit in bits:
-        values = jnp.concatenate([values, swap(values, "dp", 2 * bit)], axis=0)
+        values = jnp.concatenate([values, after(swap(values, "dp", 2 * bit), *waited)], axis=0)
     return values
 
 
@@ -850,9 +850,9 @@
     return swap(values, "dp", line)
 
 
-def line_scatter(values, bits):
+def line_scatter(values, bits, *waited):
     for bit in bits[:0:-1]:
-        values = add_low(values[:bit], swap(values[bit:], "dp", 2 * bit))
+        values = add_low(values[:bit], after(swap(values[bit:], "dp", 2 * bit), *waited))
     return [values[0], swap(values[1], "dp", 2)]
 
 
@@ -934,10 +934,12 @@
         extra = extra.at[3, :KV_WIDTH].set(bias_all[SPLIT:])
         return jnp.concatenate([rows, extra], axis=0)
 
-    def attn_finish(own_side, other_side, *waited):
+    def attn_finish(own_side, other_side, *waited, ahead=None):
         parts = [own_side, other_side]
         parts = parts + [swap(after(part, *waited), "seq", 2) for part in parts]
-        parts = parts + [swap(part, "seq", 1) for part in parts]
+        parts = parts + [swap(after(part, other_side), "seq", 1) for part in parts]
+        if ahead is not None:
+            parts[1] = after(parts[1], ahead)
         first_full, second_full, small = assemble(parts, [core, chip_x, dp_place], chip_rows)
         return (
             first_full,
@@ -955,14 +957,13 @@
     gate_shards = pack_rows(gate_blocks, down_weight, seq_place)
     attn_line = line_gather(after(shards[0], *spread), bits)
     attn_other = swap(after(attn_line, *gate_shards), "dp", 1)
-    def outward(crossed):
+    def outward(crossed, *waited):
         if line != 4:
             return crossed
-        passed = line_steps(crossed, [(1, 0), (2, 3)])
+        passed = after(line_steps(crossed, [(1, 0), (2, 3)]), *waited)
         return jnp.where((line_place == 1) | (line_place == 2), crossed, passed)
 
     near = [line_gather(after(gate_shards[0], attn_line), bits[:-1])]
-    near.append(line_gather(after(gate_shards[1], near[0]), bits[:-1]))
     near_pair = [swap(after(near[0], attn_other), "dp", 1)]
     crossed = [cross_middle(near[0])]
     far = []
@@ -983,12 +984,15 @@
     terms = [tokens.reshape(tok_len, model_width)]
     kept_state = []
     mlp_sets = []
-    attn_sets = [attn_finish(attn_line, attn_other)]
+    second_line = line_gather(after(shards[1], attn_other), bits[:1])
+    attn_sets = [attn_finish(attn_line, attn_other, ahead=second_line)]
+    for bit in bits[1:]:
+        second_line = line_gather(second_line, [bit])
     for layer in range(LAYERS):
         first_full, second_full, gain_full, mlp_gain_full, bias_first, bias_second = attn_sets[layer]
         x, normed, queries, own_kv = before_attention(
             terms,
-            after(gain_full, *near) if layer == 0 else after(gain_full, near_pair[1]),
+            after(gain_full, near[0], crossed[0], second_line) if layer == 0 else after(gain_full, near_pair[1]),
             first_full,
             second_full,
             bias_first,
@@ -1001,29 +1005,29 @@
         mixed, middle, n2 = attention(
             queries, kv_blocks, biases, x, second_full, after(mlp_gain_full, *waited)
         )
-        n2_parts = group_rows(n2)
+        if layer + 1 == LAYERS:
+            far.append(outward(after(crossed[1], kept_state[0][7][0]), own_kv))
+            far_pair = swap(far[1], "dp", 1)
+            n2_parts = group_rows(n2, far_pair)
+        else:
+            n2_parts = group_rows(n2)
         if layer == 0:
-            second_line = line_gather(after(shards[1], own_kv), bits[:1])
-            for bit in bits[1:]:
-                second_line = line_gather(after(second_line, n2), [bit])
-            second_other = swap(after(second_line, n2_parts[3]), "dp", 1)
-            far.append(outward(after(crossed[0], n2)))
+            second_other = swap(after(second_line, n2), "dp", 1)
+            far.append(outward(crossed[0], n2))
             far_pair = swap(far[0], "dp", 1)
-            crossed.append(cross_middle(after(near[1], n2)))
+            near.append(line_gather(after(gate_shards[1], n2), bits[:-1], n2_parts[3]))
+            crossed.append(cross_middle(near[1]))
             attn_sets.append(attn_finish(second_line, second_other, n2_parts[3]))
             near_pair.append(swap(after(near[1], far_pair), "dp", 1))
-            n2_parts[0] = after(n2_parts[0], attn_sets[1][2], crossed[1])
         mlp_sets.append(mlp_finish(layer, far_pair))
         gu_near, *outs_near = feed_forward(n2_parts[:2], *mlp_sets[layer])
-        if layer + 1 == LAYERS:
+        if layer == 0:
+            n2_parts[2] = after(n2_parts[2], crossed[1], gu_near)
+        else:
             low_parts = group_rows(
                 after(cotangent.reshape(tok_len, model_width), n2_parts[3]), gu_near
             )
         gu_far, *outs_far = feed_forward(n2_parts[2:], *mlp_sets[layer])
-        if layer == 0:
-            far.append(outward(crossed[1]))
-            outs_far[0] = after(outs_far[0], far[1])
-            far_pair = swap(after(far[1], outs_far[0]), "dp", 1)
         across_sum = add_low(outs_far[0], swap(outs_far[1], "seq", 1))
         terms = [middle, outs_near[0], swap(outs_near[1], "seq", 1)]
         if layer + 1 < LAYERS:
@@ -1056,15 +1060,18 @@
         state["near_sum"] = add_low(state["keep_near"], after(state["near_got"], *waited))
 
     def step_two(state, *waited):
-        near_sum = add_low(state["near_sum"], after(state["crossed"], *waited))
-        state["terms"] = line_scatter(near_sum, bits[:-1])
+        state["near_sum"] = add_low(state["near_sum"], after(state["crossed"], *waited))
+        state["terms"] = line_scatter(state["near_sum"], bits[:-1])
 
     def finish(states):
         other_side = jnp.concatenate([state["attn_sums"][1] for state in states], axis=1)
         other_side = swap(after(other_side, states[0]["near_got"]), "dp", 1)
         own_side = jnp.concatenate([state["attn_sums"][0] for state in states], axis=1)
         owned = sum(
-            term.astype(jnp.float32) for term in line_scatter(add_low(own_side, other_side), bits)
+            term.astype(jnp.float32)
+            for term in line_scatter(
+                add_low(own_side, other_side), bits, states[0]["near_sum"]
+            )
         ).reshape(LAYERS, chip_rows + 8, -1)
         extra = owned[:, chip_rows:]
         halves = owned[:, :chip_rows].reshape(LAYERS, 2, width_rows, -1)
@@ -1120,7 +1127,6 @@
         got = swap(pair_out, "seq", 1)
         out_terms = [own_out, got[0], swap(add_low(across_out, got[1]), "seq", 2)]
         got_far = swap(send_far, "dp", 1)
-        near_got = swap(after(send_near, got_far), "dp", 1)
         if before is not None:
             step_one(before, own_out)
             before["attn_sums"] = sum_attn(before, attn_sent, own_out)
@@ -1148,7 +1154,8 @@
             cos_wide,
             sin_wide,
         )
-        far_sum = add_low(keep_far, after(got_far, upstream))
+        near_got = swap(after(send_near, grad_low), "dp", 1)
+        far_sum = add_low(keep_far, after(got_far, upstream if before is None else grad_low))
         state = {
             "layer": layer,
             "far_sum": far_sum,

time: 696 us -> 667 us (0.958)
  waiting for transfers between devices: 317 us -> 277 us
  starting transfers between devices: 84.6 us -> 93.7 us
  local copies, waits for them, and re-layouts: 55.5 us -> 47.9 us
  other arithmetic: 31.4 us -> 38.7 us
    ppermute x84, waiting for transfers between devices: 312 us -> 259 us  [swap(): return lax.ppermute(values, axis, [(i, i ^ bit) for i in range(size)])]
    ppermute x8, starting transfers between devices: 18.1 us -> 31.1 us  [line_steps(): lax.ppermute(values, 'dp', [(2 * here + side, 2 * there + side) for here,...]
    ppermute x8, waiting for transfers between devices: 4.82 us -> 17.2 us  [line_steps(): lax.ppermute(values, 'dp', [(2 * here + side, 2 * there + side) for here,...]
    unnamed x200 -> x174, local copies, waits for them, and re-layouts: 39.5 us -> 36.2 us
  transfers between devices with their start and end apart: 92 -> 92, of which waited for: 39 -> 42; matrix products, arithmetic and copies ran while one was open for 7% -> 7% of each run, Pallas kernels for 22% -> 23%
where the time goes in v4:
time: 667 us; the launch traced here: 659 us
  waiting for transfers between devices  277 us (42%)
  Pallas kernels  186 us (28%)
  starting transfers between devices  93.7 us (14%)
  local copies, waits for them, and re-layouts  47.9 us (7%)
  other arithmetic  38.7 us (6%)
  between operations  15.5 us (2%)
    ppermute x84, waiting for transfers between devices, swap(): return lax.ppermute(values, axis, [(i, i ^ bit) for i in range(size)])  259 us
    pallas_call x2, Pallas kernels, feed_back(): call(kernel, [((half, packed, 2 * units), jnp.bfloat16), ((half, packed,...  65.5 us
    ppermute x84, starting transfers between devices, swap(): return lax.ppermute(values, axis, [(i, i ^ bit) for i in range(size)])  62.6 us
    pallas_call x4, Pallas kernels, feed_forward(): call(kernel, [((rows, 2 * units), jnp.bfloat16)] + [((part_rows, D), jnp....  40.8 us
    unnamed x174, local copies, waits for them, and re-layouts  36.2 us
    ppermute x8, starting transfers between devices, line_steps(): lax.ppermute(values, 'dp', [(2 * here + side, 2 * there + side) for here,...  31.1 us
    pallas_call x2, Pallas kernels, attention_back(): call(kernel, [((rows, D), jnp.float32), ((rows, D), jnp.bfloat16), ((1, D...  26.4 us
    pallas_call x2, Pallas kernels, attention(): call(kernel, [((rows, D), jnp.bfloat16), ((rows, D), jnp.float32), ((rows...  21.5 us
  transfers between devices with their start and end apart: 92, of which 42 were waited for; matrix products, arithmetic and copies ran while one was open for 7% of the time, Pallas kernels for 23%

profile of v4, /device:TPU:0, one launch (start us, length us, event | category | flops | bytes accessed | tf_op | source)
XLA Modules:
  0.0 658.9 jit_solution(13352709782478363082)
XLA Ops:
  17.1 3.4 collective-permute-done.4.refs_2_
  20.5 5.5 collective-permute-done.5.refs_3_
  30.1 18.2 %collective-permute-done.15 = bf16[1,168,2432]{2,1,0:T(8,128)(2,1)} collective-permute-done((bf16[1,168,2432]{2,1,0:T(8,128)(2,1)S(1)}, bf16[1,168,2432]{2,1,0:T(8,128)(2,1)}, u32[]{:S(2)}, u32[]{:S(2)}) %collective-permute-start.15) | collective-permute-done | bytes 817184 | tf_op jit(solution)/shard_map/ppermute | solution.py:820
  57.6 8.9 %collective-permute-done.6.refs_1_ = bf16[4,64,1024]{2,1,0:T(8,128)(2,1)S(1)} collective-permute-done((bf16[4,64,1024]{2,1,0:T(8,128)(2,1)S(1)}, bf16[4,64,1024]{2,1,0:T(8,128)(2,1)S(1)}, u32[]{:S(2)}, u32[]{:S(2)}) %collective-permute-start.6) | collective-permute-done | bytes 524320 | tf_op jit(solution)/shard_map/ppermute | solution.py:820
  66.6 4.9 collective-permute-start.8
  86.6 14.9 %collective-permute-done.17 = bf16[2,64,1024]{2,1,0:T(8,128)(2,1)S(1)} collective-permute-done((bf16[2,64,1024]{2,1,0:T(8,128)(2,1)S(1)}, bf16[2,64,1024]{2,1,0:T(8,128)(2,1)S(1)}, u32[]{:S(2)}, u32[]{:S(2)}) %collective-permute-start.17) | collective-permute-done | bytes 262176 | tf_op jit(solution)/shard_map/ppermute | solution.py:820
  116.9 3.0 assemble.2
  136.9 11.7 %attention.2 = (bf16[256,896]{1,0:T(8,128)(2,1)S(1)}, f32[256,896]{1,0:T(8,128)S(1)}, bf16[256,896]{1,0:T(8,128)(2,1)}) custom-call(bf16[2,2,896,64]{3,2,1,0:T(8,128)(2,1)S(1)} %copy-done.18, bf16[256,256]{1,0:T(8,128)(2,1)} %get-tuple-element.268.kv0.refs_8_, bf16[256,256]{1,0:T(8,128)(2,1)} %collective-permute-done.18.kv1.refs_9_, ...), custom_call_target="tpu_custom_call" | custom-call | bytes 42000 | tf_op jit(solution)/shard_map/attention/pallas_call | solution.py:159
  151.8 3.9 collective-permute-start.27
  155.7 7.9 %collective-permute-done.26.refs_0_.refs_7_ = bf16[256,896]{1,0:T(8,128)(2,1)} collective-permute-done((bf16[256,896]{1,0:T(8,128)(2,1)}, bf16[256,896]{1,0:T(8,128)(2,1)}, u32[]{:S(2)}, u32[]{:S(2)}) %collective-permute-start.26) | collective-permute-done | bytes 458784 | tf_op jit(solution)/shard_map/ppermute | solution.py:820
  165.7 8.6 %collective-permute-done.27 = bf16[1,168,2432]{2,1,0:T(8,128)(2,1)} collective-permute-done((bf16[1,168,2432]{2,1,0:T(8,128)(2,1)}, bf16[1,168,2432]{2,1,0:T(8,128)(2,1)}, u32[]{:S(2)}, u32[]{:S(2)}) %collective-permute-start.27) | collective-permute-done | bytes 817184 | tf_op jit(solution)/shard_map/ppermute | solution.py:820
  180.7 14.0 %collective-permute-start.29 = (bf16[2,168,2432]{2,1,0:T(8,128)(2,1)}, bf16[2,168,2432]{2,1,0:T(8,128)(2,1)}, u32[]{:S(2)}, u32[]{:S(2)}) collective-permute-start(bf16[2,168,2432]{2,1,0:T(8,128)(2,1)} %constant_dynamic-update-slice_fusion.refs_0_), channel_id=1, source_target_pairs={{8,16},{12,20},{16,8},{20,12},{9,17},{13,21},{17,9},{21,13},{10,18... | collective-permute-start | bytes 4902920 | tf_op jit(solution)/shard_map/ppermute | solution.py:841
  195.9 20.2 %collective-permute-done.24.refs_3_ = bf16[2,168,2432]{2,1,0:T(8,128)(2,1)} collective-permute-done((bf16[2,168,2432]{2,1,0:T(8,128)(2,1)}, bf16[2,168,2432]{2,1,0:T(8,128)(2,1)}, u32[]{:S(2)}, u32[]{:S(2)}) %collective-permute-start.24) | collective-permute-done | bytes 1634336 | tf_op jit(solution)/shard_map/ppermute | solution.py:820
  217.6 2.9 unpack.2
  223.9 10.2 %feed_forward.4 = (bf16[512,2432]{1,0:T(8,128)(2,1)}, bf16[256,896]{1,0:T(8,128)(2,1)}, bf16[256,896]{1,0:T(8,128)(2,1)}) custom-call(bf16[256,896]{1,0:T(8,128)(2,1)} %get-tuple-element.273.refs_0_.refs_5_, bf16[256,896]{1,0:T(8,128)(2,1)} %collective-permute-done.22.refs_1_.refs_6_, bf16[896,2432]{1,0:T(8,128)(2,1)} %bitcast.140, bf16[1216,896]{1,0:T(8,128)(2,1)} %bitcast.154), custom_call_target="tpu_custom_call" | custom-call | bytes 36000 | tf_op jit(solution)/shard_map/feed_forward/pallas_call | solution.py:204
  236.1 10.2 %feed_forward.5 = (bf16[512,2432]{1,0:T(8,128)(2,1)}, bf16[256,896]{1,0:T(8,128)(2,1)}, bf16[256,896]{1,0:T(8,128)(2,1)}) custom-call(bf16[256,896]{1,0:T(8,128)(2,1)} %collective-permute-done.26.refs_0_.refs_7_, bf16[256,896]{1,0:T(8,128)(2,1)} %collective-permute-done.28.refs_1_.refs_8_, bf16[896,2432]{1,0:T(8,128)(2,1)} %bitcast.141, ...), custom_call_target="tpu_custom_call" | custom-call | bytes 36000 | tf_op jit(solution)/shard_map/feed_forward/pallas_call | solution.py:204
  246.9 3.3 collective-permute-done.34.refs_3_
  253.0 3.2 assemble.3
  256.3 4.4 collective-permute-done.39.refs_2_
  260.7 4.2 collective-permute-done.31.refs_3_
  266.7 3.8 collective-permute-done.44
  274.6 4.4 collective-permute-done.41.kv2.refs_10_
  281.1 9.8 %attention.3 = (bf16[256,896]{1,0:T(8,128)(2,1)S(1)}, f32[256,896]{1,0:T(8,128)S(1)}, bf16[256,896]{1,0:T(8,128)(2,1)S(1)}) custom-call(bf16[2,2,896,64]{3,2,1,0:T(8,128)(2,1)S(1)} %get-tuple-element.297.q_ref.refs_7_, bf16[256,256]{1,0:T(8,128)(2,1)S(1)} %get-tuple-element.298.kv0.refs_8_, bf16[256,256]{1,0:T(8,128)(2,1)S(1)} %collective-permute-done.40.kv1.refs_9_, ...), custom_call_target="tpu_custom_call" | custom-call | bytes 42000 | tf_op jit(solution)/shard_map/attention/pallas_call | solution.py:159
  293.1 12.4 %collective-permute-done.47.refs_0_.refs_7_ = bf16[256,896]{1,0:T(8,128)(2,1)S(1)} collective-permute-done((bf16[256,896]{1,0:T(8,128)(2,1)S(1)}, bf16[256,896]{1,0:T(8,128)(2,1)S(1)}, u32[]{:S(2)}, u32[]{:S(2)}) %collective-permute-start.47) | collective-permute-done | bytes 458784 | tf_op jit(solution)/shard_map/ppermute | solution.py:820
  315.6 10.2 %feed_forward.6 = (bf16[512,2432]{1,0:T(8,128)(2,1)}, bf16[256,896]{1,0:T(8,128)(2,1)}, bf16[256,896]{1,0:T(8,128)(2,1)}) custom-call(bf16[256,896]{1,0:T(8,128)(2,1)} %copy-done.34, bf16[256,896]{1,0:T(8,128)(2,1)} %copy-done.65, bf16[896,2432]{1,0:T(8,128)(2,1)} %bitcast.143, bf16[1216,896]{1,0:T(8,128)(2,1)} %bitcast.157), custom_call_target="tpu_custom_call" | custom-call | bytes 36000 | tf_op jit(solution)/shard_map/feed_forward/pallas_call | solution.py:204
  326.4 10.2 %feed_forward.7 = (bf16[512,2432]{1,0:T(8,128)(2,1)}, bf16[256,896]{1,0:T(8,128)(2,1)}, bf16[256,896]{1,0:T(8,128)(2,1)}) custom-call(bf16[256,896]{1,0:T(8,128)(2,1)} %copy-done.63, bf16[256,896]{1,0:T(8,128)(2,1)} %copy-done.64, bf16[896,2432]{1,0:T(8,128)(2,1)} %bitcast.144, bf16[1216,896]{1,0:T(8,128)(2,1)} %bitcast.158), custom_call_target="tpu_custom_call" | custom-call | bytes 36000 | tf_op jit(solution)/shard_map/feed_forward/pallas_call | solution.py:204
  337.3 32.8 %feed_back.2 = (bf16[2,168,2432]{2,1,0:T(8,128)(2,1)}, bf16[2,168,2432]{2,1,0:T(8,128)(2,1)}, bf16[2,168,2432]{2,1,0:T(8,128)(2,1)}, bf16[2,168,2432]{2,1,0:T(8,...) custom-call(s32[1]{0:T(128)} %bitcast.3.refs_0_, ...), custom_call_target="tpu_custom_call" | custom-call | bytes 100000 | tf_op jit(solution)/shard_map/feed_back/pallas_call | solution.py:321
  375.7 11.0 %collective-permute-done.54.refs_5_ = bf16[256,896]{1,0:T(8,128)(2,1)S(1)} collective-permute-done((bf16[256,896]{1,0:T(8,128)(2,1)S(1)}, bf16[256,896]{1,0:T(8,128)(2,1)S(1)}, u32[]{:S(2)}, u32[]{:S(2)}) %collective-permute-start.54) | collective-permute-done | bytes 458784 | tf_op jit(solution)/shard_map/ppermute | solution.py:820
  389.1 13.2 %attention_back.2 = (f32[256,896]{1,0:T(8,128)S(1)}, bf16[256,896]{1,0:T(8,128)(2,1)S(1)}, f32[1,896]{1,0:T(1,128)S(1)}, bf16[256,896]{1,0:T(8,128)(2,1)S(1)}, f...) custom-call(bf16[256,896]{1,0:T(8,128)(2,1)} %bitcast.47.refs_1_.ref, ...), custom_call_target="tpu_custom_call" | custom-call | bytes 52000 | tf_op jit(solution)/shard_map/attention_back/pallas_call | solution.py:463
  404.7 4.1 collective-permute-done.56.refs_2_
  417.5 8.2 %collective-permute-done.58.refs_3_ = bf16[256,896]{1,0:T(8,128)(2,1)S(1)} collective-permute-done((bf16[256,896]{1,0:T(8,128)(2,1)S(1)}, bf16[256,896]{1,0:T(8,128)(2,1)S(1)}, u32[]{:S(2)}, u32[]{:S(2)}) %collective-permute-start.58) | collective-permute-done | bytes 458784 | tf_op jit(solution)/shard_map/ppermute | solution.py:820
  427.4 6.8 %collective-permute-start.68 = (bf16[2,168,2432]{2,1,0:T(8,128)(2,1)}, bf16[2,168,2432]{2,1,0:T(8,128)(2,1)}, u32[]{:S(2)}, u32[]{:S(2)}) collective-permute-start(bf16[2,168,2432]{2,1,0:T(8,128)(2,1)} %add_convert_fusion.7), channel_id=1, source_target_pairs={{0,8},{4,12},{24,16},{28,20},{1,9},{5,13},{25,17},{29,21},{2,10},{... | collective-permute-start | bytes 4902920 | tf_op jit(solution)/shard_map/ppermute | solution.py:841
  442.0 32.6 %feed_back.3 = (bf16[2,168,2432]{2,1,0:T(8,128)(2,1)}, bf16[2,168,2432]{2,1,0:T(8,128)(2,1)}, bf16[2,168,2432]{2,1,0:T(8,128)(2,1)}, bf16[2,168,2432]{2,1,0:T(8,...) custom-call(s32[1]{0:T(128)} %bitcast.3.refs_0_, ...), custom_call_target="tpu_custom_call" | custom-call | bytes 100000 | tf_op jit(solution)/shard_map/feed_back/pallas_call | solution.py:321
  479.3 3.5 add_convert_fusion.1
  484.9 6.3 collective-permute-done.70.refs_5_
  491.2 13.2 %attention_back.3 = (f32[256,896]{1,0:T(8,128)S(1)}, bf16[256,896]{1,0:T(8,128)(2,1)S(1)}, f32[1,896]{1,0:T(1,128)S(1)}, bf16[256,896]{1,0:T(8,128)(2,1)S(1)}, f...) custom-call(f32[256,896]{1,0:T(8,128)S(1)} %copy-done.38, ...), custom_call_target="tpu_custom_call" | custom-call | bytes 52000 | tf_op jit(solution)/shard_map/attention_back/pallas_call | solution.py:463
  504.4 8.7 %collective-permute-done.81 = bf16[2,168,2432]{2,1,0:T(8,128)(2,1)S(1)} collective-permute-done((bf16[2,168,2432]{2,1,0:T(8,128)(2,1)}, bf16[2,168,2432]{2,1,0:T(8,128)(2,1)S(1)}, u32[]{:S(2)}, u32[]{:S(2)}) %collective-permute-start.81) | collective-permute-done | bytes 1634336 | tf_op jit(solution)/shard_map/ppermute | solution.py:820
  519.3 4.5 collective-permute-done.72.refs_2_
  528.1 3.1 projection_grads.3
  537.9 13.5 %collective-permute-done.82 = bf16[2,168,2432]{2,1,0:T(8,128)(2,1)} collective-permute-done((bf16[2,168,2432]{2,1,0:T(8,128)(2,1)}, bf16[2,168,2432]{2,1,0:T(8,128)(2,1)}, u32[]{:S(2)}, u32[]{:S(2)}) %collective-permute-start.82) | collective-permute-done | bytes 1634336 | tf_op jit(solution)/shard_map/ppermute | solution.py:841
  555.1 9.2 %collective-permute-done.77 = bf16[4,64,1024]{2,1,0:T(8,128)(2,1)S(1)} collective-permute-done((bf16[4,64,1024]{2,1,0:T(8,128)(2,1)S(1)}, bf16[4,64,1024]{2,1,0:T(8,128)(2,1)S(1)}, u32[]{:S(2)}, u32[]{:S(2)}) %collective-permute-start.77) | collective-permute-done | bytes 524320 | tf_op jit(solution)/shard_map/ppermute | solution.py:820
  565.0 5.9 collective-permute-done.78
  574.1 21.2 %collective-permute-done.79 = bf16[4,128,1024]{2,1,0:T(8,128)(2,1)S(1)} collective-permute-done((bf16[4,128,1024]{2,1,0:T(8,128)(2,1)S(1)}, bf16[4,128,1024]{2,1,0:T(8,128)(2,1)S(1)}, u32[]{:S(2)}, u32[]{:S(2)}) %collective-permute-start.79) | collective-permute-done | bytes 1048608 | tf_op jit(solution)/shard_map/ppermute | solution.py:820
  600.0 20.5 %collective-permute-done.80 = bf16[2,128,1024]{2,1,0:T(8,128)(2,1)S(1)} collective-permute-done((bf16[2,128,1024]{2,1,0:T(8,128)(2,1)S(1)}, bf16[2,128,1024]{2,1,0:T(8,128)(2,1)S(1)}, u32[]{:S(2)}, u32[]{:S(2)}) %collective-permute-start.80) | collective-permute-done | bytes 524320 | tf_op jit(solution)/shard_map/ppermute | solution.py:820
  622.9 10.5 %collective-permute-done.84 = bf16[128,1024]{1,0:T(8,128)(2,1)S(1)} collective-permute-done((bf16[128,1024]{1,0:T(8,128)(2,1)S(1)}, bf16[128,1024]{1,0:T(8,128)(2,1)S(1)}, u32[]{:S(2)}, u32[]{:S(2)}) %collective-permute-start.84) | collective-permute-done | bytes 262176 | tf_op jit(solution)/shard_map/ppermute | solution.py:820
  641.6 7.0 %collective-permute-done.90.refs_2_ = bf16[2,28,2432]{2,1,0:T(8,128)(2,1)S(1)} collective-permute-done((bf16[2,28,2432]{2,1,0:T(8,128)(2,1)S(1)}, bf16[2,28,2432]{2,1,0:T(8,128)(2,1)S(1)}, u32[]{:S(2)}, u32[]{:S(2)}) %collective-permute-start.90) | collective-permute-done | bytes 272416 | tf_op jit(solution)/shard_map/ppermute | solution.py:820
  648.6 4.8 collective-permute-done.91.refs_3_
  655.4 3.0 copy.67
  (445 shorter events, 185.8 us)
Async XLA Ops:
  11.8 14.2 %collective-permute-start.5 = (bf16[2,28,2432]{2,1,0:T(8,128)(2,1)S(1)}, bf16[2,28,2432]{2,1,0:T(8,128)(2,1)S(1)}, u32[]{:S(2)}, u32[]{:S(2)}) collective-permute-start(bf16[2,28,2432]{2,1,0:T(8,128)(2,1)S(1)} %get-tuple-element.251), channel_id=1, source_target_pairs={{0,3},{1,2},{2,1},{3,0},{4,7},{5,6},{6,5},{7,4},{8,11},{9,10},{10,... | collective-permute-start | bytes 817160 | tf_op jit(solution)/shard_map/ppermute | solution.py:820
  14.3 14.7 %collective-permute-start.2 = (bf16[2,64,1024]{2,1,0:T(8,128)(2,1)S(1)}, bf16[2,64,1024]{2,1,0:T(8,128)(2,1)S(1)}, u32[]{:S(2)}, u32[]{:S(2)}) collective-permute-start(bf16[2,64,1024]{2,1,0:T(8,128)(2,1)S(1)} %pad_maximum_fusion.8), channel_id=1, source_target_pairs={{0,16},{4,20},{8,24},{12,28},{16,0},{20,4},{24,8},{28,12},{1,17},{... | collective-permute-start | bytes 786440 | tf_op jit(solution)/shard_map/ppermute | solution.py:820
  29.1 19.3 %collective-permute-start.15 = (bf16[1,168,2432]{2,1,0:T(8,128)(2,1)S(1)}, bf16[1,168,2432]{2,1,0:T(8,128)(2,1)}, u32[]{:S(2)}, u32[]{:S(2)}) collective-permute-start(bf16[1,168,2432]{2,1,0:T(8,128)(2,1)S(1)} %get-tuple-element.263), channel_id=1, source_target_pairs={{0,8},{4,12},{8,0},{12,4},{16,24},{20,28},{24,16},{28,20},{1,9},{5... | collective-permute-start | bytes 2451464 | tf_op jit(solution)/shard_map/ppermute | solution.py:820
  29.8 26.2 %collective-permute-start.7 = (bf16[28,1024]{1,0:T(8,128)(2,1)S(1)}, bf16[28,1024]{1,0:T(8,128)(2,1)S(1)}, u32[]{:S(2)}, u32[]{:S(2)}) collective-permute-start(bf16[28,1024]{1,0:T(8,128)(2,1)S(1)} %get-tuple-element.439), channel_id=1, source_target_pairs={{0,1},{1,0},{2,3},{3,2},{4,5},{5,4},{6,7},{7,6},{8,9},{9,8},{10,11... | collective-permute-start | bytes 172040 | tf_op jit(solution)/shard_map/ppermute | solution.py:820
  49.7 57.6 %collective-permute-start.16 = (bf16[2,168,2432]{2,1,0:T(8,128)(2,1)S(1)}, bf16[2,168,2432]{2,1,0:T(8,128)(2,1)}, u32[]{:S(2)}, u32[]{:S(2)}) collective-permute-start(bf16[2,168,2432]{2,1,0:T(8,128)(2,1)S(1)} %pad_maximum_fusion.refs_0_), channel_id=1, source_target_pairs={{8,16},{12,20},{16,8},{20,12},{9,17},{13,21},{17,9},{21,13},{10,18... | collective-permute-start | bytes 4902920 | tf_op jit(solution)/shard_map/ppermute | solution.py:841
  56.0 20.0 %collective-permute-start.9 = (bf16[4,64,1024]{2,1,0:T(8,128)(2,1)S(1)}, bf16[4,64,1024]{2,1,0:T(8,128)(2,1)S(1)}, u32[]{:S(2)}, u32[]{:S(2)}) collective-permute-start(bf16[4,64,1024]{2,1,0:T(8,128)(2,1)S(1)} %pad_maximum_fusion.2.refs_0_), channel_id=1, source_target_pairs={{0,2},{1,3},{2,0},{3,1},{4,6},{5,7},{6,4},{7,5},{8,10},{9,11},{10,... | collective-permute-start | bytes 1572872 | tf_op jit(solution)/shard_map/ppermute | solution.py:820
  71.5 58.4 %collective-permute-start.21 = (bf16[2,168,2432]{2,1,0:T(8,128)(2,1)S(1)}, bf16[2,168,2432]{2,1,0:T(8,128)(2,1)}, u32[]{:S(2)}, u32[]{:S(2)}) collective-permute-start(bf16[2,168,2432]{2,1,0:T(8,128)(2,1)S(1)} %pad_maximum_fusion.refs_0_), channel_id=1, source_target_pairs={{0,4},{4,0},{8,12},{12,8},{16,20},{20,16},{24,28},{28,24},{1,5},{5... | collective-permute-start | bytes 4902920 | tf_op jit(solution)/shard_map/ppermute | solution.py:820
  73.5 12.9 %collective-permute-start.10 = (bf16[4,64,1024]{2,1,0:T(8,128)(2,1)S(1)}, bf16[4,64,1024]{2,1,0:T(8,128)(2,1)}, u32[]{:S(2)}, u32[]{:S(2)}) collective-permute-start(bf16[4,64,1024]{2,1,0:T(8,128)(2,1)S(1)} %collective-permute-done.6.refs_1_), channel_id=1, source_target_pairs={{0,2},{1,3},{2,0},{3,1},{4,6},{5,7},{6,4},{7,5},{8,10},{9,11},{10,... | collective-permute-start | bytes 1572872 | tf_op jit(solution)/shard_map/ppermute | solution.py:820
  75.1 26.4 %collective-permute-start.11 = (bf16[4,64,1024]{2,1,0:T(8,128)(2,1)S(1)}, bf16[4,64,1024]{2,1,0:T(8,128)(2,1)S(1)}, u32[]{:S(2)}, u32[]{:S(2)}) collective-permute-start(bf16[4,64,1024]{2,1,0:T(8,128)(2,1)S(1)} %pad_maximum_fusion.2.refs_0_), channel_id=1, source_target_pairs={{0,1},{1,0},{2,3},{3,2},{4,5},{5,4},{6,7},{7,6},{8,9},{9,8},{10,11... | collective-permute-start | bytes 1572872 | tf_op jit(solution)/shard_map/ppermute | solution.py:820
  76.0 25.4 %collective-permute-start.17 = (bf16[2,64,1024]{2,1,0:T(8,128)(2,1)S(1)}, bf16[2,64,1024]{2,1,0:T(8,128)(2,1)S(1)}, u32[]{:S(2)}, u32[]{:S(2)}) collective-permute-start(bf16[2,64,1024]{2,1,0:T(8,128)(2,1)S(1)} %pad_maximum_fusion.9), channel_id=1, source_target_pairs={{0,16},{4,20},{8,24},{12,28},{16,0},{20,4},{24,8},{28,12},{1,17},{... | collective-permute-start | bytes 786440 | tf_op jit(solution)/shard_map/ppermute | solution.py:820
  86.4 25.6 %collective-permute-start.12 = (bf16[4,64,1024]{2,1,0:T(8,128)(2,1)S(1)}, bf16[4,64,1024]{2,1,0:T(8,128)(2,1)}, u32[]{:S(2)}, u32[]{:S(2)}) collective-permute-start(bf16[4,64,1024]{2,1,0:T(8,128)(2,1)S(1)} %collective-permute-done.6.refs_1_), channel_id=1, source_target_pairs={{0,1},{1,0},{2,3},{3,2},{4,5},{5,4},{6,7},{7,6},{8,9},{9,8},{10,11... | collective-permute-start | bytes 1572872 | tf_op jit(solution)/shard_map/ppermute | solution.py:820
  107.3 67.0 %collective-permute-start.23 = (bf16[2,168,2432]{2,1,0:T(8,128)(2,1)}, bf16[2,168,2432]{2,1,0:T(8,128)(2,1)}, u32[]{:S(2)}, u32[]{:S(2)}) collective-permute-start(bf16[2,168,2432]{2,1,0:T(8,128)(2,1)} %collective-permute-done.16), channel_id=1, source_target_pairs={{8,0},{12,4},{16,24},{20,28},{9,1},{13,5},{17,25},{21,29},{10,2},{... | collective-permute-start | bytes 4902920 | tf_op jit(solution)/shard_map/ppermute | solution.py:841
  150.3 13.3 %collective-permute-start.26 = (bf16[256,896]{1,0:T(8,128)(2,1)}, bf16[256,896]{1,0:T(8,128)(2,1)}, u32[]{:S(2)}, u32[]{:S(2)}) collective-permute-start(bf16[256,896]{1,0:T(8,128)(2,1)} %get-tuple-element.273.refs_0_.refs_5_), channel_id=1, source_target_pairs={{0,2},{1,3},{2,0},{3,1},{4,6},{5,7},{6,4},{7,5},{8,10},{9,11},{10,... | collective-permute-start | bytes 1376264 | tf_op jit(solution)/shard_map/ppermute | solution.py:820
  151.8 22.5 %collective-permute-start.27 = (bf16[1,168,2432]{2,1,0:T(8,128)(2,1)}, bf16[1,168,2432]{2,1,0:T(8,128)(2,1)}, u32[]{:S(2)}, u32[]{:S(2)}) collective-permute-start(bf16[1,168,2432]{2,1,0:T(8,128)(2,1)} %get-tuple-element.279), channel_id=1, source_target_pairs={{0,8},{4,12},{8,0},{12,4},{16,24},{20,28},{24,16},{28,20},{1,9},{5... | collective-permute-start | bytes 2451464 | tf_op jit(solution)/shard_map/ppermute | solution.py:820
  177.1 39.0 %collective-permute-start.24 = (bf16[2,168,2432]{2,1,0:T(8,128)(2,1)}, bf16[2,168,2432]{2,1,0:T(8,128)(2,1)}, u32[]{:S(2)}, u32[]{:S(2)}) collective-permute-start(bf16[2,168,2432]{2,1,0:T(8,128)(2,1)} %broadcast_select_fusion.1.refs_1_), channel_id=1, source_target_pairs={{0,4},{4,0},{8,12},{12,8},{16,20},{20,16},{24,28},{28,24},{1,5},{5... | collective-permute-start | bytes 4902920 | tf_op jit(solution)/shard_map/ppermute | solution.py:820
  180.7 53.4 %collective-permute-start.29 = (bf16[2,168,2432]{2,1,0:T(8,128)(2,1)}, bf16[2,168,2432]{2,1,0:T(8,128)(2,1)}, u32[]{:S(2)}, u32[]{:S(2)}) collective-permute-start(bf16[2,168,2432]{2,1,0:T(8,128)(2,1)} %constant_dynamic-update-slice_fusion.refs_0_), channel_id=1, source_target_pairs={{8,16},{12,20},{16,8},{20,12},{9,17},{13,21},{17,9},{21,13},{10,18... | collective-permute-start | bytes 4902920 | tf_op jit(solution)/shard_map/ppermute | solution.py:841
  194.7 29.2 %collective-permute-start.22 = (bf16[256,896]{1,0:T(8,128)(2,1)}, bf16[256,896]{1,0:T(8,128)(2,1)}, u32[]{:S(2)}, u32[]{:S(2)}) collective-permute-start(bf16[256,896]{1,0:T(8,128)(2,1)} %get-tuple-element.273.refs_0_.refs_5_), channel_id=1, source_target_pairs={{0,1},{1,0},{2,3},{3,2},{4,5},{5,4},{6,7},{7,6},{8,9},{9,8},{10,11... | collective-permute-start | bytes 1376264 | tf_op jit(solution)/shard_map/ppermute | solution.py:820
  194.8 40.6 %collective-permute-start.32 = (bf16[4,64,1024]{2,1,0:T(8,128)(2,1)}, bf16[4,64,1024]{2,1,0:T(8,128)(2,1)}, u32[]{:S(2)}, u32[]{:S(2)}) collective-permute-start(bf16[4,64,1024]{2,1,0:T(8,128)(2,1)} %pad_maximum_fusion.3.refs_0_), channel_id=1, source_target_pairs={{0,4},{4,0},{8,12},{12,8},{16,20},{20,16},{24,28},{28,24},{1,5},{5... | collective-permute-start | bytes 1572872 | tf_op jit(solution)/shard_map/ppermute | solution.py:820
  195.3 50.9 %collective-permute-start.33 = (bf16[4,64,1024]{2,1,0:T(8,128)(2,1)}, bf16[4,64,1024]{2,1,0:T(8,128)(2,1)}, u32[]{:S(2)}, u32[]{:S(2)}) collective-permute-start(bf16[4,64,1024]{2,1,0:T(8,128)(2,1)} %pad_maximum_fusion.3.refs_0_), channel_id=1, source_target_pairs={{0,2},{1,3},{2,0},{3,1},{4,6},{5,7},{6,4},{7,5},{8,10},{9,11},{10,... | collective-permute-start | bytes 1572872 | tf_op jit(solution)/shard_map/ppermute | solution.py:820
  216.0 44.6 %collective-permute-start.39 = (bf16[2,168,2432]{2,1,0:T(8,128)(2,1)}, bf16[2,168,2432]{2,1,0:T(8,128)(2,1)}, u32[]{:S(2)}, u32[]{:S(2)}) collective-permute-start(bf16[2,168,2432]{2,1,0:T(8,128)(2,1)} %constant_dynamic-update-slice_fusion.refs_0_), channel_id=1, source_target_pairs={{0,4},{4,0},{8,12},{12,8},{16,20},{20,16},{24,28},{28,24},{1,5},{5... | collective-permute-start | bytes 4902920 | tf_op jit(solution)/shard_map/ppermute | solution.py:820
  234.1 36.4 %collective-permute-start.44 = (bf16[2,168,2432]{2,1,0:T(8,128)(2,1)}, bf16[2,168,2432]{2,1,0:T(8,128)(2,1)}, u32[]{:S(2)}, u32[]{:S(2)}) collective-permute-start(bf16[2,168,2432]{2,1,0:T(8,128)(2,1)} %collective-permute-done.29), channel_id=1, source_target_pairs={{8,0},{12,4},{16,24},{20,28},{9,1},{13,5},{17,25},{21,29},{10,2},{... | collective-permute-start | bytes 4902920 | tf_op jit(solution)/shard_map/ppermute | solution.py:841
  235.5 14.7 %collective-permute-start.34 = (bf16[4,64,1024]{2,1,0:T(8,128)(2,1)}, bf16[4,64,1024]{2,1,0:T(8,128)(2,1)}, u32[]{:S(2)}, u32[]{:S(2)}) collective-permute-start(bf16[4,64,1024]{2,1,0:T(8,128)(2,1)} %collective-permute-done.32.refs_1_), channel_id=1, source_target_pairs={{0,2},{1,3},{2,0},{3,1},{4,6},{5,7},{6,4},{7,5},{8,10},{9,11},{10,... | collective-permute-start | bytes 1572872 | tf_op jit(solution)/shard_map/ppermute | solution.py:820
  272.1 34.2 %collective-permute-start.45 = (bf16[2,168,2432]{2,1,0:T(8,128)(2,1)S(1)}, bf16[2,168,2432]{2,1,0:T(8,128)(2,1)S(1)}, u32[]{:S(2)}, u32[]{:S(2)}) collective-permute-start(bf16[2,168,2432]{2,1,0:T(8,128)(2,1)S(1)} %broadcast_select_fusion.refs_1_), channel_id=1, source_target_pairs={{0,4},{4,0},{8,12},{12,8},{16,20},{20,16},{24,28},{28,24},{1,5},{5... | collective-permute-start | bytes 4902920 | tf_op jit(solution)/shard_map/ppermute | solution.py:820
  292.6 12.9 %collective-permute-start.47 = (bf16[256,896]{1,0:T(8,128)(2,1)S(1)}, bf16[256,896]{1,0:T(8,128)(2,1)S(1)}, u32[]{:S(2)}, u32[]{:S(2)}) collective-permute-start(bf16[256,896]{1,0:T(8,128)(2,1)S(1)} %get-tuple-element.301.refs_0_.refs_5_), channel_id=1, source_target_pairs={{0,2},{1,3},{2,0},{3,1},{4,6},{5,7},{6,4},{7,5},{8,10},{9,11},{10,... | collective-permute-start | bytes 1376264 | tf_op jit(solution)/shard_map/ppermute | solution.py:820
  308.1 17.8 %collective-permute-start.51 = (bf16[256,896]{1,0:T(8,128)(2,1)}, bf16[256,896]{1,0:T(8,128)(2,1)}, u32[]{:S(2)}, u32[]{:S(2)}) collective-permute-start(bf16[256,896]{1,0:T(8,128)(2,1)} %bitcast.47.refs_1_.refs_0_), channel_id=1, source_target_pairs={{0,2},{1,3},{2,0},{3,1},{4,6},{5,7},{6,4},{7,5},{8,10},{9,11},{10,... | collective-permute-start | bytes 1376264 | tf_op jit(solution)/shard_map/ppermute | solution.py:820
  370.4 47.1 %collective-permute-start.67 = (bf16[2,168,2432]{2,1,0:T(8,128)(2,1)}, bf16[2,168,2432]{2,1,0:T(8,128)(2,1)S(1)}, u32[]{:S(2)}, u32[]{:S(2)}) collective-permute-start(bf16[2,168,2432]{2,1,0:T(8,128)(2,1)} %get-tuple-element.347), channel_id=1, source_target_pairs={{0,4},{4,0},{8,12},{12,8},{16,20},{20,16},{24,28},{28,24},{1,5},{5... | collective-permute-start | bytes 4902920 | tf_op jit(solution)/shard_map/ppermute | solution.py:820
  413.0 12.7 %collective-permute-start.58 = (bf16[256,896]{1,0:T(8,128)(2,1)S(1)}, bf16[256,896]{1,0:T(8,128)(2,1)S(1)}, u32[]{:S(2)}, u32[]{:S(2)}) collective-permute-start(bf16[256,896]{1,0:T(8,128)(2,1)S(1)} %get-tuple-element.337.refs_1_), channel_id=1, source_target_pairs={{0,2},{1,3},{2,0},{3,1},{4,6},{5,7},{6,4},{7,5},{8,10},{9,11},{10,... | collective-permute-start | bytes 1376264 | tf_op jit(solution)/shard_map/ppermute | solution.py:820
  414.5 60.1 %collective-permute-start.66 = (bf16[2,168,2432]{2,1,0:T(8,128)(2,1)}, bf16[2,168,2432]{2,1,0:T(8,128)(2,1)}, u32[]{:S(2)}, u32[]{:S(2)}) collective-permute-start(bf16[2,168,2432]{2,1,0:T(8,128)(2,1)} %get-tuple-element.345), channel_id=1, source_target_pairs={{0,4},{4,0},{8,12},{12,8},{16,20},{20,16},{24,28},{28,24},{1,5},{5... | collective-permute-start | bytes 4902920 | tf_op jit(solution)/shard_map/ppermute | solution.py:820
  417.4 17.3 %collective-permute-start.62 = (bf16[2,4,64,1024]{3,2,1,0:T(8,128)(2,1)S(1)}, bf16[2,4,64,1024]{3,2,1,0:T(8,128)(2,1)S(1)}, u32[]{:S(2)}, u32[]{:S(2)}) collective-permute-start(bf16[2,4,64,1024]{3,2,1,0:T(8,128)(2,1)S(1)} %get-tuple-element.336), channel_id=1, source_target_pairs={{0,1},{1,0},{2,3},{3,2},{4,5},{5,4},{6,7},{7,6},{8,9},{9,8},{10,11... | collective-permute-start | bytes 3145736 | tf_op jit(solution)/shard_map/ppermute | solution.py:820
  427.4 47.3 %collective-permute-start.68 = (bf16[2,168,2432]{2,1,0:T(8,128)(2,1)}, bf16[2,168,2432]{2,1,0:T(8,128)(2,1)}, u32[]{:S(2)}, u32[]{:S(2)}) collective-permute-start(bf16[2,168,2432]{2,1,0:T(8,128)(2,1)} %add_convert_fusion.7), channel_id=1, source_target_pairs={{0,8},{4,12},{24,16},{28,20},{1,9},{5,13},{25,17},{29,21},{2,10},{... | collective-permute-start | bytes 4902920 | tf_op jit(solution)/shard_map/ppermute | solution.py:841
  437.5 37.1 %collective-permute-start.64 = (bf16[4,64,1024]{2,1,0:T(8,128)(2,1)}, bf16[4,64,1024]{2,1,0:T(8,128)(2,1)}, u32[]{:S(2)}, u32[]{:S(2)}) collective-permute-start(bf16[4,64,1024]{2,1,0:T(8,128)(2,1)} %get-tuple-element.342), channel_id=1, source_target_pairs={{0,2},{1,3},{2,0},{3,1},{4,6},{5,7},{6,4},{7,5},{8,10},{9,11},{10,... | collective-permute-start | bytes 1572872 | tf_op jit(solution)/shard_map/ppermute | solution.py:820
  439.0 35.6 %collective-permute-start.65 = (bf16[4,64,1024]{2,1,0:T(8,128)(2,1)}, bf16[4,64,1024]{2,1,0:T(8,128)(2,1)}, u32[]{:S(2)}, u32[]{:S(2)}) collective-permute-start(bf16[4,64,1024]{2,1,0:T(8,128)(2,1)} %get-tuple-element.343), channel_id=1, source_target_pairs={{0,2},{1,3},{2,0},{3,1},{4,6},{5,7},{6,4},{7,5},{8,10},{9,11},{10,... | collective-permute-start | bytes 1572872 | tf_op jit(solution)/shard_map/ppermute | solution.py:820
  440.6 34.1 %collective-permute-start.60 = (bf16[256,896]{1,0:T(8,128)(2,1)}, bf16[256,896]{1,0:T(8,128)(2,1)}, u32[]{:S(2)}, u32[]{:S(2)}) collective-permute-start(bf16[256,896]{1,0:T(8,128)(2,1)} %add_convert_fusion.15), channel_id=1, source_target_pairs={{0,2},{1,3},{2,0},{3,1},{4,6},{5,7},{6,4},{7,5},{8,10},{9,11},{10,... | collective-permute-start | bytes 1376264 | tf_op jit(solution)/shard_map/ppermute | solution.py:820
  474.7 38.3 %collective-permute-start.81 = (bf16[2,168,2432]{2,1,0:T(8,128)(2,1)}, bf16[2,168,2432]{2,1,0:T(8,128)(2,1)S(1)}, u32[]{:S(2)}, u32[]{:S(2)}) collective-permute-start(bf16[2,168,2432]{2,1,0:T(8,128)(2,1)} %get-tuple-element.378), channel_id=1, source_target_pairs={{0,4},{4,0},{8,12},{12,8},{16,20},{20,16},{24,28},{28,24},{1,5},{5... | collective-permute-start | bytes 4902920 | tf_op jit(solution)/shard_map/ppermute | solution.py:820
  482.8 52.6 %collective-permute-start.87 = (bf16[2,168,2432]{2,1,0:T(8,128)(2,1)}, bf16[2,168,2432]{2,1,0:T(8,128)(2,1)}, u32[]{:S(2)}, u32[]{:S(2)}) collective-permute-start(bf16[2,168,2432]{2,1,0:T(8,128)(2,1)} %add_convert_fusion.1), channel_id=1, source_target_pairs={{8,16},{12,20},{16,8},{20,12},{9,17},{13,21},{17,9},{21,13},{10,18... | collective-permute-start | bytes 4902920 | tf_op jit(solution)/shard_map/ppermute | solution.py:841
  514.7 36.7 %collective-permute-start.82 = (bf16[2,168,2432]{2,1,0:T(8,128)(2,1)}, bf16[2,168,2432]{2,1,0:T(8,128)(2,1)}, u32[]{:S(2)}, u32[]{:S(2)}) collective-permute-start(bf16[2,168,2432]{2,1,0:T(8,128)(2,1)} %add_convert_fusion.5), channel_id=1, source_target_pairs={{0,8},{4,12},{24,16},{28,20},{1,9},{5,13},{25,17},{29,21},{2,10},{... | collective-permute-start | bytes 4902920 | tf_op jit(solution)/shard_map/ppermute | solution.py:841
  532.5 88.3 %collective-permute-start.46 = (bf16[256,896]{1,0:T(8,128)(2,1)}, bf16[256,896]{1,0:T(8,128)(2,1)S(1)}, u32[]{:S(2)}, u32[]{:S(2)}) collective-permute-start(bf16[256,896]{1,0:T(8,128)(2,1)} %get-tuple-element.307), channel_id=1, source_target_pairs={{0,1},{1,0},{2,3},{3,2},{4,5},{5,4},{6,7},{7,6},{8,9},{9,8},{10,11... | collective-permute-start | bytes 1376264 | tf_op jit(solution)/shard_map/ppermute | solution.py:820
  532.7 38.1 %collective-permute-start.78 = (bf16[2,168,2432]{2,1,0:T(8,128)(2,1)}, bf16[2,168,2432]{2,1,0:T(8,128)(2,1)S(1)}, u32[]{:S(2)}, u32[]{:S(2)}) collective-permute-start(bf16[2,168,2432]{2,1,0:T(8,128)(2,1)} %get-tuple-element.374), channel_id=1, source_target_pairs={{0,4},{4,0},{8,12},{12,8},{16,20},{20,16},{24,28},{28,24},{1,5},{5... | collective-permute-start | bytes 4902920 | tf_op jit(solution)/shard_map/ppermute | solution.py:820
  535.4 28.8 %collective-permute-start.74 = (bf16[2,4,64,1024]{3,2,1,0:T(8,128)(2,1)S(1)}, bf16[2,4,64,1024]{3,2,1,0:T(8,128)(2,1)S(1)}, u32[]{:S(2)}, u32[]{:S(2)}) collective-permute-start(bf16[2,4,64,1024]{3,2,1,0:T(8,128)(2,1)S(1)} %copy-done.62), channel_id=1, source_target_pairs={{0,1},{1,0},{2,3},{3,2},{4,5},{5,4},{6,7},{7,6},{8,9},{9,8},{10,11... | collective-permute-start | bytes 3145736 | tf_op jit(solution)/shard_map/ppermute | solution.py:820
  537.1 17.2 %collective-permute-start.76 = (bf16[4,64,1024]{2,1,0:T(8,128)(2,1)S(1)}, bf16[4,64,1024]{2,1,0:T(8,128)(2,1)S(1)}, u32[]{:S(2)}, u32[]{:S(2)}) collective-permute-start(bf16[4,64,1024]{2,1,0:T(8,128)(2,1)S(1)} %get-tuple-element.422), channel_id=1, source_target_pairs={{0,2},{1,3},{2,0},{3,1},{4,6},{5,7},{6,4},{7,5},{8,10},{9,11},{10,... | collective-permute-start | bytes 1572872 | tf_op jit(solution)/shard_map/ppermute | solution.py:820
  551.3 12.9 %collective-permute-start.77 = (bf16[4,64,1024]{2,1,0:T(8,128)(2,1)S(1)}, bf16[4,64,1024]{2,1,0:T(8,128)(2,1)S(1)}, u32[]{:S(2)}, u32[]{:S(2)}) collective-permute-start(bf16[4,64,1024]{2,1,0:T(8,128)(2,1)S(1)} %get-tuple-element.423), channel_id=1, source_target_pairs={{0,2},{1,3},{2,0},{3,1},{4,6},{5,7},{6,4},{7,5},{8,10},{9,11},{10,... | collective-permute-start | bytes 1572872 | tf_op jit(solution)/shard_map/ppermute | solution.py:820
  554.3 41.6 %collective-permute-start.83 = (bf16[2,168,2432]{2,1,0:T(8,128)(2,1)S(1)}, bf16[2,168,2432]{2,1,0:T(8,128)(2,1)S(1)}, u32[]{:S(2)}, u32[]{:S(2)}) collective-permute-start(bf16[2,168,2432]{2,1,0:T(8,128)(2,1)S(1)} %add_convert_fusion.4), channel_id=1, source_target_pairs={{8,16},{12,20},{16,8},{20,12},{9,17},{13,21},{17,9},{21,13},{10,18... | collective-permute-start | bytes 4902920 | tf_op jit(solution)/shard_map/ppermute | solution.py:841
  570.8 24.5 %collective-permute-start.79 = (bf16[4,128,1024]{2,1,0:T(8,128)(2,1)S(1)}, bf16[4,128,1024]{2,1,0:T(8,128)(2,1)S(1)}, u32[]{:S(2)}, u32[]{:S(2)}) collective-permute-start(bf16[4,128,1024]{2,1,0:T(8,128)(2,1)S(1)} %pad_maximum_fusion.1), channel_id=1, source_target_pairs={{0,4},{4,0},{8,12},{12,8},{16,20},{20,16},{24,28},{28,24},{1,5},{5... | collective-permute-start | bytes 3145736 | tf_op jit(solution)/shard_map/ppermute | solution.py:820
  574.0 61.9 %collective-permute-start.88 = (bf16[168,2432]{1,0:T(8,128)(2,1)S(1)}, bf16[168,2432]{1,0:T(8,128)(2,1)S(1)}, u32[]{:S(2)}, u32[]{:S(2)}) collective-permute-start(bf16[168,2432]{1,0:T(8,128)(2,1)S(1)} %get-tuple-element.428), channel_id=1, source_target_pairs={{0,8},{4,12},{8,0},{12,4},{16,24},{20,28},{24,16},{28,20},{1,9},{5... | collective-permute-start | bytes 2451464 | tf_op jit(solution)/shard_map/ppermute | solution.py:820
  595.8 24.7 %collective-permute-start.80 = (bf16[2,128,1024]{2,1,0:T(8,128)(2,1)S(1)}, bf16[2,128,1024]{2,1,0:T(8,128)(2,1)S(1)}, u32[]{:S(2)}, u32[]{:S(2)}) collective-permute-start(bf16[2,128,1024]{2,1,0:T(8,128)(2,1)S(1)} %slice.390), channel_id=1, source_target_pairs={{0,16},{4,20},{8,24},{12,28},{16,0},{20,4},{24,8},{28,12},{1,17},{... | collective-permute-start | bytes 1572872 | tf_op jit(solution)/shard_map/ppermute | solution.py:820
  597.6 38.4 %collective-permute-start.86 = (bf16[168,2432]{1,0:T(8,128)(2,1)S(1)}, bf16[168,2432]{1,0:T(8,128)(2,1)S(1)}, u32[]{:S(2)}, u32[]{:S(2)}) collective-permute-start(bf16[168,2432]{1,0:T(8,128)(2,1)S(1)} %get-tuple-element.430), channel_id=1, source_target_pairs={{0,8},{4,12},{8,0},{12,4},{16,24},{20,28},{24,16},{28,20},{1,9},{5... | collective-permute-start | bytes 2451464 | tf_op jit(solution)/shard_map/ppermute | solution.py:820
  620.7 12.6 %collective-permute-start.84 = (bf16[128,1024]{1,0:T(8,128)(2,1)S(1)}, bf16[128,1024]{1,0:T(8,128)(2,1)S(1)}, u32[]{:S(2)}, u32[]{:S(2)}) collective-permute-start(bf16[128,1024]{1,0:T(8,128)(2,1)S(1)} %slice_bitcast_fusion.8), channel_id=1, source_target_pairs={{0,8},{4,12},{8,0},{12,4},{16,24},{20,28},{24,16},{28,20},{1,9},{5... | collective-permute-start | bytes 786440 | tf_op jit(solution)/shard_map/ppermute | solution.py:820
  639.0 14.4 %collective-permute-start.91 = (bf16[2,28,2432]{2,1,0:T(8,128)(2,1)S(1)}, bf16[2,28,2432]{2,1,0:T(8,128)(2,1)S(1)}, u32[]{:S(2)}, u32[]{:S(2)}) collective-permute-start(bf16[2,28,2432]{2,1,0:T(8,128)(2,1)S(1)} %get-tuple-element.388), channel_id=1, source_target_pairs={{0,3},{1,2},{2,1},{3,0},{4,7},{5,6},{6,5},{7,4},{8,11},{9,10},{10,... | collective-permute-start | bytes 817160 | tf_op jit(solution)/shard_map/ppermute | solution.py:820
  (128 other events, 1101.1 us)

commit v5 on v4

--- a/solution.py
+++ b/solution.py
@@ -226,9 +226,10 @@
     return (mine ^ place) - line // 2
 
 
-def feed_back(gz_parts, n2_parts, gu_parts, gate_up_full, down_full, dp_place, group_count):
+def feed_back(gz_parts, n2_parts, gu_parts, gate_up_full, down_full, dp_place, group_count, far_arrays):
     line = group_count // 2
     half = line // 2
+    each = half // far_arrays
     chunk = D // group_count
     count = len(gz_parts)
     gu_count = len(gu_parts)
@@ -247,9 +248,9 @@
         n2_refs = refs[count : 2 * count]
         gu_refs = refs[2 * count : 2 * count + gu_count]
         w_ref, d_ref = refs[2 * count + gu_count : 2 * count + gu_count + 2]
-        keep_near, keep_far, send_near, send_far, own_ref, across_ref, pair_ref = refs[
-            2 * count + gu_count + 2 : 2 * count + gu_count + 9
-        ]
+        outs = refs[2 * count + gu_count + 2 : -4]
+        keep_near, send_near, own_ref, across_ref, pair_ref = outs[:5]
+        keep_far, send_far = outs[5 : 5 + far_arrays], outs[5 + far_arrays :]
         total, gz, n2t, down = refs[-4:]
         side, mine = place_ref[0] % 2, place_ref[0] // 2
         step = pl.program_id(0)
@@ -273,10 +274,12 @@
                 keep_near[slot, rows, lanes] = keep
                 send_near[slot, rows, lanes] = send
 
-            @pl.when(slot >= half)
-            def _():
-                keep_far[beyond, rows, lanes] = keep
-                send_far[beyond, rows, lanes] = send
+            for number in range(far_arrays):
+
+                @pl.when((slot >= half) & (beyond // each == number))
+                def _():
+                    keep_far[number][beyond % each, rows, lanes] = keep
+                    send_far[number][beyond % each, rows, lanes] = send
 
         def work(width):
             gu = jnp.concatenate([ref[:, : 2 * width] for ref in gu_refs], axis=0).astype(jnp.float32)
@@ -323,12 +326,11 @@
         [
             ((half, packed, 2 * units), jnp.bfloat16),
             ((half, packed, 2 * units), jnp.bfloat16),
-            ((half, packed, 2 * units), jnp.bfloat16),
-            ((half, packed, 2 * units), jnp.bfloat16),
             ((part_rows, D), jnp.bfloat16),
             ((part_rows, D), jnp.bfloat16),
             ((2, part_rows, D), jnp.bfloat16),
-        ],
+        ]
+        + [((each, packed, 2 * units), jnp.bfloat16)] * (2 * far_arrays),
         25.0,
         [
             pltpu.VMEM((rows, D), jnp.float32),
@@ -348,12 +350,12 @@
         out_specs=[
             pl.BlockSpec((half, packed, 2 * units), lambda step: (0, 0, 0), pipeline_mode=once),
             pl.BlockSpec((half, packed, 2 * units), lambda step: (0, 0, 0), pipeline_mode=once),
-            pl.BlockSpec((half, packed, 2 * units), lambda step: (0, 0, 0), pipeline_mode=once),
-            pl.BlockSpec((half, packed, 2 * units), lambda step: (0, 0, 0), pipeline_mode=once),
             pl.BlockSpec((part_rows, D), whole, pipeline_mode=once),
             pl.BlockSpec((part_rows, D), whole, pipeline_mode=once),
             pl.BlockSpec((2, part_rows, D), lambda step: (0, 0, 0), pipeline_mode=once),
-        ],
+        ]
+        + [pl.BlockSpec((each, packed, 2 * units), lambda step: (0, 0, 0), pipeline_mode=once)]
+        * (2 * far_arrays),
     )(dp_place.reshape(1).astype(jnp.int32), *gz_parts, *n2_parts, *gu_parts, gate_up_full, down_full)
 
 
@@ -934,12 +936,13 @@
         extra = extra.at[3, :KV_WIDTH].set(bias_all[SPLIT:])
         return jnp.concatenate([rows, extra], axis=0)
 
-    def attn_finish(own_side, other_side, *waited, ahead=None):
+    def attn_parts(own_side, other_side, *waited):
         parts = [own_side, other_side]
-        parts = parts + [swap(after(part, *waited), "seq", 2) for part in parts]
+        return parts + [swap(after(part, *waited), "seq", 2) for part in parts]
+
+    def attn_finish(parts):
+        other_side = parts[1]
         parts = parts + [swap(after(part, other_side), "seq", 1) for part in parts]
-        if ahead is not None:
-            parts[1] = after(parts[1], ahead)
         first_full, second_full, small = assemble(parts, [core, chip_x, dp_place], chip_rows)
         return (
             first_full,
@@ -963,7 +966,8 @@
         passed = after(line_steps(crossed, [(1, 0), (2, 3)]), *waited)
         return jnp.where((line_place == 1) | (line_place == 2), crossed, passed)
 
-    near = [line_gather(after(gate_shards[0], attn_line), bits[:-1])]
+    first_parts = attn_parts(attn_line, attn_other)
+    near = [line_gather(after(gate_shards[0], attn_other), bits[:-1], first_parts[3])]
     near_pair = [swap(after(near[0], attn_other), "dp", 1)]
     crossed = [cross_middle(near[0])]
     far = []
@@ -984,15 +988,14 @@
     terms = [tokens.reshape(tok_len, model_width)]
     kept_state = []
     mlp_sets = []
-    second_line = line_gather(after(shards[1], attn_other), bits[:1])
-    attn_sets = [attn_finish(attn_line, attn_other, ahead=second_line)]
-    for bit in bits[1:]:
-        second_line = line_gather(second_line, [bit])
+    attn_sets = [attn_finish(first_parts)]
     for layer in range(LAYERS):
         first_full, second_full, gain_full, mlp_gain_full, bias_first, bias_second = attn_sets[layer]
+        if layer == 0:
+            second_line = line_gather(after(shards[1], first_full), bits[:1])
         x, normed, queries, own_kv = before_attention(
             terms,
-            after(gain_full, near[0], crossed[0], second_line) if layer == 0 else after(gain_full, near_pair[1]),
+            after(gain_full, near[0], second_line) if layer == 0 else after(gain_full, near_pair[1]),
             first_full,
             second_full,
             bias_first,
@@ -1012,12 +1015,13 @@
         else:
             n2_parts = group_rows(n2)
         if layer == 0:
-            second_other = swap(after(second_line, n2), "dp", 1)
-            far.append(outward(crossed[0], n2))
+            second_line = line_gather(second_line, bits[1:])
+            second_other = swap(after(second_line, n2_parts[3]), "dp", 1)
+            far.append(outward(after(crossed[0], n2)))
             far_pair = swap(far[0], "dp", 1)
             near.append(line_gather(after(gate_shards[1], n2), bits[:-1], n2_parts[3]))
             crossed.append(cross_middle(near[1]))
-            attn_sets.append(attn_finish(second_line, second_other, n2_parts[3]))
+            attn_sets.append(attn_finish(attn_parts(second_line, second_other, n2_parts[3])))
             near_pair.append(swap(after(near[1], far_pair), "dp", 1))
         mlp_sets.append(mlp_finish(layer, far_pair))
         gu_near, *outs_near = feed_forward(n2_parts[:2], *mlp_sets[layer])
@@ -1064,15 +1068,14 @@
         state["terms"] = line_scatter(state["near_sum"], bits[:-1])
 
     def finish(states):
-        other_side = jnp.concatenate([state["attn_sums"][1] for state in states], axis=1)
-        other_side = swap(after(other_side, states[0]["near_got"]), "dp", 1)
-        own_side = jnp.concatenate([state["attn_sums"][0] for state in states], axis=1)
-        owned = sum(
-            term.astype(jnp.float32)
-            for term in line_scatter(
-                add_low(own_side, other_side), bits, states[0]["near_sum"]
-            )
-        ).reshape(LAYERS, chip_rows + 8, -1)
+        state = states[0]
+        other_side = swap(after(state["attn_sums"][1], state["near_got"]), "dp", 1)
+        state["owned"] = line_scatter(
+            add_low(state["attn_sums"][0], other_side), bits, state["near_sum"]
+        )
+        owned = jnp.stack(
+            [sum(term.astype(jnp.float32) for term in state["owned"]) for state in states]
+        )
         extra = owned[:, chip_rows:]
         halves = owned[:, :chip_rows].reshape(LAYERS, 2, width_rows, -1)
         mine = lax.dynamic_index_in_dim(halves, core, 1, keepdims=False)
@@ -1114,19 +1117,28 @@
             low_parts[0] = after(low_parts[0], *before["attn_parts"][2:])
             attn_sent = [send_attn(before, pair, low_parts[3]) for pair in range(2)]
             last_across = swap(after(across_sum, low_parts[3]), "seq", 2)
-        keep_near, keep_far, send_near, send_far, own_out, across_out, pair_out = feed_back(
+        apart = line == 4 and layer == 0
+        keep_near, send_near, own_out, across_out, pair_out, *far_parts = feed_back(
             low_parts,
             n2_parts,
             gu_parts,
             *mlp_sets[layer],
             dp_place,
             group_count,
+            2 if apart else 1,
         )
         if before is not None:
             pair_out = after(pair_out, last_across, *attn_sent, before["near_got"], before["inward"])
         got = swap(pair_out, "seq", 1)
         out_terms = [own_out, got[0], swap(add_low(across_out, got[1]), "seq", 2)]
-        got_far = swap(send_far, "dp", 1)
+        if apart:
+            keep_far, send_far = far_parts[:2], far_parts[2:]
+            got_far = [swap(after(send_far[0], got), "dp", 1), swap(send_far[1], "dp", 1)]
+            far_sums = [None, add_low(keep_far[1], after(got_far[1], out_terms[2]))]
+            inward = [None, line_steps(far_sums[1], [(0, 1), (3, 2)])]
+        else:
+            keep_far, send_far = far_parts
+            got_far = swap(send_far, "dp", 1)
         if before is not None:
             step_one(before, own_out)
             before["attn_sums"] = sum_attn(before, attn_sent, own_out)
@@ -1142,6 +1154,8 @@
             cos_wide,
             sin_wide,
         )
+        if apart:
+            kv_terms[0] = after(kv_terms[0], inward[1])
         kv_terms = [own_term] + [swap(kv_terms[bit - 1], "seq", bit) for bit in range(1, 4)]
         upstream, upstream_low, grad_kv, attn_gain_part, bias_first, bias_second = before_back(
             kv_terms,
@@ -1155,16 +1169,29 @@
             sin_wide,
         )
         near_got = swap(after(send_near, grad_low), "dp", 1)
-        far_sum = add_low(keep_far, after(got_far, upstream if before is None else grad_low))
-        state = {
-            "layer": layer,
-            "far_sum": far_sum,
-            "keep_near": keep_near,
-            "near_got": near_got,
-            "inward": line_steps(far_sum, [(0, 1), (3, 2)]) if line == 4 else far_sum,
-        }
+        if apart:
+            across_middle = [None, cross_middle(add_low(far_sums[1], after(inward[1], grad_low)))]
+            far_sums[0] = add_low(keep_far[0], after(got_far[0], grad_low))
+            inward[0] = after(line_steps(far_sums[0], [(0, 1), (3, 2)]), upstream)
+            across_middle[0] = cross_middle(add_low(far_sums[0], inward[0]))
+            near_one = add_low(add_low(keep_near[1], near_got[1]), across_middle[1][0])
+            near_zero = add_low(add_low(keep_near[0], near_got[0]), across_middle[0][0])
+            state = {"near_got": near_got, "near_sum": near_one}
+            state["terms"] = [near_zero, swap(near_one, "dp", 2)]
+            step_two(before, far_sums[0])
+        else:
+            far_sum = add_low(keep_far, after(got_far, upstream if before is None else grad_low))
+            state = {
+                "far_sum": far_sum,
+                "keep_near": keep_near,
+                "near_got": near_got,
+                "inward": line_steps(far_sum, [(0, 1), (3, 2)]) if line == 4 else far_sum,
+            }
+            if before is not None:
+                step_two(before, far_sum)
         if before is not None:
-            step_two(before, far_sum)
+            other_side = swap(after(before["attn_sums"][1], grad_low), "dp", 1)
+            attn_pair = add_low(before["attn_sums"][0], after(other_side, upstream))
         near_x, far_x, near_other, far_other = projection_grads(
             normed,
             grad_query,
@@ -1182,9 +1209,12 @@
         got_far_other = swap(far_other, "seq", 1)
         got_near_other = swap(near_other, "seq", 1)
         state["attn_parts"] = (near_x, far_x, got_near_other, got_far_other)
+        if before is not None:
+            before["owned"] = line_scatter(attn_pair, bits, got_far_other)
         states[layer] = before = state
-    step_one(before)
-    step_two(before)
+    if line != 4:
+        step_one(before)
+        step_two(before)
     arrived = [None, send_attn(before, 1)]
     arrived[0] = send_attn(before, 0)
     before["attn_sums"] = sum_attn(before, arrived)

time: 667 us -> 663 us (level)
  other arithmetic: 38.7 us -> 29.2 us
  waiting for transfers between devices: 277 us -> 286 us
    ppermute x84 -> x88, waiting for transfers between devices: 259 us -> 272 us  [swap(): return lax.ppermute(values, axis, [(i, i ^ bit) for i in range(size)])]
    ppermute x84 -> x88, starting transfers between devices: 62.6 us -> 73 us  [swap(): return lax.ppermute(values, axis, [(i, i ^ bit) for i in range(size)])]
    ppermute x8 -> x10, starting transfers between devices: 31.1 us -> 21 us  [line_steps(): lax.ppermute(values, 'dp', [(2 * here + side, 2 * there + side) for here,...]
    convert_element_type x14 -> x18, other arithmetic: 20.2 us -> 15.1 us  [add_low(): (left.astype(jnp.float32) + right.astype(jnp.float32)).astype(jnp.bfloat16)]
    ppermute x8 -> x10, waiting for transfers between devices: 17.2 us -> 13.7 us  [line_steps(): lax.ppermute(values, 'dp', [(2 * here + side, 2 * there + side) for here,...]
    unnamed x174 -> x212, local copies, waits for them, and re-layouts: 36.2 us -> 34 us
  transfers between devices with their start and end apart: 92 -> 98, of which waited for: 42 -> 40; matrix products, arithmetic and copies ran while one was open for 7% -> 6% of each run, Pallas kernels for 23% -> 23%
where the time goes in v5:
time: 663 us; the launch traced here: 656 us
  waiting for transfers between devices  286 us (43%)
  Pallas kernels  184 us (28%)
  starting transfers between devices  93.9 us (14%)
  local copies, waits for them, and re-layouts  46.9 us (7%)
  other arithmetic  29.2 us (4%)
  between operations  15.7 us (2%)
    ppermute x88, waiting for transfers between devices, swap(): return lax.ppermute(values, axis, [(i, i ^ bit) for i in range(size)])  272 us
    ppermute x88, starting transfers between devices, swap(): return lax.ppermute(values, axis, [(i, i ^ bit) for i in range(size)])  73 us
    pallas_call x2, Pallas kernels, feed_back(): call(kernel, [((half, packed, 2 * units), jnp.bfloat16), ((half, packed,...  65.6 us
    pallas_call x4, Pallas kernels, feed_forward(): call(kernel, [((rows, 2 * units), jnp.bfloat16)] + [((part_rows, D), jnp....  41 us
    unnamed x212, local copies, waits for them, and re-layouts  34 us
    pallas_call x2, Pallas kernels, attention_back(): call(kernel, [((rows, D), jnp.float32), ((rows, D), jnp.bfloat16), ((1, D...  25.1 us
    pallas_call x2, Pallas kernels, attention(): call(kernel, [((rows, D), jnp.bfloat16), ((rows, D), jnp.float32), ((rows...  21.4 us
    ppermute x10, starting transfers between devices, line_steps(): lax.ppermute(values, 'dp', [(2 * here + side, 2 * there + side) for here,...  21 us
  transfers between devices with their start and end apart: 98, of which 40 were waited for; matrix products, arithmetic and copies ran while one was open for 6% of the time, Pallas kernels for 23%

profile of v5, /device:TPU:0, one launch (start us, length us, event | category | flops | bytes accessed | tf_op | source)
XLA Modules:
  0.0 655.9 jit_solution(221663209439097937)
XLA Ops:
  7.3 2.9 collective-permute-start.1
  14.3 2.8 collective-permute-start.2
  17.2 3.4 collective-permute-done.4.refs_2_
  20.5 5.5 collective-permute-done.5.refs_3_
  32.7 9.3 %collective-permute-done.6.refs_1_ = bf16[4,64,1024]{2,1,0:T(8,128)(2,1)S(1)} collective-permute-done((bf16[4,64,1024]{2,1,0:T(8,128)(2,1)S(1)}, bf16[4,64,1024]{2,1,0:T(8,128)(2,1)S(1)}, u32[]{:S(2)}, u32[]{:S(2)}) %collective-permute-start.6) | collective-permute-done | bytes 524320 | tf_op jit(solution)/shard_map/ppermute | solution.py:822
  55.6 2.8 collective-permute-done.8.refs_3_
  58.4 2.8 collective-permute-done.13
  77.9 3.2 assemble.2
  81.2 2.9 collective-permute-start.15
  84.1 4.1 collective-permute-done.15
  96.3 5.0 collective-permute-done.19.refs_2_
  105.6 11.5 %attention.2 = (bf16[256,896]{1,0:T(8,128)(2,1)S(1)}, f32[256,896]{1,0:T(8,128)S(1)}, bf16[256,896]{1,0:T(8,128)(2,1)}) custom-call(bf16[2,2,896,64]{3,2,1,0:T(8,128)(2,1)S(1)} %get-tuple-element.276.q_ref.refs_7_, bf16[256,256]{1,0:T(8,128)(2,1)} %get-tuple-element.277.kv0.refs_8_, bf16[256,256]{1,0:T(8,128)(2,1)S(1)} %copy-done.40, ...), custom_call_target="tpu_custom_call" | custom-call | bytes 42000 | tf_op jit(solution)/shard_map/attention/pallas_call | solution.py:159
  121.9 5.3 collective-permute-start.26
  127.2 4.5 collective-permute-done.25.refs_0_.refs_7_
  133.9 41.3 %collective-permute-done.26 = bf16[1,168,2432]{2,1,0:T(8,128)(2,1)} collective-permute-done((bf16[1,168,2432]{2,1,0:T(8,128)(2,1)}, bf16[1,168,2432]{2,1,0:T(8,128)(2,1)}, u32[]{:S(2)}, u32[]{:S(2)}) %collective-permute-start.26) | collective-permute-done | bytes 817184 | tf_op jit(solution)/shard_map/ppermute | solution.py:822
  184.4 43.4 %collective-permute-done.31 = bf16[2,64,1024]{2,1,0:T(8,128)(2,1)S(1)} collective-permute-done((bf16[2,64,1024]{2,1,0:T(8,128)(2,1)S(1)}, bf16[2,64,1024]{2,1,0:T(8,128)(2,1)S(1)}, u32[]{:S(2)}, u32[]{:S(2)}) %collective-permute-start.31) | collective-permute-done | bytes 262176 | tf_op jit(solution)/shard_map/ppermute | solution.py:822
  232.2 2.9 unpack.2
  238.4 10.2 %feed_forward.4 = (bf16[512,2432]{1,0:T(8,128)(2,1)}, bf16[256,896]{1,0:T(8,128)(2,1)}, bf16[256,896]{1,0:T(8,128)(2,1)}) custom-call(bf16[256,896]{1,0:T(8,128)(2,1)} %get-tuple-element.282.refs_0_.refs_5_, bf16[256,896]{1,0:T(8,128)(2,1)} %collective-permute-done.20.refs_1_.refs_6_, bf16[896,2432]{1,0:T(8,128)(2,1)} %bitcast.146, bf16[1216,896]{1,0:T(8,128)(2,1)} %bitcast.160), custom_call_target="tpu_custom_call" | custom-call | bytes 36000 | tf_op jit(solution)/shard_map/feed_forward/pallas_call | solution.py:204
  250.6 10.4 %feed_forward.5 = (bf16[512,2432]{1,0:T(8,128)(2,1)}, bf16[256,896]{1,0:T(8,128)(2,1)}, bf16[256,896]{1,0:T(8,128)(2,1)}) custom-call(bf16[256,896]{1,0:T(8,128)(2,1)} %copy-done.70, bf16[256,896]{1,0:T(8,128)(2,1)} %copy-done.71, bf16[896,2432]{1,0:T(8,128)(2,1)} %bitcast.147, bf16[1216,896]{1,0:T(8,128)(2,1)} %bitcast.161), custom_call_target="tpu_custom_call" | custom-call | bytes 36000 | tf_op jit(solution)/shard_map/feed_forward/pallas_call | solution.py:204
  268.0 3.0 assemble.3
  271.0 7.3 %collective-permute-done.39.refs_2_ = bf16[2,168,2432]{2,1,0:T(8,128)(2,1)} collective-permute-done((bf16[2,168,2432]{2,1,0:T(8,128)(2,1)}, bf16[2,168,2432]{2,1,0:T(8,128)(2,1)}, u32[]{:S(2)}, u32[]{:S(2)}) %collective-permute-start.39) | collective-permute-done | bytes 1634336 | tf_op jit(solution)/shard_map/ppermute | solution.py:822
  281.7 6.5 collective-permute-done.44
  292.3 4.4 collective-permute-done.41.kv2.refs_10_
  298.8 9.9 %attention.3 = (bf16[256,896]{1,0:T(8,128)(2,1)S(1)}, f32[256,896]{1,0:T(8,128)S(1)}, bf16[256,896]{1,0:T(8,128)(2,1)S(1)}) custom-call(bf16[2,2,896,64]{3,2,1,0:T(8,128)(2,1)S(1)} %get-tuple-element.305.q_ref.refs_7_, bf16[256,256]{1,0:T(8,128)(2,1)S(1)} %get-tuple-element.306.kv0.refs_8_, bf16[256,256]{1,0:T(8,128)(2,1)S(1)} %collective-permute-done.40.kv1.refs_9_, ...), custom_call_target="tpu_custom_call" | custom-call | bytes 42000 | tf_op jit(solution)/shard_map/attention/pallas_call | solution.py:159
  310.9 12.4 %collective-permute-done.47.refs_0_.refs_7_ = bf16[256,896]{1,0:T(8,128)(2,1)S(1)} collective-permute-done((bf16[256,896]{1,0:T(8,128)(2,1)S(1)}, bf16[256,896]{1,0:T(8,128)(2,1)S(1)}, u32[]{:S(2)}, u32[]{:S(2)}) %collective-permute-start.47) | collective-permute-done | bytes 458784 | tf_op jit(solution)/shard_map/ppermute | solution.py:822
  323.3 3.0 collective-permute-done.45.refs_3_
  329.5 2.9 unpack.3
  336.5 10.2 %feed_forward.6 = (bf16[512,2432]{1,0:T(8,128)(2,1)}, bf16[256,896]{1,0:T(8,128)(2,1)}, bf16[256,896]{1,0:T(8,128)(2,1)}) custom-call(bf16[256,896]{1,0:T(8,128)(2,1)} %copy-done.31, bf16[256,896]{1,0:T(8,128)(2,1)} %copy-done.74, bf16[896,2432]{1,0:T(8,128)(2,1)} %bitcast.149, bf16[1216,896]{1,0:T(8,128)(2,1)} %bitcast.163), custom_call_target="tpu_custom_call" | custom-call | bytes 36000 | tf_op jit(solution)/shard_map/feed_forward/pallas_call | solution.py:204
  347.2 10.2 %feed_forward.7 = (bf16[512,2432]{1,0:T(8,128)(2,1)}, bf16[256,896]{1,0:T(8,128)(2,1)}, bf16[256,896]{1,0:T(8,128)(2,1)}) custom-call(bf16[256,896]{1,0:T(8,128)(2,1)} %copy-done.72, bf16[256,896]{1,0:T(8,128)(2,1)} %copy-done.73, bf16[896,2432]{1,0:T(8,128)(2,1)} %bitcast.150, bf16[1216,896]{1,0:T(8,128)(2,1)} %bitcast.164), custom_call_target="tpu_custom_call" | custom-call | bytes 36000 | tf_op jit(solution)/shard_map/feed_forward/pallas_call | solution.py:204
  358.2 33.0 %feed_back.2 = (bf16[2,168,2432]{2,1,0:T(8,128)(2,1)}, bf16[2,168,2432]{2,1,0:T(8,128)(2,1)}, bf16[256,896]{1,0:T(8,128)(2,1)}, bf16[256,896]{1,0:T(8,128)(2,1)}...) custom-call(s32[1]{0:T(128)} %bitcast.3.refs_0_, ...), custom_call_target="tpu_custom_call" | custom-call | bytes 100000 | tf_op jit(solution)/shard_map/feed_back/pallas_call | solution.py:324
  396.6 11.1 %collective-permute-done.54.refs_5_ = bf16[256,896]{1,0:T(8,128)(2,1)S(1)} collective-permute-done((bf16[256,896]{1,0:T(8,128)(2,1)S(1)}, bf16[256,896]{1,0:T(8,128)(2,1)S(1)}, u32[]{:S(2)}, u32[]{:S(2)}) %collective-permute-start.54) | collective-permute-done | bytes 458784 | tf_op jit(solution)/shard_map/ppermute | solution.py:822
  411.1 12.1 %attention_back.2 = (f32[256,896]{1,0:T(8,128)S(1)}, bf16[256,896]{1,0:T(8,128)(2,1)S(1)}, f32[1,896]{1,0:T(1,128)S(1)}, bf16[256,896]{1,0:T(8,128)(2,1)S(1)}, f...) custom-call(bf16[256,896]{1,0:T(8,128)(2,1)S(1)} %bitcast.173, ...), custom_call_target="tpu_custom_call" | custom-call | bytes 52000 | tf_op jit(solution)/shard_map/attention_back/pallas_call | solution.py:465
  425.5 4.5 collective-permute-done.56.refs_2_
  438.4 8.5 %collective-permute-done.58.refs_3_ = bf16[256,896]{1,0:T(8,128)(2,1)S(1)} collective-permute-done((bf16[256,896]{1,0:T(8,128)(2,1)S(1)}, bf16[256,896]{1,0:T(8,128)(2,1)S(1)}, u32[]{:S(2)}, u32[]{:S(2)}) %collective-permute-start.58) | collective-permute-done | bytes 458784 | tf_op jit(solution)/shard_map/ppermute | solution.py:822
  458.3 32.6 %feed_back.3 = (bf16[2,168,2432]{2,1,0:T(8,128)(2,1)}, bf16[2,168,2432]{2,1,0:T(8,128)(2,1)}, bf16[256,896]{1,0:T(8,128)(2,1)}, bf16[256,896]{1,0:T(8,128)(2,1)}...) custom-call(s32[1]{0:T(128)} %bitcast.3.refs_0_, ...), custom_call_target="tpu_custom_call" | custom-call | bytes 100000 | tf_op jit(solution)/shard_map/feed_back/pallas_call | solution.py:324
  499.9 12.5 %collective-permute-done.71 = bf16[1,168,2432]{2,1,0:T(8,128)(2,1)S(1)} collective-permute-done((bf16[1,168,2432]{2,1,0:T(8,128)(2,1)}, bf16[1,168,2432]{2,1,0:T(8,128)(2,1)S(1)}, u32[]{:S(2)}, u32[]{:S(2)}) %collective-permute-start.71) | collective-permute-done | bytes 817184 | tf_op jit(solution)/shard_map/ppermute | solution.py:822
  515.4 13.1 %attention_back.3 = (f32[256,896]{1,0:T(8,128)S(1)}, bf16[256,896]{1,0:T(8,128)(2,1)S(1)}, f32[1,896]{1,0:T(1,128)S(1)}, bf16[256,896]{1,0:T(8,128)(2,1)S(1)}, f...) custom-call(f32[256,896]{1,0:T(8,128)S(1)} %copy-done.37, ...), custom_call_target="tpu_custom_call" | custom-call | bytes 52000 | tf_op jit(solution)/shard_map/attention_back/pallas_call | solution.py:465
  530.2 7.9 %collective-permute-start.90 = (bf16[1,168,2432]{2,1,0:T(8,128)(2,1)S(1)}, bf16[1,168,2432]{2,1,0:T(8,128)(2,1)S(1)}, u32[]{:S(2)}, u32[]{:S(2)}) collective-permute-start(bf16[1,168,2432]{2,1,0:T(8,128)(2,1)S(1)} %add_convert_fusion.7), channel_id=1, source_target_pairs={{0,8},{4,12},{24,16},{28,20},{1,9},{5,13},{25,17},{29,21},{2,10},{... | collective-permute-start | bytes 2451464 | tf_op jit(solution)/shard_map/ppermute | solution.py:843
  547.3 7.2 %collective-permute-done.90 = bf16[1,168,2432]{2,1,0:T(8,128)(2,1)S(1)} collective-permute-done((bf16[1,168,2432]{2,1,0:T(8,128)(2,1)S(1)}, bf16[1,168,2432]{2,1,0:T(8,128)(2,1)S(1)}, u32[]{:S(2)}, u32[]{:S(2)}) %collective-permute-start.90) | collective-permute-done | bytes 817184 | tf_op jit(solution)/shard_map/ppermute | solution.py:843
  559.1 11.2 %collective-permute-done.79 = bf16[4,64,1024]{2,1,0:T(8,128)(2,1)S(1)} collective-permute-done((bf16[4,64,1024]{2,1,0:T(8,128)(2,1)S(1)}, bf16[4,64,1024]{2,1,0:T(8,128)(2,1)S(1)}, u32[]{:S(2)}, u32[]{:S(2)}) %collective-permute-start.79) | collective-permute-done | bytes 524320 | tf_op jit(solution)/shard_map/ppermute | solution.py:822
  570.4 5.2 collective-permute-start.94
  575.8 3.4 collective-permute-done.80
  582.0 17.2 %collective-permute-done.86 = bf16[2,64,1024]{2,1,0:T(8,128)(2,1)S(1)} collective-permute-done((bf16[2,64,1024]{2,1,0:T(8,128)(2,1)S(1)}, bf16[2,64,1024]{2,1,0:T(8,128)(2,1)S(1)}, u32[]{:S(2)}, u32[]{:S(2)}) %collective-permute-start.86) | collective-permute-done | bytes 262176 | tf_op jit(solution)/shard_map/ppermute | solution.py:822
  602.1 3.2 collective-permute-start.82
  607.3 20.5 %collective-permute-done.87 = bf16[64,1024]{1,0:T(8,128)(2,1)S(1)} collective-permute-done((bf16[64,1024]{1,0:T(8,128)(2,1)S(1)}, bf16[64,1024]{1,0:T(8,128)(2,1)S(1)}, u32[]{:S(2)}, u32[]{:S(2)}) %collective-permute-start.87) | collective-permute-done | bytes 131104 | tf_op jit(solution)/shard_map/ppermute | solution.py:822
  631.9 8.1 %collective-permute-done.96.refs_2_ = bf16[2,28,2432]{2,1,0:T(8,128)(2,1)S(1)} collective-permute-done((bf16[2,28,2432]{2,1,0:T(8,128)(2,1)S(1)}, bf16[2,28,2432]{2,1,0:T(8,128)(2,1)S(1)}, u32[]{:S(2)}, u32[]{:S(2)}) %collective-permute-start.96) | collective-permute-done | bytes 272416 | tf_op jit(solution)/shard_map/ppermute | solution.py:822
  640.0 5.9 collective-permute-done.97.refs_3_
  647.9 3.0 copy.58
  (502 shorter events, 176.2 us)
Async XLA Ops:
  11.8 14.2 %collective-permute-start.5 = (bf16[2,28,2432]{2,1,0:T(8,128)(2,1)S(1)}, bf16[2,28,2432]{2,1,0:T(8,128)(2,1)S(1)}, u32[]{:S(2)}, u32[]{:S(2)}) collective-permute-start(bf16[2,28,2432]{2,1,0:T(8,128)(2,1)S(1)} %get-tuple-element.260), channel_id=1, source_target_pairs={{0,3},{1,2},{2,1},{3,0},{4,7},{5,6},{6,5},{7,4},{8,11},{9,10},{10,... | collective-permute-start | bytes 817160 | tf_op jit(solution)/shard_map/ppermute | solution.py:822
  14.3 14.7 %collective-permute-start.2 = (bf16[2,64,1024]{2,1,0:T(8,128)(2,1)S(1)}, bf16[2,64,1024]{2,1,0:T(8,128)(2,1)S(1)}, u32[]{:S(2)}, u32[]{:S(2)}) collective-permute-start(bf16[2,64,1024]{2,1,0:T(8,128)(2,1)S(1)} %pad_maximum_fusion.6), channel_id=1, source_target_pairs={{0,16},{4,20},{8,24},{12,28},{16,0},{20,4},{24,8},{28,12},{1,17},{... | collective-permute-start | bytes 786440 | tf_op jit(solution)/shard_map/ppermute | solution.py:822
  30.6 37.6 %collective-permute-start.14 = (bf16[28,1024]{1,0:T(8,128)(2,1)S(1)}, bf16[28,1024]{1,0:T(8,128)(2,1)S(1)}, u32[]{:S(2)}, u32[]{:S(2)}) collective-permute-start(bf16[28,1024]{1,0:T(8,128)(2,1)S(1)} %get-tuple-element.453), channel_id=1, source_target_pairs={{0,1},{1,0},{2,3},{3,2},{4,5},{5,4},{6,7},{7,6},{8,9},{9,8},{10,11... | collective-permute-start | bytes 172040 | tf_op jit(solution)/shard_map/ppermute | solution.py:822
  42.0 19.2 %collective-permute-start.13 = (bf16[1,168,2432]{2,1,0:T(8,128)(2,1)S(1)}, bf16[1,168,2432]{2,1,0:T(8,128)(2,1)}, u32[]{:S(2)}, u32[]{:S(2)}) collective-permute-start(bf16[1,168,2432]{2,1,0:T(8,128)(2,1)S(1)} %get-tuple-element.270), channel_id=1, source_target_pairs={{0,8},{4,12},{8,0},{12,4},{16,24},{20,28},{24,16},{28,20},{1,9},{5... | collective-permute-start | bytes 2451464 | tf_op jit(solution)/shard_map/ppermute | solution.py:822
  44.1 14.3 %collective-permute-start.8 = (bf16[4,64,1024]{2,1,0:T(8,128)(2,1)S(1)}, bf16[4,64,1024]{2,1,0:T(8,128)(2,1)S(1)}, u32[]{:S(2)}, u32[]{:S(2)}) collective-permute-start(bf16[4,64,1024]{2,1,0:T(8,128)(2,1)S(1)} %collective-permute-done.6.refs_1_), channel_id=1, source_target_pairs={{0,2},{1,3},{2,0},{3,1},{4,6},{5,7},{6,4},{7,5},{8,10},{9,11},{10,... | collective-permute-start | bytes 1572872 | tf_op jit(solution)/shard_map/ppermute | solution.py:822
  54.1 14.2 %collective-permute-start.7 = (bf16[4,64,1024]{2,1,0:T(8,128)(2,1)S(1)}, bf16[4,64,1024]{2,1,0:T(8,128)(2,1)}, u32[]{:S(2)}, u32[]{:S(2)}) collective-permute-start(bf16[4,64,1024]{2,1,0:T(8,128)(2,1)S(1)} %pad_maximum_fusion.refs_0_), channel_id=1, source_target_pairs={{0,2},{1,3},{2,0},{3,1},{4,6},{5,7},{6,4},{7,5},{8,10},{9,11},{10,... | collective-permute-start | bytes 1572872 | tf_op jit(solution)/shard_map/ppermute | solution.py:822
  63.3 55.5 %collective-permute-start.21 = (bf16[2,168,2432]{2,1,0:T(8,128)(2,1)}, bf16[2,168,2432]{2,1,0:T(8,128)(2,1)}, u32[]{:S(2)}, u32[]{:S(2)}) collective-permute-start(bf16[2,168,2432]{2,1,0:T(8,128)(2,1)} %constant_dynamic-update-slice_fusion.refs_0_), channel_id=1, source_target_pairs={{8,16},{12,20},{16,8},{20,12},{9,17},{13,21},{17,9},{21,13},{10,18... | collective-permute-start | bytes 4902920 | tf_op jit(solution)/shard_map/ppermute | solution.py:843
  65.2 36.0 %collective-permute-start.19 = (bf16[2,168,2432]{2,1,0:T(8,128)(2,1)}, bf16[2,168,2432]{2,1,0:T(8,128)(2,1)}, u32[]{:S(2)}, u32[]{:S(2)}) collective-permute-start(bf16[2,168,2432]{2,1,0:T(8,128)(2,1)} %constant_dynamic-update-slice_fusion.refs_0_), channel_id=1, source_target_pairs={{0,4},{4,0},{8,12},{12,8},{16,20},{20,16},{24,28},{28,24},{1,5},{5... | collective-permute-start | bytes 4902920 | tf_op jit(solution)/shard_map/ppermute | solution.py:822
  118.8 57.2 %collective-permute-start.22 = (bf16[2,168,2432]{2,1,0:T(8,128)(2,1)}, bf16[2,168,2432]{2,1,0:T(8,128)(2,1)}, u32[]{:S(2)}, u32[]{:S(2)}) collective-permute-start(bf16[2,168,2432]{2,1,0:T(8,128)(2,1)} %collective-permute-done.21), channel_id=1, source_target_pairs={{8,0},{12,4},{16,24},{20,28},{9,1},{13,5},{17,25},{21,29},{10,2},{... | collective-permute-start | bytes 4902920 | tf_op jit(solution)/shard_map/ppermute | solution.py:843
  121.9 53.4 %collective-permute-start.26 = (bf16[1,168,2432]{2,1,0:T(8,128)(2,1)}, bf16[1,168,2432]{2,1,0:T(8,128)(2,1)}, u32[]{:S(2)}, u32[]{:S(2)}) collective-permute-start(bf16[1,168,2432]{2,1,0:T(8,128)(2,1)} %get-tuple-element.288), channel_id=1, source_target_pairs={{0,8},{4,12},{8,0},{12,4},{16,24},{20,28},{24,16},{28,20},{1,9},{5... | collective-permute-start | bytes 2451464 | tf_op jit(solution)/shard_map/ppermute | solution.py:822
  131.7 43.6 %collective-permute-start.27 = (bf16[256,896]{1,0:T(8,128)(2,1)S(1)}, bf16[256,896]{1,0:T(8,128)(2,1)S(1)}, u32[]{:S(2)}, u32[]{:S(2)}) collective-permute-start(bf16[256,896]{1,0:T(8,128)(2,1)S(1)} %collective-permute-done.25.refs_0_.refs_7_), channel_id=1, source_target_pairs={{0,1},{1,0},{2,3},{3,2},{4,5},{5,4},{6,7},{7,6},{8,9},{9,8},{10,11... | collective-permute-start | bytes 1376264 | tf_op jit(solution)/shard_map/ppermute | solution.py:822
  177.7 52.9 %collective-permute-start.23 = (bf16[2,168,2432]{2,1,0:T(8,128)(2,1)S(1)}, bf16[2,168,2432]{2,1,0:T(8,128)(2,1)}, u32[]{:S(2)}, u32[]{:S(2)}) collective-permute-start(bf16[2,168,2432]{2,1,0:T(8,128)(2,1)S(1)} %broadcast_select_fusion.1.refs_1_), channel_id=1, source_target_pairs={{0,4},{4,0},{8,12},{12,8},{16,20},{20,16},{24,28},{28,24},{1,5},{5... | collective-permute-start | bytes 4902920 | tf_op jit(solution)/shard_map/ppermute | solution.py:822
  181.4 67.3 %collective-permute-start.28 = (bf16[2,168,2432]{2,1,0:T(8,128)(2,1)}, bf16[2,168,2432]{2,1,0:T(8,128)(2,1)}, u32[]{:S(2)}, u32[]{:S(2)}) collective-permute-start(bf16[2,168,2432]{2,1,0:T(8,128)(2,1)} %constant_dynamic-update-slice_fusion.2.refs_0_), channel_id=1, source_target_pairs={{8,16},{12,20},{16,8},{20,12},{9,17},{13,21},{17,9},{21,13},{10,18... | collective-permute-start | bytes 4902920 | tf_op jit(solution)/shard_map/ppermute | solution.py:843
  183.3 44.5 %collective-permute-start.31 = (bf16[2,64,1024]{2,1,0:T(8,128)(2,1)S(1)}, bf16[2,64,1024]{2,1,0:T(8,128)(2,1)S(1)}, u32[]{:S(2)}, u32[]{:S(2)}) collective-permute-start(bf16[2,64,1024]{2,1,0:T(8,128)(2,1)S(1)} %copy-done.94), channel_id=1, source_target_pairs={{0,16},{4,20},{8,24},{12,28},{16,0},{20,4},{24,8},{28,12},{1,17},{... | collective-permute-start | bytes 786440 | tf_op jit(solution)/shard_map/ppermute | solution.py:822
  228.6 21.3 %collective-permute-start.32 = (bf16[4,64,1024]{2,1,0:T(8,128)(2,1)}, bf16[4,64,1024]{2,1,0:T(8,128)(2,1)}, u32[]{:S(2)}, u32[]{:S(2)}) collective-permute-start(bf16[4,64,1024]{2,1,0:T(8,128)(2,1)} %pad_maximum_fusion.2.refs_0_), channel_id=1, source_target_pairs={{0,4},{4,0},{8,12},{12,8},{16,20},{20,16},{24,28},{28,24},{1,5},{5... | collective-permute-start | bytes 1572872 | tf_op jit(solution)/shard_map/ppermute | solution.py:822
  229.1 32.0 %collective-permute-start.33 = (bf16[4,64,1024]{2,1,0:T(8,128)(2,1)}, bf16[4,64,1024]{2,1,0:T(8,128)(2,1)}, u32[]{:S(2)}, u32[]{:S(2)}) collective-permute-start(bf16[4,64,1024]{2,1,0:T(8,128)(2,1)} %pad_maximum_fusion.2.refs_0_), channel_id=1, source_target_pairs={{0,2},{1,3},{2,0},{3,1},{4,6},{5,7},{6,4},{7,5},{8,10},{9,11},{10,... | collective-permute-start | bytes 1572872 | tf_op jit(solution)/shard_map/ppermute | solution.py:822
  230.5 47.7 %collective-permute-start.39 = (bf16[2,168,2432]{2,1,0:T(8,128)(2,1)}, bf16[2,168,2432]{2,1,0:T(8,128)(2,1)}, u32[]{:S(2)}, u32[]{:S(2)}) collective-permute-start(bf16[2,168,2432]{2,1,0:T(8,128)(2,1)} %constant_dynamic-update-slice_fusion.2.refs_0_), channel_id=1, source_target_pairs={{0,4},{4,0},{8,12},{12,8},{16,20},{20,16},{24,28},{28,24},{1,5},{5... | collective-permute-start | bytes 4902920 | tf_op jit(solution)/shard_map/ppermute | solution.py:822
  248.6 39.5 %collective-permute-start.44 = (bf16[2,168,2432]{2,1,0:T(8,128)(2,1)}, bf16[2,168,2432]{2,1,0:T(8,128)(2,1)}, u32[]{:S(2)}, u32[]{:S(2)}) collective-permute-start(bf16[2,168,2432]{2,1,0:T(8,128)(2,1)} %collective-permute-done.28), channel_id=1, source_target_pairs={{8,0},{12,4},{16,24},{20,28},{9,1},{13,5},{17,25},{21,29},{10,2},{... | collective-permute-start | bytes 4902920 | tf_op jit(solution)/shard_map/ppermute | solution.py:843
  289.8 36.4 %collective-permute-start.45 = (bf16[2,168,2432]{2,1,0:T(8,128)(2,1)S(1)}, bf16[2,168,2432]{2,1,0:T(8,128)(2,1)S(1)}, u32[]{:S(2)}, u32[]{:S(2)}) collective-permute-start(bf16[2,168,2432]{2,1,0:T(8,128)(2,1)S(1)} %broadcast_select_fusion.refs_1_), channel_id=1, source_target_pairs={{0,4},{4,0},{8,12},{12,8},{16,20},{20,16},{24,28},{28,24},{1,5},{5... | collective-permute-start | bytes 4902920 | tf_op jit(solution)/shard_map/ppermute | solution.py:822
  328.9 17.9 %collective-permute-start.51 = (bf16[256,896]{1,0:T(8,128)(2,1)S(1)}, bf16[256,896]{1,0:T(8,128)(2,1)}, u32[]{:S(2)}, u32[]{:S(2)}) collective-permute-start(bf16[256,896]{1,0:T(8,128)(2,1)S(1)} %bitcast.171), channel_id=1, source_target_pairs={{0,2},{1,3},{2,0},{3,1},{4,6},{5,7},{6,4},{7,5},{8,10},{9,11},{10,... | collective-permute-start | bytes 1376264 | tf_op jit(solution)/shard_map/ppermute | solution.py:822
  391.3 47.1 %collective-permute-start.67 = (bf16[2,168,2432]{2,1,0:T(8,128)(2,1)}, bf16[2,168,2432]{2,1,0:T(8,128)(2,1)S(1)}, u32[]{:S(2)}, u32[]{:S(2)}) collective-permute-start(bf16[2,168,2432]{2,1,0:T(8,128)(2,1)} %get-tuple-element.355), channel_id=1, source_target_pairs={{0,4},{4,0},{8,12},{12,8},{16,20},{20,16},{24,28},{28,24},{1,5},{5... | collective-permute-start | bytes 4902920 | tf_op jit(solution)/shard_map/ppermute | solution.py:822
  435.7 55.3 %collective-permute-start.66 = (bf16[2,168,2432]{2,1,0:T(8,128)(2,1)}, bf16[2,168,2432]{2,1,0:T(8,128)(2,1)}, u32[]{:S(2)}, u32[]{:S(2)}) collective-permute-start(bf16[2,168,2432]{2,1,0:T(8,128)(2,1)} %get-tuple-element.353), channel_id=1, source_target_pairs={{0,4},{4,0},{8,12},{12,8},{16,20},{20,16},{24,28},{28,24},{1,5},{5... | collective-permute-start | bytes 4902920 | tf_op jit(solution)/shard_map/ppermute | solution.py:822
  448.6 42.4 %collective-permute-start.68 = (bf16[2,168,2432]{2,1,0:T(8,128)(2,1)}, bf16[2,168,2432]{2,1,0:T(8,128)(2,1)}, u32[]{:S(2)}, u32[]{:S(2)}) collective-permute-start(bf16[2,168,2432]{2,1,0:T(8,128)(2,1)} %add_convert_fusion.3), channel_id=1, source_target_pairs={{0,8},{4,12},{24,16},{28,20},{1,9},{5,13},{25,17},{29,21},{2,10},{... | collective-permute-start | bytes 4902920 | tf_op jit(solution)/shard_map/ppermute | solution.py:843
  454.7 36.3 %collective-permute-start.64 = (bf16[4,64,1024]{2,1,0:T(8,128)(2,1)}, bf16[4,64,1024]{2,1,0:T(8,128)(2,1)}, u32[]{:S(2)}, u32[]{:S(2)}) collective-permute-start(bf16[4,64,1024]{2,1,0:T(8,128)(2,1)} %get-tuple-element.350), channel_id=1, source_target_pairs={{0,2},{1,3},{2,0},{3,1},{4,6},{5,7},{6,4},{7,5},{8,10},{9,11},{10,... | collective-permute-start | bytes 1572872 | tf_op jit(solution)/shard_map/ppermute | solution.py:822
  456.1 34.9 %collective-permute-start.65 = (bf16[4,64,1024]{2,1,0:T(8,128)(2,1)}, bf16[4,64,1024]{2,1,0:T(8,128)(2,1)}, u32[]{:S(2)}, u32[]{:S(2)}) collective-permute-start(bf16[4,64,1024]{2,1,0:T(8,128)(2,1)} %get-tuple-element.351), channel_id=1, source_target_pairs={{0,2},{1,3},{2,0},{3,1},{4,6},{5,7},{6,4},{7,5},{8,10},{9,11},{10,... | collective-permute-start | bytes 1572872 | tf_op jit(solution)/shard_map/ppermute | solution.py:822
  456.9 34.1 %collective-permute-start.60 = (bf16[256,896]{1,0:T(8,128)(2,1)S(1)}, bf16[256,896]{1,0:T(8,128)(2,1)}, u32[]{:S(2)}, u32[]{:S(2)}) collective-permute-start(bf16[256,896]{1,0:T(8,128)(2,1)S(1)} %add_convert_fusion.19), channel_id=1, source_target_pairs={{0,2},{1,3},{2,0},{3,1},{4,6},{5,7},{6,4},{7,5},{8,10},{9,11},{10,... | collective-permute-start | bytes 1376264 | tf_op jit(solution)/shard_map/ppermute | solution.py:822
  491.1 21.3 %collective-permute-start.71 = (bf16[1,168,2432]{2,1,0:T(8,128)(2,1)}, bf16[1,168,2432]{2,1,0:T(8,128)(2,1)S(1)}, u32[]{:S(2)}, u32[]{:S(2)}) collective-permute-start(bf16[1,168,2432]{2,1,0:T(8,128)(2,1)} %get-tuple-element.362), channel_id=1, source_target_pairs={{0,4},{4,0},{8,12},{12,8},{16,20},{20,16},{24,28},{28,24},{1,5},{5... | collective-permute-start | bytes 2451464 | tf_op jit(solution)/shard_map/ppermute | solution.py:822
  495.1 17.3 %collective-permute-start.70 = (bf16[256,896]{1,0:T(8,128)(2,1)S(1)}, bf16[256,896]{1,0:T(8,128)(2,1)S(1)}, u32[]{:S(2)}, u32[]{:S(2)}) collective-permute-start(bf16[256,896]{1,0:T(8,128)(2,1)S(1)} %fusion.4), channel_id=1, source_target_pairs={{0,2},{1,3},{2,0},{3,1},{4,6},{5,7},{6,4},{7,5},{8,10},{9,11},{10,... | collective-permute-start | bytes 1376264 | tf_op jit(solution)/shard_map/ppermute | solution.py:822
  498.1 32.1 %collective-permute-start.93 = (bf16[2,168,2432]{2,1,0:T(8,128)(2,1)S(1)}, bf16[2,168,2432]{2,1,0:T(8,128)(2,1)S(1)}, u32[]{:S(2)}, u32[]{:S(2)}) collective-permute-start(bf16[2,168,2432]{2,1,0:T(8,128)(2,1)S(1)} %add_convert_fusion.1), channel_id=1, source_target_pairs={{8,16},{12,20},{16,8},{20,12},{9,17},{13,21},{17,9},{21,13},{10,18... | collective-permute-start | bytes 4902920 | tf_op jit(solution)/shard_map/ppermute | solution.py:843
  498.9 30.6 %collective-permute-start.89 = (bf16[1,168,2432]{2,1,0:T(8,128)(2,1)S(1)}, bf16[1,168,2432]{2,1,0:T(8,128)(2,1)S(1)}, u32[]{:S(2)}, u32[]{:S(2)}) collective-permute-start(bf16[1,168,2432]{2,1,0:T(8,128)(2,1)S(1)} %copy-done.100), channel_id=1, source_target_pairs={{0,4},{4,0},{8,12},{12,8},{16,20},{20,16},{24,28},{28,24},{1,5},{5... | collective-permute-start | bytes 2451464 | tf_op jit(solution)/shard_map/ppermute | solution.py:822
  512.7 25.5 %collective-permute-start.72 = (bf16[1,168,2432]{2,1,0:T(8,128)(2,1)S(1)}, bf16[1,168,2432]{2,1,0:T(8,128)(2,1)S(1)}, u32[]{:S(2)}, u32[]{:S(2)}) collective-permute-start(bf16[1,168,2432]{2,1,0:T(8,128)(2,1)S(1)} %add_convert_fusion.11), channel_id=1, source_target_pairs={{0,8},{4,12},{24,16},{28,20},{1,9},{5,13},{25,17},{29,21},{2,10},{... | collective-permute-start | bytes 2451464 | tf_op jit(solution)/shard_map/ppermute | solution.py:843
  529.5 26.5 %collective-permute-start.85 = (bf16[4,64,1024]{2,1,0:T(8,128)(2,1)S(1)}, bf16[4,64,1024]{2,1,0:T(8,128)(2,1)S(1)}, u32[]{:S(2)}, u32[]{:S(2)}) collective-permute-start(bf16[4,64,1024]{2,1,0:T(8,128)(2,1)S(1)} %fusion), channel_id=1, source_target_pairs={{0,4},{4,0},{8,12},{12,8},{16,20},{20,16},{24,28},{28,24},{1,5},{5... | collective-permute-start | bytes 1572872 | tf_op jit(solution)/shard_map/ppermute | solution.py:822
  530.2 24.3 %collective-permute-start.90 = (bf16[1,168,2432]{2,1,0:T(8,128)(2,1)S(1)}, bf16[1,168,2432]{2,1,0:T(8,128)(2,1)S(1)}, u32[]{:S(2)}, u32[]{:S(2)}) collective-permute-start(bf16[1,168,2432]{2,1,0:T(8,128)(2,1)S(1)} %add_convert_fusion.7), channel_id=1, source_target_pairs={{0,8},{4,12},{24,16},{28,20},{1,9},{5,13},{25,17},{29,21},{2,10},{... | collective-permute-start | bytes 2451464 | tf_op jit(solution)/shard_map/ppermute | solution.py:843
  540.5 38.7 %collective-permute-start.80 = (bf16[2,168,2432]{2,1,0:T(8,128)(2,1)S(1)}, bf16[2,168,2432]{2,1,0:T(8,128)(2,1)S(1)}, u32[]{:S(2)}, u32[]{:S(2)}) collective-permute-start(bf16[2,168,2432]{2,1,0:T(8,128)(2,1)S(1)} %copy-done.99), channel_id=1, source_target_pairs={{0,4},{4,0},{8,12},{12,8},{16,20},{20,16},{24,28},{28,24},{1,5},{5... | collective-permute-start | bytes 4902920 | tf_op jit(solution)/shard_map/ppermute | solution.py:822
  546.6 32.6 %collective-permute-start.83 = (bf16[1,168,2432]{2,1,0:T(8,128)(2,1)S(1)}, bf16[1,168,2432]{2,1,0:T(8,128)(2,1)S(1)}, u32[]{:S(2)}, u32[]{:S(2)}) collective-permute-start(bf16[1,168,2432]{2,1,0:T(8,128)(2,1)S(1)} %add_convert_fusion.9), channel_id=1, source_target_pairs={{8,16},{12,20},{16,8},{20,12},{9,17},{13,21},{17,9},{21,13},{10,18... | collective-permute-start | bytes 2451464 | tf_op jit(solution)/shard_map/ppermute | solution.py:843
  554.5 15.8 %collective-permute-start.76 = (bf16[2,4,64,1024]{3,2,1,0:T(8,128)(2,1)S(1)}, bf16[2,4,64,1024]{3,2,1,0:T(8,128)(2,1)S(1)}, u32[]{:S(2)}, u32[]{:S(2)}) collective-permute-start(bf16[2,4,64,1024]{3,2,1,0:T(8,128)(2,1)S(1)} %get-tuple-element.379), channel_id=1, source_target_pairs={{0,1},{1,0},{2,3},{3,2},{4,5},{5,4},{6,7},{7,6},{8,9},{9,8},{10,11... | collective-permute-start | bytes 3145736 | tf_op jit(solution)/shard_map/ppermute | solution.py:822
  554.8 25.7 %collective-permute-start.91 = (bf16[1,168,2432]{2,1,0:T(8,128)(2,1)S(1)}, bf16[1,168,2432]{2,1,0:T(8,128)(2,1)S(1)}, u32[]{:S(2)}, u32[]{:S(2)}) collective-permute-start(bf16[1,168,2432]{2,1,0:T(8,128)(2,1)S(1)} %add_convert_fusion.6), channel_id=1, source_target_pairs={{8,16},{12,20},{16,8},{20,12},{9,17},{13,21},{17,9},{21,13},{10,18... | collective-permute-start | bytes 2451464 | tf_op jit(solution)/shard_map/ppermute | solution.py:843
  555.9 14.4 %collective-permute-start.79 = (bf16[4,64,1024]{2,1,0:T(8,128)(2,1)S(1)}, bf16[4,64,1024]{2,1,0:T(8,128)(2,1)S(1)}, u32[]{:S(2)}, u32[]{:S(2)}) collective-permute-start(bf16[4,64,1024]{2,1,0:T(8,128)(2,1)S(1)} %get-tuple-element.441), channel_id=1, source_target_pairs={{0,2},{1,3},{2,0},{3,1},{4,6},{5,7},{6,4},{7,5},{8,10},{9,11},{10,... | collective-permute-start | bytes 1572872 | tf_op jit(solution)/shard_map/ppermute | solution.py:822
  570.4 34.9 %collective-permute-start.46 = (bf16[256,896]{1,0:T(8,128)(2,1)S(1)}, bf16[256,896]{1,0:T(8,128)(2,1)S(1)}, u32[]{:S(2)}, u32[]{:S(2)}) collective-permute-start(bf16[256,896]{1,0:T(8,128)(2,1)S(1)} %copy-done.101), channel_id=1, source_target_pairs={{0,1},{1,0},{2,3},{3,2},{4,5},{5,4},{6,7},{7,6},{8,9},{9,8},{10,11... | collective-permute-start | bytes 1376264 | tf_op jit(solution)/shard_map/ppermute | solution.py:822
  570.4 57.6 %collective-permute-start.94 = (bf16[168,2432]{1,0:T(8,128)(2,1)S(1)}, bf16[168,2432]{1,0:T(8,128)(2,1)S(1)}, u32[]{:S(2)}, u32[]{:S(2)}) collective-permute-start(bf16[168,2432]{1,0:T(8,128)(2,1)S(1)} %get-tuple-element.444), channel_id=1, source_target_pairs={{0,8},{4,12},{8,0},{12,4},{16,24},{20,28},{24,16},{28,20},{1,9},{5... | collective-permute-start | bytes 2451464 | tf_op jit(solution)/shard_map/ppermute | solution.py:822
  579.2 20.0 %collective-permute-start.86 = (bf16[2,64,1024]{2,1,0:T(8,128)(2,1)S(1)}, bf16[2,64,1024]{2,1,0:T(8,128)(2,1)S(1)}, u32[]{:S(2)}, u32[]{:S(2)}) collective-permute-start(bf16[2,64,1024]{2,1,0:T(8,128)(2,1)S(1)} %slice.419), channel_id=1, source_target_pairs={{0,16},{4,20},{8,24},{12,28},{16,0},{20,4},{24,8},{28,12},{1,17},{... | collective-permute-start | bytes 786440 | tf_op jit(solution)/shard_map/ppermute | solution.py:822
  579.2 22.4 %collective-permute-start.78 = (bf16[4,64,1024]{2,1,0:T(8,128)(2,1)S(1)}, bf16[4,64,1024]{2,1,0:T(8,128)(2,1)S(1)}, u32[]{:S(2)}, u32[]{:S(2)}) collective-permute-start(bf16[4,64,1024]{2,1,0:T(8,128)(2,1)S(1)} %get-tuple-element.440), channel_id=1, source_target_pairs={{0,2},{1,3},{2,0},{3,1},{4,6},{5,7},{6,4},{7,5},{8,10},{9,11},{10,... | collective-permute-start | bytes 1572872 | tf_op jit(solution)/shard_map/ppermute | solution.py:822
  580.5 21.2 %collective-permute-start.81 = (bf16[4,64,1024]{2,1,0:T(8,128)(2,1)S(1)}, bf16[4,64,1024]{2,1,0:T(8,128)(2,1)S(1)}, u32[]{:S(2)}, u32[]{:S(2)}) collective-permute-start(bf16[4,64,1024]{2,1,0:T(8,128)(2,1)S(1)} %fusion.2), channel_id=1, source_target_pairs={{0,4},{4,0},{8,12},{12,8},{16,20},{20,16},{24,28},{28,24},{1,5},{5... | collective-permute-start | bytes 1572872 | tf_op jit(solution)/shard_map/ppermute | solution.py:822
  599.2 28.7 %collective-permute-start.92 = (bf16[168,2432]{1,0:T(8,128)(2,1)S(1)}, bf16[168,2432]{1,0:T(8,128)(2,1)S(1)}, u32[]{:S(2)}, u32[]{:S(2)}) collective-permute-start(bf16[168,2432]{1,0:T(8,128)(2,1)S(1)} %get-tuple-element.439), channel_id=1, source_target_pairs={{0,8},{4,12},{8,0},{12,4},{16,24},{20,28},{24,16},{28,20},{1,9},{5... | collective-permute-start | bytes 2451464 | tf_op jit(solution)/shard_map/ppermute | solution.py:822
  601.6 26.3 %collective-permute-start.87 = (bf16[64,1024]{1,0:T(8,128)(2,1)S(1)}, bf16[64,1024]{1,0:T(8,128)(2,1)S(1)}, u32[]{:S(2)}, u32[]{:S(2)}) collective-permute-start(bf16[64,1024]{1,0:T(8,128)(2,1)S(1)} %slice_bitcast_fusion.6), channel_id=1, source_target_pairs={{0,8},{4,12},{8,0},{12,4},{16,24},{20,28},{24,16},{28,20},{1,9},{5... | collective-permute-start | bytes 393224 | tf_op jit(solution)/shard_map/ppermute | solution.py:822
  602.1 29.6 %collective-permute-start.82 = (bf16[2,64,1024]{2,1,0:T(8,128)(2,1)S(1)}, bf16[2,64,1024]{2,1,0:T(8,128)(2,1)S(1)}, u32[]{:S(2)}, u32[]{:S(2)}) collective-permute-start(bf16[2,64,1024]{2,1,0:T(8,128)(2,1)S(1)} %slice.412), channel_id=1, source_target_pairs={{0,16},{4,20},{8,24},{12,28},{16,0},{20,4},{24,8},{28,12},{1,17},{... | collective-permute-start | bytes 786440 | tf_op jit(solution)/shard_map/ppermute | solution.py:822
  631.1 14.8 %collective-permute-start.97 = (bf16[2,28,2432]{2,1,0:T(8,128)(2,1)S(1)}, bf16[2,28,2432]{2,1,0:T(8,128)(2,1)S(1)}, u32[]{:S(2)}, u32[]{:S(2)}) collective-permute-start(bf16[2,28,2432]{2,1,0:T(8,128)(2,1)S(1)} %get-tuple-element.406), channel_id=1, source_target_pairs={{0,3},{1,2},{2,1},{3,0},{4,7},{5,6},{6,5},{7,4},{8,11},{9,10},{10,... | collective-permute-start | bytes 817160 | tf_op jit(solution)/shard_map/ppermute | solution.py:822
  631.8 19.2 %collective-permute-start.84 = (bf16[64,1024]{1,0:T(8,128)(2,1)S(1)}, bf16[64,1024]{1,0:T(8,128)(2,1)S(1)}, u32[]{:S(2)}, u32[]{:S(2)}) collective-permute-start(bf16[64,1024]{1,0:T(8,128)(2,1)S(1)} %slice_bitcast_fusion.8), channel_id=1, source_target_pairs={{0,8},{4,12},{8,0},{12,4},{16,24},{20,28},{24,16},{28,20},{1,9},{5... | collective-permute-start | bytes 393224 | tf_op jit(solution)/shard_map/ppermute | solution.py:822
  (153 other events, 1625.7 us)

commit v6 on v5

--- a/solution.py
+++ b/solution.py
@@ -992,10 +992,11 @@
     for layer in range(LAYERS):
         first_full, second_full, gain_full, mlp_gain_full, bias_first, bias_second = attn_sets[layer]
         if layer == 0:
-            second_line = line_gather(after(shards[1], first_full), bits[:1])
+            second_start = line_gather(after(shards[1], first_full), bits[:1])
+            second_line = line_gather(second_start, bits[1:])
         x, normed, queries, own_kv = before_attention(
             terms,
-            after(gain_full, near[0], second_line) if layer == 0 else after(gain_full, near_pair[1]),
+            after(gain_full, near[0], second_start) if layer == 0 else after(gain_full, near_pair[1]),
             first_full,
             second_full,
             bias_first,
@@ -1004,7 +1005,7 @@
             sin_wide,
         )
         kv_blocks = [own_kv] + [swap(own_kv, "seq", bit) for bit in range(1, 4)]
-        waited = (near_pair[0],) if layer == 0 else ()
+        waited = (near_pair[0], crossed[0], second_line) if layer == 0 else ()
         mixed, middle, n2 = attention(
             queries, kv_blocks, biases, x, second_full, after(mlp_gain_full, *waited)
         )
@@ -1015,11 +1016,10 @@
         else:
             n2_parts = group_rows(n2)
         if layer == 0:
-            second_line = line_gather(second_line, bits[1:])
             second_other = swap(after(second_line, n2_parts[3]), "dp", 1)
-            far.append(outward(after(crossed[0], n2)))
+            far.append(outward(crossed[0], n2))
             far_pair = swap(far[0], "dp", 1)
-            near.append(line_gather(after(gate_shards[1], n2), bits[:-1], n2_parts[3]))
+            near.append(line_gather(after(gate_shards[1], n2), bits[:-1], n2_parts[3], far[0]))
             crossed.append(cross_middle(near[1]))
             attn_sets.append(attn_finish(attn_parts(second_line, second_other, n2_parts[3])))
             near_pair.append(swap(after(near[1], far_pair), "dp", 1))
@@ -1128,7 +1128,7 @@
             2 if apart else 1,
         )
         if before is not None:
-            pair_out = after(pair_out, last_across, *attn_sent, before["near_got"], before["inward"])
+            pair_out = after(pair_out, terms[2], last_across, *attn_sent, before["near_got"], before["inward"])
         got = swap(pair_out, "seq", 1)
         out_terms = [own_out, got[0], swap(add_low(across_out, got[1]), "seq", 2)]
         if apart:
@@ -1210,7 +1210,9 @@
         got_near_other = swap(near_other, "seq", 1)
         state["attn_parts"] = (near_x, far_x, got_near_other, got_far_other)
         if before is not None:
-            before["owned"] = line_scatter(attn_pair, bits, got_far_other)
+            before["owned"] = line_scatter(
+                attn_pair, bits, state["near_sum"] if apart else got_far_other
+            )
         states[layer] = before = state
     if line != 4:
         step_one(before)

time: 663 us -> 655 us (0.988)
  waiting for transfers between devices: 286 us -> 267 us
  starting transfers between devices: 93.9 us -> 107 us
    ppermute x88, waiting for transfers between devices: 272 us -> 253 us  [swap(): return lax.ppermute(values, axis, [(i, i ^ bit) for i in range(size)])]
    ppermute x88, starting transfers between devices: 73 us -> 85.6 us  [swap(): return lax.ppermute(values, axis, [(i, i ^ bit) for i in range(size)])]
    unnamed x212 -> x228, local copies, waits for them, and re-layouts: 34 us -> 31 us
  transfers between devices with their start and end apart: 98 -> 98, of which waited for: 40 -> 40; matrix products, arithmetic and copies ran while one was open for 6% -> 7% of each run, Pallas kernels for 23% -> 23%
where the time goes in v6:
time: 655 us; the launch traced here: 647 us
  waiting for transfers between devices  267 us (41%)
  Pallas kernels  182 us (28%)
  starting transfers between devices  107 us (16%)
  local copies, waits for them, and re-layouts  41.6 us (6%)
  other arithmetic  33.9 us (5%)
  between operations  15.9 us (2%)
    ppermute x88, waiting for transfers between devices, swap(): return lax.ppermute(values, axis, [(i, i ^ bit) for i in range(size)])  253 us
    ppermute x88, starting transfers between devices, swap(): return lax.ppermute(values, axis, [(i, i ^ bit) for i in range(size)])  85.6 us
    pallas_call x2, Pallas kernels, feed_back(): call(kernel, [((half, packed, 2 * units), jnp.bfloat16), ((half, packed,...  65.7 us
    pallas_call x4, Pallas kernels, feed_forward(): call(kernel, [((rows, 2 * units), jnp.bfloat16)] + [((part_rows, D), jnp....  40.8 us
    unnamed x228, local copies, waits for them, and re-layouts  31 us
    pallas_call x2, Pallas kernels, attention_back(): call(kernel, [((rows, D), jnp.float32), ((rows, D), jnp.bfloat16), ((1, D...  25.1 us
    pallas_call x2, Pallas kernels, attention(): call(kernel, [((rows, D), jnp.bfloat16), ((rows, D), jnp.float32), ((rows...  21.4 us
    ppermute x10, starting transfers between devices, line_steps(): lax.ppermute(values, 'dp', [(2 * here + side, 2 * there + side) for here,...  21.3 us
  transfers between devices with their start and end apart: 98, of which 40 were waited for; matrix products, arithmetic and copies ran while one was open for 7% of the time, Pallas kernels for 23%

profile of v6, /device:TPU:0, one launch (start us, length us, event | category | flops | bytes accessed | tf_op | source)
XLA Modules:
  0.0 647.4 jit_solution(9955202762087385714)
XLA Ops:
  7.9 2.9 collective-permute-start.1
  14.9 2.8 collective-permute-start.2
  17.8 3.4 collective-permute-done.4.refs_2_
  21.1 5.5 collective-permute-done.5.refs_3_
  31.2 11.4 %collective-permute-done.6.refs_1_ = bf16[4,64,1024]{2,1,0:T(8,128)(2,1)S(1)} collective-permute-done((bf16[4,64,1024]{2,1,0:T(8,128)(2,1)S(1)}, bf16[4,64,1024]{2,1,0:T(8,128)(2,1)S(1)}, u32[]{:S(2)}, u32[]{:S(2)}) %collective-permute-start.6) | collective-permute-done | bytes 524320 | tf_op jit(solution)/shard_map/ppermute | solution.py:822
  46.7 10.3 %collective-permute-done.8.refs_3_ = bf16[4,64,1024]{2,1,0:T(8,128)(2,1)S(1)} collective-permute-done((bf16[4,64,1024]{2,1,0:T(8,128)(2,1)S(1)}, bf16[4,64,1024]{2,1,0:T(8,128)(2,1)S(1)}, u32[]{:S(2)}, u32[]{:S(2)}) %collective-permute-start.8) | collective-permute-done | bytes 524320 | tf_op jit(solution)/shard_map/ppermute | solution.py:822
  56.9 4.8 collective-permute-done.13
  94.5 2.9 assemble.2
  97.4 17.6 %collective-permute-start.15 = (bf16[1,64,1024]{2,1,0:T(8,128)(2,1)}, bf16[1,64,1024]{2,1,0:T(8,128)(2,1)S(1)}, u32[]{:S(2)}, u32[]{:S(2)}) collective-permute-start(bf16[1,64,1024]{2,1,0:T(8,128)(2,1)} %maximum_bitcast_fusion.1), channel_id=1, source_target_pairs={{0,8},{4,12},{8,0},{12,4},{16,24},{20,28},{24,16},{28,20},{1,9},{5... | collective-permute-start | bytes 393224 | tf_op jit(solution)/shard_map/ppermute | solution.py:822
  115.1 26.2 %collective-permute-done.15 = bf16[1,64,1024]{2,1,0:T(8,128)(2,1)S(1)} collective-permute-done((bf16[1,64,1024]{2,1,0:T(8,128)(2,1)}, bf16[1,64,1024]{2,1,0:T(8,128)(2,1)S(1)}, u32[]{:S(2)}, u32[]{:S(2)}) %collective-permute-start.15) | collective-permute-done | bytes 131104 | tf_op jit(solution)/shard_map/ppermute | solution.py:822
  147.2 6.7 %collective-permute-done.21 = bf16[2,64,1024]{2,1,0:T(8,128)(2,1)S(1)} collective-permute-done((bf16[2,64,1024]{2,1,0:T(8,128)(2,1)S(1)}, bf16[2,64,1024]{2,1,0:T(8,128)(2,1)S(1)}, u32[]{:S(2)}, u32[]{:S(2)}) %collective-permute-start.21) | collective-permute-done | bytes 262176 | tf_op jit(solution)/shard_map/ppermute | solution.py:822
  159.7 11.5 %attention.2 = (bf16[256,896]{1,0:T(8,128)(2,1)S(1)}, f32[256,896]{1,0:T(8,128)S(1)}, bf16[256,896]{1,0:T(8,128)(2,1)}) custom-call(bf16[2,2,896,64]{3,2,1,0:T(8,128)(2,1)S(1)} %get-tuple-element.276.q_ref.refs_7_, bf16[256,256]{1,0:T(8,128)(2,1)S(1)} %get-tuple-element.277.kv0.refs_8_, bf16[256,256]{1,0:T(8,128)(2,1)S(1)} %collective-permute-done.16.kv1.refs_9_, ...), custom_call_target="tpu_custom_call" | custom-call | bytes 42000 | tf_op jit(solution)/shard_map/attention/pallas_call | solution.py:159
  176.0 9.9 %collective-permute-done.26.refs_0_.refs_7_ = bf16[256,896]{1,0:T(8,128)(2,1)} collective-permute-done((bf16[256,896]{1,0:T(8,128)(2,1)}, bf16[256,896]{1,0:T(8,128)(2,1)}, u32[]{:S(2)}, u32[]{:S(2)}) %collective-permute-start.26) | collective-permute-done | bytes 458784 | tf_op jit(solution)/shard_map/ppermute | solution.py:822
  189.3 4.5 collective-permute-done.27
  199.6 26.8 %collective-permute-done.24.refs_3_ = bf16[2,168,2432]{2,1,0:T(8,128)(2,1)} collective-permute-done((bf16[2,168,2432]{2,1,0:T(8,128)(2,1)S(1)}, bf16[2,168,2432]{2,1,0:T(8,128)(2,1)}, u32[]{:S(2)}, u32[]{:S(2)}) %collective-permute-start.24) | collective-permute-done | bytes 1634336 | tf_op jit(solution)/shard_map/ppermute | solution.py:822
  228.0 2.9 unpack.2
  234.3 10.2 %feed_forward.4 = (bf16[512,2432]{1,0:T(8,128)(2,1)}, bf16[256,896]{1,0:T(8,128)(2,1)}, bf16[256,896]{1,0:T(8,128)(2,1)}) custom-call(bf16[256,896]{1,0:T(8,128)(2,1)} %get-tuple-element.282.refs_0_.refs_5_, bf16[256,896]{1,0:T(8,128)(2,1)} %collective-permute-done.22.refs_1_.refs_6_, bf16[896,2432]{1,0:T(8,128)(2,1)} %bitcast.146, bf16[1216,896]{1,0:T(8,128)(2,1)} %bitcast.160), custom_call_target="tpu_custom_call" | custom-call | bytes 36000 | tf_op jit(solution)/shard_map/feed_forward/pallas_call | solution.py:204
  246.4 10.2 %feed_forward.5 = (bf16[512,2432]{1,0:T(8,128)(2,1)}, bf16[256,896]{1,0:T(8,128)(2,1)}, bf16[256,896]{1,0:T(8,128)(2,1)}) custom-call(bf16[256,896]{1,0:T(8,128)(2,1)} %collective-permute-done.26.refs_0_.refs_7_, bf16[256,896]{1,0:T(8,128)(2,1)} %collective-permute-done.28.refs_1_.refs_8_, bf16[896,2432]{1,0:T(8,128)(2,1)} %bitcast.147, ...), custom_call_target="tpu_custom_call" | custom-call | bytes 36000 | tf_op jit(solution)/shard_map/feed_forward/pallas_call | solution.py:204
  262.6 3.0 assemble.3
  265.6 6.6 %collective-permute-done.39.refs_2_ = bf16[2,168,2432]{2,1,0:T(8,128)(2,1)} collective-permute-done((bf16[2,168,2432]{2,1,0:T(8,128)(2,1)}, bf16[2,168,2432]{2,1,0:T(8,128)(2,1)}, u32[]{:S(2)}, u32[]{:S(2)}) %collective-permute-start.39) | collective-permute-done | bytes 1634336 | tf_op jit(solution)/shard_map/ppermute | solution.py:822
  272.3 2.9 collective-permute-done.31.refs_3_
  276.9 6.5 collective-permute-done.44
  287.5 4.4 collective-permute-done.41.kv2.refs_10_
  294.0 9.9 %attention.3 = (bf16[256,896]{1,0:T(8,128)(2,1)S(1)}, f32[256,896]{1,0:T(8,128)S(1)}, bf16[256,896]{1,0:T(8,128)(2,1)S(1)}) custom-call(bf16[2,2,896,64]{3,2,1,0:T(8,128)(2,1)S(1)} %get-tuple-element.305.q_ref.refs_7_, bf16[256,256]{1,0:T(8,128)(2,1)S(1)} %get-tuple-element.306.kv0.refs_8_, bf16[256,256]{1,0:T(8,128)(2,1)S(1)} %collective-permute-done.40.kv1.refs_9_, ...), custom_call_target="tpu_custom_call" | custom-call | bytes 42000 | tf_op jit(solution)/shard_map/attention/pallas_call | solution.py:159
  306.1 12.4 %collective-permute-done.47.refs_0_.refs_7_ = bf16[256,896]{1,0:T(8,128)(2,1)S(1)} collective-permute-done((bf16[256,896]{1,0:T(8,128)(2,1)S(1)}, bf16[256,896]{1,0:T(8,128)(2,1)S(1)}, u32[]{:S(2)}, u32[]{:S(2)}) %collective-permute-start.47) | collective-permute-done | bytes 458784 | tf_op jit(solution)/shard_map/ppermute | solution.py:822
  324.0 2.8 unpack.3
  330.9 10.2 %feed_forward.6 = (bf16[512,2432]{1,0:T(8,128)(2,1)}, bf16[256,896]{1,0:T(8,128)(2,1)}, bf16[256,896]{1,0:T(8,128)(2,1)}) custom-call(bf16[256,896]{1,0:T(8,128)(2,1)} %copy-done.31, bf16[256,896]{1,0:T(8,128)(2,1)} %copy-done.73, bf16[896,2432]{1,0:T(8,128)(2,1)} %bitcast.149, bf16[1216,896]{1,0:T(8,128)(2,1)} %bitcast.163), custom_call_target="tpu_custom_call" | custom-call | bytes 36000 | tf_op jit(solution)/shard_map/feed_forward/pallas_call | solution.py:204
  341.7 10.2 %feed_forward.7 = (bf16[512,2432]{1,0:T(8,128)(2,1)}, bf16[256,896]{1,0:T(8,128)(2,1)}, bf16[256,896]{1,0:T(8,128)(2,1)}) custom-call(bf16[256,896]{1,0:T(8,128)(2,1)} %copy-done.71, bf16[256,896]{1,0:T(8,128)(2,1)} %copy-done.72, bf16[896,2432]{1,0:T(8,128)(2,1)} %bitcast.150, bf16[1216,896]{1,0:T(8,128)(2,1)} %bitcast.164), custom_call_target="tpu_custom_call" | custom-call | bytes 36000 | tf_op jit(solution)/shard_map/feed_forward/pallas_call | solution.py:204
  352.7 33.0 %feed_back.2 = (bf16[2,168,2432]{2,1,0:T(8,128)(2,1)}, bf16[2,168,2432]{2,1,0:T(8,128)(2,1)}, bf16[256,896]{1,0:T(8,128)(2,1)}, bf16[256,896]{1,0:T(8,128)(2,1)}...) custom-call(s32[1]{0:T(128)} %bitcast.3.refs_0_, ...), custom_call_target="tpu_custom_call" | custom-call | bytes 100000 | tf_op jit(solution)/shard_map/feed_back/pallas_call | solution.py:324
  391.3 11.0 %collective-permute-done.54.refs_5_ = bf16[256,896]{1,0:T(8,128)(2,1)S(1)} collective-permute-done((bf16[256,896]{1,0:T(8,128)(2,1)S(1)}, bf16[256,896]{1,0:T(8,128)(2,1)S(1)}, u32[]{:S(2)}, u32[]{:S(2)}) %collective-permute-start.54) | collective-permute-done | bytes 458784 | tf_op jit(solution)/shard_map/ppermute | solution.py:822
  405.7 12.1 %attention_back.2 = (f32[256,896]{1,0:T(8,128)S(1)}, bf16[256,896]{1,0:T(8,128)(2,1)S(1)}, f32[1,896]{1,0:T(1,128)S(1)}, bf16[256,896]{1,0:T(8,128)(2,1)S(1)}, f...) custom-call(bf16[256,896]{1,0:T(8,128)(2,1)S(1)} %bitcast.173, ...), custom_call_target="tpu_custom_call" | custom-call | bytes 52000 | tf_op jit(solution)/shard_map/attention_back/pallas_call | solution.py:465
  420.1 4.5 collective-permute-done.56.refs_2_
  433.2 8.3 %collective-permute-done.58.refs_3_ = bf16[256,896]{1,0:T(8,128)(2,1)S(1)} collective-permute-done((bf16[256,896]{1,0:T(8,128)(2,1)S(1)}, bf16[256,896]{1,0:T(8,128)(2,1)S(1)}, u32[]{:S(2)}, u32[]{:S(2)}) %collective-permute-start.58) | collective-permute-done | bytes 458784 | tf_op jit(solution)/shard_map/ppermute | solution.py:822
  453.8 32.6 %feed_back.3 = (bf16[2,168,2432]{2,1,0:T(8,128)(2,1)}, bf16[2,168,2432]{2,1,0:T(8,128)(2,1)}, bf16[256,896]{1,0:T(8,128)(2,1)}, bf16[256,896]{1,0:T(8,128)(2,1)}...) custom-call(s32[1]{0:T(128)} %bitcast.3.refs_0_, ...), custom_call_target="tpu_custom_call" | custom-call | bytes 100000 | tf_op jit(solution)/shard_map/feed_back/pallas_call | solution.py:324
  495.4 12.5 %collective-permute-done.71 = bf16[1,168,2432]{2,1,0:T(8,128)(2,1)S(1)} collective-permute-done((bf16[1,168,2432]{2,1,0:T(8,128)(2,1)}, bf16[1,168,2432]{2,1,0:T(8,128)(2,1)S(1)}, u32[]{:S(2)}, u32[]{:S(2)}) %collective-permute-start.71) | collective-permute-done | bytes 817184 | tf_op jit(solution)/shard_map/ppermute | solution.py:822
  511.0 13.1 %attention_back.3 = (f32[256,896]{1,0:T(8,128)S(1)}, bf16[256,896]{1,0:T(8,128)(2,1)S(1)}, f32[1,896]{1,0:T(1,128)S(1)}, bf16[256,896]{1,0:T(8,128)(2,1)S(1)}, f...) custom-call(f32[256,896]{1,0:T(8,128)S(1)} %copy-done.37, ...), custom_call_target="tpu_custom_call" | custom-call | bytes 52000 | tf_op jit(solution)/shard_map/attention_back/pallas_call | solution.py:465
  525.6 7.9 %collective-permute-start.90 = (bf16[1,168,2432]{2,1,0:T(8,128)(2,1)S(1)}, bf16[1,168,2432]{2,1,0:T(8,128)(2,1)S(1)}, u32[]{:S(2)}, u32[]{:S(2)}) collective-permute-start(bf16[1,168,2432]{2,1,0:T(8,128)(2,1)S(1)} %add_convert_fusion.7), channel_id=1, source_target_pairs={{0,8},{4,12},{24,16},{28,20},{1,9},{5,13},{25,17},{29,21},{2,10},{... | collective-permute-start | bytes 2451464 | tf_op jit(solution)/shard_map/ppermute | solution.py:843
  542.7 7.2 %collective-permute-done.90 = bf16[1,168,2432]{2,1,0:T(8,128)(2,1)S(1)} collective-permute-done((bf16[1,168,2432]{2,1,0:T(8,128)(2,1)S(1)}, bf16[1,168,2432]{2,1,0:T(8,128)(2,1)S(1)}, u32[]{:S(2)}, u32[]{:S(2)}) %collective-permute-start.90) | collective-permute-done | bytes 817184 | tf_op jit(solution)/shard_map/ppermute | solution.py:843
  554.3 11.4 %collective-permute-done.79 = bf16[4,64,1024]{2,1,0:T(8,128)(2,1)S(1)} collective-permute-done((bf16[4,64,1024]{2,1,0:T(8,128)(2,1)S(1)}, bf16[4,64,1024]{2,1,0:T(8,128)(2,1)S(1)}, u32[]{:S(2)}, u32[]{:S(2)}) %collective-permute-start.79) | collective-permute-done | bytes 524320 | tf_op jit(solution)/shard_map/ppermute | solution.py:822
  565.8 4.2 collective-permute-start.94
  570.9 3.7 collective-permute-done.80
  577.0 5.5 collective-permute-start.92
  582.4 11.9 %collective-permute-done.86 = bf16[2,64,1024]{2,1,0:T(8,128)(2,1)S(1)} collective-permute-done((bf16[2,64,1024]{2,1,0:T(8,128)(2,1)S(1)}, bf16[2,64,1024]{2,1,0:T(8,128)(2,1)S(1)}, u32[]{:S(2)}, u32[]{:S(2)}) %collective-permute-start.86) | collective-permute-done | bytes 262176 | tf_op jit(solution)/shard_map/ppermute | solution.py:822
  594.4 3.2 collective-permute-start.87
  600.4 19.0 %collective-permute-done.87 = bf16[64,1024]{1,0:T(8,128)(2,1)S(1)} collective-permute-done((bf16[64,1024]{1,0:T(8,128)(2,1)S(1)}, bf16[64,1024]{1,0:T(8,128)(2,1)S(1)}, u32[]{:S(2)}, u32[]{:S(2)}) %collective-permute-start.87) | collective-permute-done | bytes 131104 | tf_op jit(solution)/shard_map/ppermute | solution.py:822
  623.4 8.1 %collective-permute-done.96.refs_2_ = bf16[2,28,2432]{2,1,0:T(8,128)(2,1)S(1)} collective-permute-done((bf16[2,28,2432]{2,1,0:T(8,128)(2,1)S(1)}, bf16[2,28,2432]{2,1,0:T(8,128)(2,1)S(1)}, u32[]{:S(2)}, u32[]{:S(2)}) %collective-permute-start.96) | collective-permute-done | bytes 272416 | tf_op jit(solution)/shard_map/ppermute | solution.py:822
  631.4 5.9 collective-permute-done.97.refs_3_
  639.4 3.0 copy.58
  (518 shorter events, 174.2 us)
Async XLA Ops:
  12.4 14.2 %collective-permute-start.5 = (bf16[2,28,2432]{2,1,0:T(8,128)(2,1)S(1)}, bf16[2,28,2432]{2,1,0:T(8,128)(2,1)S(1)}, u32[]{:S(2)}, u32[]{:S(2)}) collective-permute-start(bf16[2,28,2432]{2,1,0:T(8,128)(2,1)S(1)} %get-tuple-element.260), channel_id=1, source_target_pairs={{0,3},{1,2},{2,1},{3,0},{4,7},{5,6},{6,5},{7,4},{8,11},{9,10},{10,... | collective-permute-start | bytes 817160 | tf_op jit(solution)/shard_map/ppermute | solution.py:822
  14.9 14.7 %collective-permute-start.2 = (bf16[2,64,1024]{2,1,0:T(8,128)(2,1)S(1)}, bf16[2,64,1024]{2,1,0:T(8,128)(2,1)S(1)}, u32[]{:S(2)}, u32[]{:S(2)}) collective-permute-start(bf16[2,64,1024]{2,1,0:T(8,128)(2,1)S(1)} %pad_maximum_fusion.6), channel_id=1, source_target_pairs={{0,16},{4,20},{8,24},{12,28},{16,0},{20,4},{24,8},{28,12},{1,17},{... | collective-permute-start | bytes 786440 | tf_op jit(solution)/shard_map/ppermute | solution.py:822
  42.6 19.1 %collective-permute-start.13 = (bf16[1,168,2432]{2,1,0:T(8,128)(2,1)S(1)}, bf16[1,168,2432]{2,1,0:T(8,128)(2,1)S(1)}, u32[]{:S(2)}, u32[]{:S(2)}) collective-permute-start(bf16[1,168,2432]{2,1,0:T(8,128)(2,1)S(1)} %get-tuple-element.270), channel_id=1, source_target_pairs={{0,8},{4,12},{8,0},{12,4},{16,24},{20,28},{24,16},{28,20},{1,9},{5... | collective-permute-start | bytes 2451464 | tf_op jit(solution)/shard_map/ppermute | solution.py:822
  62.7 24.3 %collective-permute-start.20 = (bf16[2,168,2432]{2,1,0:T(8,128)(2,1)}, bf16[2,168,2432]{2,1,0:T(8,128)(2,1)}, u32[]{:S(2)}, u32[]{:S(2)}) collective-permute-start(bf16[2,168,2432]{2,1,0:T(8,128)(2,1)} %constant_dynamic-update-slice_fusion.refs_0_), channel_id=1, source_target_pairs={{8,16},{12,20},{16,8},{20,12},{9,17},{13,21},{17,9},{21,13},{10,18... | collective-permute-start | bytes 4902920 | tf_op jit(solution)/shard_map/ppermute | solution.py:843
  64.6 20.4 %collective-permute-start.14 = (bf16[28,1024]{1,0:T(8,128)(2,1)S(1)}, bf16[28,1024]{1,0:T(8,128)(2,1)S(1)}, u32[]{:S(2)}, u32[]{:S(2)}) collective-permute-start(bf16[28,1024]{1,0:T(8,128)(2,1)S(1)} %get-tuple-element.453), channel_id=1, source_target_pairs={{0,1},{1,0},{2,3},{3,2},{4,5},{5,4},{6,7},{7,6},{8,9},{9,8},{10,11... | collective-permute-start | bytes 172040 | tf_op jit(solution)/shard_map/ppermute | solution.py:822
  66.7 18.1 %collective-permute-start.7 = (bf16[4,64,1024]{2,1,0:T(8,128)(2,1)S(1)}, bf16[4,64,1024]{2,1,0:T(8,128)(2,1)S(1)}, u32[]{:S(2)}, u32[]{:S(2)}) collective-permute-start(bf16[4,64,1024]{2,1,0:T(8,128)(2,1)S(1)} %pad_maximum_fusion.refs_0_), channel_id=1, source_target_pairs={{0,2},{1,3},{2,0},{3,1},{4,6},{5,7},{6,4},{7,5},{8,10},{9,11},{10,... | collective-permute-start | bytes 1572872 | tf_op jit(solution)/shard_map/ppermute | solution.py:822
  68.2 17.1 %collective-permute-start.9 = (bf16[4,64,1024]{2,1,0:T(8,128)(2,1)S(1)}, bf16[4,64,1024]{2,1,0:T(8,128)(2,1)S(1)}, u32[]{:S(2)}, u32[]{:S(2)}) collective-permute-start(bf16[4,64,1024]{2,1,0:T(8,128)(2,1)S(1)} %pad_maximum_fusion.refs_0_), channel_id=1, source_target_pairs={{0,1},{1,0},{2,3},{3,2},{4,5},{5,4},{6,7},{7,6},{8,9},{9,8},{10,11... | collective-permute-start | bytes 1572872 | tf_op jit(solution)/shard_map/ppermute | solution.py:822
  74.0 84.5 %collective-permute-start.19 = (bf16[2,168,2432]{2,1,0:T(8,128)(2,1)}, bf16[2,168,2432]{2,1,0:T(8,128)(2,1)}, u32[]{:S(2)}, u32[]{:S(2)}) collective-permute-start(bf16[2,168,2432]{2,1,0:T(8,128)(2,1)} %constant_dynamic-update-slice_fusion.refs_0_), channel_id=1, source_target_pairs={{0,4},{4,0},{8,12},{12,8},{16,20},{20,16},{24,28},{28,24},{1,5},{5... | collective-permute-start | bytes 4902920 | tf_op jit(solution)/shard_map/ppermute | solution.py:822
  87.0 98.9 %collective-permute-start.23 = (bf16[2,168,2432]{2,1,0:T(8,128)(2,1)}, bf16[2,168,2432]{2,1,0:T(8,128)(2,1)}, u32[]{:S(2)}, u32[]{:S(2)}) collective-permute-start(bf16[2,168,2432]{2,1,0:T(8,128)(2,1)} %collective-permute-done.20), channel_id=1, source_target_pairs={{8,0},{12,4},{16,24},{20,28},{9,1},{13,5},{17,25},{21,29},{10,2},{... | collective-permute-start | bytes 4902920 | tf_op jit(solution)/shard_map/ppermute | solution.py:843
  97.4 43.9 %collective-permute-start.15 = (bf16[1,64,1024]{2,1,0:T(8,128)(2,1)}, bf16[1,64,1024]{2,1,0:T(8,128)(2,1)S(1)}, u32[]{:S(2)}, u32[]{:S(2)}) collective-permute-start(bf16[1,64,1024]{2,1,0:T(8,128)(2,1)} %maximum_bitcast_fusion.1), channel_id=1, source_target_pairs={{0,8},{4,12},{8,0},{12,4},{16,24},{20,28},{24,16},{28,20},{1,9},{5... | collective-permute-start | bytes 393224 | tf_op jit(solution)/shard_map/ppermute | solution.py:822
  173.8 19.9 %collective-permute-start.27 = (bf16[1,168,2432]{2,1,0:T(8,128)(2,1)}, bf16[1,168,2432]{2,1,0:T(8,128)(2,1)S(1)}, u32[]{:S(2)}, u32[]{:S(2)}) collective-permute-start(bf16[1,168,2432]{2,1,0:T(8,128)(2,1)} %copy-done.38), channel_id=1, source_target_pairs={{0,8},{4,12},{8,0},{12,4},{16,24},{20,28},{24,16},{28,20},{1,9},{5... | collective-permute-start | bytes 2451464 | tf_op jit(solution)/shard_map/ppermute | solution.py:822
  187.7 38.7 %collective-permute-start.24 = (bf16[2,168,2432]{2,1,0:T(8,128)(2,1)S(1)}, bf16[2,168,2432]{2,1,0:T(8,128)(2,1)}, u32[]{:S(2)}, u32[]{:S(2)}) collective-permute-start(bf16[2,168,2432]{2,1,0:T(8,128)(2,1)S(1)} %broadcast_select_fusion.1.refs_1_), channel_id=1, source_target_pairs={{0,4},{4,0},{8,12},{12,8},{16,20},{20,16},{24,28},{28,24},{1,5},{5... | collective-permute-start | bytes 4902920 | tf_op jit(solution)/shard_map/ppermute | solution.py:822
  194.7 49.7 %collective-permute-start.29 = (bf16[2,168,2432]{2,1,0:T(8,128)(2,1)}, bf16[2,168,2432]{2,1,0:T(8,128)(2,1)}, u32[]{:S(2)}, u32[]{:S(2)}) collective-permute-start(bf16[2,168,2432]{2,1,0:T(8,128)(2,1)} %constant_dynamic-update-slice_fusion.2.refs_0_), channel_id=1, source_target_pairs={{8,16},{12,20},{16,8},{20,12},{9,17},{13,21},{17,9},{21,13},{10,18... | collective-permute-start | bytes 4902920 | tf_op jit(solution)/shard_map/ppermute | solution.py:843
  196.6 37.7 %collective-permute-start.22 = (bf16[256,896]{1,0:T(8,128)(2,1)}, bf16[256,896]{1,0:T(8,128)(2,1)}, u32[]{:S(2)}, u32[]{:S(2)}) collective-permute-start(bf16[256,896]{1,0:T(8,128)(2,1)} %get-tuple-element.282.refs_0_.refs_5_), channel_id=1, source_target_pairs={{0,1},{1,0},{2,3},{3,2},{4,5},{5,4},{6,7},{7,6},{8,9},{9,8},{10,11... | collective-permute-start | bytes 1376264 | tf_op jit(solution)/shard_map/ppermute | solution.py:822
  196.6 49.2 %collective-permute-start.32 = (bf16[4,64,1024]{2,1,0:T(8,128)(2,1)}, bf16[4,64,1024]{2,1,0:T(8,128)(2,1)}, u32[]{:S(2)}, u32[]{:S(2)}) collective-permute-start(bf16[4,64,1024]{2,1,0:T(8,128)(2,1)} %pad_maximum_fusion.2.refs_0_), channel_id=1, source_target_pairs={{0,4},{4,0},{8,12},{12,8},{16,20},{20,16},{24,28},{28,24},{1,5},{5... | collective-permute-start | bytes 1572872 | tf_op jit(solution)/shard_map/ppermute | solution.py:822
  198.1 58.5 %collective-permute-start.33 = (bf16[4,64,1024]{2,1,0:T(8,128)(2,1)}, bf16[4,64,1024]{2,1,0:T(8,128)(2,1)}, u32[]{:S(2)}, u32[]{:S(2)}) collective-permute-start(bf16[4,64,1024]{2,1,0:T(8,128)(2,1)} %pad_maximum_fusion.2.refs_0_), channel_id=1, source_target_pairs={{0,2},{1,3},{2,0},{3,1},{4,6},{5,7},{6,4},{7,5},{8,10},{9,11},{10,... | collective-permute-start | bytes 1572872 | tf_op jit(solution)/shard_map/ppermute | solution.py:822
  226.4 45.9 %collective-permute-start.39 = (bf16[2,168,2432]{2,1,0:T(8,128)(2,1)}, bf16[2,168,2432]{2,1,0:T(8,128)(2,1)}, u32[]{:S(2)}, u32[]{:S(2)}) collective-permute-start(bf16[2,168,2432]{2,1,0:T(8,128)(2,1)} %constant_dynamic-update-slice_fusion.2.refs_0_), channel_id=1, source_target_pairs={{0,4},{4,0},{8,12},{12,8},{16,20},{20,16},{24,28},{28,24},{1,5},{5... | collective-permute-start | bytes 4902920 | tf_op jit(solution)/shard_map/ppermute | solution.py:822
  244.5 38.9 %collective-permute-start.44 = (bf16[2,168,2432]{2,1,0:T(8,128)(2,1)}, bf16[2,168,2432]{2,1,0:T(8,128)(2,1)}, u32[]{:S(2)}, u32[]{:S(2)}) collective-permute-start(bf16[2,168,2432]{2,1,0:T(8,128)(2,1)} %collective-permute-done.29), channel_id=1, source_target_pairs={{8,0},{12,4},{16,24},{20,28},{9,1},{13,5},{17,25},{21,29},{10,2},{... | collective-permute-start | bytes 4902920 | tf_op jit(solution)/shard_map/ppermute | solution.py:843
  285.0 35.8 %collective-permute-start.45 = (bf16[2,168,2432]{2,1,0:T(8,128)(2,1)S(1)}, bf16[2,168,2432]{2,1,0:T(8,128)(2,1)S(1)}, u32[]{:S(2)}, u32[]{:S(2)}) collective-permute-start(bf16[2,168,2432]{2,1,0:T(8,128)(2,1)S(1)} %broadcast_select_fusion.refs_1_), channel_id=1, source_target_pairs={{0,4},{4,0},{8,12},{12,8},{16,20},{20,16},{24,28},{28,24},{1,5},{5... | collective-permute-start | bytes 4902920 | tf_op jit(solution)/shard_map/ppermute | solution.py:822
  323.4 17.7 %collective-permute-start.51 = (bf16[256,896]{1,0:T(8,128)(2,1)S(1)}, bf16[256,896]{1,0:T(8,128)(2,1)}, u32[]{:S(2)}, u32[]{:S(2)}) collective-permute-start(bf16[256,896]{1,0:T(8,128)(2,1)S(1)} %bitcast.171), channel_id=1, source_target_pairs={{0,2},{1,3},{2,0},{3,1},{4,6},{5,7},{6,4},{7,5},{8,10},{9,11},{10,... | collective-permute-start | bytes 1376264 | tf_op jit(solution)/shard_map/ppermute | solution.py:822
  385.9 47.3 %collective-permute-start.67 = (bf16[2,168,2432]{2,1,0:T(8,128)(2,1)}, bf16[2,168,2432]{2,1,0:T(8,128)(2,1)S(1)}, u32[]{:S(2)}, u32[]{:S(2)}) collective-permute-start(bf16[2,168,2432]{2,1,0:T(8,128)(2,1)} %get-tuple-element.355), channel_id=1, source_target_pairs={{0,4},{4,0},{8,12},{12,8},{16,20},{20,16},{24,28},{28,24},{1,5},{5... | collective-permute-start | bytes 4902920 | tf_op jit(solution)/shard_map/ppermute | solution.py:822
  430.3 15.6 %collective-permute-start.46 = (bf16[256,896]{1,0:T(8,128)(2,1)S(1)}, bf16[256,896]{1,0:T(8,128)(2,1)S(1)}, u32[]{:S(2)}, u32[]{:S(2)}) collective-permute-start(bf16[256,896]{1,0:T(8,128)(2,1)S(1)} %copy-done.110), channel_id=1, source_target_pairs={{0,1},{1,0},{2,3},{3,2},{4,5},{5,4},{6,7},{7,6},{8,9},{9,8},{10,11... | collective-permute-start | bytes 1376264 | tf_op jit(solution)/shard_map/ppermute | solution.py:822
  430.3 56.2 %collective-permute-start.66 = (bf16[2,168,2432]{2,1,0:T(8,128)(2,1)}, bf16[2,168,2432]{2,1,0:T(8,128)(2,1)}, u32[]{:S(2)}, u32[]{:S(2)}) collective-permute-start(bf16[2,168,2432]{2,1,0:T(8,128)(2,1)} %get-tuple-element.353), channel_id=1, source_target_pairs={{0,4},{4,0},{8,12},{12,8},{16,20},{20,16},{24,28},{28,24},{1,5},{5... | collective-permute-start | bytes 4902920 | tf_op jit(solution)/shard_map/ppermute | solution.py:822
  443.1 43.4 %collective-permute-start.68 = (bf16[2,168,2432]{2,1,0:T(8,128)(2,1)}, bf16[2,168,2432]{2,1,0:T(8,128)(2,1)}, u32[]{:S(2)}, u32[]{:S(2)}) collective-permute-start(bf16[2,168,2432]{2,1,0:T(8,128)(2,1)} %add_convert_fusion.3), channel_id=1, source_target_pairs={{0,8},{4,12},{24,16},{28,20},{1,9},{5,13},{25,17},{29,21},{2,10},{... | collective-permute-start | bytes 4902920 | tf_op jit(solution)/shard_map/ppermute | solution.py:843
  449.2 37.3 %collective-permute-start.64 = (bf16[4,64,1024]{2,1,0:T(8,128)(2,1)}, bf16[4,64,1024]{2,1,0:T(8,128)(2,1)}, u32[]{:S(2)}, u32[]{:S(2)}) collective-permute-start(bf16[4,64,1024]{2,1,0:T(8,128)(2,1)} %get-tuple-element.350), channel_id=1, source_target_pairs={{0,2},{1,3},{2,0},{3,1},{4,6},{5,7},{6,4},{7,5},{8,10},{9,11},{10,... | collective-permute-start | bytes 1572872 | tf_op jit(solution)/shard_map/ppermute | solution.py:822
  450.7 35.8 %collective-permute-start.65 = (bf16[4,64,1024]{2,1,0:T(8,128)(2,1)}, bf16[4,64,1024]{2,1,0:T(8,128)(2,1)}, u32[]{:S(2)}, u32[]{:S(2)}) collective-permute-start(bf16[4,64,1024]{2,1,0:T(8,128)(2,1)} %get-tuple-element.351), channel_id=1, source_target_pairs={{0,2},{1,3},{2,0},{3,1},{4,6},{5,7},{6,4},{7,5},{8,10},{9,11},{10,... | collective-permute-start | bytes 1572872 | tf_op jit(solution)/shard_map/ppermute | solution.py:822
  452.4 34.0 %collective-permute-start.60 = (bf16[256,896]{1,0:T(8,128)(2,1)S(1)}, bf16[256,896]{1,0:T(8,128)(2,1)}, u32[]{:S(2)}, u32[]{:S(2)}) collective-permute-start(bf16[256,896]{1,0:T(8,128)(2,1)S(1)} %add_convert_fusion.19), channel_id=1, source_target_pairs={{0,2},{1,3},{2,0},{3,1},{4,6},{5,7},{6,4},{7,5},{8,10},{9,11},{10,... | collective-permute-start | bytes 1376264 | tf_op jit(solution)/shard_map/ppermute | solution.py:822
  486.6 21.3 %collective-permute-start.71 = (bf16[1,168,2432]{2,1,0:T(8,128)(2,1)}, bf16[1,168,2432]{2,1,0:T(8,128)(2,1)S(1)}, u32[]{:S(2)}, u32[]{:S(2)}) collective-permute-start(bf16[1,168,2432]{2,1,0:T(8,128)(2,1)} %get-tuple-element.362), channel_id=1, source_target_pairs={{0,4},{4,0},{8,12},{12,8},{16,20},{20,16},{24,28},{28,24},{1,5},{5... | collective-permute-start | bytes 2451464 | tf_op jit(solution)/shard_map/ppermute | solution.py:822
  490.6 17.3 %collective-permute-start.70 = (bf16[256,896]{1,0:T(8,128)(2,1)S(1)}, bf16[256,896]{1,0:T(8,128)(2,1)S(1)}, u32[]{:S(2)}, u32[]{:S(2)}) collective-permute-start(bf16[256,896]{1,0:T(8,128)(2,1)S(1)} %fusion.4), channel_id=1, source_target_pairs={{0,2},{1,3},{2,0},{3,1},{4,6},{5,7},{6,4},{7,5},{8,10},{9,11},{10,... | collective-permute-start | bytes 1376264 | tf_op jit(solution)/shard_map/ppermute | solution.py:822
  493.6 32.0 %collective-permute-start.93 = (bf16[2,168,2432]{2,1,0:T(8,128)(2,1)S(1)}, bf16[2,168,2432]{2,1,0:T(8,128)(2,1)S(1)}, u32[]{:S(2)}, u32[]{:S(2)}) collective-permute-start(bf16[2,168,2432]{2,1,0:T(8,128)(2,1)S(1)} %add_convert_fusion.1), channel_id=1, source_target_pairs={{8,16},{12,20},{16,8},{20,12},{9,17},{13,21},{17,9},{21,13},{10,18... | collective-permute-start | bytes 4902920 | tf_op jit(solution)/shard_map/ppermute | solution.py:843
  494.4 30.6 %collective-permute-start.89 = (bf16[1,168,2432]{2,1,0:T(8,128)(2,1)S(1)}, bf16[1,168,2432]{2,1,0:T(8,128)(2,1)S(1)}, u32[]{:S(2)}, u32[]{:S(2)}) collective-permute-start(bf16[1,168,2432]{2,1,0:T(8,128)(2,1)S(1)} %copy-done.108), channel_id=1, source_target_pairs={{0,4},{4,0},{8,12},{12,8},{16,20},{20,16},{24,28},{28,24},{1,5},{5... | collective-permute-start | bytes 2451464 | tf_op jit(solution)/shard_map/ppermute | solution.py:822
  508.2 25.4 %collective-permute-start.72 = (bf16[1,168,2432]{2,1,0:T(8,128)(2,1)S(1)}, bf16[1,168,2432]{2,1,0:T(8,128)(2,1)S(1)}, u32[]{:S(2)}, u32[]{:S(2)}) collective-permute-start(bf16[1,168,2432]{2,1,0:T(8,128)(2,1)S(1)} %add_convert_fusion.11), channel_id=1, source_target_pairs={{0,8},{4,12},{24,16},{28,20},{1,9},{5,13},{25,17},{29,21},{2,10},{... | collective-permute-start | bytes 2451464 | tf_op jit(solution)/shard_map/ppermute | solution.py:843
  524.9 26.4 %collective-permute-start.85 = (bf16[4,64,1024]{2,1,0:T(8,128)(2,1)S(1)}, bf16[4,64,1024]{2,1,0:T(8,128)(2,1)S(1)}, u32[]{:S(2)}, u32[]{:S(2)}) collective-permute-start(bf16[4,64,1024]{2,1,0:T(8,128)(2,1)S(1)} %fusion), channel_id=1, source_target_pairs={{0,4},{4,0},{8,12},{12,8},{16,20},{20,16},{24,28},{28,24},{1,5},{5... | collective-permute-start | bytes 1572872 | tf_op jit(solution)/shard_map/ppermute | solution.py:822
  525.6 24.3 %collective-permute-start.90 = (bf16[1,168,2432]{2,1,0:T(8,128)(2,1)S(1)}, bf16[1,168,2432]{2,1,0:T(8,128)(2,1)S(1)}, u32[]{:S(2)}, u32[]{:S(2)}) collective-permute-start(bf16[1,168,2432]{2,1,0:T(8,128)(2,1)S(1)} %add_convert_fusion.7), channel_id=1, source_target_pairs={{0,8},{4,12},{24,16},{28,20},{1,9},{5,13},{25,17},{29,21},{2,10},{... | collective-permute-start | bytes 2451464 | tf_op jit(solution)/shard_map/ppermute | solution.py:843
  535.9 38.7 %collective-permute-start.80 = (bf16[2,168,2432]{2,1,0:T(8,128)(2,1)S(1)}, bf16[2,168,2432]{2,1,0:T(8,128)(2,1)S(1)}, u32[]{:S(2)}, u32[]{:S(2)}) collective-permute-start(bf16[2,168,2432]{2,1,0:T(8,128)(2,1)S(1)} %copy-done.107), channel_id=1, source_target_pairs={{0,4},{4,0},{8,12},{12,8},{16,20},{20,16},{24,28},{28,24},{1,5},{5... | collective-permute-start | bytes 4902920 | tf_op jit(solution)/shard_map/ppermute | solution.py:822
  542.0 33.8 %collective-permute-start.83 = (bf16[1,168,2432]{2,1,0:T(8,128)(2,1)S(1)}, bf16[1,168,2432]{2,1,0:T(8,128)(2,1)S(1)}, u32[]{:S(2)}, u32[]{:S(2)}) collective-permute-start(bf16[1,168,2432]{2,1,0:T(8,128)(2,1)S(1)} %add_convert_fusion.9), channel_id=1, source_target_pairs={{8,16},{12,20},{16,8},{20,12},{9,17},{13,21},{17,9},{21,13},{10,18... | collective-permute-start | bytes 2451464 | tf_op jit(solution)/shard_map/ppermute | solution.py:843
  550.0 20.1 %collective-permute-start.76 = (bf16[2,4,64,1024]{3,2,1,0:T(8,128)(2,1)S(1)}, bf16[2,4,64,1024]{3,2,1,0:T(8,128)(2,1)S(1)}, u32[]{:S(2)}, u32[]{:S(2)}) collective-permute-start(bf16[2,4,64,1024]{3,2,1,0:T(8,128)(2,1)S(1)} %get-tuple-element.379), channel_id=1, source_target_pairs={{0,1},{1,0},{2,3},{3,2},{4,5},{5,4},{6,7},{7,6},{8,9},{9,8},{10,11... | collective-permute-start | bytes 3145736 | tf_op jit(solution)/shard_map/ppermute | solution.py:822
  550.2 26.2 %collective-permute-start.91 = (bf16[1,168,2432]{2,1,0:T(8,128)(2,1)S(1)}, bf16[1,168,2432]{2,1,0:T(8,128)(2,1)S(1)}, u32[]{:S(2)}, u32[]{:S(2)}) collective-permute-start(bf16[1,168,2432]{2,1,0:T(8,128)(2,1)S(1)} %add_convert_fusion.6), channel_id=1, source_target_pairs={{8,16},{12,20},{16,8},{20,12},{9,17},{13,21},{17,9},{21,13},{10,18... | collective-permute-start | bytes 2451464 | tf_op jit(solution)/shard_map/ppermute | solution.py:843
  551.4 14.4 %collective-permute-start.79 = (bf16[4,64,1024]{2,1,0:T(8,128)(2,1)S(1)}, bf16[4,64,1024]{2,1,0:T(8,128)(2,1)S(1)}, u32[]{:S(2)}, u32[]{:S(2)}) collective-permute-start(bf16[4,64,1024]{2,1,0:T(8,128)(2,1)S(1)} %get-tuple-element.441), channel_id=1, source_target_pairs={{0,2},{1,3},{2,0},{3,1},{4,6},{5,7},{6,4},{7,5},{8,10},{9,11},{10,... | collective-permute-start | bytes 1572872 | tf_op jit(solution)/shard_map/ppermute | solution.py:822
  565.8 53.6 %collective-permute-start.94 = (bf16[168,2432]{1,0:T(8,128)(2,1)S(1)}, bf16[168,2432]{1,0:T(8,128)(2,1)S(1)}, u32[]{:S(2)}, u32[]{:S(2)}) collective-permute-start(bf16[168,2432]{1,0:T(8,128)(2,1)S(1)} %get-tuple-element.444), channel_id=1, source_target_pairs={{0,8},{4,12},{8,0},{12,4},{16,24},{20,28},{24,16},{28,20},{1,9},{5... | collective-permute-start | bytes 2451464 | tf_op jit(solution)/shard_map/ppermute | solution.py:822
  570.0 24.3 %collective-permute-start.86 = (bf16[2,64,1024]{2,1,0:T(8,128)(2,1)S(1)}, bf16[2,64,1024]{2,1,0:T(8,128)(2,1)S(1)}, u32[]{:S(2)}, u32[]{:S(2)}) collective-permute-start(bf16[2,64,1024]{2,1,0:T(8,128)(2,1)S(1)} %slice.419), channel_id=1, source_target_pairs={{0,16},{4,20},{8,24},{12,28},{16,0},{20,4},{24,8},{28,12},{1,17},{... | collective-permute-start | bytes 786440 | tf_op jit(solution)/shard_map/ppermute | solution.py:822
  574.6 23.0 %collective-permute-start.78 = (bf16[4,64,1024]{2,1,0:T(8,128)(2,1)S(1)}, bf16[4,64,1024]{2,1,0:T(8,128)(2,1)S(1)}, u32[]{:S(2)}, u32[]{:S(2)}) collective-permute-start(bf16[4,64,1024]{2,1,0:T(8,128)(2,1)S(1)} %get-tuple-element.440), channel_id=1, source_target_pairs={{0,2},{1,3},{2,0},{3,1},{4,6},{5,7},{6,4},{7,5},{8,10},{9,11},{10,... | collective-permute-start | bytes 1572872 | tf_op jit(solution)/shard_map/ppermute | solution.py:822
  575.8 21.8 %collective-permute-start.81 = (bf16[4,64,1024]{2,1,0:T(8,128)(2,1)S(1)}, bf16[4,64,1024]{2,1,0:T(8,128)(2,1)S(1)}, u32[]{:S(2)}, u32[]{:S(2)}) collective-permute-start(bf16[4,64,1024]{2,1,0:T(8,128)(2,1)S(1)} %fusion.2), channel_id=1, source_target_pairs={{0,4},{4,0},{8,12},{12,8},{16,20},{20,16},{24,28},{28,24},{1,5},{5... | collective-permute-start | bytes 1572872 | tf_op jit(solution)/shard_map/ppermute | solution.py:822
  577.0 42.4 %collective-permute-start.92 = (bf16[168,2432]{1,0:T(8,128)(2,1)S(1)}, bf16[168,2432]{1,0:T(8,128)(2,1)S(1)}, u32[]{:S(2)}, u32[]{:S(2)}) collective-permute-start(bf16[168,2432]{1,0:T(8,128)(2,1)S(1)} %get-tuple-element.439), channel_id=1, source_target_pairs={{0,8},{4,12},{8,0},{12,4},{16,24},{20,28},{24,16},{28,20},{1,9},{5... | collective-permute-start | bytes 2451464 | tf_op jit(solution)/shard_map/ppermute | solution.py:822
  594.4 24.9 %collective-permute-start.87 = (bf16[64,1024]{1,0:T(8,128)(2,1)S(1)}, bf16[64,1024]{1,0:T(8,128)(2,1)S(1)}, u32[]{:S(2)}, u32[]{:S(2)}) collective-permute-start(bf16[64,1024]{1,0:T(8,128)(2,1)S(1)} %slice_bitcast_fusion.6), channel_id=1, source_target_pairs={{0,8},{4,12},{8,0},{12,4},{16,24},{20,28},{24,16},{28,20},{1,9},{5... | collective-permute-start | bytes 393224 | tf_op jit(solution)/shard_map/ppermute | solution.py:822
  598.0 25.2 %collective-permute-start.82 = (bf16[2,64,1024]{2,1,0:T(8,128)(2,1)S(1)}, bf16[2,64,1024]{2,1,0:T(8,128)(2,1)S(1)}, u32[]{:S(2)}, u32[]{:S(2)}) collective-permute-start(bf16[2,64,1024]{2,1,0:T(8,128)(2,1)S(1)} %slice.412), channel_id=1, source_target_pairs={{0,16},{4,20},{8,24},{12,28},{16,0},{20,4},{24,8},{28,12},{1,17},{... | collective-permute-start | bytes 786440 | tf_op jit(solution)/shard_map/ppermute | solution.py:822
  622.6 14.8 %collective-permute-start.97 = (bf16[2,28,2432]{2,1,0:T(8,128)(2,1)S(1)}, bf16[2,28,2432]{2,1,0:T(8,128)(2,1)S(1)}, u32[]{:S(2)}, u32[]{:S(2)}) collective-permute-start(bf16[2,28,2432]{2,1,0:T(8,128)(2,1)S(1)} %get-tuple-element.406), channel_id=1, source_target_pairs={{0,3},{1,2},{2,1},{3,0},{4,7},{5,6},{6,5},{7,4},{8,11},{9,10},{10,... | collective-permute-start | bytes 817160 | tf_op jit(solution)/shard_map/ppermute | solution.py:822
  623.2 19.2 %collective-permute-start.84 = (bf16[64,1024]{1,0:T(8,128)(2,1)S(1)}, bf16[64,1024]{1,0:T(8,128)(2,1)S(1)}, u32[]{:S(2)}, u32[]{:S(2)}) collective-permute-start(bf16[64,1024]{1,0:T(8,128)(2,1)S(1)} %slice_bitcast_fusion.8), channel_id=1, source_target_pairs={{0,8},{4,12},{8,0},{12,4},{16,24},{20,28},{24,16},{28,20},{1,9},{5... | collective-permute-start | bytes 393224 | tf_op jit(solution)/shard_map/ppermute | solution.py:822
  (161 other events, 1817.5 us)

commit v7 on v6

--- a/solution.py
+++ b/solution.py
@@ -991,12 +991,9 @@
     attn_sets = [attn_finish(first_parts)]
     for layer in range(LAYERS):
         first_full, second_full, gain_full, mlp_gain_full, bias_first, bias_second = attn_sets[layer]
-        if layer == 0:
-            second_start = line_gather(after(shards[1], first_full), bits[:1])
-            second_line = line_gather(second_start, bits[1:])
         x, normed, queries, own_kv = before_attention(
             terms,
-            after(gain_full, near[0], second_start) if layer == 0 else after(gain_full, near_pair[1]),
+            after(gain_full, near[0]) if layer == 0 else after(gain_full, near_pair[1]),
             first_full,
             second_full,
             bias_first,
@@ -1005,7 +1002,7 @@
             sin_wide,
         )
         kv_blocks = [own_kv] + [swap(own_kv, "seq", bit) for bit in range(1, 4)]
-        waited = (near_pair[0], crossed[0], second_line) if layer == 0 else ()
+        waited = (near_pair[0],) if layer == 0 else ()
         mixed, middle, n2 = attention(
             queries, kv_blocks, biases, x, second_full, after(mlp_gain_full, *waited)
         )
@@ -1014,13 +1011,14 @@
             far_pair = swap(far[1], "dp", 1)
             n2_parts = group_rows(n2, far_pair)
         else:
-            n2_parts = group_rows(n2)
-        if layer == 0:
-            second_other = swap(after(second_line, n2_parts[3]), "dp", 1)
             far.append(outward(crossed[0], n2))
             far_pair = swap(far[0], "dp", 1)
-            near.append(line_gather(after(gate_shards[1], n2), bits[:-1], n2_parts[3], far[0]))
-            crossed.append(cross_middle(near[1]))
+            n2_parts = group_rows(after(n2, far[0]))
+            second_start = line_gather(after(shards[1], n2_parts[2]), bits[:1])
+            second_line = line_gather(second_start, bits[1:])
+            second_other = swap(after(second_line, n2_parts[3]), "dp", 1)
+            near.append(line_gather(after(gate_shards[1], second_start), bits[:-1], n2_parts[3]))
+            crossed.append(cross_middle(after(near[1], second_line)))
             attn_sets.append(attn_finish(attn_parts(second_line, second_other, n2_parts[3])))
             near_pair.append(swap(after(near[1], far_pair), "dp", 1))
         mlp_sets.append(mlp_finish(layer, far_pair))
@@ -1068,13 +1066,20 @@
         state["terms"] = line_scatter(state["near_sum"], bits[:-1])
 
     def finish(states):
+        gate_rows, down_owned = split_rows(
+            [state["terms"] for state in states], seq_devices * width_rows, seq_place, seq_devices
+        )
         state = states[0]
         other_side = swap(after(state["attn_sums"][1], state["near_got"]), "dp", 1)
         state["owned"] = line_scatter(
             add_low(state["attn_sums"][0], other_side), bits, state["near_sum"]
         )
         owned = jnp.stack(
-            [sum(term.astype(jnp.float32) for term in state["owned"]) for state in states]
+            [
+                state["owned"][0].astype(jnp.float32)
+                + after(state["owned"][1], gate_rows[0]).astype(jnp.float32)
+                for state in states
+            ]
         )
         extra = owned[:, chip_rows:]
         halves = owned[:, :chip_rows].reshape(LAYERS, 2, width_rows, -1)
@@ -1089,9 +1094,6 @@
             start = (0, row, device * width)
             return lax.dynamic_slice(extra[:, :, :stop], start, (LAYERS, 1, width))[:, 0]
 
-        gate_rows, down_owned = split_rows(
-            [state["terms"] for state in states], seq_devices * width_rows, seq_place, seq_devices
-        )
         gate_owned = collect_columns(
             [gate_rows[0]] + [swap(gate_rows[bit], "seq", bit) for bit in range(1, 4)],
             seq_place,

time: 655 us -> 658 us (level)
  waiting for transfers between devices: 267 us -> 242 us
  starting transfers between devices: 107 us -> 125 us
  local copies, waits for them, and re-layouts: 41.6 us -> 54.3 us
    ppermute x88, waiting for transfers between devices: 253 us -> 209 us  [swap(): return lax.ppermute(values, axis, [(i, i ^ bit) for i in range(size)])]
    ppermute x10, waiting for transfers between devices: 13.7 us -> 33.2 us  [line_steps(): lax.ppermute(values, 'dp', [(2 * here + side, 2 * there + side) for here,...]
    ppermute x88, starting transfers between devices: 85.6 us -> 103 us  [swap(): return lax.ppermute(values, axis, [(i, i ^ bit) for i in range(size)])]
    unnamed x228 -> x214, local copies, waits for them, and re-layouts: 31 us -> 33.2 us
  transfers between devices with their start and end apart: 98 -> 98, of which waited for: 40 -> 39; matrix products, arithmetic and copies ran while one was open for 7% -> 8% of each run, Pallas kernels for 23% -> 23%
where the time goes in v7:
time: 658 us; the launch traced here: 651 us
  waiting for transfers between devices  242 us (37%)
  Pallas kernels  184 us (28%)
  starting transfers between devices  125 us (19%)
  local copies, waits for them, and re-layouts  54.3 us (8%)
  other arithmetic  30.4 us (5%)
  between operations  15.8 us (2%)
    ppermute x88, waiting for transfers between devices, swap(): return lax.ppermute(values, axis, [(i, i ^ bit) for i in range(size)])  209 us
    ppermute x88, starting transfers between devices, swap(): return lax.ppermute(values, axis, [(i, i ^ bit) for i in range(size)])  103 us
    pallas_call x2, Pallas kernels, feed_back(): call(kernel, [((half, packed, 2 * units), jnp.bfloat16), ((half, packed,...  65.7 us
    pallas_call x4, Pallas kernels, feed_forward(): call(kernel, [((rows, 2 * units), jnp.bfloat16)] + [((part_rows, D), jnp....  41 us
    ppermute x10, waiting for transfers between devices, line_steps(): lax.ppermute(values, 'dp', [(2 * here + side, 2 * there + side) for here,...  33.2 us
    unnamed x214, local copies, waits for them, and re-layouts  33.2 us
    pallas_call x2, Pallas kernels, attention_back(): call(kernel, [((rows, D), jnp.float32), ((rows, D), jnp.bfloat16), ((1, D...  25.1 us
    ppermute x10, starting transfers between devices, line_steps(): lax.ppermute(values, 'dp', [(2 * here + side, 2 * there + side) for here,...  22.4 us
  transfers between devices with their start and end apart: 98, of which 39 were waited for; matrix products, arithmetic and copies ran while one was open for 8% of the time, Pallas kernels for 23%

profile of v7, /device:TPU:0, one launch (start us, length us, event | category | flops | bytes accessed | tf_op | source)
XLA Modules:
  0.0 651.5 jit_solution(13624863231535376981)
XLA Ops:
  9.5 2.8 collective-permute-start.1
  16.5 2.8 collective-permute-start.2
  19.3 3.4 collective-permute-done.4.refs_2_
  22.7 5.4 collective-permute-done.5.refs_3_
  32.8 11.4 %collective-permute-done.6.refs_1_ = bf16[4,64,1024]{2,1,0:T(8,128)(2,1)S(1)} collective-permute-done((bf16[4,64,1024]{2,1,0:T(8,128)(2,1)S(1)}, bf16[4,64,1024]{2,1,0:T(8,128)(2,1)S(1)}, u32[]{:S(2)}, u32[]{:S(2)}) %collective-permute-start.6) | collective-permute-done | bytes 524320 | tf_op jit(solution)/shard_map/ppermute | solution.py:822
  48.3 10.3 %collective-permute-done.8.refs_3_ = bf16[4,64,1024]{2,1,0:T(8,128)(2,1)S(1)} collective-permute-done((bf16[4,64,1024]{2,1,0:T(8,128)(2,1)S(1)}, bf16[4,64,1024]{2,1,0:T(8,128)(2,1)S(1)}, u32[]{:S(2)}, u32[]{:S(2)}) %collective-permute-start.8) | collective-permute-done | bytes 524320 | tf_op jit(solution)/shard_map/ppermute | solution.py:822
  58.6 4.8 collective-permute-done.13
  74.7 8.8 %collective-permute-done.7.refs_2_ = bf16[4,64,1024]{2,1,0:T(8,128)(2,1)S(1)} collective-permute-done((bf16[4,64,1024]{2,1,0:T(8,128)(2,1)S(1)}, bf16[4,64,1024]{2,1,0:T(8,128)(2,1)S(1)}, u32[]{:S(2)}, u32[]{:S(2)}) %collective-permute-start.7) | collective-permute-done | bytes 524320 | tf_op jit(solution)/shard_map/ppermute | solution.py:822
  99.2 3.0 assemble.2
  116.9 11.7 %attention.2 = (bf16[256,896]{1,0:T(8,128)(2,1)S(1)}, f32[256,896]{1,0:T(8,128)S(1)}, bf16[256,896]{1,0:T(8,128)(2,1)}) custom-call(bf16[2,2,896,64]{3,2,1,0:T(8,128)(2,1)S(1)} %get-tuple-element.279.q_ref.refs_7_, bf16[256,256]{1,0:T(8,128)(2,1)} %get-tuple-element.280.kv0.refs_8_, bf16[256,256]{1,0:T(8,128)(2,1)S(1)} %copy-done.41, ...), custom_call_target="tpu_custom_call" | custom-call | bytes 42000 | tf_op jit(solution)/shard_map/attention/pallas_call | solution.py:159
  128.6 11.6 %collective-permute-done.19 = bf16[2,168,2432]{2,1,0:T(8,128)(2,1)} collective-permute-done((bf16[2,168,2432]{2,1,0:T(8,128)(2,1)}, bf16[2,168,2432]{2,1,0:T(8,128)(2,1)}, u32[]{:S(2)}, u32[]{:S(2)}) %collective-permute-start.19) | collective-permute-done | bytes 1634336 | tf_op jit(solution)/shard_map/ppermute | solution.py:843
  155.0 25.6 %collective-permute-start.25 = (bf16[1,64,1024]{2,1,0:T(8,128)(2,1)S(1)}, bf16[1,64,1024]{2,1,0:T(8,128)(2,1)S(1)}, u32[]{:S(2)}, u32[]{:S(2)}) collective-permute-start(bf16[1,64,1024]{2,1,0:T(8,128)(2,1)S(1)} %maximum_bitcast_fusion.1), channel_id=1, source_target_pairs={{0,8},{4,12},{8,0},{12,4},{16,24},{20,28},{24,16},{28,20},{1,9},{5... | collective-permute-start | bytes 393224 | tf_op jit(solution)/shard_map/ppermute | solution.py:822
  180.6 4.1 collective-permute-done.25
  191.2 18.5 %collective-permute-done.28 = bf16[2,64,1024]{2,1,0:T(8,128)(2,1)S(1)} collective-permute-done((bf16[2,64,1024]{2,1,0:T(8,128)(2,1)S(1)}, bf16[2,64,1024]{2,1,0:T(8,128)(2,1)S(1)}, u32[]{:S(2)}, u32[]{:S(2)}) %collective-permute-start.28) | collective-permute-done | bytes 262176 | tf_op jit(solution)/shard_map/ppermute | solution.py:822
  214.8 10.5 %collective-permute-done.21.refs_3_ = bf16[2,168,2432]{2,1,0:T(8,128)(2,1)} collective-permute-done((bf16[2,168,2432]{2,1,0:T(8,128)(2,1)S(1)}, bf16[2,168,2432]{2,1,0:T(8,128)(2,1)}, u32[]{:S(2)}, u32[]{:S(2)}) %collective-permute-start.21) | collective-permute-done | bytes 1634336 | tf_op jit(solution)/shard_map/ppermute | solution.py:822
  226.8 2.9 unpack.2
  233.0 10.2 %feed_forward.4 = (bf16[512,2432]{1,0:T(8,128)(2,1)}, bf16[256,896]{1,0:T(8,128)(2,1)}, bf16[256,896]{1,0:T(8,128)(2,1)}) custom-call(bf16[256,896]{1,0:T(8,128)(2,1)} %get-tuple-element.287.refs_0_.refs_5_, bf16[256,896]{1,0:T(8,128)(2,1)} %collective-permute-done.20.refs_1_.refs_6_, bf16[896,2432]{1,0:T(8,128)(2,1)} %bitcast.146, bf16[1216,896]{1,0:T(8,128)(2,1)} %bitcast.160), custom_call_target="tpu_custom_call" | custom-call | bytes 36000 | tf_op jit(solution)/shard_map/feed_forward/pallas_call | solution.py:204
  245.1 10.4 %feed_forward.5 = (bf16[512,2432]{1,0:T(8,128)(2,1)}, bf16[256,896]{1,0:T(8,128)(2,1)}, bf16[256,896]{1,0:T(8,128)(2,1)}) custom-call(bf16[256,896]{1,0:T(8,128)(2,1)} %collective-permute-done.23.refs_0_.refs_7_, bf16[256,896]{1,0:T(8,128)(2,1)} %collective-permute-done.27.refs_1_.refs_8_, bf16[896,2432]{1,0:T(8,128)(2,1)} %bitcast.147, ...), custom_call_target="tpu_custom_call" | custom-call | bytes 36000 | tf_op jit(solution)/shard_map/feed_forward/pallas_call | solution.py:204
  261.1 3.0 assemble.3
  264.1 5.8 collective-permute-done.39.refs_2_
  274.1 14.5 %collective-permute-done.44 = bf16[2,168,2432]{2,1,0:T(8,128)(2,1)} collective-permute-done((bf16[2,168,2432]{2,1,0:T(8,128)(2,1)}, bf16[2,168,2432]{2,1,0:T(8,128)(2,1)}, u32[]{:S(2)}, u32[]{:S(2)}) %collective-permute-start.44) | collective-permute-done | bytes 1634336 | tf_op jit(solution)/shard_map/ppermute | solution.py:843
  293.7 4.4 collective-permute-done.41.kv2.refs_10_
  300.2 9.9 %attention.3 = (bf16[256,896]{1,0:T(8,128)(2,1)S(1)}, f32[256,896]{1,0:T(8,128)S(1)}, bf16[256,896]{1,0:T(8,128)(2,1)S(1)}) custom-call(bf16[2,2,896,64]{3,2,1,0:T(8,128)(2,1)S(1)} %get-tuple-element.311.q_ref.refs_7_, bf16[256,256]{1,0:T(8,128)(2,1)S(1)} %get-tuple-element.312.kv0.refs_8_, bf16[256,256]{1,0:T(8,128)(2,1)S(1)} %collective-permute-done.40.kv1.refs_9_, ...), custom_call_target="tpu_custom_call" | custom-call | bytes 42000 | tf_op jit(solution)/shard_map/attention/pallas_call | solution.py:159
  312.3 12.4 %collective-permute-done.47.refs_0_.refs_7_ = bf16[256,896]{1,0:T(8,128)(2,1)S(1)} collective-permute-done((bf16[256,896]{1,0:T(8,128)(2,1)S(1)}, bf16[256,896]{1,0:T(8,128)(2,1)S(1)}, u32[]{:S(2)}, u32[]{:S(2)}) %collective-permute-start.47) | collective-permute-done | bytes 458784 | tf_op jit(solution)/shard_map/ppermute | solution.py:822
  327.7 2.9 unpack.3
  334.7 10.2 %feed_forward.6 = (bf16[512,2432]{1,0:T(8,128)(2,1)}, bf16[256,896]{1,0:T(8,128)(2,1)}, bf16[256,896]{1,0:T(8,128)(2,1)}) custom-call(bf16[256,896]{1,0:T(8,128)(2,1)} %copy-done.31, bf16[256,896]{1,0:T(8,128)(2,1)} %copy-done.75, bf16[896,2432]{1,0:T(8,128)(2,1)} %bitcast.149, bf16[1216,896]{1,0:T(8,128)(2,1)} %bitcast.163), custom_call_target="tpu_custom_call" | custom-call | bytes 36000 | tf_op jit(solution)/shard_map/feed_forward/pallas_call | solution.py:204
  345.5 10.2 %feed_forward.7 = (bf16[512,2432]{1,0:T(8,128)(2,1)}, bf16[256,896]{1,0:T(8,128)(2,1)}, bf16[256,896]{1,0:T(8,128)(2,1)}) custom-call(bf16[256,896]{1,0:T(8,128)(2,1)} %copy-done.73, bf16[256,896]{1,0:T(8,128)(2,1)} %copy-done.74, bf16[896,2432]{1,0:T(8,128)(2,1)} %bitcast.150, bf16[1216,896]{1,0:T(8,128)(2,1)} %bitcast.164), custom_call_target="tpu_custom_call" | custom-call | bytes 36000 | tf_op jit(solution)/shard_map/feed_forward/pallas_call | solution.py:204
  356.5 33.0 %feed_back.2 = (bf16[2,168,2432]{2,1,0:T(8,128)(2,1)}, bf16[2,168,2432]{2,1,0:T(8,128)(2,1)}, bf16[256,896]{1,0:T(8,128)(2,1)}, bf16[256,896]{1,0:T(8,128)(2,1)}...) custom-call(s32[1]{0:T(128)} %bitcast.3.refs_0_, ...), custom_call_target="tpu_custom_call" | custom-call | bytes 100000 | tf_op jit(solution)/shard_map/feed_back/pallas_call | solution.py:324
  395.5 10.8 %collective-permute-done.54.refs_5_ = bf16[256,896]{1,0:T(8,128)(2,1)S(1)} collective-permute-done((bf16[256,896]{1,0:T(8,128)(2,1)S(1)}, bf16[256,896]{1,0:T(8,128)(2,1)S(1)}, u32[]{:S(2)}, u32[]{:S(2)}) %collective-permute-start.54) | collective-permute-done | bytes 458784 | tf_op jit(solution)/shard_map/ppermute | solution.py:822
  409.7 12.1 %attention_back.2 = (f32[256,896]{1,0:T(8,128)S(1)}, bf16[256,896]{1,0:T(8,128)(2,1)S(1)}, f32[1,896]{1,0:T(1,128)S(1)}, bf16[256,896]{1,0:T(8,128)(2,1)S(1)}, f...) custom-call(bf16[256,896]{1,0:T(8,128)(2,1)S(1)} %bitcast.173, ...), custom_call_target="tpu_custom_call" | custom-call | bytes 52000 | tf_op jit(solution)/shard_map/attention_back/pallas_call | solution.py:465
  424.2 4.4 collective-permute-done.56.refs_2_
  438.5 7.0 %collective-permute-done.58.refs_3_ = bf16[256,896]{1,0:T(8,128)(2,1)S(1)} collective-permute-done((bf16[256,896]{1,0:T(8,128)(2,1)S(1)}, bf16[256,896]{1,0:T(8,128)(2,1)S(1)}, u32[]{:S(2)}, u32[]{:S(2)}) %collective-permute-start.58) | collective-permute-done | bytes 458784 | tf_op jit(solution)/shard_map/ppermute | solution.py:822
  447.1 4.3 collective-permute-start.68
  458.6 32.7 %feed_back.3 = (bf16[2,168,2432]{2,1,0:T(8,128)(2,1)}, bf16[2,168,2432]{2,1,0:T(8,128)(2,1)}, bf16[256,896]{1,0:T(8,128)(2,1)}, bf16[256,896]{1,0:T(8,128)(2,1)}...) custom-call(s32[1]{0:T(128)} %bitcast.3.refs_0_, ...), custom_call_target="tpu_custom_call" | custom-call | bytes 100000 | tf_op jit(solution)/shard_map/feed_back/pallas_call | solution.py:324
  501.5 11.2 %collective-permute-done.71 = bf16[1,168,2432]{2,1,0:T(8,128)(2,1)S(1)} collective-permute-done((bf16[1,168,2432]{2,1,0:T(8,128)(2,1)}, bf16[1,168,2432]{2,1,0:T(8,128)(2,1)S(1)}, u32[]{:S(2)}, u32[]{:S(2)}) %collective-permute-start.71) | collective-permute-done | bytes 817184 | tf_op jit(solution)/shard_map/ppermute | solution.py:822
  515.8 13.1 %attention_back.3 = (f32[256,896]{1,0:T(8,128)S(1)}, bf16[256,896]{1,0:T(8,128)(2,1)S(1)}, f32[1,896]{1,0:T(1,128)S(1)}, bf16[256,896]{1,0:T(8,128)(2,1)S(1)}, f...) custom-call(f32[256,896]{1,0:T(8,128)S(1)} %copy-done.37, ...), custom_call_target="tpu_custom_call" | custom-call | bytes 52000 | tf_op jit(solution)/shard_map/attention_back/pallas_call | solution.py:465
  532.1 7.5 %collective-permute-start.86 = (bf16[1,168,2432]{2,1,0:T(8,128)(2,1)S(1)}, bf16[1,168,2432]{2,1,0:T(8,128)(2,1)S(1)}, u32[]{:S(2)}, u32[]{:S(2)}) collective-permute-start(bf16[1,168,2432]{2,1,0:T(8,128)(2,1)S(1)} %add_convert_fusion.7), channel_id=1, source_target_pairs={{0,8},{4,12},{24,16},{28,20},{1,9},{5,13},{25,17},{29,21},{2,10},{... | collective-permute-start | bytes 2451464 | tf_op jit(solution)/shard_map/ppermute | solution.py:843
  548.8 7.1 %collective-permute-done.86 = bf16[1,168,2432]{2,1,0:T(8,128)(2,1)S(1)} collective-permute-done((bf16[1,168,2432]{2,1,0:T(8,128)(2,1)S(1)}, bf16[1,168,2432]{2,1,0:T(8,128)(2,1)S(1)}, u32[]{:S(2)}, u32[]{:S(2)}) %collective-permute-start.86) | collective-permute-done | bytes 817184 | tf_op jit(solution)/shard_map/ppermute | solution.py:843
  560.3 11.4 %collective-permute-done.79 = bf16[4,64,1024]{2,1,0:T(8,128)(2,1)S(1)} collective-permute-done((bf16[4,64,1024]{2,1,0:T(8,128)(2,1)S(1)}, bf16[4,64,1024]{2,1,0:T(8,128)(2,1)S(1)}, u32[]{:S(2)}, u32[]{:S(2)}) %collective-permute-start.79) | collective-permute-done | bytes 524320 | tf_op jit(solution)/shard_map/ppermute | solution.py:822
  571.7 4.0 collective-permute-start.90
  576.9 3.2 collective-permute-done.80
  582.9 5.5 collective-permute-start.88
  588.5 11.5 %collective-permute-done.92 = bf16[2,64,1024]{2,1,0:T(8,128)(2,1)S(1)} collective-permute-done((bf16[2,64,1024]{2,1,0:T(8,128)(2,1)S(1)}, bf16[2,64,1024]{2,1,0:T(8,128)(2,1)S(1)}, u32[]{:S(2)}, u32[]{:S(2)}) %collective-permute-start.92) | collective-permute-done | bytes 262176 | tf_op jit(solution)/shard_map/ppermute | solution.py:822
  600.1 3.4 collective-permute-start.93
  606.1 17.5 %collective-permute-done.88.refs_1_ = bf16[168,2432]{1,0:T(8,128)(2,1)S(1)} collective-permute-done((bf16[168,2432]{1,0:T(8,128)(2,1)S(1)}, bf16[168,2432]{1,0:T(8,128)(2,1)S(1)}, u32[]{:S(2)}, u32[]{:S(2)}) %collective-permute-start.88) | collective-permute-done | bytes 817184 | tf_op jit(solution)/shard_map/ppermute | solution.py:822
  627.8 7.8 %collective-permute-done.96.refs_2_ = bf16[2,28,2432]{2,1,0:T(8,128)(2,1)S(1)} collective-permute-done((bf16[2,28,2432]{2,1,0:T(8,128)(2,1)S(1)}, bf16[2,28,2432]{2,1,0:T(8,128)(2,1)S(1)}, u32[]{:S(2)}, u32[]{:S(2)}) %collective-permute-start.96) | collective-permute-done | bytes 272416 | tf_op jit(solution)/shard_map/ppermute | solution.py:822
  635.6 5.9 collective-permute-done.97.refs_3_
  643.5 3.0 copy.58
  (504 shorter events, 187.8 us)
Async XLA Ops:
  14.0 14.1 %collective-permute-start.5 = (bf16[2,28,2432]{2,1,0:T(8,128)(2,1)S(1)}, bf16[2,28,2432]{2,1,0:T(8,128)(2,1)S(1)}, u32[]{:S(2)}, u32[]{:S(2)}) collective-permute-start(bf16[2,28,2432]{2,1,0:T(8,128)(2,1)S(1)} %get-tuple-element.264), channel_id=1, source_target_pairs={{0,3},{1,2},{2,1},{3,0},{4,7},{5,6},{6,5},{7,4},{8,11},{9,10},{10,... | collective-permute-start | bytes 817160 | tf_op jit(solution)/shard_map/ppermute | solution.py:822
  16.5 14.7 %collective-permute-start.2 = (bf16[2,64,1024]{2,1,0:T(8,128)(2,1)S(1)}, bf16[2,64,1024]{2,1,0:T(8,128)(2,1)S(1)}, u32[]{:S(2)}, u32[]{:S(2)}) collective-permute-start(bf16[2,64,1024]{2,1,0:T(8,128)(2,1)S(1)} %pad_maximum_fusion.6), channel_id=1, source_target_pairs={{0,16},{4,20},{8,24},{12,28},{16,0},{20,4},{24,8},{28,12},{1,17},{... | collective-permute-start | bytes 786440 | tf_op jit(solution)/shard_map/ppermute | solution.py:822
  44.2 19.1 %collective-permute-start.13 = (bf16[1,168,2432]{2,1,0:T(8,128)(2,1)S(1)}, bf16[1,168,2432]{2,1,0:T(8,128)(2,1)S(1)}, u32[]{:S(2)}, u32[]{:S(2)}) collective-permute-start(bf16[1,168,2432]{2,1,0:T(8,128)(2,1)S(1)} %get-tuple-element.274), channel_id=1, source_target_pairs={{0,8},{4,12},{8,0},{12,4},{16,24},{20,28},{24,16},{28,20},{1,9},{5... | collective-permute-start | bytes 2451464 | tf_op jit(solution)/shard_map/ppermute | solution.py:822
  68.2 42.7 %collective-permute-start.17 = (bf16[2,168,2432]{2,1,0:T(8,128)(2,1)}, bf16[2,168,2432]{2,1,0:T(8,128)(2,1)}, u32[]{:S(2)}, u32[]{:S(2)}) collective-permute-start(bf16[2,168,2432]{2,1,0:T(8,128)(2,1)} %constant_dynamic-update-slice_fusion.refs_0_), channel_id=1, source_target_pairs={{0,4},{4,0},{8,12},{12,8},{16,20},{20,16},{24,28},{28,24},{1,5},{5... | collective-permute-start | bytes 4902920 | tf_op jit(solution)/shard_map/ppermute | solution.py:822
  69.8 70.4 %collective-permute-start.19 = (bf16[2,168,2432]{2,1,0:T(8,128)(2,1)}, bf16[2,168,2432]{2,1,0:T(8,128)(2,1)}, u32[]{:S(2)}, u32[]{:S(2)}) collective-permute-start(bf16[2,168,2432]{2,1,0:T(8,128)(2,1)} %collective-permute-done.18), channel_id=1, source_target_pairs={{8,0},{12,4},{16,24},{20,28},{9,1},{13,5},{17,25},{21,29},{10,2},{... | collective-permute-start | bytes 4902920 | tf_op jit(solution)/shard_map/ppermute | solution.py:843
  74.1 21.9 %collective-permute-start.10 = (bf16[4,64,1024]{2,1,0:T(8,128)(2,1)S(1)}, bf16[4,64,1024]{2,1,0:T(8,128)(2,1)}, u32[]{:S(2)}, u32[]{:S(2)}) collective-permute-start(bf16[4,64,1024]{2,1,0:T(8,128)(2,1)S(1)} %collective-permute-done.6.refs_1_), channel_id=1, source_target_pairs={{0,1},{1,0},{2,3},{3,2},{4,5},{5,4},{6,7},{7,6},{8,9},{9,8},{10,11... | collective-permute-start | bytes 1572872 | tf_op jit(solution)/shard_map/ppermute | solution.py:822
  155.0 29.7 %collective-permute-start.25 = (bf16[1,64,1024]{2,1,0:T(8,128)(2,1)S(1)}, bf16[1,64,1024]{2,1,0:T(8,128)(2,1)S(1)}, u32[]{:S(2)}, u32[]{:S(2)}) collective-permute-start(bf16[1,64,1024]{2,1,0:T(8,128)(2,1)S(1)} %maximum_bitcast_fusion.1), channel_id=1, source_target_pairs={{0,8},{4,12},{8,0},{12,4},{16,24},{20,28},{24,16},{28,20},{1,9},{5... | collective-permute-start | bytes 393224 | tf_op jit(solution)/shard_map/ppermute | solution.py:822
  184.7 25.9 %collective-permute-start.26 = (bf16[1,168,2432]{2,1,0:T(8,128)(2,1)}, bf16[1,168,2432]{2,1,0:T(8,128)(2,1)S(1)}, u32[]{:S(2)}, u32[]{:S(2)}) collective-permute-start(bf16[1,168,2432]{2,1,0:T(8,128)(2,1)} %copy-done.38), channel_id=1, source_target_pairs={{0,8},{4,12},{8,0},{12,4},{16,24},{20,28},{24,16},{28,20},{1,9},{5... | collective-permute-start | bytes 2451464 | tf_op jit(solution)/shard_map/ppermute | solution.py:822
  186.5 38.8 %collective-permute-start.21 = (bf16[2,168,2432]{2,1,0:T(8,128)(2,1)S(1)}, bf16[2,168,2432]{2,1,0:T(8,128)(2,1)}, u32[]{:S(2)}, u32[]{:S(2)}) collective-permute-start(bf16[2,168,2432]{2,1,0:T(8,128)(2,1)S(1)} %broadcast_select_fusion.1.refs_1_), channel_id=1, source_target_pairs={{0,4},{4,0},{8,12},{12,8},{16,20},{20,16},{24,28},{28,24},{1,5},{5... | collective-permute-start | bytes 4902920 | tf_op jit(solution)/shard_map/ppermute | solution.py:822
  187.9 22.6 %collective-permute-start.27 = (bf16[256,896]{1,0:T(8,128)(2,1)}, bf16[256,896]{1,0:T(8,128)(2,1)}, u32[]{:S(2)}, u32[]{:S(2)}) collective-permute-start(bf16[256,896]{1,0:T(8,128)(2,1)} %collective-permute-done.23.refs_0_.refs_7_), channel_id=1, source_target_pairs={{0,1},{1,0},{2,3},{3,2},{4,5},{5,4},{6,7},{7,6},{8,9},{9,8},{10,11... | collective-permute-start | bytes 1376264 | tf_op jit(solution)/shard_map/ppermute | solution.py:822
  187.9 21.7 %collective-permute-start.28 = (bf16[2,64,1024]{2,1,0:T(8,128)(2,1)S(1)}, bf16[2,64,1024]{2,1,0:T(8,128)(2,1)S(1)}, u32[]{:S(2)}, u32[]{:S(2)}) collective-permute-start(bf16[2,64,1024]{2,1,0:T(8,128)(2,1)S(1)} %pad_maximum_fusion.7), channel_id=1, source_target_pairs={{0,16},{4,20},{8,24},{12,28},{16,0},{20,4},{24,8},{28,12},{1,17},{... | collective-permute-start | bytes 786440 | tf_op jit(solution)/shard_map/ppermute | solution.py:822
  211.6 31.6 %collective-permute-start.29 = (bf16[2,168,2432]{2,1,0:T(8,128)(2,1)}, bf16[2,168,2432]{2,1,0:T(8,128)(2,1)}, u32[]{:S(2)}, u32[]{:S(2)}) collective-permute-start(bf16[2,168,2432]{2,1,0:T(8,128)(2,1)} %constant_dynamic-update-slice_fusion.2.refs_0_), channel_id=1, source_target_pairs={{8,16},{12,20},{16,8},{20,12},{9,17},{13,21},{17,9},{21,13},{10,18... | collective-permute-start | bytes 4902920 | tf_op jit(solution)/shard_map/ppermute | solution.py:843
  213.4 19.6 %collective-permute-start.20 = (bf16[256,896]{1,0:T(8,128)(2,1)}, bf16[256,896]{1,0:T(8,128)(2,1)}, u32[]{:S(2)}, u32[]{:S(2)}) collective-permute-start(bf16[256,896]{1,0:T(8,128)(2,1)} %get-tuple-element.287.refs_0_.refs_5_), channel_id=1, source_target_pairs={{0,1},{1,0},{2,3},{3,2},{4,5},{5,4},{6,7},{7,6},{8,9},{9,8},{10,11... | collective-permute-start | bytes 1376264 | tf_op jit(solution)/shard_map/ppermute | solution.py:822
  213.4 31.1 %collective-permute-start.32 = (bf16[4,64,1024]{2,1,0:T(8,128)(2,1)}, bf16[4,64,1024]{2,1,0:T(8,128)(2,1)}, u32[]{:S(2)}, u32[]{:S(2)}) collective-permute-start(bf16[4,64,1024]{2,1,0:T(8,128)(2,1)} %pad_maximum_fusion.2.refs_0_), channel_id=1, source_target_pairs={{0,4},{4,0},{8,12},{12,8},{16,20},{20,16},{24,28},{28,24},{1,5},{5... | collective-permute-start | bytes 1572872 | tf_op jit(solution)/shard_map/ppermute | solution.py:822
  214.8 40.8 %collective-permute-start.33 = (bf16[4,64,1024]{2,1,0:T(8,128)(2,1)}, bf16[4,64,1024]{2,1,0:T(8,128)(2,1)}, u32[]{:S(2)}, u32[]{:S(2)}) collective-permute-start(bf16[4,64,1024]{2,1,0:T(8,128)(2,1)} %pad_maximum_fusion.2.refs_0_), channel_id=1, source_target_pairs={{0,2},{1,3},{2,0},{3,1},{4,6},{5,7},{6,4},{7,5},{8,10},{9,11},{10,... | collective-permute-start | bytes 1572872 | tf_op jit(solution)/shard_map/ppermute | solution.py:822
  225.3 44.6 %collective-permute-start.39 = (bf16[2,168,2432]{2,1,0:T(8,128)(2,1)}, bf16[2,168,2432]{2,1,0:T(8,128)(2,1)}, u32[]{:S(2)}, u32[]{:S(2)}) collective-permute-start(bf16[2,168,2432]{2,1,0:T(8,128)(2,1)} %constant_dynamic-update-slice_fusion.2.refs_0_), channel_id=1, source_target_pairs={{0,4},{4,0},{8,12},{12,8},{16,20},{20,16},{24,28},{28,24},{1,5},{5... | collective-permute-start | bytes 4902920 | tf_op jit(solution)/shard_map/ppermute | solution.py:822
  243.2 45.4 %collective-permute-start.44 = (bf16[2,168,2432]{2,1,0:T(8,128)(2,1)}, bf16[2,168,2432]{2,1,0:T(8,128)(2,1)}, u32[]{:S(2)}, u32[]{:S(2)}) collective-permute-start(bf16[2,168,2432]{2,1,0:T(8,128)(2,1)} %collective-permute-done.29), channel_id=1, source_target_pairs={{8,0},{12,4},{16,24},{20,28},{9,1},{13,5},{17,25},{21,29},{10,2},{... | collective-permute-start | bytes 4902920 | tf_op jit(solution)/shard_map/ppermute | solution.py:843
  290.3 34.9 %collective-permute-start.45 = (bf16[2,168,2432]{2,1,0:T(8,128)(2,1)S(1)}, bf16[2,168,2432]{2,1,0:T(8,128)(2,1)S(1)}, u32[]{:S(2)}, u32[]{:S(2)}) collective-permute-start(bf16[2,168,2432]{2,1,0:T(8,128)(2,1)S(1)} %broadcast_select_fusion.refs_1_), channel_id=1, source_target_pairs={{0,4},{4,0},{8,12},{12,8},{16,20},{20,16},{24,28},{28,24},{1,5},{5... | collective-permute-start | bytes 4902920 | tf_op jit(solution)/shard_map/ppermute | solution.py:822
  327.7 17.4 %collective-permute-start.51 = (bf16[256,896]{1,0:T(8,128)(2,1)S(1)}, bf16[256,896]{1,0:T(8,128)(2,1)}, u32[]{:S(2)}, u32[]{:S(2)}) collective-permute-start(bf16[256,896]{1,0:T(8,128)(2,1)S(1)} %bitcast.171), channel_id=1, source_target_pairs={{0,2},{1,3},{2,0},{3,1},{4,6},{5,7},{6,4},{7,5},{8,10},{9,11},{10,... | collective-permute-start | bytes 1376264 | tf_op jit(solution)/shard_map/ppermute | solution.py:822
  389.7 48.8 %collective-permute-start.67 = (bf16[2,168,2432]{2,1,0:T(8,128)(2,1)}, bf16[2,168,2432]{2,1,0:T(8,128)(2,1)S(1)}, u32[]{:S(2)}, u32[]{:S(2)}) collective-permute-start(bf16[2,168,2432]{2,1,0:T(8,128)(2,1)} %get-tuple-element.361), channel_id=1, source_target_pairs={{0,4},{4,0},{8,12},{12,8},{16,20},{20,16},{24,28},{28,24},{1,5},{5... | collective-permute-start | bytes 4902920 | tf_op jit(solution)/shard_map/ppermute | solution.py:822
  434.6 16.9 %collective-permute-start.46 = (bf16[256,896]{1,0:T(8,128)(2,1)S(1)}, bf16[256,896]{1,0:T(8,128)(2,1)S(1)}, u32[]{:S(2)}, u32[]{:S(2)}) collective-permute-start(bf16[256,896]{1,0:T(8,128)(2,1)S(1)} %copy-done.103), channel_id=1, source_target_pairs={{0,1},{1,0},{2,3},{3,2},{4,5},{5,4},{6,7},{7,6},{8,9},{9,8},{10,11... | collective-permute-start | bytes 1376264 | tf_op jit(solution)/shard_map/ppermute | solution.py:822
  434.6 56.7 %collective-permute-start.66 = (bf16[2,168,2432]{2,1,0:T(8,128)(2,1)}, bf16[2,168,2432]{2,1,0:T(8,128)(2,1)}, u32[]{:S(2)}, u32[]{:S(2)}) collective-permute-start(bf16[2,168,2432]{2,1,0:T(8,128)(2,1)} %get-tuple-element.359), channel_id=1, source_target_pairs={{0,4},{4,0},{8,12},{12,8},{16,20},{20,16},{24,28},{28,24},{1,5},{5... | collective-permute-start | bytes 4902920 | tf_op jit(solution)/shard_map/ppermute | solution.py:822
  438.2 13.8 %collective-permute-start.62 = (bf16[2,4,64,1024]{3,2,1,0:T(8,128)(2,1)S(1)}, bf16[2,4,64,1024]{3,2,1,0:T(8,128)(2,1)S(1)}, u32[]{:S(2)}, u32[]{:S(2)}) collective-permute-start(bf16[2,4,64,1024]{3,2,1,0:T(8,128)(2,1)S(1)} %get-tuple-element.350), channel_id=1, source_target_pairs={{0,1},{1,0},{2,3},{3,2},{4,5},{5,4},{6,7},{7,6},{8,9},{9,8},{10,11... | collective-permute-start | bytes 3145736 | tf_op jit(solution)/shard_map/ppermute | solution.py:822
  447.1 44.2 %collective-permute-start.68 = (bf16[2,168,2432]{2,1,0:T(8,128)(2,1)}, bf16[2,168,2432]{2,1,0:T(8,128)(2,1)}, u32[]{:S(2)}, u32[]{:S(2)}) collective-permute-start(bf16[2,168,2432]{2,1,0:T(8,128)(2,1)} %add_convert_fusion.3), channel_id=1, source_target_pairs={{0,8},{4,12},{24,16},{28,20},{1,9},{5,13},{25,17},{29,21},{2,10},{... | collective-permute-start | bytes 4902920 | tf_op jit(solution)/shard_map/ppermute | solution.py:843
  454.8 36.5 %collective-permute-start.64 = (bf16[4,64,1024]{2,1,0:T(8,128)(2,1)}, bf16[4,64,1024]{2,1,0:T(8,128)(2,1)}, u32[]{:S(2)}, u32[]{:S(2)}) collective-permute-start(bf16[4,64,1024]{2,1,0:T(8,128)(2,1)} %get-tuple-element.356), channel_id=1, source_target_pairs={{0,2},{1,3},{2,0},{3,1},{4,6},{5,7},{6,4},{7,5},{8,10},{9,11},{10,... | collective-permute-start | bytes 1572872 | tf_op jit(solution)/shard_map/ppermute | solution.py:822
  455.5 35.9 %collective-permute-start.65 = (bf16[4,64,1024]{2,1,0:T(8,128)(2,1)}, bf16[4,64,1024]{2,1,0:T(8,128)(2,1)}, u32[]{:S(2)}, u32[]{:S(2)}) collective-permute-start(bf16[4,64,1024]{2,1,0:T(8,128)(2,1)} %get-tuple-element.357), channel_id=1, source_target_pairs={{0,2},{1,3},{2,0},{3,1},{4,6},{5,7},{6,4},{7,5},{8,10},{9,11},{10,... | collective-permute-start | bytes 1572872 | tf_op jit(solution)/shard_map/ppermute | solution.py:822
  458.0 33.3 %collective-permute-start.60 = (bf16[256,896]{1,0:T(8,128)(2,1)S(1)}, bf16[256,896]{1,0:T(8,128)(2,1)}, u32[]{:S(2)}, u32[]{:S(2)}) collective-permute-start(bf16[256,896]{1,0:T(8,128)(2,1)S(1)} %add_convert_fusion.19), channel_id=1, source_target_pairs={{0,2},{1,3},{2,0},{3,1},{4,6},{5,7},{6,4},{7,5},{8,10},{9,11},{10,... | collective-permute-start | bytes 1376264 | tf_op jit(solution)/shard_map/ppermute | solution.py:822
  491.4 21.3 %collective-permute-start.71 = (bf16[1,168,2432]{2,1,0:T(8,128)(2,1)}, bf16[1,168,2432]{2,1,0:T(8,128)(2,1)S(1)}, u32[]{:S(2)}, u32[]{:S(2)}) collective-permute-start(bf16[1,168,2432]{2,1,0:T(8,128)(2,1)} %get-tuple-element.368), channel_id=1, source_target_pairs={{0,4},{4,0},{8,12},{12,8},{16,20},{20,16},{24,28},{28,24},{1,5},{5... | collective-permute-start | bytes 2451464 | tf_op jit(solution)/shard_map/ppermute | solution.py:822
  495.8 16.9 %collective-permute-start.70 = (bf16[256,896]{1,0:T(8,128)(2,1)S(1)}, bf16[256,896]{1,0:T(8,128)(2,1)S(1)}, u32[]{:S(2)}, u32[]{:S(2)}) collective-permute-start(bf16[256,896]{1,0:T(8,128)(2,1)S(1)} %fusion.4), channel_id=1, source_target_pairs={{0,2},{1,3},{2,0},{3,1},{4,6},{5,7},{6,4},{7,5},{8,10},{9,11},{10,... | collective-permute-start | bytes 1376264 | tf_op jit(solution)/shard_map/ppermute | solution.py:822
  499.6 32.5 %collective-permute-start.89 = (bf16[2,168,2432]{2,1,0:T(8,128)(2,1)S(1)}, bf16[2,168,2432]{2,1,0:T(8,128)(2,1)S(1)}, u32[]{:S(2)}, u32[]{:S(2)}) collective-permute-start(bf16[2,168,2432]{2,1,0:T(8,128)(2,1)S(1)} %add_convert_fusion.1), channel_id=1, source_target_pairs={{8,16},{12,20},{16,8},{20,12},{9,17},{13,21},{17,9},{21,13},{10,18... | collective-permute-start | bytes 4902920 | tf_op jit(solution)/shard_map/ppermute | solution.py:843
  500.4 30.0 %collective-permute-start.85 = (bf16[1,168,2432]{2,1,0:T(8,128)(2,1)S(1)}, bf16[1,168,2432]{2,1,0:T(8,128)(2,1)S(1)}, u32[]{:S(2)}, u32[]{:S(2)}) collective-permute-start(bf16[1,168,2432]{2,1,0:T(8,128)(2,1)S(1)} %copy-done.101), channel_id=1, source_target_pairs={{0,4},{4,0},{8,12},{12,8},{16,20},{20,16},{24,28},{28,24},{1,5},{5... | collective-permute-start | bytes 2451464 | tf_op jit(solution)/shard_map/ppermute | solution.py:822
  513.0 26.5 %collective-permute-start.72 = (bf16[1,168,2432]{2,1,0:T(8,128)(2,1)S(1)}, bf16[1,168,2432]{2,1,0:T(8,128)(2,1)S(1)}, u32[]{:S(2)}, u32[]{:S(2)}) collective-permute-start(bf16[1,168,2432]{2,1,0:T(8,128)(2,1)S(1)} %add_convert_fusion.11), channel_id=1, source_target_pairs={{0,8},{4,12},{24,16},{28,20},{1,9},{5,13},{25,17},{29,21},{2,10},{... | collective-permute-start | bytes 2451464 | tf_op jit(solution)/shard_map/ppermute | solution.py:843
  530.3 27.0 %collective-permute-start.91 = (bf16[4,64,1024]{2,1,0:T(8,128)(2,1)S(1)}, bf16[4,64,1024]{2,1,0:T(8,128)(2,1)S(1)}, u32[]{:S(2)}, u32[]{:S(2)}) collective-permute-start(bf16[4,64,1024]{2,1,0:T(8,128)(2,1)S(1)} %fusion), channel_id=1, source_target_pairs={{0,4},{4,0},{8,12},{12,8},{16,20},{20,16},{24,28},{28,24},{1,5},{5... | collective-permute-start | bytes 1572872 | tf_op jit(solution)/shard_map/ppermute | solution.py:822
  532.1 23.8 %collective-permute-start.86 = (bf16[1,168,2432]{2,1,0:T(8,128)(2,1)S(1)}, bf16[1,168,2432]{2,1,0:T(8,128)(2,1)S(1)}, u32[]{:S(2)}, u32[]{:S(2)}) collective-permute-start(bf16[1,168,2432]{2,1,0:T(8,128)(2,1)S(1)} %add_convert_fusion.7), channel_id=1, source_target_pairs={{0,8},{4,12},{24,16},{28,20},{1,9},{5,13},{25,17},{29,21},{2,10},{... | collective-permute-start | bytes 2451464 | tf_op jit(solution)/shard_map/ppermute | solution.py:843
  541.9 38.1 %collective-permute-start.80 = (bf16[2,168,2432]{2,1,0:T(8,128)(2,1)S(1)}, bf16[2,168,2432]{2,1,0:T(8,128)(2,1)S(1)}, u32[]{:S(2)}, u32[]{:S(2)}) collective-permute-start(bf16[2,168,2432]{2,1,0:T(8,128)(2,1)S(1)} %copy-done.100), channel_id=1, source_target_pairs={{0,4},{4,0},{8,12},{12,8},{16,20},{20,16},{24,28},{28,24},{1,5},{5... | collective-permute-start | bytes 4902920 | tf_op jit(solution)/shard_map/ppermute | solution.py:822
  548.1 32.9 %collective-permute-start.83 = (bf16[1,168,2432]{2,1,0:T(8,128)(2,1)S(1)}, bf16[1,168,2432]{2,1,0:T(8,128)(2,1)S(1)}, u32[]{:S(2)}, u32[]{:S(2)}) collective-permute-start(bf16[1,168,2432]{2,1,0:T(8,128)(2,1)S(1)} %add_convert_fusion.9), channel_id=1, source_target_pairs={{8,16},{12,20},{16,8},{20,12},{9,17},{13,21},{17,9},{21,13},{10,18... | collective-permute-start | bytes 2451464 | tf_op jit(solution)/shard_map/ppermute | solution.py:843
  555.9 19.8 %collective-permute-start.76 = (bf16[2,4,64,1024]{3,2,1,0:T(8,128)(2,1)S(1)}, bf16[2,4,64,1024]{3,2,1,0:T(8,128)(2,1)S(1)}, u32[]{:S(2)}, u32[]{:S(2)}) collective-permute-start(bf16[2,4,64,1024]{3,2,1,0:T(8,128)(2,1)S(1)} %get-tuple-element.385), channel_id=1, source_target_pairs={{0,1},{1,0},{2,3},{3,2},{4,5},{5,4},{6,7},{7,6},{8,9},{9,8},{10,11... | collective-permute-start | bytes 3145736 | tf_op jit(solution)/shard_map/ppermute | solution.py:822
  556.1 26.2 %collective-permute-start.87 = (bf16[1,168,2432]{2,1,0:T(8,128)(2,1)S(1)}, bf16[1,168,2432]{2,1,0:T(8,128)(2,1)S(1)}, u32[]{:S(2)}, u32[]{:S(2)}) collective-permute-start(bf16[1,168,2432]{2,1,0:T(8,128)(2,1)S(1)} %add_convert_fusion.6), channel_id=1, source_target_pairs={{8,16},{12,20},{16,8},{20,12},{9,17},{13,21},{17,9},{21,13},{10,18... | collective-permute-start | bytes 2451464 | tf_op jit(solution)/shard_map/ppermute | solution.py:843
  557.3 14.4 %collective-permute-start.79 = (bf16[4,64,1024]{2,1,0:T(8,128)(2,1)S(1)}, bf16[4,64,1024]{2,1,0:T(8,128)(2,1)S(1)}, u32[]{:S(2)}, u32[]{:S(2)}) collective-permute-start(bf16[4,64,1024]{2,1,0:T(8,128)(2,1)S(1)} %get-tuple-element.449), channel_id=1, source_target_pairs={{0,2},{1,3},{2,0},{3,1},{4,6},{5,7},{6,4},{7,5},{8,10},{9,11},{10,... | collective-permute-start | bytes 1572872 | tf_op jit(solution)/shard_map/ppermute | solution.py:822
  571.7 34.3 %collective-permute-start.90 = (bf16[168,2432]{1,0:T(8,128)(2,1)S(1)}, bf16[168,2432]{1,0:T(8,128)(2,1)S(1)}, u32[]{:S(2)}, u32[]{:S(2)}) collective-permute-start(bf16[168,2432]{1,0:T(8,128)(2,1)S(1)} %get-tuple-element.452), channel_id=1, source_target_pairs={{0,8},{4,12},{8,0},{12,4},{16,24},{20,28},{24,16},{28,20},{1,9},{5... | collective-permute-start | bytes 2451464 | tf_op jit(solution)/shard_map/ppermute | solution.py:822
  575.7 24.3 %collective-permute-start.92 = (bf16[2,64,1024]{2,1,0:T(8,128)(2,1)S(1)}, bf16[2,64,1024]{2,1,0:T(8,128)(2,1)S(1)}, u32[]{:S(2)}, u32[]{:S(2)}) collective-permute-start(bf16[2,64,1024]{2,1,0:T(8,128)(2,1)S(1)} %slice.422), channel_id=1, source_target_pairs={{0,16},{4,20},{8,24},{12,28},{16,0},{20,4},{24,8},{28,12},{1,17},{... | collective-permute-start | bytes 786440 | tf_op jit(solution)/shard_map/ppermute | solution.py:822
  580.0 23.5 %collective-permute-start.78 = (bf16[4,64,1024]{2,1,0:T(8,128)(2,1)S(1)}, bf16[4,64,1024]{2,1,0:T(8,128)(2,1)S(1)}, u32[]{:S(2)}, u32[]{:S(2)}) collective-permute-start(bf16[4,64,1024]{2,1,0:T(8,128)(2,1)S(1)} %get-tuple-element.448), channel_id=1, source_target_pairs={{0,2},{1,3},{2,0},{3,1},{4,6},{5,7},{6,4},{7,5},{8,10},{9,11},{10,... | collective-permute-start | bytes 1572872 | tf_op jit(solution)/shard_map/ppermute | solution.py:822
  581.0 22.5 %collective-permute-start.81 = (bf16[4,64,1024]{2,1,0:T(8,128)(2,1)S(1)}, bf16[4,64,1024]{2,1,0:T(8,128)(2,1)S(1)}, u32[]{:S(2)}, u32[]{:S(2)}) collective-permute-start(bf16[4,64,1024]{2,1,0:T(8,128)(2,1)S(1)} %fusion.2), channel_id=1, source_target_pairs={{0,4},{4,0},{8,12},{12,8},{16,20},{20,16},{24,28},{28,24},{1,5},{5... | collective-permute-start | bytes 1572872 | tf_op jit(solution)/shard_map/ppermute | solution.py:822
  582.9 40.6 %collective-permute-start.88 = (bf16[168,2432]{1,0:T(8,128)(2,1)S(1)}, bf16[168,2432]{1,0:T(8,128)(2,1)S(1)}, u32[]{:S(2)}, u32[]{:S(2)}) collective-permute-start(bf16[168,2432]{1,0:T(8,128)(2,1)S(1)} %get-tuple-element.447), channel_id=1, source_target_pairs={{0,8},{4,12},{8,0},{12,4},{16,24},{20,28},{24,16},{28,20},{1,9},{5... | collective-permute-start | bytes 2451464 | tf_op jit(solution)/shard_map/ppermute | solution.py:822
  600.1 25.3 %collective-permute-start.93 = (bf16[64,1024]{1,0:T(8,128)(2,1)S(1)}, bf16[64,1024]{1,0:T(8,128)(2,1)S(1)}, u32[]{:S(2)}, u32[]{:S(2)}) collective-permute-start(bf16[64,1024]{1,0:T(8,128)(2,1)S(1)} %slice_bitcast_fusion.6), channel_id=1, source_target_pairs={{0,8},{4,12},{8,0},{12,4},{16,24},{20,28},{24,16},{28,20},{1,9},{5... | collective-permute-start | bytes 393224 | tf_op jit(solution)/shard_map/ppermute | solution.py:822
  603.9 23.4 %collective-permute-start.82 = (bf16[2,64,1024]{2,1,0:T(8,128)(2,1)S(1)}, bf16[2,64,1024]{2,1,0:T(8,128)(2,1)S(1)}, u32[]{:S(2)}, u32[]{:S(2)}) collective-permute-start(bf16[2,64,1024]{2,1,0:T(8,128)(2,1)S(1)} %slice.412), channel_id=1, source_target_pairs={{0,16},{4,20},{8,24},{12,28},{16,0},{20,4},{24,8},{28,12},{1,17},{... | collective-permute-start | bytes 786440 | tf_op jit(solution)/shard_map/ppermute | solution.py:822
  626.1 15.3 %collective-permute-start.97 = (bf16[2,28,2432]{2,1,0:T(8,128)(2,1)S(1)}, bf16[2,28,2432]{2,1,0:T(8,128)(2,1)S(1)}, u32[]{:S(2)}, u32[]{:S(2)}) collective-permute-start(bf16[2,28,2432]{2,1,0:T(8,128)(2,1)S(1)} %get-tuple-element.414), channel_id=1, source_target_pairs={{0,3},{1,2},{2,1},{3,0},{4,7},{5,6},{6,5},{7,4},{8,11},{9,10},{10,... | collective-permute-start | bytes 817160 | tf_op jit(solution)/shard_map/ppermute | solution.py:822
  627.4 19.1 %collective-permute-start.84 = (bf16[64,1024]{1,0:T(8,128)(2,1)S(1)}, bf16[64,1024]{1,0:T(8,128)(2,1)S(1)}, u32[]{:S(2)}, u32[]{:S(2)}) collective-permute-start(bf16[64,1024]{1,0:T(8,128)(2,1)S(1)} %slice_bitcast_fusion.8), channel_id=1, source_target_pairs={{0,8},{4,12},{8,0},{12,4},{16,24},{20,28},{24,16},{28,20},{1,9},{5... | collective-permute-start | bytes 393224 | tf_op jit(solution)/shard_map/ppermute | solution.py:822
  (154 other events, 1553.0 us)

commit v8 on v7

--- a/solution.py
+++ b/solution.py
@@ -1007,24 +1007,24 @@
             queries, kv_blocks, biases, x, second_full, after(mlp_gain_full, *waited)
         )
         if layer + 1 == LAYERS:
-            far.append(outward(after(crossed[1], kept_state[0][7][0]), own_kv))
+            far.append(outward(after(crossed[1], kept_state[0][7][1]), own_kv))
             far_pair = swap(far[1], "dp", 1)
             n2_parts = group_rows(n2, far_pair)
         else:
             far.append(outward(crossed[0], n2))
             far_pair = swap(far[0], "dp", 1)
             n2_parts = group_rows(after(n2, far[0]))
-            second_start = line_gather(after(shards[1], n2_parts[2]), bits[:1])
+            second_start = line_gather(after(shards[1], far_pair), bits[:1])
             second_line = line_gather(second_start, bits[1:])
             second_other = swap(after(second_line, n2_parts[3]), "dp", 1)
-            near.append(line_gather(after(gate_shards[1], second_start), bits[:-1], n2_parts[3]))
+            near.append(line_gather(after(gate_shards[1], far[0]), bits[:-1], n2_parts[3]))
             crossed.append(cross_middle(after(near[1], second_line)))
             attn_sets.append(attn_finish(attn_parts(second_line, second_other, n2_parts[3])))
             near_pair.append(swap(after(near[1], far_pair), "dp", 1))
         mlp_sets.append(mlp_finish(layer, far_pair))
         gu_near, *outs_near = feed_forward(n2_parts[:2], *mlp_sets[layer])
         if layer == 0:
-            n2_parts[2] = after(n2_parts[2], crossed[1], gu_near)
+            n2_parts[2] = after(n2_parts[2], gu_near)
         else:
             low_parts = group_rows(
                 after(cotangent.reshape(tok_len, model_width), n2_parts[3]), gu_near

time: 658 us -> 666 us (1.012)
  starting transfers between devices: 125 us -> 147 us
  waiting for transfers between devices: 242 us -> 230 us
    ppermute x88, starting transfers between devices: 103 us -> 125 us  [swap(): return lax.ppermute(values, axis, [(i, i ^ bit) for i in range(size)])]
    ppermute x88, waiting for transfers between devices: 209 us -> 201 us  [swap(): return lax.ppermute(values, axis, [(i, i ^ bit) for i in range(size)])]
  transfers between devices with their start and end apart: 98 -> 98, of which waited for: 39 -> 38; matrix products, arithmetic and copies ran while one was open for 8% -> 7% of each run, Pallas kernels for 23% -> 23%
where the time goes in v8:
time: 666 us; the launch traced here: 660 us
  waiting for transfers between devices  230 us (35%)
  Pallas kernels  183 us (27%)
  starting transfers between devices  147 us (22%)
  local copies, waits for them, and re-layouts  55.1 us (8%)
  other arithmetic  29 us (4%)
  between operations  15.9 us (2%)
    ppermute x88, waiting for transfers between devices, swap(): return lax.ppermute(values, axis, [(i, i ^ bit) for i in range(size)])  201 us
    ppermute x88, starting transfers between devices, swap(): return lax.ppermute(values, axis, [(i, i ^ bit) for i in range(size)])  125 us
    pallas_call x2, Pallas kernels, feed_back(): call(kernel, [((half, packed, 2 * units), jnp.bfloat16), ((half, packed,...  65.7 us
    pallas_call x4, Pallas kernels, feed_forward(): call(kernel, [((rows, 2 * units), jnp.bfloat16)] + [((part_rows, D), jnp....  40.9 us
    unnamed x214, local copies, waits for them, and re-layouts  34.1 us
    ppermute x10, waiting for transfers between devices, line_steps(): lax.ppermute(values, 'dp', [(2 * here + side, 2 * there + side) for here,...  28.2 us
    pallas_call x2, Pallas kernels, attention_back(): call(kernel, [((rows, D), jnp.float32), ((rows, D), jnp.bfloat16), ((1, D...  25.1 us
    ppermute x10, starting transfers between devices, line_steps(): lax.ppermute(values, 'dp', [(2 * here + side, 2 * there + side) for here,...  22.7 us
  transfers between devices with their start and end apart: 98, of which 38 were waited for; matrix products, arithmetic and copies ran while one was open for 7% of the time, Pallas kernels for 23%

profile of v8, /device:TPU:0, one launch (start us, length us, event | category | flops | bytes accessed | tf_op | source)
XLA Modules:
  0.0 660.0 jit_solution(16825537941428563254)
XLA Ops:
  9.6 2.8 collective-permute-start.1
  16.6 2.8 collective-permute-start.2
  19.4 3.4 collective-permute-done.4.refs_2_
  22.8 5.4 collective-permute-done.5.refs_3_
  32.9 11.4 %collective-permute-done.6.refs_1_ = bf16[4,64,1024]{2,1,0:T(8,128)(2,1)S(1)} collective-permute-done((bf16[4,64,1024]{2,1,0:T(8,128)(2,1)S(1)}, bf16[4,64,1024]{2,1,0:T(8,128)(2,1)S(1)}, u32[]{:S(2)}, u32[]{:S(2)}) %collective-permute-start.6) | collective-permute-done | bytes 524320 | tf_op jit(solution)/shard_map/ppermute | solution.py:822
  48.4 10.3 %collective-permute-done.8.refs_3_ = bf16[4,64,1024]{2,1,0:T(8,128)(2,1)S(1)} collective-permute-done((bf16[4,64,1024]{2,1,0:T(8,128)(2,1)S(1)}, bf16[4,64,1024]{2,1,0:T(8,128)(2,1)S(1)}, u32[]{:S(2)}, u32[]{:S(2)}) %collective-permute-start.8) | collective-permute-done | bytes 524320 | tf_op jit(solution)/shard_map/ppermute | solution.py:822
  58.6 4.8 collective-permute-done.13
  74.7 8.8 %collective-permute-done.7.refs_2_ = bf16[4,64,1024]{2,1,0:T(8,128)(2,1)S(1)} collective-permute-done((bf16[4,64,1024]{2,1,0:T(8,128)(2,1)S(1)}, bf16[4,64,1024]{2,1,0:T(8,128)(2,1)S(1)}, u32[]{:S(2)}, u32[]{:S(2)}) %collective-permute-start.7) | collective-permute-done | bytes 524320 | tf_op jit(solution)/shard_map/ppermute | solution.py:822
  98.8 3.0 assemble.2
  116.5 11.7 %attention.2 = (bf16[256,896]{1,0:T(8,128)(2,1)S(1)}, f32[256,896]{1,0:T(8,128)S(1)}, bf16[256,896]{1,0:T(8,128)(2,1)}) custom-call(bf16[2,2,896,64]{3,2,1,0:T(8,128)(2,1)S(1)} %get-tuple-element.279.q_ref.refs_7_, bf16[256,256]{1,0:T(8,128)(2,1)} %get-tuple-element.280.kv0.refs_8_, bf16[256,256]{1,0:T(8,128)(2,1)S(1)} %copy-done.41, ...), custom_call_target="tpu_custom_call" | custom-call | bytes 42000 | tf_op jit(solution)/shard_map/attention/pallas_call | solution.py:159
  128.3 12.0 %collective-permute-done.19 = bf16[2,168,2432]{2,1,0:T(8,128)(2,1)} collective-permute-done((bf16[2,168,2432]{2,1,0:T(8,128)(2,1)}, bf16[2,168,2432]{2,1,0:T(8,128)(2,1)}, u32[]{:S(2)}, u32[]{:S(2)}) %collective-permute-start.19) | collective-permute-done | bytes 1634336 | tf_op jit(solution)/shard_map/ppermute | solution.py:843
  145.9 24.8 %collective-permute-start.37 = (bf16[1,168,2432]{2,1,0:T(8,128)(2,1)}, bf16[1,168,2432]{2,1,0:T(8,128)(2,1)}, u32[]{:S(2)}, u32[]{:S(2)}) collective-permute-start(bf16[1,168,2432]{2,1,0:T(8,128)(2,1)} %copy-done.38), channel_id=1, source_target_pairs={{0,8},{4,12},{8,0},{12,4},{16,24},{20,28},{24,16},{28,20},{1,9},{5... | collective-permute-start | bytes 2451464 | tf_op jit(solution)/shard_map/ppermute | solution.py:822
  181.9 23.1 %collective-permute-start.28 = (bf16[1,64,1024]{2,1,0:T(8,128)(2,1)S(1)}, bf16[1,64,1024]{2,1,0:T(8,128)(2,1)S(1)}, u32[]{:S(2)}, u32[]{:S(2)}) collective-permute-start(bf16[1,64,1024]{2,1,0:T(8,128)(2,1)S(1)} %maximum_bitcast_fusion.1), channel_id=1, source_target_pairs={{0,8},{4,12},{8,0},{12,4},{16,24},{20,28},{24,16},{28,20},{1,9},{5... | collective-permute-start | bytes 393224 | tf_op jit(solution)/shard_map/ppermute | solution.py:822
  208.2 2.8 collective-permute-start.29
  213.1 8.8 %collective-permute-done.29 = bf16[2,64,1024]{2,1,0:T(8,128)(2,1)S(1)} collective-permute-done((bf16[2,64,1024]{2,1,0:T(8,128)(2,1)S(1)}, bf16[2,64,1024]{2,1,0:T(8,128)(2,1)S(1)}, u32[]{:S(2)}, u32[]{:S(2)}) %collective-permute-start.29) | collective-permute-done | bytes 262176 | tf_op jit(solution)/shard_map/ppermute | solution.py:822
  228.1 2.9 unpack.2
  234.3 10.2 %feed_forward.4 = (bf16[512,2432]{1,0:T(8,128)(2,1)}, bf16[256,896]{1,0:T(8,128)(2,1)}, bf16[256,896]{1,0:T(8,128)(2,1)}) custom-call(bf16[256,896]{1,0:T(8,128)(2,1)} %get-tuple-element.287.refs_0_.refs_5_, bf16[256,896]{1,0:T(8,128)(2,1)} %collective-permute-done.20.refs_1_.refs_6_, bf16[896,2432]{1,0:T(8,128)(2,1)} %bitcast.146, bf16[1216,896]{1,0:T(8,128)(2,1)} %bitcast.160), custom_call_target="tpu_custom_call" | custom-call | bytes 36000 | tf_op jit(solution)/shard_map/feed_forward/pallas_call | solution.py:204
  244.5 10.3 %feed_forward.5 = (bf16[512,2432]{1,0:T(8,128)(2,1)}, bf16[256,896]{1,0:T(8,128)(2,1)}, bf16[256,896]{1,0:T(8,128)(2,1)}) custom-call(bf16[256,896]{1,0:T(8,128)(2,1)} %collective-permute-done.23.refs_0_.refs_7_, bf16[256,896]{1,0:T(8,128)(2,1)} %collective-permute-done.24.refs_1_.refs_8_, bf16[896,2432]{1,0:T(8,128)(2,1)} %bitcast.147, ...), custom_call_target="tpu_custom_call" | custom-call | bytes 36000 | tf_op jit(solution)/shard_map/feed_forward/pallas_call | solution.py:204
  259.3 10.8 %collective-permute-done.32.refs_3_ = bf16[4,64,1024]{2,1,0:T(8,128)(2,1)S(1)} collective-permute-done((bf16[4,64,1024]{2,1,0:T(8,128)(2,1)}, bf16[4,64,1024]{2,1,0:T(8,128)(2,1)S(1)}, u32[]{:S(2)}, u32[]{:S(2)}) %collective-permute-start.32) | collective-permute-done | bytes 524320 | tf_op jit(solution)/shard_map/ppermute | solution.py:822
  273.7 3.0 assemble.3
  276.7 8.7 %collective-permute-done.26.refs_3_ = bf16[256,896]{1,0:T(8,128)(2,1)S(1)} collective-permute-done((bf16[256,896]{1,0:T(8,128)(2,1)S(1)}, bf16[256,896]{1,0:T(8,128)(2,1)S(1)}, u32[]{:S(2)}, u32[]{:S(2)}) %collective-permute-start.26) | collective-permute-done | bytes 458784 | tf_op jit(solution)/shard_map/ppermute | solution.py:822
  288.0 9.0 %collective-permute-done.44 = bf16[2,168,2432]{2,1,0:T(8,128)(2,1)S(1)} collective-permute-done((bf16[2,168,2432]{2,1,0:T(8,128)(2,1)}, bf16[2,168,2432]{2,1,0:T(8,128)(2,1)S(1)}, u32[]{:S(2)}, u32[]{:S(2)}) %collective-permute-start.44) | collective-permute-done | bytes 1634336 | tf_op jit(solution)/shard_map/ppermute | solution.py:843
  300.7 4.4 collective-permute-done.40.kv2.refs_10_
  307.2 9.9 %attention.3 = (bf16[256,896]{1,0:T(8,128)(2,1)S(1)}, f32[256,896]{1,0:T(8,128)S(1)}, bf16[256,896]{1,0:T(8,128)(2,1)S(1)}) custom-call(bf16[2,2,896,64]{3,2,1,0:T(8,128)(2,1)S(1)} %get-tuple-element.310.q_ref.refs_7_, bf16[256,256]{1,0:T(8,128)(2,1)S(1)} %get-tuple-element.311.kv0.refs_8_, bf16[256,256]{1,0:T(8,128)(2,1)S(1)} %collective-permute-done.39.kv1.refs_9_, ...), custom_call_target="tpu_custom_call" | custom-call | bytes 42000 | tf_op jit(solution)/shard_map/attention/pallas_call | solution.py:159
  320.5 11.2 %collective-permute-done.47.refs_0_.refs_7_ = bf16[256,896]{1,0:T(8,128)(2,1)S(1)} collective-permute-done((bf16[256,896]{1,0:T(8,128)(2,1)S(1)}, bf16[256,896]{1,0:T(8,128)(2,1)S(1)}, u32[]{:S(2)}, u32[]{:S(2)}) %collective-permute-start.47) | collective-permute-done | bytes 458784 | tf_op jit(solution)/shard_map/ppermute | solution.py:822
  343.5 10.2 %feed_forward.6 = (bf16[512,2432]{1,0:T(8,128)(2,1)}, bf16[256,896]{1,0:T(8,128)(2,1)}, bf16[256,896]{1,0:T(8,128)(2,1)}) custom-call(bf16[256,896]{1,0:T(8,128)(2,1)} %copy-done.31, bf16[256,896]{1,0:T(8,128)(2,1)} %copy-done.75, bf16[896,2432]{1,0:T(8,128)(2,1)} %bitcast.149, bf16[1216,896]{1,0:T(8,128)(2,1)} %bitcast.163), custom_call_target="tpu_custom_call" | custom-call | bytes 36000 | tf_op jit(solution)/shard_map/feed_forward/pallas_call | solution.py:204
  354.2 10.2 %feed_forward.7 = (bf16[512,2432]{1,0:T(8,128)(2,1)}, bf16[256,896]{1,0:T(8,128)(2,1)}, bf16[256,896]{1,0:T(8,128)(2,1)}) custom-call(bf16[256,896]{1,0:T(8,128)(2,1)} %copy-done.73, bf16[256,896]{1,0:T(8,128)(2,1)} %copy-done.74, bf16[896,2432]{1,0:T(8,128)(2,1)} %bitcast.150, bf16[1216,896]{1,0:T(8,128)(2,1)} %bitcast.164), custom_call_target="tpu_custom_call" | custom-call | bytes 36000 | tf_op jit(solution)/shard_map/feed_forward/pallas_call | solution.py:204
  365.3 33.0 %feed_back.2 = (bf16[2,168,2432]{2,1,0:T(8,128)(2,1)}, bf16[2,168,2432]{2,1,0:T(8,128)(2,1)}, bf16[256,896]{1,0:T(8,128)(2,1)}, bf16[256,896]{1,0:T(8,128)(2,1)}...) custom-call(s32[1]{0:T(128)} %bitcast.3.refs_0_, ...), custom_call_target="tpu_custom_call" | custom-call | bytes 100000 | tf_op jit(solution)/shard_map/feed_back/pallas_call | solution.py:324
  402.4 12.4 %collective-permute-done.54.refs_5_ = bf16[256,896]{1,0:T(8,128)(2,1)S(1)} collective-permute-done((bf16[256,896]{1,0:T(8,128)(2,1)S(1)}, bf16[256,896]{1,0:T(8,128)(2,1)S(1)}, u32[]{:S(2)}, u32[]{:S(2)}) %collective-permute-start.54) | collective-permute-done | bytes 458784 | tf_op jit(solution)/shard_map/ppermute | solution.py:822
  418.2 12.1 %attention_back.2 = (f32[256,896]{1,0:T(8,128)S(1)}, bf16[256,896]{1,0:T(8,128)(2,1)S(1)}, f32[1,896]{1,0:T(1,128)S(1)}, bf16[256,896]{1,0:T(8,128)(2,1)S(1)}, f...) custom-call(bf16[256,896]{1,0:T(8,128)(2,1)S(1)} %bitcast.173, ...), custom_call_target="tpu_custom_call" | custom-call | bytes 52000 | tf_op jit(solution)/shard_map/attention_back/pallas_call | solution.py:465
  432.6 4.5 collective-permute-done.56.refs_2_
  445.6 8.4 %collective-permute-done.58.refs_3_ = bf16[256,896]{1,0:T(8,128)(2,1)S(1)} collective-permute-done((bf16[256,896]{1,0:T(8,128)(2,1)S(1)}, bf16[256,896]{1,0:T(8,128)(2,1)S(1)}, u32[]{:S(2)}, u32[]{:S(2)}) %collective-permute-start.58) | collective-permute-done | bytes 458784 | tf_op jit(solution)/shard_map/ppermute | solution.py:822
  455.6 4.4 collective-permute-start.68
  467.1 32.7 %feed_back.3 = (bf16[2,168,2432]{2,1,0:T(8,128)(2,1)}, bf16[2,168,2432]{2,1,0:T(8,128)(2,1)}, bf16[256,896]{1,0:T(8,128)(2,1)}, bf16[256,896]{1,0:T(8,128)(2,1)}...) custom-call(s32[1]{0:T(128)} %bitcast.3.refs_0_, ...), custom_call_target="tpu_custom_call" | custom-call | bytes 100000 | tf_op jit(solution)/shard_map/feed_back/pallas_call | solution.py:324
  510.0 11.2 %collective-permute-done.71 = bf16[1,168,2432]{2,1,0:T(8,128)(2,1)S(1)} collective-permute-done((bf16[1,168,2432]{2,1,0:T(8,128)(2,1)}, bf16[1,168,2432]{2,1,0:T(8,128)(2,1)S(1)}, u32[]{:S(2)}, u32[]{:S(2)}) %collective-permute-start.71) | collective-permute-done | bytes 817184 | tf_op jit(solution)/shard_map/ppermute | solution.py:822
  524.3 13.1 %attention_back.3 = (f32[256,896]{1,0:T(8,128)S(1)}, bf16[256,896]{1,0:T(8,128)(2,1)S(1)}, f32[1,896]{1,0:T(1,128)S(1)}, bf16[256,896]{1,0:T(8,128)(2,1)S(1)}, f...) custom-call(f32[256,896]{1,0:T(8,128)S(1)} %copy-done.37, ...), custom_call_target="tpu_custom_call" | custom-call | bytes 52000 | tf_op jit(solution)/shard_map/attention_back/pallas_call | solution.py:465
  540.6 7.5 %collective-permute-start.86 = (bf16[1,168,2432]{2,1,0:T(8,128)(2,1)S(1)}, bf16[1,168,2432]{2,1,0:T(8,128)(2,1)S(1)}, u32[]{:S(2)}, u32[]{:S(2)}) collective-permute-start(bf16[1,168,2432]{2,1,0:T(8,128)(2,1)S(1)} %add_convert_fusion.7), channel_id=1, source_target_pairs={{0,8},{4,12},{24,16},{28,20},{1,9},{5,13},{25,17},{29,21},{2,10},{... | collective-permute-start | bytes 2451464 | tf_op jit(solution)/shard_map/ppermute | solution.py:843
  557.3 7.1 %collective-permute-done.86 = bf16[1,168,2432]{2,1,0:T(8,128)(2,1)S(1)} collective-permute-done((bf16[1,168,2432]{2,1,0:T(8,128)(2,1)S(1)}, bf16[1,168,2432]{2,1,0:T(8,128)(2,1)S(1)}, u32[]{:S(2)}, u32[]{:S(2)}) %collective-permute-start.86) | collective-permute-done | bytes 817184 | tf_op jit(solution)/shard_map/ppermute | solution.py:843
  568.8 11.4 %collective-permute-done.79 = bf16[4,64,1024]{2,1,0:T(8,128)(2,1)S(1)} collective-permute-done((bf16[4,64,1024]{2,1,0:T(8,128)(2,1)S(1)}, bf16[4,64,1024]{2,1,0:T(8,128)(2,1)S(1)}, u32[]{:S(2)}, u32[]{:S(2)}) %collective-permute-start.79) | collective-permute-done | bytes 524320 | tf_op jit(solution)/shard_map/ppermute | solution.py:822
  580.2 4.0 collective-permute-start.90
  585.4 3.2 collective-permute-done.80
  591.5 5.5 collective-permute-start.88
  597.0 11.5 %collective-permute-done.92 = bf16[2,64,1024]{2,1,0:T(8,128)(2,1)S(1)} collective-permute-done((bf16[2,64,1024]{2,1,0:T(8,128)(2,1)S(1)}, bf16[2,64,1024]{2,1,0:T(8,128)(2,1)S(1)}, u32[]{:S(2)}, u32[]{:S(2)}) %collective-permute-start.92) | collective-permute-done | bytes 262176 | tf_op jit(solution)/shard_map/ppermute | solution.py:822
  608.6 3.4 collective-permute-start.93
  614.6 17.5 %collective-permute-done.88.refs_1_ = bf16[168,2432]{1,0:T(8,128)(2,1)S(1)} collective-permute-done((bf16[168,2432]{1,0:T(8,128)(2,1)S(1)}, bf16[168,2432]{1,0:T(8,128)(2,1)S(1)}, u32[]{:S(2)}, u32[]{:S(2)}) %collective-permute-start.88) | collective-permute-done | bytes 817184 | tf_op jit(solution)/shard_map/ppermute | solution.py:822
  636.3 7.8 %collective-permute-done.96.refs_2_ = bf16[2,28,2432]{2,1,0:T(8,128)(2,1)S(1)} collective-permute-done((bf16[2,28,2432]{2,1,0:T(8,128)(2,1)S(1)}, bf16[2,28,2432]{2,1,0:T(8,128)(2,1)S(1)}, u32[]{:S(2)}, u32[]{:S(2)}) %collective-permute-start.96) | collective-permute-done | bytes 272416 | tf_op jit(solution)/shard_map/ppermute | solution.py:822
  644.1 5.9 collective-permute-done.97.refs_3_
  652.0 3.0 copy.58
  (504 shorter events, 187.7 us)
Async XLA Ops:
  14.1 14.1 %collective-permute-start.5 = (bf16[2,28,2432]{2,1,0:T(8,128)(2,1)S(1)}, bf16[2,28,2432]{2,1,0:T(8,128)(2,1)S(1)}, u32[]{:S(2)}, u32[]{:S(2)}) collective-permute-start(bf16[2,28,2432]{2,1,0:T(8,128)(2,1)S(1)} %get-tuple-element.264), channel_id=1, source_target_pairs={{0,3},{1,2},{2,1},{3,0},{4,7},{5,6},{6,5},{7,4},{8,11},{9,10},{10,... | collective-permute-start | bytes 817160 | tf_op jit(solution)/shard_map/ppermute | solution.py:822
  16.6 14.7 %collective-permute-start.2 = (bf16[2,64,1024]{2,1,0:T(8,128)(2,1)S(1)}, bf16[2,64,1024]{2,1,0:T(8,128)(2,1)S(1)}, u32[]{:S(2)}, u32[]{:S(2)}) collective-permute-start(bf16[2,64,1024]{2,1,0:T(8,128)(2,1)S(1)} %pad_maximum_fusion.6), channel_id=1, source_target_pairs={{0,16},{4,20},{8,24},{12,28},{16,0},{20,4},{24,8},{28,12},{1,17},{... | collective-permute-start | bytes 786440 | tf_op jit(solution)/shard_map/ppermute | solution.py:822
  44.3 19.1 %collective-permute-start.13 = (bf16[1,168,2432]{2,1,0:T(8,128)(2,1)S(1)}, bf16[1,168,2432]{2,1,0:T(8,128)(2,1)S(1)}, u32[]{:S(2)}, u32[]{:S(2)}) collective-permute-start(bf16[1,168,2432]{2,1,0:T(8,128)(2,1)S(1)} %get-tuple-element.274), channel_id=1, source_target_pairs={{0,8},{4,12},{8,0},{12,4},{16,24},{20,28},{24,16},{28,20},{1,9},{5... | collective-permute-start | bytes 2451464 | tf_op jit(solution)/shard_map/ppermute | solution.py:822
  68.2 41.0 %collective-permute-start.17 = (bf16[2,168,2432]{2,1,0:T(8,128)(2,1)}, bf16[2,168,2432]{2,1,0:T(8,128)(2,1)}, u32[]{:S(2)}, u32[]{:S(2)}) collective-permute-start(bf16[2,168,2432]{2,1,0:T(8,128)(2,1)} %constant_dynamic-update-slice_fusion.refs_0_), channel_id=1, source_target_pairs={{0,4},{4,0},{8,12},{12,8},{16,20},{20,16},{24,28},{28,24},{1,5},{5... | collective-permute-start | bytes 4902920 | tf_op jit(solution)/shard_map/ppermute | solution.py:822
  69.8 70.5 %collective-permute-start.19 = (bf16[2,168,2432]{2,1,0:T(8,128)(2,1)}, bf16[2,168,2432]{2,1,0:T(8,128)(2,1)}, u32[]{:S(2)}, u32[]{:S(2)}) collective-permute-start(bf16[2,168,2432]{2,1,0:T(8,128)(2,1)} %collective-permute-done.18), channel_id=1, source_target_pairs={{8,0},{12,4},{16,24},{20,28},{9,1},{13,5},{17,25},{21,29},{10,2},{... | collective-permute-start | bytes 4902920 | tf_op jit(solution)/shard_map/ppermute | solution.py:843
  74.1 21.5 %collective-permute-start.10 = (bf16[4,64,1024]{2,1,0:T(8,128)(2,1)S(1)}, bf16[4,64,1024]{2,1,0:T(8,128)(2,1)}, u32[]{:S(2)}, u32[]{:S(2)}) collective-permute-start(bf16[4,64,1024]{2,1,0:T(8,128)(2,1)S(1)} %collective-permute-done.6.refs_1_), channel_id=1, source_target_pairs={{0,1},{1,0},{2,3},{3,2},{4,5},{5,4},{6,7},{7,6},{8,9},{9,8},{10,11... | collective-permute-start | bytes 1572872 | tf_op jit(solution)/shard_map/ppermute | solution.py:822
  142.0 39.9 %collective-permute-start.21 = (bf16[2,168,2432]{2,1,0:T(8,128)(2,1)S(1)}, bf16[2,168,2432]{2,1,0:T(8,128)(2,1)}, u32[]{:S(2)}, u32[]{:S(2)}) collective-permute-start(bf16[2,168,2432]{2,1,0:T(8,128)(2,1)S(1)} %broadcast_select_fusion.1.refs_1_), channel_id=1, source_target_pairs={{0,4},{4,0},{8,12},{12,8},{16,20},{20,16},{24,28},{28,24},{1,5},{5... | collective-permute-start | bytes 4902920 | tf_op jit(solution)/shard_map/ppermute | solution.py:822
  143.6 37.0 %collective-permute-start.23 = (bf16[256,896]{1,0:T(8,128)(2,1)}, bf16[256,896]{1,0:T(8,128)(2,1)}, u32[]{:S(2)}, u32[]{:S(2)}) collective-permute-start(bf16[256,896]{1,0:T(8,128)(2,1)} %get-tuple-element.287.refs_0_.refs_5_), channel_id=1, source_target_pairs={{0,2},{1,3},{2,0},{3,1},{4,6},{5,7},{6,4},{7,5},{8,10},{9,11},{10,... | collective-permute-start | bytes 1376264 | tf_op jit(solution)/shard_map/ppermute | solution.py:822
  145.7 31.7 %collective-permute-start.27 = (bf16[28,1024]{1,0:T(8,128)(2,1)}, bf16[28,1024]{1,0:T(8,128)(2,1)}, u32[]{:S(2)}, u32[]{:S(2)}) collective-permute-start(bf16[28,1024]{1,0:T(8,128)(2,1)} %get-tuple-element.461), channel_id=1, source_target_pairs={{0,1},{1,0},{2,3},{3,2},{4,5},{5,4},{6,7},{7,6},{8,9},{9,8},{10,11... | collective-permute-start | bytes 172040 | tf_op jit(solution)/shard_map/ppermute | solution.py:822
  145.9 61.1 %collective-permute-start.37 = (bf16[1,168,2432]{2,1,0:T(8,128)(2,1)}, bf16[1,168,2432]{2,1,0:T(8,128)(2,1)}, u32[]{:S(2)}, u32[]{:S(2)}) collective-permute-start(bf16[1,168,2432]{2,1,0:T(8,128)(2,1)} %copy-done.38), channel_id=1, source_target_pairs={{0,8},{4,12},{8,0},{12,4},{16,24},{20,28},{24,16},{28,20},{1,9},{5... | collective-permute-start | bytes 2451464 | tf_op jit(solution)/shard_map/ppermute | solution.py:822
  180.6 26.5 %collective-permute-start.24 = (bf16[256,896]{1,0:T(8,128)(2,1)}, bf16[256,896]{1,0:T(8,128)(2,1)}, u32[]{:S(2)}, u32[]{:S(2)}) collective-permute-start(bf16[256,896]{1,0:T(8,128)(2,1)} %collective-permute-done.23.refs_0_.refs_7_), channel_id=1, source_target_pairs={{0,1},{1,0},{2,3},{3,2},{4,5},{5,4},{6,7},{7,6},{8,9},{9,8},{10,11... | collective-permute-start | bytes 1376264 | tf_op jit(solution)/shard_map/ppermute | solution.py:822
  181.9 26.3 %collective-permute-start.28 = (bf16[1,64,1024]{2,1,0:T(8,128)(2,1)S(1)}, bf16[1,64,1024]{2,1,0:T(8,128)(2,1)S(1)}, u32[]{:S(2)}, u32[]{:S(2)}) collective-permute-start(bf16[1,64,1024]{2,1,0:T(8,128)(2,1)S(1)} %maximum_bitcast_fusion.1), channel_id=1, source_target_pairs={{0,8},{4,12},{8,0},{12,4},{16,24},{20,28},{24,16},{28,20},{1,9},{5... | collective-permute-start | bytes 393224 | tf_op jit(solution)/shard_map/ppermute | solution.py:822
  222.8 32.0 %collective-permute-start.43 = (bf16[2,168,2432]{2,1,0:T(8,128)(2,1)}, bf16[2,168,2432]{2,1,0:T(8,128)(2,1)}, u32[]{:S(2)}, u32[]{:S(2)}) collective-permute-start(bf16[2,168,2432]{2,1,0:T(8,128)(2,1)} %constant_dynamic-update-slice_fusion.2.refs_0_), channel_id=1, source_target_pairs={{8,16},{12,20},{16,8},{20,12},{9,17},{13,21},{17,9},{21,13},{10,18... | collective-permute-start | bytes 4902920 | tf_op jit(solution)/shard_map/ppermute | solution.py:843
  224.7 31.7 %collective-permute-start.30 = (bf16[4,64,1024]{2,1,0:T(8,128)(2,1)}, bf16[4,64,1024]{2,1,0:T(8,128)(2,1)}, u32[]{:S(2)}, u32[]{:S(2)}) collective-permute-start(bf16[4,64,1024]{2,1,0:T(8,128)(2,1)} %pad_maximum_fusion.2.refs_0_), channel_id=1, source_target_pairs={{0,4},{4,0},{8,12},{12,8},{16,20},{20,16},{24,28},{28,24},{1,5},{5... | collective-permute-start | bytes 1572872 | tf_op jit(solution)/shard_map/ppermute | solution.py:822
  226.2 31.0 %collective-permute-start.31 = (bf16[4,64,1024]{2,1,0:T(8,128)(2,1)}, bf16[4,64,1024]{2,1,0:T(8,128)(2,1)}, u32[]{:S(2)}, u32[]{:S(2)}) collective-permute-start(bf16[4,64,1024]{2,1,0:T(8,128)(2,1)} %pad_maximum_fusion.2.refs_0_), channel_id=1, source_target_pairs={{0,2},{1,3},{2,0},{3,1},{4,6},{5,7},{6,4},{7,5},{8,10},{9,11},{10,... | collective-permute-start | bytes 1572872 | tf_op jit(solution)/shard_map/ppermute | solution.py:822
  227.8 49.0 %collective-permute-start.38 = (bf16[2,168,2432]{2,1,0:T(8,128)(2,1)}, bf16[2,168,2432]{2,1,0:T(8,128)(2,1)}, u32[]{:S(2)}, u32[]{:S(2)}) collective-permute-start(bf16[2,168,2432]{2,1,0:T(8,128)(2,1)} %constant_dynamic-update-slice_fusion.2.refs_0_), channel_id=1, source_target_pairs={{0,4},{4,0},{8,12},{12,8},{16,20},{20,16},{24,28},{28,24},{1,5},{5... | collective-permute-start | bytes 4902920 | tf_op jit(solution)/shard_map/ppermute | solution.py:822
  254.8 42.1 %collective-permute-start.44 = (bf16[2,168,2432]{2,1,0:T(8,128)(2,1)}, bf16[2,168,2432]{2,1,0:T(8,128)(2,1)S(1)}, u32[]{:S(2)}, u32[]{:S(2)}) collective-permute-start(bf16[2,168,2432]{2,1,0:T(8,128)(2,1)} %collective-permute-done.43), channel_id=1, source_target_pairs={{8,0},{12,4},{16,24},{20,28},{9,1},{13,5},{17,25},{21,29},{10,2},{... | collective-permute-start | bytes 4902920 | tf_op jit(solution)/shard_map/ppermute | solution.py:843
  297.2 35.2 %collective-permute-start.45 = (bf16[2,168,2432]{2,1,0:T(8,128)(2,1)S(1)}, bf16[2,168,2432]{2,1,0:T(8,128)(2,1)S(1)}, u32[]{:S(2)}, u32[]{:S(2)}) collective-permute-start(bf16[2,168,2432]{2,1,0:T(8,128)(2,1)S(1)} %broadcast_select_fusion.refs_1_), channel_id=1, source_target_pairs={{0,4},{4,0},{8,12},{12,8},{16,20},{20,16},{24,28},{28,24},{1,5},{5... | collective-permute-start | bytes 4902920 | tf_op jit(solution)/shard_map/ppermute | solution.py:822
  335.0 18.7 %collective-permute-start.51 = (bf16[256,896]{1,0:T(8,128)(2,1)S(1)}, bf16[256,896]{1,0:T(8,128)(2,1)}, u32[]{:S(2)}, u32[]{:S(2)}) collective-permute-start(bf16[256,896]{1,0:T(8,128)(2,1)S(1)} %bitcast.171), channel_id=1, source_target_pairs={{0,2},{1,3},{2,0},{3,1},{4,6},{5,7},{6,4},{7,5},{8,10},{9,11},{10,... | collective-permute-start | bytes 1376264 | tf_op jit(solution)/shard_map/ppermute | solution.py:822
  398.5 47.1 %collective-permute-start.67 = (bf16[2,168,2432]{2,1,0:T(8,128)(2,1)}, bf16[2,168,2432]{2,1,0:T(8,128)(2,1)S(1)}, u32[]{:S(2)}, u32[]{:S(2)}) collective-permute-start(bf16[2,168,2432]{2,1,0:T(8,128)(2,1)} %get-tuple-element.361), channel_id=1, source_target_pairs={{0,4},{4,0},{8,12},{12,8},{16,20},{20,16},{24,28},{28,24},{1,5},{5... | collective-permute-start | bytes 4902920 | tf_op jit(solution)/shard_map/ppermute | solution.py:822
  441.6 18.4 %collective-permute-start.46 = (bf16[256,896]{1,0:T(8,128)(2,1)S(1)}, bf16[256,896]{1,0:T(8,128)(2,1)S(1)}, u32[]{:S(2)}, u32[]{:S(2)}) collective-permute-start(bf16[256,896]{1,0:T(8,128)(2,1)S(1)} %copy-done.102), channel_id=1, source_target_pairs={{0,1},{1,0},{2,3},{3,2},{4,5},{5,4},{6,7},{7,6},{8,9},{9,8},{10,11... | collective-permute-start | bytes 1376264 | tf_op jit(solution)/shard_map/ppermute | solution.py:822
  441.7 58.2 %collective-permute-start.66 = (bf16[2,168,2432]{2,1,0:T(8,128)(2,1)}, bf16[2,168,2432]{2,1,0:T(8,128)(2,1)}, u32[]{:S(2)}, u32[]{:S(2)}) collective-permute-start(bf16[2,168,2432]{2,1,0:T(8,128)(2,1)} %get-tuple-element.359), channel_id=1, source_target_pairs={{0,4},{4,0},{8,12},{12,8},{16,20},{20,16},{24,28},{28,24},{1,5},{5... | collective-permute-start | bytes 4902920 | tf_op jit(solution)/shard_map/ppermute | solution.py:822
  445.3 15.3 %collective-permute-start.62 = (bf16[2,4,64,1024]{3,2,1,0:T(8,128)(2,1)S(1)}, bf16[2,4,64,1024]{3,2,1,0:T(8,128)(2,1)S(1)}, u32[]{:S(2)}, u32[]{:S(2)}) collective-permute-start(bf16[2,4,64,1024]{3,2,1,0:T(8,128)(2,1)S(1)} %get-tuple-element.351), channel_id=1, source_target_pairs={{0,1},{1,0},{2,3},{3,2},{4,5},{5,4},{6,7},{7,6},{8,9},{9,8},{10,11... | collective-permute-start | bytes 3145736 | tf_op jit(solution)/shard_map/ppermute | solution.py:822
  455.6 44.2 %collective-permute-start.68 = (bf16[2,168,2432]{2,1,0:T(8,128)(2,1)}, bf16[2,168,2432]{2,1,0:T(8,128)(2,1)}, u32[]{:S(2)}, u32[]{:S(2)}) collective-permute-start(bf16[2,168,2432]{2,1,0:T(8,128)(2,1)} %add_convert_fusion.3), channel_id=1, source_target_pairs={{0,8},{4,12},{24,16},{28,20},{1,9},{5,13},{25,17},{29,21},{2,10},{... | collective-permute-start | bytes 4902920 | tf_op jit(solution)/shard_map/ppermute | solution.py:843
  463.3 36.5 %collective-permute-start.64 = (bf16[4,64,1024]{2,1,0:T(8,128)(2,1)}, bf16[4,64,1024]{2,1,0:T(8,128)(2,1)}, u32[]{:S(2)}, u32[]{:S(2)}) collective-permute-start(bf16[4,64,1024]{2,1,0:T(8,128)(2,1)} %get-tuple-element.356), channel_id=1, source_target_pairs={{0,2},{1,3},{2,0},{3,1},{4,6},{5,7},{6,4},{7,5},{8,10},{9,11},{10,... | collective-permute-start | bytes 1572872 | tf_op jit(solution)/shard_map/ppermute | solution.py:822
  464.0 35.9 %collective-permute-start.65 = (bf16[4,64,1024]{2,1,0:T(8,128)(2,1)}, bf16[4,64,1024]{2,1,0:T(8,128)(2,1)}, u32[]{:S(2)}, u32[]{:S(2)}) collective-permute-start(bf16[4,64,1024]{2,1,0:T(8,128)(2,1)} %get-tuple-element.357), channel_id=1, source_target_pairs={{0,2},{1,3},{2,0},{3,1},{4,6},{5,7},{6,4},{7,5},{8,10},{9,11},{10,... | collective-permute-start | bytes 1572872 | tf_op jit(solution)/shard_map/ppermute | solution.py:822
  466.5 33.3 %collective-permute-start.60 = (bf16[256,896]{1,0:T(8,128)(2,1)S(1)}, bf16[256,896]{1,0:T(8,128)(2,1)}, u32[]{:S(2)}, u32[]{:S(2)}) collective-permute-start(bf16[256,896]{1,0:T(8,128)(2,1)S(1)} %add_convert_fusion.19), channel_id=1, source_target_pairs={{0,2},{1,3},{2,0},{3,1},{4,6},{5,7},{6,4},{7,5},{8,10},{9,11},{10,... | collective-permute-start | bytes 1376264 | tf_op jit(solution)/shard_map/ppermute | solution.py:822
  500.0 21.3 %collective-permute-start.71 = (bf16[1,168,2432]{2,1,0:T(8,128)(2,1)}, bf16[1,168,2432]{2,1,0:T(8,128)(2,1)S(1)}, u32[]{:S(2)}, u32[]{:S(2)}) collective-permute-start(bf16[1,168,2432]{2,1,0:T(8,128)(2,1)} %get-tuple-element.368), channel_id=1, source_target_pairs={{0,4},{4,0},{8,12},{12,8},{16,20},{20,16},{24,28},{28,24},{1,5},{5... | collective-permute-start | bytes 2451464 | tf_op jit(solution)/shard_map/ppermute | solution.py:822
  504.4 16.9 %collective-permute-start.70 = (bf16[256,896]{1,0:T(8,128)(2,1)S(1)}, bf16[256,896]{1,0:T(8,128)(2,1)S(1)}, u32[]{:S(2)}, u32[]{:S(2)}) collective-permute-start(bf16[256,896]{1,0:T(8,128)(2,1)S(1)} %fusion.4), channel_id=1, source_target_pairs={{0,2},{1,3},{2,0},{3,1},{4,6},{5,7},{6,4},{7,5},{8,10},{9,11},{10,... | collective-permute-start | bytes 1376264 | tf_op jit(solution)/shard_map/ppermute | solution.py:822
  508.1 32.5 %collective-permute-start.89 = (bf16[2,168,2432]{2,1,0:T(8,128)(2,1)S(1)}, bf16[2,168,2432]{2,1,0:T(8,128)(2,1)S(1)}, u32[]{:S(2)}, u32[]{:S(2)}) collective-permute-start(bf16[2,168,2432]{2,1,0:T(8,128)(2,1)S(1)} %add_convert_fusion.1), channel_id=1, source_target_pairs={{8,16},{12,20},{16,8},{20,12},{9,17},{13,21},{17,9},{21,13},{10,18... | collective-permute-start | bytes 4902920 | tf_op jit(solution)/shard_map/ppermute | solution.py:843
  508.9 30.0 %collective-permute-start.85 = (bf16[1,168,2432]{2,1,0:T(8,128)(2,1)S(1)}, bf16[1,168,2432]{2,1,0:T(8,128)(2,1)S(1)}, u32[]{:S(2)}, u32[]{:S(2)}) collective-permute-start(bf16[1,168,2432]{2,1,0:T(8,128)(2,1)S(1)} %copy-done.100), channel_id=1, source_target_pairs={{0,4},{4,0},{8,12},{12,8},{16,20},{20,16},{24,28},{28,24},{1,5},{5... | collective-permute-start | bytes 2451464 | tf_op jit(solution)/shard_map/ppermute | solution.py:822
  521.6 26.5 %collective-permute-start.72 = (bf16[1,168,2432]{2,1,0:T(8,128)(2,1)S(1)}, bf16[1,168,2432]{2,1,0:T(8,128)(2,1)S(1)}, u32[]{:S(2)}, u32[]{:S(2)}) collective-permute-start(bf16[1,168,2432]{2,1,0:T(8,128)(2,1)S(1)} %add_convert_fusion.11), channel_id=1, source_target_pairs={{0,8},{4,12},{24,16},{28,20},{1,9},{5,13},{25,17},{29,21},{2,10},{... | collective-permute-start | bytes 2451464 | tf_op jit(solution)/shard_map/ppermute | solution.py:843
  538.9 27.0 %collective-permute-start.91 = (bf16[4,64,1024]{2,1,0:T(8,128)(2,1)S(1)}, bf16[4,64,1024]{2,1,0:T(8,128)(2,1)S(1)}, u32[]{:S(2)}, u32[]{:S(2)}) collective-permute-start(bf16[4,64,1024]{2,1,0:T(8,128)(2,1)S(1)} %fusion), channel_id=1, source_target_pairs={{0,4},{4,0},{8,12},{12,8},{16,20},{20,16},{24,28},{28,24},{1,5},{5... | collective-permute-start | bytes 1572872 | tf_op jit(solution)/shard_map/ppermute | solution.py:822
  540.6 23.8 %collective-permute-start.86 = (bf16[1,168,2432]{2,1,0:T(8,128)(2,1)S(1)}, bf16[1,168,2432]{2,1,0:T(8,128)(2,1)S(1)}, u32[]{:S(2)}, u32[]{:S(2)}) collective-permute-start(bf16[1,168,2432]{2,1,0:T(8,128)(2,1)S(1)} %add_convert_fusion.7), channel_id=1, source_target_pairs={{0,8},{4,12},{24,16},{28,20},{1,9},{5,13},{25,17},{29,21},{2,10},{... | collective-permute-start | bytes 2451464 | tf_op jit(solution)/shard_map/ppermute | solution.py:843
  550.4 38.1 %collective-permute-start.80 = (bf16[2,168,2432]{2,1,0:T(8,128)(2,1)S(1)}, bf16[2,168,2432]{2,1,0:T(8,128)(2,1)S(1)}, u32[]{:S(2)}, u32[]{:S(2)}) collective-permute-start(bf16[2,168,2432]{2,1,0:T(8,128)(2,1)S(1)} %copy-done.99), channel_id=1, source_target_pairs={{0,4},{4,0},{8,12},{12,8},{16,20},{20,16},{24,28},{28,24},{1,5},{5... | collective-permute-start | bytes 4902920 | tf_op jit(solution)/shard_map/ppermute | solution.py:822
  556.6 32.9 %collective-permute-start.83 = (bf16[1,168,2432]{2,1,0:T(8,128)(2,1)S(1)}, bf16[1,168,2432]{2,1,0:T(8,128)(2,1)S(1)}, u32[]{:S(2)}, u32[]{:S(2)}) collective-permute-start(bf16[1,168,2432]{2,1,0:T(8,128)(2,1)S(1)} %add_convert_fusion.9), channel_id=1, source_target_pairs={{8,16},{12,20},{16,8},{20,12},{9,17},{13,21},{17,9},{21,13},{10,18... | collective-permute-start | bytes 2451464 | tf_op jit(solution)/shard_map/ppermute | solution.py:843
  564.4 19.8 %collective-permute-start.76 = (bf16[2,4,64,1024]{3,2,1,0:T(8,128)(2,1)S(1)}, bf16[2,4,64,1024]{3,2,1,0:T(8,128)(2,1)S(1)}, u32[]{:S(2)}, u32[]{:S(2)}) collective-permute-start(bf16[2,4,64,1024]{3,2,1,0:T(8,128)(2,1)S(1)} %get-tuple-element.385), channel_id=1, source_target_pairs={{0,1},{1,0},{2,3},{3,2},{4,5},{5,4},{6,7},{7,6},{8,9},{9,8},{10,11... | collective-permute-start | bytes 3145736 | tf_op jit(solution)/shard_map/ppermute | solution.py:822
  564.6 26.2 %collective-permute-start.87 = (bf16[1,168,2432]{2,1,0:T(8,128)(2,1)S(1)}, bf16[1,168,2432]{2,1,0:T(8,128)(2,1)S(1)}, u32[]{:S(2)}, u32[]{:S(2)}) collective-permute-start(bf16[1,168,2432]{2,1,0:T(8,128)(2,1)S(1)} %add_convert_fusion.6), channel_id=1, source_target_pairs={{8,16},{12,20},{16,8},{20,12},{9,17},{13,21},{17,9},{21,13},{10,18... | collective-permute-start | bytes 2451464 | tf_op jit(solution)/shard_map/ppermute | solution.py:843
  565.8 14.4 %collective-permute-start.79 = (bf16[4,64,1024]{2,1,0:T(8,128)(2,1)S(1)}, bf16[4,64,1024]{2,1,0:T(8,128)(2,1)S(1)}, u32[]{:S(2)}, u32[]{:S(2)}) collective-permute-start(bf16[4,64,1024]{2,1,0:T(8,128)(2,1)S(1)} %get-tuple-element.449), channel_id=1, source_target_pairs={{0,2},{1,3},{2,0},{3,1},{4,6},{5,7},{6,4},{7,5},{8,10},{9,11},{10,... | collective-permute-start | bytes 1572872 | tf_op jit(solution)/shard_map/ppermute | solution.py:822
  580.2 34.3 %collective-permute-start.90 = (bf16[168,2432]{1,0:T(8,128)(2,1)S(1)}, bf16[168,2432]{1,0:T(8,128)(2,1)S(1)}, u32[]{:S(2)}, u32[]{:S(2)}) collective-permute-start(bf16[168,2432]{1,0:T(8,128)(2,1)S(1)} %get-tuple-element.452), channel_id=1, source_target_pairs={{0,8},{4,12},{8,0},{12,4},{16,24},{20,28},{24,16},{28,20},{1,9},{5... | collective-permute-start | bytes 2451464 | tf_op jit(solution)/shard_map/ppermute | solution.py:822
  584.2 24.3 %collective-permute-start.92 = (bf16[2,64,1024]{2,1,0:T(8,128)(2,1)S(1)}, bf16[2,64,1024]{2,1,0:T(8,128)(2,1)S(1)}, u32[]{:S(2)}, u32[]{:S(2)}) collective-permute-start(bf16[2,64,1024]{2,1,0:T(8,128)(2,1)S(1)} %slice.422), channel_id=1, source_target_pairs={{0,16},{4,20},{8,24},{12,28},{16,0},{20,4},{24,8},{28,12},{1,17},{... | collective-permute-start | bytes 786440 | tf_op jit(solution)/shard_map/ppermute | solution.py:822
  588.6 23.5 %collective-permute-start.78 = (bf16[4,64,1024]{2,1,0:T(8,128)(2,1)S(1)}, bf16[4,64,1024]{2,1,0:T(8,128)(2,1)S(1)}, u32[]{:S(2)}, u32[]{:S(2)}) collective-permute-start(bf16[4,64,1024]{2,1,0:T(8,128)(2,1)S(1)} %get-tuple-element.448), channel_id=1, source_target_pairs={{0,2},{1,3},{2,0},{3,1},{4,6},{5,7},{6,4},{7,5},{8,10},{9,11},{10,... | collective-permute-start | bytes 1572872 | tf_op jit(solution)/shard_map/ppermute | solution.py:822
  589.5 22.5 %collective-permute-start.81 = (bf16[4,64,1024]{2,1,0:T(8,128)(2,1)S(1)}, bf16[4,64,1024]{2,1,0:T(8,128)(2,1)S(1)}, u32[]{:S(2)}, u32[]{:S(2)}) collective-permute-start(bf16[4,64,1024]{2,1,0:T(8,128)(2,1)S(1)} %fusion.2), channel_id=1, source_target_pairs={{0,4},{4,0},{8,12},{12,8},{16,20},{20,16},{24,28},{28,24},{1,5},{5... | collective-permute-start | bytes 1572872 | tf_op jit(solution)/shard_map/ppermute | solution.py:822
  591.5 40.6 %collective-permute-start.88 = (bf16[168,2432]{1,0:T(8,128)(2,1)S(1)}, bf16[168,2432]{1,0:T(8,128)(2,1)S(1)}, u32[]{:S(2)}, u32[]{:S(2)}) collective-permute-start(bf16[168,2432]{1,0:T(8,128)(2,1)S(1)} %get-tuple-element.447), channel_id=1, source_target_pairs={{0,8},{4,12},{8,0},{12,4},{16,24},{20,28},{24,16},{28,20},{1,9},{5... | collective-permute-start | bytes 2451464 | tf_op jit(solution)/shard_map/ppermute | solution.py:822
  608.6 25.3 %collective-permute-start.93 = (bf16[64,1024]{1,0:T(8,128)(2,1)S(1)}, bf16[64,1024]{1,0:T(8,128)(2,1)S(1)}, u32[]{:S(2)}, u32[]{:S(2)}) collective-permute-start(bf16[64,1024]{1,0:T(8,128)(2,1)S(1)} %slice_bitcast_fusion.6), channel_id=1, source_target_pairs={{0,8},{4,12},{8,0},{12,4},{16,24},{20,28},{24,16},{28,20},{1,9},{5... | collective-permute-start | bytes 393224 | tf_op jit(solution)/shard_map/ppermute | solution.py:822
  612.4 23.4 %collective-permute-start.82 = (bf16[2,64,1024]{2,1,0:T(8,128)(2,1)S(1)}, bf16[2,64,1024]{2,1,0:T(8,128)(2,1)S(1)}, u32[]{:S(2)}, u32[]{:S(2)}) collective-permute-start(bf16[2,64,1024]{2,1,0:T(8,128)(2,1)S(1)} %slice.412), channel_id=1, source_target_pairs={{0,16},{4,20},{8,24},{12,28},{16,0},{20,4},{24,8},{28,12},{1,17},{... | collective-permute-start | bytes 786440 | tf_op jit(solution)/shard_map/ppermute | solution.py:822
  634.7 15.3 %collective-permute-start.97 = (bf16[2,28,2432]{2,1,0:T(8,128)(2,1)S(1)}, bf16[2,28,2432]{2,1,0:T(8,128)(2,1)S(1)}, u32[]{:S(2)}, u32[]{:S(2)}) collective-permute-start(bf16[2,28,2432]{2,1,0:T(8,128)(2,1)S(1)} %get-tuple-element.414), channel_id=1, source_target_pairs={{0,3},{1,2},{2,1},{3,0},{4,7},{5,6},{6,5},{7,4},{8,11},{9,10},{10,... | collective-permute-start | bytes 817160 | tf_op jit(solution)/shard_map/ppermute | solution.py:822
  635.9 19.1 %collective-permute-start.84 = (bf16[64,1024]{1,0:T(8,128)(2,1)S(1)}, bf16[64,1024]{1,0:T(8,128)(2,1)S(1)}, u32[]{:S(2)}, u32[]{:S(2)}) collective-permute-start(bf16[64,1024]{1,0:T(8,128)(2,1)S(1)} %slice_bitcast_fusion.8), channel_id=1, source_target_pairs={{0,8},{4,12},{8,0},{12,4},{16,24},{20,28},{24,16},{28,20},{1,9},{5... | collective-permute-start | bytes 393224 | tf_op jit(solution)/shard_map/ppermute | solution.py:822
  (154 other events, 1539.5 us)
